TPU v7x, 512 devices: a whole 4x4x16 slice. The times are simulated.
512 devices in a mesh: blk: 16 (over z), uly: 8 (over x, core), dp: 4 (over y).
Axes of the slice: x: 4, y: 4, z: 16, core: 2. Of those that a mesh axis runs over, the one named last changes fastest.
Arguments:
- queries: bfloat16 [32768, 3072], P(('dp', 'blk', 'uly')), parts along dimension 0, may hold values from -6 to 6, as said below
- keys: bfloat16 [32768, 3072], P(('dp', 'blk', 'uly')), parts along dimension 0, may hold values from -6 to 6, as said below
- values: bfloat16 [32768, 3072], P(('dp', 'blk', 'uly')), parts along dimension 0, may hold values from -6 to 6
- tile_order: int32 [128], P('dp'), parts along dimension 0, may hold values from 0 to 31, as said below
- neighbors: int32 [128, 9], P('dp'), parts along dimension 0, may hold values from 0 to 31, as said below
Outputs:
- attended: bfloat16 [32768, 3072], P(('dp', 'blk', 'uly')), parts along dimension 0
There are 4 independent parts, one for each index of `dp`. A program takes and returns all parts, laid end to end along the dimension named above; each array names one. Nothing has to cross between parts.
Inputs may be any that keep to these rules, and one draw needn't show every extreme that they name: `queries`: of order one; a few tokens carry larger entries. `keys`: of order one; a few tokens carry larger entries. `tile_order`: A permutation of the tile ids. The slots k * 4 to (k + 1) * 4 - 1 hold all tiles of one tile column w, and w = (k + r) % 8 with r drawn from the seed; index b of blk stores slots b * 2 to (b + 1) * 2 - 1. `neighbors`: row s lists, without repeats, the slots of all tiles with any time index, height index ch - 1, ch, ch + 1 and width index cw - 1, cw, cw + 1, where ch and cw are the height and width indices of the tile in slot s clamped to 1 .. 2 and 1 .. 6. Every listed slot lies in a shard (slot // 2) within cyclic distance 5 of shard s // 2, and distance 5 occurs.
All inputs are finite; a program needn't handle non-finite values.
Results may differ from a plain program's by a relative error of at most 0.0096.
Values may be sent and summed in bfloat16 or wider, within the bound.
No kernel may reach another device: no remote copies, remote signals or barrier semaphores. Data moves between devices by JAX's collectives and lax.ppermute only.
A program may use at most 64 MiB of HBM per device.

v0:
```python
import jax
import jax.numpy as jnp
from jax import lax
from jax.sharding import PartitionSpec as P

HD = 128
TILE_T = 4
TILE_H = 8
TILE_W = 8
TT = 1
TH = 4
TW = 8
TOK_TILE = 256


def passed_along(block, axis, distance):
    devices = range(lax.axis_size(axis))
    route = [((i - distance) % len(devices), i) for i in devices]
    return lax.ppermute(block, axis, route)


def angle_tables(tokens, tile_order):
    slot = tokens // TOK_TILE
    local = tokens % TOK_TILE
    tile = jnp.take(tile_order, slot)
    frame = tile // (TH * TW) * TILE_T + local // (TILE_H * TILE_W)
    row = tile // TW % TH * TILE_H + local // TILE_W % TILE_H
    column = tile % TW * TILE_W + local % TILE_W
    dt = HD - 4 * (HD // 6)
    dhw = 2 * (HD // 6)
    freq_t = jnp.power(10000.0, -2.0 * jnp.arange(dt // 2, dtype=jnp.float32) / dt)
    freq_s = jnp.power(10000.0, -2.0 * jnp.arange(dhw // 2, dtype=jnp.float32) / dhw)
    angles = jnp.concatenate(
        [
            frame.astype(jnp.float32)[:, None] * freq_t[None, :],
            row.astype(jnp.float32)[:, None] * freq_s[None, :],
            column.astype(jnp.float32)[:, None] * freq_s[None, :],
        ],
        axis=1,
    )
    return (jnp.cos(angles), jnp.sin(angles))


def rotate(field, cosine, sine):
    rows = field.shape[0]
    pairs = field.astype(jnp.float32).reshape(rows, -1, HD // 2, 2)
    first = pairs[..., 0]
    second = pairs[..., 1]
    cosine = cosine[:, None, :]
    sine = sine[:, None, :]
    turned = jnp.stack([first * cosine - second * sine, first * sine + second * cosine], axis=-1)
    return turned.reshape(rows, -1).astype(jnp.bfloat16)


def shards(queries, keys, values, tile_order, neighbors):
    block = lax.axis_index("blk")
    lane = lax.axis_index("uly")
    lanes = lax.axis_size("uly")
    blocks = lax.axis_size("blk")
    rows = queries.shape[0]
    tokens = (block * lanes + lane) * rows + jnp.arange(rows, dtype=jnp.int32)
    cosine, sine = angle_tables(tokens, tile_order)
    q_rot = rotate(queries, cosine, sine)
    k_rot = rotate(keys, cosine, sine)
    q_local, k_local, v_local = (
        lax.all_to_all(q_rot, "uly", split_axis=1, concat_axis=0, tiled=True),
        lax.all_to_all(k_rot, "uly", split_axis=1, concat_axis=0, tiled=True),
        lax.all_to_all(values, "uly", split_axis=1, concat_axis=0, tiled=True),
    )
    shard_rows = q_local.shape[0]
    tiles_dev = shard_rows // TOK_TILE
    column_tiles = TT * TH
    reach = (2 * column_tiles + tiles_dev - 1) // tiles_dev + max(column_tiles // tiles_dev - 1, 0)
    width = q_local.shape[1]
    heads_here = width // HD
    stacked = jnp.stack([k_local, v_local])
    own_lists = lax.dynamic_slice_in_dim(neighbors, block * tiles_dev, tiles_dev, 0)
    earlier = []
    later = []
    for distance in range(1, reach + 1):
        earlier.append(passed_along(stacked, "blk", distance))
        later.append(passed_along(stacked, "blk", -distance))
    joined = jnp.concatenate(earlier[::-1] + [stacked] + later, axis=1)
    pool = joined.reshape(2, (2 * reach + 1) * tiles_dev, TOK_TILE, width)
    shard_of = own_lists // tiles_dev
    picks = (shard_of - block + reach) % blocks * tiles_dev + own_lists % tiles_dev
    scale = HD ** (-0.5)
    q_tiles = q_local.reshape(tiles_dev, TOK_TILE, heads_here, HD)

    def one_tile(item):
        q_tile, chosen = item
        gathered = jnp.take(pool, chosen, axis=1).reshape(2, -1, heads_here, HD)
        scores = (
            jnp.einsum("qhd,khd->hqk", q_tile, gathered[0], preferred_element_type=jnp.float32)
            * scale
        )
        top = jnp.max(scores, axis=-1, keepdims=True)
        weights = jnp.exp(scores - top)
        total = jnp.sum(weights, axis=-1)
        weights_bf = weights.astype(jnp.bfloat16)
        summed = jnp.einsum(
            "hqk,khd->qhd", weights_bf, gathered[1], preferred_element_type=jnp.float32
        )
        result = summed / jnp.transpose(total)[:, :, None]
        return result.reshape(TOK_TILE, width).astype(jnp.bfloat16)

    attended_local = lax.map(one_tile, (q_tiles, picks)).reshape(shard_rows, width)
    return lax.all_to_all(attended_local, "uly", split_axis=0, concat_axis=1, tiled=True)


def solution(mesh):
    placed = (
        P(("dp", "blk", "uly"), None),
        P(("dp", "blk", "uly"), None),
        P(("dp", "blk", "uly"), None),
        P("dp"),
        P("dp", None),
    )
    return jax.shard_map(
        shards, mesh=mesh, in_specs=placed, out_specs=P(("dp", "blk", "uly"), None), check_vma=False
    )
```

profile of v0, /device:TPU:32, one launch (start us, length us, event | category | flops | bytes accessed | tf_op | source)
XLA Modules:
  0.0 537.1 jit_solution(15556947079096841533)
XLA Ops:
  0.1 1.4 gather_fusion.1
  1.6 1.4 copy.33
  2.9 0.7 convert.18
  3.6 1.4 copy.36
  5.0 0.7 convert.19
  6.0 4.3 subtract_convert_fusion
  10.3 4.2 pad_maximum_fusion
  14.5 1.0 copy.34
  15.5 4.3 all-to-all-start
  19.9 8.9 %all-to-all-done = bf16[64,8,384]{2,0,1:T(8,128)(2,1)S(1)} async-done(((bf16[64,8,384]{2,0,1:T(8,128)(2,1)}), bf16[64,8,384]{2,0,1:T(8,128)(2,1)S(1)}, u32[]{:S(2)}, u32[]{:S(2)}) %all-to-all-start) | async-done | bytes 393248 | tf_op jit(solution)/shard_map/all_to_all | solution.py:67
  28.8 11.3 %all_to_all.61 = bf16[64,8,384]{2,0,1:T(8,128)(2,1)S(1)} all-to-all(bf16[64,8,384]{2,0,1:T(8,128)(2,1)S(1)} %bitcast.80), channel_id=1, replica_groups=mesh['blk'=16,'uly'=8,'dp'=4] {'uly'}, dimensions={1} | all-to-all | bytes 786432 | tf_op jit(solution)/shard_map/all_to_all | solution.py:68
  40.2 10.5 %collective-permute-start = (bf16[2,512,384]{2,1,0:T(8,128)(2,1)S(1)}, bf16[2,512,384]{2,1,0:T(8,128)(2,1)}, u32[]{:S(2)}, u32[]{:S(2)}) collective-permute-start(bf16[2,512,384]{2,1,0:T(8,128)(2,1)S(1)} %pad_maximum_fusion.1), channel_id=1, source_target_pairs={{352,0},{384,32},{416,64},{448,96},{480,128},{0,160},{32,192},{64,... | collective-permute-start | bytes 2359304 | tf_op jit(solution)/shard_map/ppermute | solution.py:19
  50.6 7.3 %collective-permute-start.1 = (bf16[2,512,384]{2,1,0:T(8,128)(2,1)S(1)}, bf16[2,512,384]{2,1,0:T(8,128)(2,1)}, u32[]{:S(2)}, u32[]{:S(2)}) collective-permute-start(bf16[2,512,384]{2,1,0:T(8,128)(2,1)S(1)} %pad_maximum_fusion.1), channel_id=1, source_target_pairs={{384,0},{416,32},{448,64},{480,96},{0,128},{32,160},{64,192},{96,2... | collective-permute-start | bytes 2359304 | tf_op jit(solution)/shard_map/ppermute | solution.py:19
  57.9 3.8 collective-permute-start.2
  61.8 3.4 collective-permute-start.3
  65.2 1.0 copy.37
  66.2 3.5 all-to-all-start.2
  69.7 1.9 collective-permute-start.4
  71.8 6.7 %all-to-all-done.2 = bf16[64,8,384]{2,0,1:T(8,128)(2,1)S(1)} async-done(((bf16[64,8,384]{2,0,1:T(8,128)(2,1)}), bf16[64,8,384]{2,0,1:T(8,128)(2,1)S(1)}, u32[]{:S(2)}, u32[]{:S(2)}) %all-to-all-start.2) | async-done | bytes 393248 | tf_op jit(solution)/shard_map/all_to_all | solution.py:66
  78.6 0.8 copy.38
  79.4 61.3 %collective-permute-done = bf16[2,512,384]{2,1,0:T(8,128)(2,1)} collective-permute-done((bf16[2,512,384]{2,1,0:T(8,128)(2,1)S(1)}, bf16[2,512,384]{2,1,0:T(8,128)(2,1)}, u32[]{:S(2)}, u32[]{:S(2)}) %collective-permute-start) | collective-permute-done | bytes 786464 | tf_op jit(solution)/shard_map/ppermute | solution.py:19
  140.8 1.9 collective-permute-start.5
  142.7 1.2 constant_dynamic-update-slice_fusion.11
  143.9 66.9 %collective-permute-done.1 = bf16[2,512,384]{2,1,0:T(8,128)(2,1)} collective-permute-done((bf16[2,512,384]{2,1,0:T(8,128)(2,1)S(1)}, bf16[2,512,384]{2,1,0:T(8,128)(2,1)}, u32[]{:S(2)}, u32[]{:S(2)}) %collective-permute-start.1) | collective-permute-done | bytes 786464 | tf_op jit(solution)/shard_map/ppermute | solution.py:19
  210.8 1.9 collective-permute-start.6
  212.8 1.3 constant_dynamic-update-slice_fusion.10
  214.0 41.3 %collective-permute-done.2 = bf16[2,512,384]{2,1,0:T(8,128)(2,1)} collective-permute-done((bf16[2,512,384]{2,1,0:T(8,128)(2,1)S(1)}, bf16[2,512,384]{2,1,0:T(8,128)(2,1)}, u32[]{:S(2)}, u32[]{:S(2)}) %collective-permute-start.2) | collective-permute-done | bytes 786464 | tf_op jit(solution)/shard_map/ppermute | solution.py:19
  255.4 5.4 %collective-permute-start.7 = (bf16[2,512,384]{2,1,0:T(8,128)(2,1)S(1)}, bf16[2,512,384]{2,1,0:T(8,128)(2,1)S(1)}, u32[]{:S(2)}, u32[]{:S(2)}) collective-permute-start(bf16[2,512,384]{2,1,0:T(8,128)(2,1)S(1)} %pad_maximum_fusion.1), channel_id=1, source_target_pairs={{96,0},{128,32},{160,64},{192,96},{224,128},{256,160},{288,192},{3... | collective-permute-start | bytes 2359304 | tf_op jit(solution)/shard_map/ppermute | solution.py:19
  260.8 1.3 constant_dynamic-update-slice_fusion.9
  262.1 26.1 %collective-permute-done.3 = bf16[2,512,384]{2,1,0:T(8,128)(2,1)S(1)} collective-permute-done((bf16[2,512,384]{2,1,0:T(8,128)(2,1)S(1)}, bf16[2,512,384]{2,1,0:T(8,128)(2,1)S(1)}, u32[]{:S(2)}, u32[]{:S(2)}) %collective-permute-start.3) | collective-permute-done | bytes 786464 | tf_op jit(solution)/shard_map/ppermute | solution.py:19
  288.2 6.0 %collective-permute-start.8 = (bf16[2,512,384]{2,1,0:T(8,128)(2,1)S(1)}, bf16[2,512,384]{2,1,0:T(8,128)(2,1)S(1)}, u32[]{:S(2)}, u32[]{:S(2)}) collective-permute-start(bf16[2,512,384]{2,1,0:T(8,128)(2,1)S(1)} %pad_maximum_fusion.1), channel_id=1, source_target_pairs={{128,0},{160,32},{192,64},{224,96},{256,128},{288,160},{320,192},{... | collective-permute-start | bytes 2359304 | tf_op jit(solution)/shard_map/ppermute | solution.py:19
  294.2 0.2 constant_dynamic-update-slice_fusion.8
  294.3 9.7 %collective-permute-done.4 = bf16[2,512,384]{2,1,0:T(8,128)(2,1)} collective-permute-done((bf16[2,512,384]{2,1,0:T(8,128)(2,1)S(1)}, bf16[2,512,384]{2,1,0:T(8,128)(2,1)}, u32[]{:S(2)}, u32[]{:S(2)}) %collective-permute-start.4) | collective-permute-done | bytes 786464 | tf_op jit(solution)/shard_map/ppermute | solution.py:19
  304.0 6.4 %collective-permute-start.9 = (bf16[2,512,384]{2,1,0:T(8,128)(2,1)S(1)}, bf16[2,512,384]{2,1,0:T(8,128)(2,1)S(1)}, u32[]{:S(2)}, u32[]{:S(2)}) collective-permute-start(bf16[2,512,384]{2,1,0:T(8,128)(2,1)S(1)} %pad_maximum_fusion.1), channel_id=1, source_target_pairs={{160,0},{192,32},{224,64},{256,96},{288,128},{320,160},{352,192},{... | collective-permute-start | bytes 2359304 | tf_op jit(solution)/shard_map/ppermute | solution.py:19
  310.4 1.3 constant_dynamic-update-slice_fusion.7
  312.1 16.2 %collective-permute-done.7 = bf16[2,512,384]{2,1,0:T(8,128)(2,1)S(1)} collective-permute-done((bf16[2,512,384]{2,1,0:T(8,128)(2,1)S(1)}, bf16[2,512,384]{2,1,0:T(8,128)(2,1)S(1)}, u32[]{:S(2)}, u32[]{:S(2)}) %collective-permute-start.7) | collective-permute-done | bytes 786464 | tf_op jit(solution)/shard_map/ppermute | solution.py:19
  328.5 6.1 %collective-permute-done.8 = bf16[2,512,384]{2,1,0:T(8,128)(2,1)S(1)} collective-permute-done((bf16[2,512,384]{2,1,0:T(8,128)(2,1)S(1)}, bf16[2,512,384]{2,1,0:T(8,128)(2,1)S(1)}, u32[]{:S(2)}, u32[]{:S(2)}) %collective-permute-start.8) | collective-permute-done | bytes 786464 | tf_op jit(solution)/shard_map/ppermute | solution.py:19
  334.8 132.1 %collective-permute-done.9 = bf16[2,512,384]{2,1,0:T(8,128)(2,1)S(1)} collective-permute-done((bf16[2,512,384]{2,1,0:T(8,128)(2,1)S(1)}, bf16[2,512,384]{2,1,0:T(8,128)(2,1)S(1)}, u32[]{:S(2)}, u32[]{:S(2)}) %collective-permute-start.9) | collective-permute-done | bytes 786464 | tf_op jit(solution)/shard_map/ppermute | solution.py:19
  467.1 3.4 copy-done.3
  470.4 53.6 %while.10 = (s32[]{:T(128)}, bf16[2,256,384]{2,1,0:T(8,128)(2,1)}, s32[2,9]{1,0:T(2,128)S(1)}, bf16[2,22,256,384]{3,2,1,0:T(8,128)(2,1)}, bf16[2,256,3,128]{3,1,2,0:T(8,128)(2,1)}, /*index=5*/s32[]{:T(128)}) while((s32[]{:T(128)}, bf16[2,256,384]{2,1,0:T(8,128)(2,1)}, s32[2,9]{1,0:T(2,128)S(1)}, bf16[2,22,256,384]{3,2,1,0:T(8,128)(2,1)}, ...), condition=%wide.region_3.4_spmd, body=%wide.region_0.3_spmd.sunk | while | flops 922091136 | bytes 94981536 | solution.py:107
  470.4 4.9 gather_fusion
  475.3 0.5 select_bitcast_fusion.2
  475.8 2.3 fusion.53
  478.1 4.6 squeeze.22
  482.7 1.2 multiply_reduce_fusion.2
  483.9 3.0 copy-done.1
  486.8 1.3 fusion.54
  488.1 2.7 squeeze.23
  490.8 5.4 %fusion.55 = bf16[256,3,128]{0,2,1:T(8,128)(2,1)S(1)} fusion(f32[3,256,2304]{2,1,0:T(8,128)} %copy-done.1, f32[3,256]{1,0:T(4,128)S(1)} %get-tuple-element.115, bf16[2304,3,128]{2,1,0:T(4,128)(2,1)} %squeeze.23, f32[256,3]{0,1:T(4,128)S(1)} %bitcast.84), kind=kOutput, calls=%fused_computation.15.clone.1 | convolution fusion | flops 458489856 | bytes 9050112 | tf_op jit(solution)/shard_map/while/body/eval_jaxpr/hqk,khd->qhd/dot_general | solution.py:101
  496.3 0.2 copy.65
  496.5 0.7 copy-done.7
  497.2 4.9 gather_fusion
  502.1 0.5 select_bitcast_fusion.2
  502.6 2.3 fusion.53
  504.9 4.6 squeeze.22
  509.5 1.2 multiply_reduce_fusion.2
  510.7 3.0 copy-done.1
  513.6 1.3 fusion.54
  514.9 2.7 squeeze.23
  517.6 5.4 %fusion.55 = bf16[256,3,128]{0,2,1:T(8,128)(2,1)S(1)} fusion(f32[3,256,2304]{2,1,0:T(8,128)} %copy-done.1, f32[3,256]{1,0:T(4,128)S(1)} %get-tuple-element.115, bf16[2304,3,128]{2,1,0:T(4,128)(2,1)} %squeeze.23, f32[256,3]{0,1:T(4,128)S(1)} %bitcast.84), kind=kOutput, calls=%fused_computation.15.clone.1 | convolution fusion | flops 458489856 | bytes 9050112 | tf_op jit(solution)/shard_map/while/body/eval_jaxpr/hqk,khd->qhd/dot_general | solution.py:101
  523.0 0.2 copy.65
  523.3 0.7 copy-done.7
  524.0 12.3 %all_to_all.62 = bf16[8,64,384]{2,1,0:T(8,128)(2,1)S(1)} all-to-all(bf16[8,64,384]{2,1,0:T(8,128)(2,1)} %bitcast.83), channel_id=1, replica_groups=mesh['blk'=16,'uly'=8,'dp'=4] {'uly'}, dimensions={0} | all-to-all | bytes 786432 | tf_op jit(solution)/shard_map/all_to_all | solution.py:108
  536.3 0.8 copy.45
  (53 shorter events, 1.9 us)
Async XLA Ops:
  0.0 71.6 %copy-start = (s32[32,9]{0,1:T(8,128)S(1)}, s32[32,9]{0,1:T(8,128)}, u32[]{:S(2)}) copy-start(s32[32,9]{0,1:T(8,128)} %param.11) | copy-start | bytes 3460
  5.7 14.2 %copy-start.5 = (bf16[64,3072]{1,0:T(8,128)(2,1)S(1)}, bf16[64,3072]{1,0:T(8,128)(2,1)}, u32[]{:S(2)}) copy-start(bf16[64,3072]{1,0:T(8,128)(2,1)} %param.9) | copy-start | bytes 1179652
  15.5 13.2 %all-to-all-start = ((bf16[64,8,384]{2,0,1:T(8,128)(2,1)}), bf16[64,8,384]{2,0,1:T(8,128)(2,1)S(1)}, u32[]{:S(2)}, u32[]{:S(2)}) async-start(bf16[64,8,384]{2,0,1:T(8,128)(2,1)} %copy.34), calls=%async_computation | async-start | bytes 786432 | tf_op jit(solution)/shard_map/all_to_all | solution.py:67
  40.2 100.6 %collective-permute-start = (bf16[2,512,384]{2,1,0:T(8,128)(2,1)S(1)}, bf16[2,512,384]{2,1,0:T(8,128)(2,1)}, u32[]{:S(2)}, u32[]{:S(2)}) collective-permute-start(bf16[2,512,384]{2,1,0:T(8,128)(2,1)S(1)} %pad_maximum_fusion.1), channel_id=1, source_target_pairs={{352,0},{384,32},{416,64},{448,96},{480,128},{0,160},{32,192},{64,... | collective-permute-start | bytes 2359304 | tf_op jit(solution)/shard_map/ppermute | solution.py:19
  50.6 160.2 %collective-permute-start.1 = (bf16[2,512,384]{2,1,0:T(8,128)(2,1)S(1)}, bf16[2,512,384]{2,1,0:T(8,128)(2,1)}, u32[]{:S(2)}, u32[]{:S(2)}) collective-permute-start(bf16[2,512,384]{2,1,0:T(8,128)(2,1)S(1)} %pad_maximum_fusion.1), channel_id=1, source_target_pairs={{384,0},{416,32},{448,64},{480,96},{0,128},{32,160},{64,192},{96,2... | collective-permute-start | bytes 2359304 | tf_op jit(solution)/shard_map/ppermute | solution.py:19
  57.9 197.4 %collective-permute-start.2 = (bf16[2,512,384]{2,1,0:T(8,128)(2,1)S(1)}, bf16[2,512,384]{2,1,0:T(8,128)(2,1)}, u32[]{:S(2)}, u32[]{:S(2)}) collective-permute-start(bf16[2,512,384]{2,1,0:T(8,128)(2,1)S(1)} %pad_maximum_fusion.1), channel_id=1, source_target_pairs={{416,0},{448,32},{480,64},{0,96},{32,128},{64,160},{96,192},{128,2... | collective-permute-start | bytes 2359304 | tf_op jit(solution)/shard_map/ppermute | solution.py:19
  61.8 226.4 %collective-permute-start.3 = (bf16[2,512,384]{2,1,0:T(8,128)(2,1)S(1)}, bf16[2,512,384]{2,1,0:T(8,128)(2,1)S(1)}, u32[]{:S(2)}, u32[]{:S(2)}) collective-permute-start(bf16[2,512,384]{2,1,0:T(8,128)(2,1)S(1)} %pad_maximum_fusion.1), channel_id=1, source_target_pairs={{448,0},{480,32},{0,64},{32,96},{64,128},{96,160},{128,192},{160,2... | collective-permute-start | bytes 2359304 | tf_op jit(solution)/shard_map/ppermute | solution.py:19
  66.2 12.3 %all-to-all-start.2 = ((bf16[64,8,384]{2,0,1:T(8,128)(2,1)}), bf16[64,8,384]{2,0,1:T(8,128)(2,1)S(1)}, u32[]{:S(2)}, u32[]{:S(2)}) async-start(bf16[64,8,384]{2,0,1:T(8,128)(2,1)} %copy.37), calls=%async_computation.2 | async-start | bytes 786432 | tf_op jit(solution)/shard_map/all_to_all | solution.py:66
  69.7 234.3 %collective-permute-start.4 = (bf16[2,512,384]{2,1,0:T(8,128)(2,1)S(1)}, bf16[2,512,384]{2,1,0:T(8,128)(2,1)}, u32[]{:S(2)}, u32[]{:S(2)}) collective-permute-start(bf16[2,512,384]{2,1,0:T(8,128)(2,1)S(1)} %pad_maximum_fusion.1), channel_id=1, source_target_pairs={{480,0},{0,32},{32,64},{64,96},{96,128},{128,160},{160,192},{192,2... | collective-permute-start | bytes 2359304 | tf_op jit(solution)/shard_map/ppermute | solution.py:19
  140.8 171.0 %collective-permute-start.5 = (bf16[2,512,384]{2,1,0:T(8,128)(2,1)S(1)}, bf16[2,512,384]{2,1,0:T(8,128)(2,1)S(1)}, u32[]{:S(2)}, u32[]{:S(2)}) collective-permute-start(bf16[2,512,384]{2,1,0:T(8,128)(2,1)S(1)} %pad_maximum_fusion.1), channel_id=1, source_target_pairs={{32,0},{64,32},{96,64},{128,96},{160,128},{192,160},{224,192},{256... | collective-permute-start | bytes 2359304 | tf_op jit(solution)/shard_map/ppermute | solution.py:19
  210.8 101.1 %collective-permute-start.6 = (bf16[2,512,384]{2,1,0:T(8,128)(2,1)S(1)}, bf16[2,512,384]{2,1,0:T(8,128)(2,1)S(1)}, u32[]{:S(2)}, u32[]{:S(2)}) collective-permute-start(bf16[2,512,384]{2,1,0:T(8,128)(2,1)S(1)} %pad_maximum_fusion.1), channel_id=1, source_target_pairs={{64,0},{96,32},{128,64},{160,96},{192,128},{224,160},{256,192},{28... | collective-permute-start | bytes 2359304 | tf_op jit(solution)/shard_map/ppermute | solution.py:19
  255.4 73.0 %collective-permute-start.7 = (bf16[2,512,384]{2,1,0:T(8,128)(2,1)S(1)}, bf16[2,512,384]{2,1,0:T(8,128)(2,1)S(1)}, u32[]{:S(2)}, u32[]{:S(2)}) collective-permute-start(bf16[2,512,384]{2,1,0:T(8,128)(2,1)S(1)} %pad_maximum_fusion.1), channel_id=1, source_target_pairs={{96,0},{128,32},{160,64},{192,96},{224,128},{256,160},{288,192},{3... | collective-permute-start | bytes 2359304 | tf_op jit(solution)/shard_map/ppermute | solution.py:19
  288.2 46.4 %collective-permute-start.8 = (bf16[2,512,384]{2,1,0:T(8,128)(2,1)S(1)}, bf16[2,512,384]{2,1,0:T(8,128)(2,1)S(1)}, u32[]{:S(2)}, u32[]{:S(2)}) collective-permute-start(bf16[2,512,384]{2,1,0:T(8,128)(2,1)S(1)} %pad_maximum_fusion.1), channel_id=1, source_target_pairs={{128,0},{160,32},{192,64},{224,96},{256,128},{288,160},{320,192},{... | collective-permute-start | bytes 2359304 | tf_op jit(solution)/shard_map/ppermute | solution.py:19
  304.0 162.9 %collective-permute-start.9 = (bf16[2,512,384]{2,1,0:T(8,128)(2,1)S(1)}, bf16[2,512,384]{2,1,0:T(8,128)(2,1)S(1)}, u32[]{:S(2)}, u32[]{:S(2)}) collective-permute-start(bf16[2,512,384]{2,1,0:T(8,128)(2,1)S(1)} %pad_maximum_fusion.1), channel_id=1, source_target_pairs={{160,0},{192,32},{224,64},{256,96},{288,128},{320,160},{352,192},{... | collective-permute-start | bytes 2359304 | tf_op jit(solution)/shard_map/ppermute | solution.py:19
  467.1 3.4 copy-start.3
  475.8 6.9 %copy-start.4 = (bf16[2,256,3,128]{3,1,2,0:T(8,128)(2,1)S(1)}, bf16[2,256,3,128]{3,1,2,0:T(8,128)(2,1)}, u32[]{:S(2)}) copy-start(bf16[2,256,3,128]{3,1,2,0:T(8,128)(2,1)} %get-tuple-element.133) | copy-start | bytes 1179652 | tf_op jit(solution)/shard_map/while
  483.8 3.0 copy-start.1
  483.9 4.3 copy-start.2
  488.1 8.3 %copy-start.6 = (bf16[2,256,384]{2,1,0:T(8,128)(2,1)S(1)}, bf16[2,256,384]{2,1,0:T(8,128)(2,1)}, u32[]{:S(2)}) copy-start(bf16[2,256,384]{2,1,0:T(8,128)(2,1)} %get-tuple-element.124) | copy-start | bytes 1179652 | tf_op jit(solution)/shard_map/while
  496.5 0.7 copy-start.7
  502.6 6.9 %copy-start.4 = (bf16[2,256,3,128]{3,1,2,0:T(8,128)(2,1)S(1)}, bf16[2,256,3,128]{3,1,2,0:T(8,128)(2,1)}, u32[]{:S(2)}) copy-start(bf16[2,256,3,128]{3,1,2,0:T(8,128)(2,1)} %get-tuple-element.133) | copy-start | bytes 1179652 | tf_op jit(solution)/shard_map/while
  510.6 3.0 copy-start.1
  510.6 4.3 copy-start.2
  514.9 8.3 %copy-start.6 = (bf16[2,256,384]{2,1,0:T(8,128)(2,1)S(1)}, bf16[2,256,384]{2,1,0:T(8,128)(2,1)}, u32[]{:S(2)}) copy-start(bf16[2,256,384]{2,1,0:T(8,128)(2,1)} %get-tuple-element.124) | copy-start | bytes 1179652 | tf_op jit(solution)/shard_map/while
  523.3 0.7 copy-start.7
where the time goes:
time: 538 us; the launch traced here: 537 us
  waiting for transfers between devices  375 us (70%)
  starting transfers between devices  56.2 us (10%)
  local copies, waits for them, and re-layouts  54.1 us (10%)
  blocking collectives  23.6 us (4%)
  other arithmetic  14 us (3%)
  matrix products  13.2 us (2%)
    ppermute x10, waiting for transfers between devices, passed_along(): return lax.ppermute(block, axis, route)  360 us
    ppermute x10, starting transfers between devices, passed_along(): return lax.ppermute(block, axis, route)  48.4 us
    all_to_all x1, blocking collectives, shards(): lax.all_to_all(attended_local, 'uly', split_axis=0, concat_axis=1, tiled=...  12.3 us
    unnamed x18, local copies, waits for them, and re-layouts  12 us
    all_to_all x1, blocking collectives, shards(): lax.all_to_all(values, 'uly', split_axis=1, concat_axis=0, tiled=True)  11.3 us
    dot_general x2, matrix products, one_tile(): jnp.einsum('hqk,khd->qhd', weights_bf, gathered[1], preferred_element_typ...  10.8 us
  transfers between devices with their start and end apart: 12, of which 10 were waited for; matrix products, arithmetic and copies ran while one was open for 2% of the time, Pallas kernels for 0%

commit v1 on v0

v1 whole, which is shorter than its diff:
```python
import functools

import jax
import jax.numpy as jnp
import numpy as np
from jax import lax
from jax.experimental import pallas as pl
from jax.experimental.pallas import tpu as pltpu
from jax.sharding import Mesh
from jax.sharding import PartitionSpec as P

HD = 128
TOK_TILE = 256
WIN = 9
COLS = 8
GROUP = ("half", "x", "core")
VMEM = pl.BlockSpec(memory_space=pltpu.VMEM)
SMEM = pl.BlockSpec(memory_space=pltpu.SMEM)
BF = jnp.bfloat16
F32 = jnp.float32
LIMIT = 48 * 1024 * 1024


def frequencies():
    pair = np.arange(HD) // 2
    dt = HD - 4 * (HD // 6)
    dhw = 2 * (HD // 6)
    nt, ns = dt // 2, dhw // 2
    kind = np.where(pair < nt, 0, np.where(pair < nt + ns, 1, 2))
    within = np.where(kind == 0, pair, np.where(kind == 1, pair - nt, pair - nt - ns))
    freq = np.power(10000.0, -2.0 * within / np.where(kind == 0, dt, dhw))
    table = np.zeros((8, HD), np.float32)
    table[0] = freq
    for which in range(3):
        table[1 + which] = np.where(kind == which, freq, 0.0)
    return table


def rotate_kernel(meta, freq, q_ref, k_ref, v_ref, out_ref):
    tile = meta[2]
    frame = (tile // 32 * 4 + meta[3]).astype(F32)
    row0 = (tile // 8 % 4 * 8).astype(F32)
    col0 = (tile % 8 * 8).astype(F32)
    rows = q_ref.shape[0]
    token = lax.broadcasted_iota(jnp.int32, (rows, HD), 0)
    row = row0 + (token // 8).astype(F32)
    col = col0 + (token % 8).astype(F32)
    angle = frame * freq[1:2, :] + row * freq[2:3, :] + col * freq[3:4, :]
    cosine = jnp.cos(angle)
    sine = jnp.sin(angle)
    even = lax.broadcasted_iota(jnp.int32, (rows, HD), 1) % 2 == 0
    from_next = jnp.where(even, -sine, 0.0)
    from_last = jnp.where(even, 0.0, sine)
    scale = HD ** (-0.5) * 1.4426950408889634

    def turned(x, c, n, l):
        x = x.astype(F32)
        return (x * c + pltpu.roll(x, HD - 1, 1) * n + pltpu.roll(x, 1, 1) * l).astype(BF)

    qc, qn, ql = cosine * scale, from_next * scale, from_last * scale
    for which, ref in enumerate((q_ref, k_ref, v_ref)):
        for g in range(8):
            for h in range(3):
                x = ref[:, (3 * g + h) * HD : (3 * g + h + 1) * HD]
                if which == 0:
                    x = turned(x, qc, qn, ql)
                elif which == 1:
                    x = turned(x, cosine, from_next, from_last)
                if h < 2:
                    out_ref[2 * g + h, which, 0:64, :] = x
                else:
                    out_ref[2 * g, which, 64:96, :] = x[0:32]
                    out_ref[2 * g + 1, which, 64:96, :] = x[32:64]


def attend(q, kp, vp, picks, s_ref):
    rows = q.shape[0]
    top = None
    for j in range(WIN):
        s = lax.dot_general(q, kp[picks[j]], (((1,), (1,)), ((), ())), preferred_element_type=F32)
        s_ref[j, 0:rows, :] = s
        top = s if top is None else jnp.maximum(top, s)
    top = jnp.max(top, axis=1, keepdims=True)
    total = jnp.zeros((rows, TOK_TILE), F32)
    acc = jnp.zeros((rows, HD), F32)
    for j in range(WIN):
        p = jnp.exp2(s_ref[j, 0:rows, :] - top)
        total = total + p
        acc = acc + jnp.dot(p.astype(BF), vp[picks[j]], preferred_element_type=F32)
    return (acc / jnp.sum(total, axis=1, keepdims=True)).astype(BF)


def attention_kernel(
    meta, nb, own, r1, r2, r3, l1, l2, l3, s0, sx, sy, o_own, o_oth, kh, vh, k2, v2, s_ref
):
    k = meta[0]
    w = meta[1]
    for t in range(4):
        rows = slice(t * TOK_TILE, (t + 1) * TOK_TILE)
        kh[t] = own[4 * t : 4 * t + 4, 1, 0:64, :].reshape(TOK_TILE, HD)
        vh[t] = own[4 * t : 4 * t + 4, 2, 0:64, :].reshape(TOK_TILE, HD)
        kh[4 + t] = r2[rows]
        vh[4 + t] = r3[rows]
        kh[8 + t] = l2[rows]
        vh[8 + t] = l3[rows]

    def shared(base, mine, other):
        for t in range(4):
            rk = slice(t * 128, (t + 1) * 128)
            rv = slice(512 + t * 128, 512 + (t + 1) * 128)
            k2[base + t, 128:256] = other[rk]
            v2[base + t, 128:256] = other[rv]
            k2[base + t, 0:128] = mine[rk]
            v2[base + t, 0:128] = mine[rv]

    for t in range(4):
        k2[t, 0:128] = own[4 * t : 4 * t + 4, 1, 64:96, :].reshape(128, HD)
        v2[t, 0:128] = own[4 * t : 4 * t + 4, 2, 64:96, :].reshape(128, HD)
        k2[t, 128:256] = s0[t * 128 : (t + 1) * 128]
        v2[t, 128:256] = s0[512 + t * 128 : 512 + (t + 1) * 128]

    @pl.when(w != 7)
    def _():
        shared(4, r1, sx)

    @pl.when(w == 7)
    def _():
        shared(4, l1, sx)
        shared(8, l2, sy)

    @pl.when(w == 0)
    def _():
        shared(8, r2, sy)

    @pl.when((w != 0) & (w != 7))
    def _():
        shared(8, l1, sy)

    from_left = (w == 1) | (w == 7)
    k_oth = lax.rem(jnp.where(from_left, k + 7, k + 1), 8)
    near = jnp.where(w == 7, 7, 1)

    def picks_of(slot, one):
        picks = []
        for j in range(WIN):
            n = nb[slot, j]
            d = lax.rem(n // 4 - k + 8, 8)
            picks.append(jnp.where(d == 0, 0, jnp.where(d == one, 4, 8)) + lax.rem(n, 4))
        return picks

    edge = (w == 0) | (w == 7)
    inner = (w == 1) | (w == 6)

    @pl.when(inner)
    def _():
        @pl.loop(0, 4)
        def _(t):
            rows = pl.ds(pl.multiple_of(t * TOK_TILE, TOK_TILE), TOK_TILE)
            q = jnp.where(from_left, l1[rows], r1[rows])
            o_oth[rows] = attend(q, kh, vh, picks_of(k_oth * 4 + t, 1), s_ref)

    @pl.when(edge)
    def _():
        @pl.loop(0, 4)
        def _(t):
            rows = pl.ds(pl.multiple_of(t * 128, 128), 128)
            q = jnp.where(from_left, l3[rows], r3[rows])
            o_oth[rows] = attend(q, k2, v2, picks_of(k_oth * 4 + t, near), s_ref)

    @pl.when(jnp.logical_not(edge))
    def _():
        @pl.loop(0, 4)
        def _(t):
            q = own[pl.ds(t * 4, 4), 0, 0:64, :].reshape(TOK_TILE, HD)
            o = attend(q, kh, vh, picks_of(k * 4 + t, 1), s_ref)
            o_own[pl.ds(t * 4, 4), 0:64, :] = o.reshape(4, 64, HD)

    @pl.when(jnp.logical_not(inner))
    def _():
        @pl.loop(0, 4)
        def _(t):
            q = own[pl.ds(t * 4, 4), 0, 64:96, :].reshape(128, HD)
            o = attend(q, k2, v2, picks_of(k * 4 + t, near), s_ref)
            o_own[pl.ds(t * 4, 4), 64:96, :] = o.reshape(4, 32, HD)


def unpack_kernel(in_ref, out_ref):
    for g in range(8):
        for h in range(2):
            out_ref[:, (3 * g + h) * HD : (3 * g + h + 1) * HD] = in_ref[2 * g + h, 0:64, :]
        last = slice((3 * g + 2) * HD, (3 * g + 3) * HD)
        out_ref[0:32, last] = in_ref[2 * g, 64:96, :]
        out_ref[32:64, last] = in_ref[2 * g + 1, 64:96, :]


def along_columns(block, distance):
    n = 2 * COLS
    return lax.ppermute(block, ("col", "half"), [(i, (i + 2 * distance) % n) for i in range(n)])


def swapped(block):
    return lax.ppermute(block, "core", [(0, 1), (1, 0)])


def shards(freq, queries, keys, values, tile_order, neighbors):
    col = lax.axis_index("col")
    half = lax.axis_index("half")
    x = lax.axis_index("x")
    core = lax.axis_index("core")
    slot = col * 4 + half * 2 + x // 2
    w = tile_order[col * 4] % COLS
    meta = jnp.stack([col, w, tile_order[slot], (x % 2) * 2 + core]).astype(jnp.int32)
    packed = pl.pallas_call(
        rotate_kernel,
        out_shape=jax.ShapeDtypeStruct((16, 3, 96, HD), BF),
        in_specs=[SMEM, VMEM, VMEM, VMEM, VMEM],
        out_specs=VMEM,
        compiler_params=pltpu.CompilerParams(vmem_limit_bytes=LIMIT),
        name="rotate",
    )(meta, freq, queries, keys, values)
    own = lax.all_to_all(packed, GROUP, split_axis=0, concat_axis=0, tiled=True)
    q_head = own[:, 0, 0:64].reshape(1024, HD)
    k_head = own[:, 1, 0:64].reshape(1024, HD)
    v_head = own[:, 2, 0:64].reshape(1024, HD)
    q_shared = own[:, 0, 64:96].reshape(512, HD)
    kv_shared = jnp.concatenate(
        [own[:, 1, 64:96].reshape(512, HD), own[:, 2, 64:96].reshape(512, HD)]
    )
    q_shared = jnp.concatenate([q_shared, q_shared])
    s0 = swapped(kv_shared)
    r1 = along_columns(jnp.where(w == 7, q_head, kv_shared), -1)
    l1 = along_columns(jnp.where(w == 0, q_head, kv_shared), 1)
    r3 = along_columns(jnp.where(w == 1, q_shared, v_head), -1)
    l3 = along_columns(jnp.where(w == 6, q_shared, v_head), 1)
    r2 = along_columns(jnp.where(w == 1, r1, k_head), -1)
    l2 = along_columns(jnp.where(w == 6, l1, k_head), 1)
    sx = swapped(jnp.where(w == 7, l1, r1))
    sy = swapped(jnp.where(w == 0, r2, jnp.where(w == 7, l2, l1)))
    o_own, o_oth = pl.pallas_call(
        attention_kernel,
        out_shape=(
            jax.ShapeDtypeStruct((16, 96, HD), BF),
            jax.ShapeDtypeStruct((1024, HD), BF),
        ),
        in_specs=[SMEM, SMEM] + [VMEM] * 10,
        out_specs=(VMEM, VMEM),
        scratch_shapes=[pltpu.VMEM((12, TOK_TILE, HD), BF)] * 4
        + [pltpu.VMEM((WIN, TOK_TILE, TOK_TILE), F32)],
        compiler_params=pltpu.CompilerParams(vmem_limit_bytes=LIMIT),
        name="attend",
    )(meta, neighbors, own, r1, r2, r3, l1, l2, l3, s0, sx, sy)
    o_right = along_columns(o_oth, -1)
    o_left = along_columns(o_oth, 1)
    o_head = jnp.where(
        w == 0,
        o_right.reshape(16, 64, HD),
        jnp.where(w == 7, o_left.reshape(16, 64, HD), o_own[:, 0:64]),
    )
    o_shared = jnp.where(
        w == 1,
        o_left[0:512].reshape(16, 32, HD),
        jnp.where(w == 6, o_right[0:512].reshape(16, 32, HD), o_own[:, 64:96]),
    )
    sent = jnp.concatenate([o_head, o_shared], axis=1)
    back = lax.all_to_all(sent, GROUP, split_axis=0, concat_axis=0, tiled=True)
    return pl.pallas_call(
        unpack_kernel,
        out_shape=jax.ShapeDtypeStruct(queries.shape, BF),
        in_specs=[VMEM],
        out_specs=VMEM,
        compiler_params=pltpu.CompilerParams(vmem_limit_bytes=LIMIT),
        name="unpack",
    )(back)


def solution(mesh):
    blk, uly, dp = (mesh.shape[name] for name in ("blk", "uly", "dp"))
    fine = Mesh(
        mesh.devices.reshape(blk // 2, 2, uly // 2, 2, dp), ("col", "half", "x", "core", "dp")
    )
    tokens = ("dp", "col", "half", "x", "core")
    placed = (P(), P(tokens, None), P(tokens, None), P(tokens, None), P("dp"), P("dp", None))
    body = jax.shard_map(
        shards, mesh=fine, in_specs=placed, out_specs=P(tokens, None), check_vma=False
    )

    def run(queries, keys, values, tile_order, neighbors):
        return body(jnp.asarray(frequencies()), queries, keys, values, tile_order, neighbors)

    return run
```

time: 538 us -> 137 us (0.25)
  the two profiles are of different devices: /device:TPU:32 before, /device:TPU:24 now
where the time goes in v1:
time: 137 us; the launch traced here: 135 us
  starting transfers between devices  52.8 us (39%)
  waiting for transfers between devices  43.8 us (32%)
  blocking collectives  15.3 us (11%)
  Pallas kernels  10.7 us (8%)
  local copies, waits for them, and re-layouts  7.21 us (5%)
  other arithmetic  3.48 us (3%)
  between operations  2.19 us (2%)
    ppermute x8, starting transfers between devices, along_columns(): lax.ppermute(block, ('col', 'half'), [(i, (i + 2 * distance) % n) for i i...  40.8 us
    ppermute x8, waiting for transfers between devices, along_columns(): lax.ppermute(block, ('col', 'half'), [(i, (i + 2 * distance) % n) for i i...  25.7 us
    all_to_all x1, waiting for transfers between devices, shards(): own = lax.all_to_all(packed, GROUP, split_axis=0, concat_axis=0, tiled=True)  18.1 us
    all_to_all x1, blocking collectives, shards(): back = lax.all_to_all(sent, GROUP, split_axis=0, concat_axis=0, tiled=True)  15.3 us
    pallas_call x1, Pallas kernels, shards(): pl.pallas_call(attention_kernel, out_shape=(jax.ShapeDtypeStruct((16, 96,...  7.5 us
    ppermute x3, starting transfers between devices, swapped(): return lax.ppermute(block, 'core', [(0, 1), (1, 0)])  6.23 us
    all_to_all x1, starting transfers between devices, shards(): own = lax.all_to_all(packed, GROUP, split_axis=0, concat_axis=0, tiled=True)  5.76 us
    unnamed x13, local copies, waits for them, and re-layouts  5.69 us
  transfers between devices with their start and end apart: 12, of which 6 were waited for; matrix products, arithmetic and copies ran while one was open for 2% of the time, Pallas kernels for 0%

profile of v1, /device:TPU:24, one launch (start us, length us, event | category | flops | bytes accessed | tf_op | source)
XLA Modules:
  0.0 135.5 jit_solution(23050471938055033)
XLA Ops:
  0.0 1.4 %fusion.2 = (s32[1]{0:T(128)}, s32[1]{0:T(128)}) fusion(s32[32]{0:T(128)} %param.9, s32[]{:T(128)S(6)} %select_n.95, s32[]{:T(128)S(6)} %select_n.99), kind=kLoop, calls=%fused_computation.16 | loop fusion | bytes 24 | tf_op jit(solution)/shard_map/dynamic_slice | solution.py:211
  3.3 0.7 pad_add_fusion.meta
  4.1 0.0 copy-start
  4.1 1.0 copy-done
  5.1 0.0 copy-start.1
  5.1 1.0 copy-done.1
  6.1 0.0 copy-start.2
  6.1 1.0 copy-done.2
  7.1 0.0 copy-start.5
  7.1 0.7 copy-done.5
  7.8 2.4 %rotate.1 = bf16[16,3,96,128]{3,2,1,0:T(8,128)(2,1)} custom-call(s32[4]{0:T(128)S(1)} %pad_add_fusion.meta, f32[8,128]{1,0:T(8,128)S(1)} %copy-done.5, bf16[64,3072]{1,0:T(8,128)(2,1)S(1)} %copy-done, bf16[64,3072]{1,0:T(8,128)(2,1)S(1)} %copy-done.1, bf16[64,3072]{1,0:T(8,128)(2,1)S(1)} %copy-done.2), custom_call_target="tpu_custom_call" | custom-call | tf_op jit(solution)/shard_map/rotate/pallas_call | solution.py:213
  10.1 0.0 copy-start.3
  10.1 0.6 copy-done.3
  10.7 5.8 %all-to-all-start = ((bf16[16,3,96,128]{3,2,1,0:T(8,128)(2,1)}), bf16[16,3,96,128]{3,2,1,0:T(8,128)(2,1)S(1)}, u32[]{:S(2)}, u32[]{:S(2)}) async-start(bf16[16,3,96,128]{3,2,1,0:T(8,128)(2,1)} %rotate.1), calls=%async_computation | async-start | bytes 2359296 | tf_op jit(solution)/shard_map/all_to_all | solution.py:221
  16.5 18.1 %all-to-all-done.own = bf16[16,3,96,128]{3,2,1,0:T(8,128)(2,1)S(1)} async-done(((bf16[16,3,96,128]{3,2,1,0:T(8,128)(2,1)}), bf16[16,3,96,128]{3,2,1,0:T(8,128)(2,1)S(1)}, u32[]{:S(2)}, u32[]{:S(2)}) %all-to-all-start) | async-done | bytes 1179680 | tf_op jit(solution)/shard_map/all_to_all | solution.py:221
  34.6 0.1 fusion.1
  34.7 0.8 bitcast_select_fusion.4
  35.5 5.2 %collective-permute-start.3 = (bf16[1024,128]{1,0:T(8,128)(2,1)S(1)}, bf16[1024,128]{1,0:T(8,128)(2,1)S(1)}, u32[]{:S(2)}, u32[]{:S(2)}) collective-permute-start(bf16[1024,128]{1,0:T(8,128)(2,1)S(1)} %get-tuple-element.15), channel_id=1, source_target_pairs={{0,64},{32,96},{64,128},{96,160},{128,192},{160,224},{192,256},{22... | collective-permute-start | bytes 786440 | tf_op jit(solution)/shard_map/ppermute | solution.py:198
  40.7 7.7 %collective-permute-start = (bf16[1024,128]{1,0:T(8,128)(2,1)S(1)}, bf16[1024,128]{1,0:T(8,128)(2,1)S(1)}, u32[]{:S(2)}, u32[]{:S(2)}) collective-permute-start(bf16[1024,128]{1,0:T(8,128)(2,1)S(1)} %get-tuple-element.16), channel_id=1, source_target_pairs={{0,448},{32,480},{64,0},{96,32},{128,64},{160,96},{192,128},{224,1... | collective-permute-start | bytes 786440 | tf_op jit(solution)/shard_map/ppermute | solution.py:198
  48.4 9.4 %collective-permute-done.3.l1 = bf16[1024,128]{1,0:T(8,128)(2,1)S(1)} collective-permute-done((bf16[1024,128]{1,0:T(8,128)(2,1)S(1)}, bf16[1024,128]{1,0:T(8,128)(2,1)S(1)}, u32[]{:S(2)}, u32[]{:S(2)}) %collective-permute-start.3) | collective-permute-done | bytes 262176 | tf_op jit(solution)/shard_map/ppermute | solution.py:198
  57.8 0.8 collective-permute-done.r1
  58.5 0.1 bitcast_select_fusion.2
  58.6 5.7 %collective-permute-start.4 = (bf16[1024,128]{1,0:T(8,128)(2,1)S(1)}, bf16[1024,128]{1,0:T(8,128)(2,1)S(1)}, u32[]{:S(2)}, u32[]{:S(2)}) collective-permute-start(bf16[1024,128]{1,0:T(8,128)(2,1)S(1)} %get-tuple-element.22), channel_id=1, source_target_pairs={{0,64},{32,96},{64,128},{96,160},{128,192},{160,224},{192,256},{22... | collective-permute-start | bytes 786440 | tf_op jit(solution)/shard_map/ppermute | solution.py:198
  64.3 2.3 %collective-permute-start.1 = (bf16[1024,128]{1,0:T(8,128)(2,1)S(1)}, bf16[1024,128]{1,0:T(8,128)(2,1)S(1)}, u32[]{:S(2)}, u32[]{:S(2)}) collective-permute-start(bf16[1024,128]{1,0:T(8,128)(2,1)S(1)} %get-tuple-element.23), channel_id=1, source_target_pairs={{0,448},{32,480},{64,0},{96,32},{128,64},{160,96},{192,128},{224,1... | collective-permute-start | bytes 786440 | tf_op jit(solution)/shard_map/ppermute | solution.py:198
  66.6 0.9 bitcast_select_fusion
  67.5 4.5 %collective-permute-start.5 = (bf16[1024,128]{1,0:T(8,128)(2,1)}, bf16[1024,128]{1,0:T(8,128)(2,1)S(1)}, u32[]{:S(2)}, u32[]{:S(2)}) collective-permute-start(bf16[1024,128]{1,0:T(8,128)(2,1)} %get-tuple-element.17), channel_id=1, source_target_pairs={{0,64},{32,96},{64,128},{96,160},{128,192},{160,224},{192,256},{22... | collective-permute-start | bytes 786440 | tf_op jit(solution)/shard_map/ppermute | solution.py:198
  72.0 3.4 %collective-permute-start.2 = (bf16[1024,128]{1,0:T(8,128)(2,1)}, bf16[1024,128]{1,0:T(8,128)(2,1)S(1)}, u32[]{:S(2)}, u32[]{:S(2)}) collective-permute-start(bf16[1024,128]{1,0:T(8,128)(2,1)} %get-tuple-element.18), channel_id=1, source_target_pairs={{0,448},{32,480},{64,0},{96,32},{128,64},{160,96},{192,128},{224,1... | collective-permute-start | bytes 786440 | tf_op jit(solution)/shard_map/ppermute | solution.py:198
  75.4 1.9 %collective-permute-start.6 = (bf16[1024,128]{1,0:T(8,128)(2,1)}, bf16[1024,128]{1,0:T(8,128)(2,1)S(1)}, u32[]{:S(2)}, u32[]{:S(2)}) collective-permute-start(bf16[1024,128]{1,0:T(8,128)(2,1)} %get-tuple-element.21), channel_id=1, source_target_pairs={{0,4},{4,0},{1,5},{5,1},{2,6},{6,2},{3,7},{7,3},{8,12},{12,8},{9,1... | collective-permute-start | bytes 786440 | tf_op jit(solution)/shard_map/ppermute | solution.py:202
  77.4 0.0 collective-permute-done.4.l2
  77.4 0.0 collective-permute-done.1.r2
  77.4 0.9 select_select_fusion.1
  78.3 2.4 %collective-permute-start.8 = (bf16[1024,128]{1,0:T(8,128)(2,1)}, bf16[1024,128]{1,0:T(8,128)(2,1)S(1)}, u32[]{:S(2)}, u32[]{:S(2)}) collective-permute-start(bf16[1024,128]{1,0:T(8,128)(2,1)} %get-tuple-element.19), channel_id=1, source_target_pairs={{0,4},{4,0},{1,5},{5,1},{2,6},{6,2},{3,7},{7,3},{8,12},{12,8},{9,1... | collective-permute-start | bytes 786440 | tf_op jit(solution)/shard_map/ppermute | solution.py:202
  80.7 1.9 %collective-permute-start.7 = (bf16[1024,128]{1,0:T(8,128)(2,1)}, bf16[1024,128]{1,0:T(8,128)(2,1)S(1)}, u32[]{:S(2)}, u32[]{:S(2)}) collective-permute-start(bf16[1024,128]{1,0:T(8,128)(2,1)} %get-tuple-element.20), channel_id=1, source_target_pairs={{0,4},{4,0},{1,5},{5,1},{2,6},{6,2},{3,7},{7,3},{8,12},{12,8},{9,1... | collective-permute-start | bytes 786440 | tf_op jit(solution)/shard_map/ppermute | solution.py:202
  82.6 0.8 copy.7.nb
  83.4 5.4 %collective-permute-done.5.l3 = bf16[1024,128]{1,0:T(8,128)(2,1)S(1)} collective-permute-done((bf16[1024,128]{1,0:T(8,128)(2,1)}, bf16[1024,128]{1,0:T(8,128)(2,1)S(1)}, u32[]{:S(2)}, u32[]{:S(2)}) %collective-permute-start.5) | collective-permute-done | bytes 262176 | tf_op jit(solution)/shard_map/ppermute | solution.py:198
  88.8 0.0 collective-permute-done.2.r3
  88.8 0.0 collective-permute-done.6.s0
  88.8 0.0 collective-permute-done.8.sy
  88.8 0.0 collective-permute-done.7.sx
  88.8 0.0 copy-start.4
  88.8 0.7 copy-done.4
  89.5 7.5 %attend.1 = (bf16[16,96,128]{2,1,0:T(8,128)(2,1)S(1)}, bf16[1024,128]{1,0:T(8,128)(2,1)S(1)}) custom-call(s32[4]{0:T(128)S(1)} %copy-done.4, s32[32,9]{1,0:T(8,128)S(1)} %copy.7.nb, bf16[16,3,96,128]{3,2,1,0:T(8,128)(2,1)S(1)} %all-to-all-done.own, bf16[1024,128]{1,0:T(8,128)(2,1)S(1)} %collective-permute-done.r1, ...), custom_call_target="tpu_custom_call" | custom-call | tf_op jit(solution)/shard_map/attend/pallas_call | solution.py:239
  97.0 10.1 %collective-permute-start.10 = (bf16[1024,128]{1,0:T(8,128)(2,1)S(1)}, bf16[1024,128]{1,0:T(8,128)(2,1)S(1)}, u32[]{:S(2)}, u32[]{:S(2)}) collective-permute-start(bf16[1024,128]{1,0:T(8,128)(2,1)S(1)} %get-tuple-element.7), channel_id=1, source_target_pairs={{0,64},{32,96},{64,128},{96,160},{128,192},{160,224},{192,256},{22... | collective-permute-start | bytes 786440 | tf_op jit(solution)/shard_map/ppermute | solution.py:198
  107.1 1.9 %collective-permute-start.9 = (bf16[1024,128]{1,0:T(8,128)(2,1)S(1)}, bf16[1024,128]{1,0:T(8,128)(2,1)S(1)}, u32[]{:S(2)}, u32[]{:S(2)}) collective-permute-start(bf16[1024,128]{1,0:T(8,128)(2,1)S(1)} %get-tuple-element.7), channel_id=1, source_target_pairs={{0,448},{32,480},{64,0},{96,32},{128,64},{160,96},{192,128},{224,1... | collective-permute-start | bytes 786440 | tf_op jit(solution)/shard_map/ppermute | solution.py:198
  109.1 7.9 %collective-permute-done.10 = bf16[1024,128]{1,0:T(8,128)(2,1)S(1)} collective-permute-done((bf16[1024,128]{1,0:T(8,128)(2,1)S(1)}, bf16[1024,128]{1,0:T(8,128)(2,1)S(1)}, u32[]{:S(2)}, u32[]{:S(2)}) %collective-permute-start.10) | collective-permute-done | bytes 262176 | tf_op jit(solution)/shard_map/ppermute | solution.py:198
  116.9 2.2 %collective-permute-done.9 = bf16[1024,128]{1,0:T(8,128)(2,1)S(1)} collective-permute-done((bf16[1024,128]{1,0:T(8,128)(2,1)S(1)}, bf16[1024,128]{1,0:T(8,128)(2,1)S(1)}, u32[]{:S(2)}, u32[]{:S(2)}) %collective-permute-start.9) | collective-permute-done | bytes 262176 | tf_op jit(solution)/shard_map/ppermute | solution.py:198
  119.3 15.3 %all_to_all.10.in_ref = bf16[16,96,128]{2,1,0:T(8,128)(2,1)S(1)} all-to-all(bf16[16,96,128]{2,1,0:T(8,128)(2,1)S(1)} %pad_maximum_fusion), channel_id=1, replica_groups=mesh['col'=8,'half'=2,'x'=4,'core'=2,'dp'=4] {'half','x','core'}, dimensions={0} | all-to-all | bytes 786432 | tf_op jit(solution)/shard_map/all_to_all | solution.py:265
  134.6 0.8 unpack.1
  (6 shorter events, 0.1 us)
Async XLA Ops:
  4.1 1.0 copy-start
  5.1 1.0 copy-start.1
  6.1 1.0 copy-start.2
  7.1 0.7 copy-start.5
  10.1 0.6 copy-start.3
  10.7 23.8 %all-to-all-start = ((bf16[16,3,96,128]{3,2,1,0:T(8,128)(2,1)}), bf16[16,3,96,128]{3,2,1,0:T(8,128)(2,1)S(1)}, u32[]{:S(2)}, u32[]{:S(2)}) async-start(bf16[16,3,96,128]{3,2,1,0:T(8,128)(2,1)} %rotate.1), calls=%async_computation | async-start | bytes 2359296 | tf_op jit(solution)/shard_map/all_to_all | solution.py:221
  35.5 22.3 %collective-permute-start.3 = (bf16[1024,128]{1,0:T(8,128)(2,1)S(1)}, bf16[1024,128]{1,0:T(8,128)(2,1)S(1)}, u32[]{:S(2)}, u32[]{:S(2)}) collective-permute-start(bf16[1024,128]{1,0:T(8,128)(2,1)S(1)} %get-tuple-element.15), channel_id=1, source_target_pairs={{0,64},{32,96},{64,128},{96,160},{128,192},{160,224},{192,256},{22... | collective-permute-start | bytes 786440 | tf_op jit(solution)/shard_map/ppermute | solution.py:198
  40.7 17.9 %collective-permute-start = (bf16[1024,128]{1,0:T(8,128)(2,1)S(1)}, bf16[1024,128]{1,0:T(8,128)(2,1)S(1)}, u32[]{:S(2)}, u32[]{:S(2)}) collective-permute-start(bf16[1024,128]{1,0:T(8,128)(2,1)S(1)} %get-tuple-element.16), channel_id=1, source_target_pairs={{0,448},{32,480},{64,0},{96,32},{128,64},{160,96},{192,128},{224,1... | collective-permute-start | bytes 786440 | tf_op jit(solution)/shard_map/ppermute | solution.py:198
  58.6 18.8 %collective-permute-start.4 = (bf16[1024,128]{1,0:T(8,128)(2,1)S(1)}, bf16[1024,128]{1,0:T(8,128)(2,1)S(1)}, u32[]{:S(2)}, u32[]{:S(2)}) collective-permute-start(bf16[1024,128]{1,0:T(8,128)(2,1)S(1)} %get-tuple-element.22), channel_id=1, source_target_pairs={{0,64},{32,96},{64,128},{96,160},{128,192},{160,224},{192,256},{22... | collective-permute-start | bytes 786440 | tf_op jit(solution)/shard_map/ppermute | solution.py:198
  64.3 13.1 %collective-permute-start.1 = (bf16[1024,128]{1,0:T(8,128)(2,1)S(1)}, bf16[1024,128]{1,0:T(8,128)(2,1)S(1)}, u32[]{:S(2)}, u32[]{:S(2)}) collective-permute-start(bf16[1024,128]{1,0:T(8,128)(2,1)S(1)} %get-tuple-element.23), channel_id=1, source_target_pairs={{0,448},{32,480},{64,0},{96,32},{128,64},{160,96},{192,128},{224,1... | collective-permute-start | bytes 786440 | tf_op jit(solution)/shard_map/ppermute | solution.py:198
  67.5 21.3 %collective-permute-start.5 = (bf16[1024,128]{1,0:T(8,128)(2,1)}, bf16[1024,128]{1,0:T(8,128)(2,1)S(1)}, u32[]{:S(2)}, u32[]{:S(2)}) collective-permute-start(bf16[1024,128]{1,0:T(8,128)(2,1)} %get-tuple-element.17), channel_id=1, source_target_pairs={{0,64},{32,96},{64,128},{96,160},{128,192},{160,224},{192,256},{22... | collective-permute-start | bytes 786440 | tf_op jit(solution)/shard_map/ppermute | solution.py:198
  72.0 16.8 %collective-permute-start.2 = (bf16[1024,128]{1,0:T(8,128)(2,1)}, bf16[1024,128]{1,0:T(8,128)(2,1)S(1)}, u32[]{:S(2)}, u32[]{:S(2)}) collective-permute-start(bf16[1024,128]{1,0:T(8,128)(2,1)} %get-tuple-element.18), channel_id=1, source_target_pairs={{0,448},{32,480},{64,0},{96,32},{128,64},{160,96},{192,128},{224,1... | collective-permute-start | bytes 786440 | tf_op jit(solution)/shard_map/ppermute | solution.py:198
  75.4 13.3 %collective-permute-start.6 = (bf16[1024,128]{1,0:T(8,128)(2,1)}, bf16[1024,128]{1,0:T(8,128)(2,1)S(1)}, u32[]{:S(2)}, u32[]{:S(2)}) collective-permute-start(bf16[1024,128]{1,0:T(8,128)(2,1)} %get-tuple-element.21), channel_id=1, source_target_pairs={{0,4},{4,0},{1,5},{5,1},{2,6},{6,2},{3,7},{7,3},{8,12},{12,8},{9,1... | collective-permute-start | bytes 786440 | tf_op jit(solution)/shard_map/ppermute | solution.py:202
  78.3 10.5 %collective-permute-start.8 = (bf16[1024,128]{1,0:T(8,128)(2,1)}, bf16[1024,128]{1,0:T(8,128)(2,1)S(1)}, u32[]{:S(2)}, u32[]{:S(2)}) collective-permute-start(bf16[1024,128]{1,0:T(8,128)(2,1)} %get-tuple-element.19), channel_id=1, source_target_pairs={{0,4},{4,0},{1,5},{5,1},{2,6},{6,2},{3,7},{7,3},{8,12},{12,8},{9,1... | collective-permute-start | bytes 786440 | tf_op jit(solution)/shard_map/ppermute | solution.py:202
  80.7 8.1 %collective-permute-start.7 = (bf16[1024,128]{1,0:T(8,128)(2,1)}, bf16[1024,128]{1,0:T(8,128)(2,1)S(1)}, u32[]{:S(2)}, u32[]{:S(2)}) collective-permute-start(bf16[1024,128]{1,0:T(8,128)(2,1)} %get-tuple-element.20), channel_id=1, source_target_pairs={{0,4},{4,0},{1,5},{5,1},{2,6},{6,2},{3,7},{7,3},{8,12},{12,8},{9,1... | collective-permute-start | bytes 786440 | tf_op jit(solution)/shard_map/ppermute | solution.py:202
  88.8 0.7 copy-start.4
  97.0 19.9 %collective-permute-start.10 = (bf16[1024,128]{1,0:T(8,128)(2,1)S(1)}, bf16[1024,128]{1,0:T(8,128)(2,1)S(1)}, u32[]{:S(2)}, u32[]{:S(2)}) collective-permute-start(bf16[1024,128]{1,0:T(8,128)(2,1)S(1)} %get-tuple-element.7), channel_id=1, source_target_pairs={{0,64},{32,96},{64,128},{96,160},{128,192},{160,224},{192,256},{22... | collective-permute-start | bytes 786440 | tf_op jit(solution)/shard_map/ppermute | solution.py:198
  107.1 12.0 %collective-permute-start.9 = (bf16[1024,128]{1,0:T(8,128)(2,1)S(1)}, bf16[1024,128]{1,0:T(8,128)(2,1)S(1)}, u32[]{:S(2)}, u32[]{:S(2)}) collective-permute-start(bf16[1024,128]{1,0:T(8,128)(2,1)S(1)} %get-tuple-element.7), channel_id=1, source_target_pairs={{0,448},{32,480},{64,0},{96,32},{128,64},{160,96},{192,128},{224,1... | collective-permute-start | bytes 786440 | tf_op jit(solution)/shard_map/ppermute | solution.py:198

commit v2 on v1

v2 whole, which is shorter than its diff:
```python
import functools

import jax
import jax.numpy as jnp
import numpy as np
from jax import lax
from jax.experimental import pallas as pl
from jax.experimental.pallas import tpu as pltpu
from jax.sharding import Mesh
from jax.sharding import PartitionSpec as P

HD = 128
TOK_TILE = 256
WIN = 9
COLS = 8
GROUP = ("half", "x", "core")
VMEM = pl.BlockSpec(memory_space=pltpu.VMEM)
SMEM = pl.BlockSpec(memory_space=pltpu.SMEM)
BF = jnp.bfloat16
F32 = jnp.float32
LIMIT = 48 * 1024 * 1024


def frequency_rows():
    pair = lax.broadcasted_iota(jnp.int32, (8, HD), 1) // 2
    nt = (HD - 4 * (HD // 6)) // 2
    ns = HD // 6
    rows = []
    for first, count in ((0, nt), (nt, ns), (nt + ns, ns)):
        within = (pair - first).astype(F32)
        freq = jnp.exp(within * float(-np.log(10000.0) / count))
        rows.append(jnp.where((pair >= first) & (pair < first + count), freq, 0.0)[0:1])
    return rows


def rotate_kernel(order, q_hbm, k_hbm, v_hbm, kv_ref, qv_ref, held, sems):
    x = lax.axis_index("x")
    frame_in_tile = lax.rem(x, 2) * 2 + lax.axis_index("core")
    slot = lax.axis_index("col") * 4 + lax.axis_index("half") * 2 + x // 2
    rows = held.shape[1]
    width = 2 * 3 * HD
    copies = []
    for part in range(4):
        for which, ref in enumerate((k_hbm, q_hbm, v_hbm)):
            columns = pl.ds(part * width, width)
            copies.append(
                pltpu.make_async_copy(
                    ref.at[:, columns], held.at[which, :, columns], sems.at[3 * part + which]
                )
            )
    for copy in copies:
        copy.start()
    tile = order[slot]
    frame = (tile // 32 * 4 + frame_in_tile).astype(F32)
    row0 = (tile // 8 % 4 * 8).astype(F32)
    col0 = (tile % 8 * 8).astype(F32)
    token = lax.broadcasted_iota(jnp.int32, (rows, HD), 0)
    row = row0 + (token // 8).astype(F32)
    col = col0 + (token % 8).astype(F32)
    by_frame, by_row, by_col = frequency_rows()
    angle = frame * by_frame + row * by_row + col * by_col
    cosine = jnp.cos(angle)
    sine = jnp.sin(angle)
    even = lax.broadcasted_iota(jnp.int32, (rows, HD), 1) % 2 == 0
    from_next = jnp.where(even, -sine, 0.0)
    from_last = jnp.where(even, 0.0, sine)
    scale = HD ** (-0.5) * 1.4426950408889634

    def turned(x, c, n, l):
        x = x.astype(F32)
        return (x * c + pltpu.roll(x, HD - 1, 1) * n + pltpu.roll(x, 1, 1) * l).astype(BF)

    qc, qn, ql = cosine * scale, from_next * scale, from_last * scale
    for part in range(4):
        for which in range(3):
            copies[3 * part + which].wait()
            for g in range(2 * part, 2 * part + 2):
                for h in range(3):
                    y = held[which, :, (3 * g + h) * HD : (3 * g + h + 1) * HD]
                    if which == 0:
                        y = turned(y, cosine, from_next, from_last)
                        out, head_row, shared_row = kv_ref, 0, 64
                    elif which == 1:
                        y = turned(y, qc, qn, ql)
                        out, head_row, shared_row = qv_ref, 0, 64
                    else:
                        out, head_row, shared_row = qv_ref, 96, 96
                    if h < 2:
                        out[2 * g + h, head_row : head_row + 64, :] = y
                    else:
                        if which == 2:
                            out = kv_ref
                        out[2 * g, shared_row : shared_row + 32, :] = y[0:32]
                        out[2 * g + 1, shared_row : shared_row + 32, :] = y[32:64]


def attend(q, kp, vp, picks, s_ref):
    rows = q.shape[0]
    top = None
    for j in range(WIN):
        s = lax.dot_general(q, kp[picks[j]], (((1,), (1,)), ((), ())), preferred_element_type=F32)
        s_ref[j, 0:rows, :] = s
        top = s if top is None else jnp.maximum(top, s)
    top = jnp.max(top, axis=1, keepdims=True)
    total = jnp.zeros((rows, TOK_TILE), F32)
    acc = jnp.zeros((rows, HD), F32)
    for j in range(WIN):
        p = jnp.exp2(s_ref[j, 0:rows, :] - top)
        total = total + p
        acc = acc + jnp.dot(p.astype(BF), vp[picks[j]], preferred_element_type=F32)
    return (acc / jnp.sum(total, axis=1, keepdims=True)).astype(BF)


def place(order):
    k = lax.axis_index("col")
    w = lax.rem(order[k * 4], COLS)
    from_left = (w == 1) | (w == 7)
    k_oth = lax.rem(jnp.where(from_left, k + 7, k + 1), COLS)
    return k, w, k_oth


def picks_of(nb, k, slot, one):
    picks = []
    for j in range(WIN):
        n = nb[slot, j]
        d = lax.rem(n // 4 - k + 8, 8)
        picks.append(jnp.where(d == 0, 0, jnp.where(d == one, 4, 8)) + lax.rem(n, 4))
    return picks


def whole(ref, *index):
    return ref[index].reshape(-1, HD)


def fill_head(w, kv, qv, r1, r2, l1, l2, kh, vh):
    for t in range(4):
        four = slice(4 * t, 4 * t + 4)
        kh[t] = whole(kv, four, slice(0, 64))
        vh[t] = whole(qv, four, slice(96, 160))
        vh[4 + t] = whole(r2, 1, four)
        vh[8 + t] = whole(l2, 1, four)

    for base, special, early, late in ((4, 6, r1, r2), (8, 1, l1, l2)):
        for condition, first in ((w == special, True), (w != special, False)):

            @pl.when(condition)
            def _(base=base, first=first, early=early, late=late):
                for t in range(4):
                    four = slice(4 * t, 4 * t + 4)
                    kh[base + t] = whole(early, four) if first else whole(late, 0, four)


def fill_shared(w, kv, r1, r2, l1, l2, sw, se, k2, v2):
    def put(base, mine, other):
        for t in range(4):
            four = slice(4 * t, 4 * t + 4)
            for pool, part in ((k2, slice(0, 32)), (v2, slice(32, 64))):
                pool[base + t, 0:128] = mine(four, part)
                pool[base + t, 128:256] = other(four, part)

    put(
        0,
        lambda f, p: whole(kv, f, slice(64 + p.start, 64 + p.stop)),
        lambda f, p: whole(sw, 0, f, p),
    )

    @pl.when(w != 7)
    def _():
        put(4, lambda f, p: whole(r1, f, p), lambda f, p: whole(sw, 2, f, p))

    @pl.when(w == 7)
    def _():
        put(4, lambda f, p: whole(l1, f, p), lambda f, p: whole(sw, 1, f, p))
        put(8, lambda f, p: whole(l2, 0, f, p), lambda f, p: whole(se, f, p))

    @pl.when(w == 0)
    def _():
        put(8, lambda f, p: whole(r2, 0, f, p), lambda f, p: whole(se, f, p))

    @pl.when((w != 0) & (w != 7))
    def _():
        put(8, lambda f, p: whole(l1, f, p), lambda f, p: whole(sw, 1, f, p))


def first_kernel(order, nb, kv, qv, r1, r2, l1, l2, o_head, o_oth, kh, vh, s_ref):
    k, w, k_oth = place(order)
    inner = (w == 1) | (w == 6)
    edge = (w == 0) | (w == 7)

    @pl.when(jnp.logical_not(edge))
    def _():
        fill_head(w, kv, qv, r1, r2, l1, l2, kh, vh)

    @pl.when(inner)
    def _():
        @pl.loop(0, 4)
        def _(t):
            four = pl.ds(t * 4, 4)
            q = jnp.where(w == 1, whole(l2, 0, four), whole(r2, 0, four))
            o = attend(q, kh, vh, picks_of(nb, k, k_oth * 4 + t, 1), s_ref)
            o_oth[four] = o.reshape(4, 64, HD)

    @pl.when(jnp.logical_not(inner | edge))
    def _():
        @pl.loop(0, 4)
        def _(t):
            four = pl.ds(t * 4, 4)
            q = whole(qv, four, slice(0, 64))
            o = attend(q, kh, vh, picks_of(nb, k, k * 4 + t, 1), s_ref)
            o_head[four] = o.reshape(4, 64, HD)


def edge_kernel(order, nb, kv, r1, r2, l1, l2, sw, se, o_in, o_oth, k2, v2, s_ref):
    del o_in
    k, w, k_oth = place(order)
    near = jnp.where(w == 7, 7, 1)

    @pl.when((w == 0) | (w == 7))
    def _():
        fill_shared(w, kv, r1, r2, l1, l2, sw, se, k2, v2)

        @pl.loop(0, 4)
        def _(t):
            four = pl.ds(t * 4, 4)
            q = jnp.where(
                w == 7, whole(l2, 1, four, slice(0, 32)), whole(r2, 1, four, slice(0, 32))
            )
            o = attend(q, k2, v2, picks_of(nb, k, k_oth * 4 + t, near), s_ref)
            o_oth[four, 0:32] = o.reshape(4, 32, HD)


def last_kernel(
    order, nb, kv, qv, r1, r2, l1, l2, sw, se, o_first, o_head, o_shared, kh, vh, k2, v2, s_ref
):
    k, w, _ = place(order)
    inner = (w == 1) | (w == 6)
    near = jnp.where(w == 7, 7, 1)

    @pl.when(inner)
    def _():
        fill_head(w, kv, qv, r1, r2, l1, l2, kh, vh)

        @pl.loop(0, 4)
        def _(t):
            four = pl.ds(t * 4, 4)
            q = whole(qv, four, slice(0, 64))
            o = attend(q, kh, vh, picks_of(nb, k, k * 4 + t, 1), s_ref)
            o_head[four] = o.reshape(4, 64, HD)

    @pl.when(jnp.logical_not(inner))
    def _():
        o_head[...] = o_first[...]
        fill_shared(w, kv, r1, r2, l1, l2, sw, se, k2, v2)

        @pl.loop(0, 4)
        def _(t):
            four = pl.ds(t * 4, 4)
            q = whole(qv, four, slice(64, 96))
            o = attend(q, k2, v2, picks_of(nb, k, k * 4 + t, near), s_ref)
            o_shared[four] = o.reshape(4, 32, HD)


def unpack_kernel(in_ref, out_ref):
    for g in range(8):
        for h in range(2):
            out_ref[:, (3 * g + h) * HD : (3 * g + h + 1) * HD] = in_ref[2 * g + h, 0:64, :]
        last = slice((3 * g + 2) * HD, (3 * g + 3) * HD)
        out_ref[0:32, last] = in_ref[2 * g, 64:96, :]
        out_ref[32:64, last] = in_ref[2 * g + 1, 64:96, :]


def along_columns(block, distance):
    n = 2 * COLS
    return lax.ppermute(block, ("col", "half"), [(i, (i + 2 * distance) % n) for i in range(n)])


def swapped(block):
    return lax.ppermute(block, "core", [(0, 1), (1, 0)])


POOL = pltpu.VMEM((12, TOK_TILE, HD), BF)
SCORES = pltpu.VMEM((WIN, TOK_TILE, TOK_TILE), F32)


def kernel(body, name, shapes, inputs, scratch=(), memory=None, aliases={}, limit=LIMIT):
    specs = [SMEM] * sum(i.dtype == jnp.int32 for i in inputs)
    specs += [memory or VMEM] * (len(inputs) - len(specs))
    return pl.pallas_call(
        body,
        out_shape=tuple(jax.ShapeDtypeStruct(shape, BF) for shape in shapes),
        in_specs=specs,
        out_specs=(VMEM,) * len(shapes),
        scratch_shapes=list(scratch),
        input_output_aliases=aliases,
        compiler_params=pltpu.CompilerParams(vmem_limit_bytes=limit),
        name=name,
    )(*inputs)


def shards(queries, keys, values, order, nb):
    w = order[lax.axis_index("col") * 4] % COLS
    kv, qv = kernel(
        rotate_kernel,
        "rotate",
        ((16, 128, HD), (16, 160, HD)),
        (order, queries, keys, values),
        (pltpu.VMEM((3,) + queries.shape, BF), pltpu.SemaphoreType.DMA((12,))),
        memory=pl.BlockSpec(memory_space=pl.ANY),
        limit=60 * 1024 * 1024,
    )
    kv = lax.all_to_all(kv, GROUP, split_axis=0, concat_axis=0, tiled=True)
    k_head, shared = kv[:, 0:64], kv[:, 64:128]
    r1 = along_columns(jnp.where(w == 7, k_head, shared), -1)
    l1 = along_columns(jnp.where(w == 0, k_head, shared), 1)
    qv = lax.all_to_all(qv, GROUP, split_axis=0, concat_axis=0, tiled=True)
    q_head, q_shared, v_head = qv[:, 0:64], qv[:, 64:128], qv[:, 96:160]

    def second(early, near_edge, far_edge):
        return jnp.stack(
            [
                jnp.where(w == near_edge, early, jnp.where(w == far_edge, q_head, k_head)),
                jnp.where(w == near_edge, q_shared, v_head),
            ]
        )

    r2 = along_columns(second(r1, 1, 7), -1)
    l2 = along_columns(second(l1, 6, 0), 1)
    sw = swapped(jnp.stack([shared, l1, r1]))
    se = swapped(jnp.where(w == 0, r2[0], l2[0]))
    o_first, o_oth = kernel(
        first_kernel,
        "attend_first",
        ((16, 64, HD), (16, 64, HD)),
        (order, nb, kv, qv, r1, r2, l1, l2),
        (POOL, POOL, SCORES),
    )
    (o_oth,) = kernel(
        edge_kernel,
        "attend_edge",
        ((16, 64, HD),),
        (order, nb, kv, r1, r2, l1, l2, sw, se, o_oth),
        (POOL, POOL, SCORES),
        aliases={9: 0},
    )
    o_right = along_columns(o_oth, -1)
    o_left = along_columns(o_oth, 1)
    o_head, o_shared = kernel(
        last_kernel,
        "attend_last",
        ((16, 64, HD), (16, 32, HD)),
        (order, nb, kv, qv, r1, r2, l1, l2, sw, se, o_first),
        (POOL, POOL, POOL, POOL, SCORES),
    )
    o_head = jnp.where(w == 0, o_right, jnp.where(w == 7, o_left, o_head))
    o_shared = jnp.where(
        w == 1, o_left[:, 0:32], jnp.where(w == 6, o_right[:, 0:32], o_shared)
    )
    sent = jnp.concatenate([o_head, o_shared], axis=1)
    back = lax.all_to_all(sent, GROUP, split_axis=0, concat_axis=0, tiled=True)
    return kernel(unpack_kernel, "unpack", (queries.shape,), (back,))[0]


def solution(mesh):
    blk, uly, dp = (mesh.shape[name] for name in ("blk", "uly", "dp"))
    fine = Mesh(
        mesh.devices.reshape(blk // 2, 2, uly // 2, 2, dp), ("col", "half", "x", "core", "dp")
    )
    tokens = ("dp", "col", "half", "x", "core")
    placed = (P(tokens, None), P(tokens, None), P(tokens, None), P("dp"), P("dp", None))
    return jax.shard_map(
        shards, mesh=fine, in_specs=placed, out_specs=P(tokens, None), check_vma=False
    )
```

time: 137 us -> 132 us (0.964)
  starting transfers between devices: 52.8 us -> 33.8 us
  blocking collectives: 15.3 us -> 30.8 us
  Pallas kernels: 10.7 us -> 15.9 us
  local copies, waits for them, and re-layouts: 7.21 us -> 2.67 us
  other arithmetic: 3.48 us -> 2.08 us
    ppermute x8 -> x6, waiting for transfers between devices: 25.7 us -> 44 us  [along_columns(): lax.ppermute(block, ('col', 'half'), [(i, (i + 2 * distance) % n) for i i...]
    all_to_all x1, waiting for transfers between devices: 18.1 us -> 0.01 us  [shards(): qv = lax.all_to_all(qv, GROUP, split_axis=0, concat_axis=0, tiled=True)]
    all_to_all x0 -> x1, blocking collectives: none -> 16.6 us  [shards(): kv = lax.all_to_all(kv, GROUP, split_axis=0, concat_axis=0, tiled=True)]
    ppermute x8 -> x6, starting transfers between devices: 40.8 us -> 26.4 us  [along_columns(): lax.ppermute(block, ('col', 'half'), [(i, (i + 2 * distance) % n) for i i...]
    pallas_call x3 -> x5, Pallas kernels: 10.7 us -> 15.9 us  [kernel(): pl.pallas_call(body, out_shape=tuple((jax.ShapeDtypeStruct(shape, BF) for...]
    unnamed x13 -> x5, local copies, waits for them, and re-layouts: 5.69 us -> 2.08 us
    ppermute x3 -> x2, starting transfers between devices: 6.23 us -> 3.82 us  [swapped(): return lax.ppermute(block, 'core', [(0, 1), (1, 0)])]
    all_to_all x1, starting transfers between devices: 5.76 us -> 3.59 us  [shards(): qv = lax.all_to_all(qv, GROUP, split_axis=0, concat_axis=0, tiled=True)]
  transfers between devices with their start and end apart: 12 -> 9, of which waited for: 6 -> 6; matrix products, arithmetic and copies ran while one was open for 2% -> 2% of each run, Pallas kernels for 0% -> 8%
where the time goes in v2:
time: 132 us; the launch traced here: 131 us
  waiting for transfers between devices  44 us (33%)
  starting transfers between devices  33.8 us (26%)
  blocking collectives  30.8 us (23%)
  Pallas kernels  15.9 us (12%)
  local copies, waits for them, and re-layouts  2.67 us (2%)
  between operations  2.14 us (2%)
  other arithmetic  2.08 us (2%)
    ppermute x6, waiting for transfers between devices, along_columns(): lax.ppermute(block, ('col', 'half'), [(i, (i + 2 * distance) % n) for i i...  44 us
    ppermute x6, starting transfers between devices, along_columns(): lax.ppermute(block, ('col', 'half'), [(i, (i + 2 * distance) % n) for i i...  26.4 us
    all_to_all x1, blocking collectives, shards(): kv = lax.all_to_all(kv, GROUP, split_axis=0, concat_axis=0, tiled=True)  16.6 us
    pallas_call x5, Pallas kernels, kernel(): pl.pallas_call(body, out_shape=tuple((jax.ShapeDtypeStruct(shape, BF) for...  15.9 us
    all_to_all x1, blocking collectives, shards(): back = lax.all_to_all(sent, GROUP, split_axis=0, concat_axis=0, tiled=True)  14.1 us
    ppermute x2, starting transfers between devices, swapped(): return lax.ppermute(block, 'core', [(0, 1), (1, 0)])  3.82 us
    all_to_all x1, starting transfers between devices, shards(): qv = lax.all_to_all(qv, GROUP, split_axis=0, concat_axis=0, tiled=True)  3.59 us
  transfers between devices with their start and end apart: 9, of which 6 were waited for; matrix products, arithmetic and copies ran while one was open for 2% of the time, Pallas kernels for 8%

profile of v2, /device:TPU:24, one launch (start us, length us, event | category | flops | bytes accessed | tf_op | source)
XLA Modules:
  0.0 131.3 jit_solution(17573534863890535340)
XLA Ops:
  0.0 3.8 %rotate.1 = (bf16[16,128,128]{2,1,0:T(8,128)(2,1)}, bf16[16,160,128]{2,1,0:T(8,128)(2,1)}) custom-call(s32[32]{0:T(128)} %order.7, bf16[64,3072]{1,0:T(8,128)(2,1)} %q_hbm.1, bf16[64,3072]{1,0:T(8,128)(2,1)} %k_hbm.1, bf16[64,3072]{1,0:T(8,128)(2,1)} %v_hbm.1), custom_call_target="tpu_custom_call" | custom-call | tf_op jit(solution)/shard_map/rotate/pallas_call | solution.py:288
  3.8 16.6 %all_to_all.15.kv = bf16[16,128,128]{2,1,0:T(8,128)(2,1)S(1)} all-to-all(bf16[16,128,128]{2,1,0:T(8,128)(2,1)} %get-tuple-element.11), channel_id=1, replica_groups=mesh['col'=8,'half'=2,'x'=4,'core'=2,'dp'=4] {'half','x','core'}, dimensions={0} | all-to-all | bytes 1048576 | tf_op jit(solution)/shard_map/all_to_all | solution.py:311
  20.5 3.6 %all-to-all-start.1 = ((bf16[16,160,128]{2,1,0:T(8,128)(2,1)}), bf16[16,160,128]{2,1,0:T(8,128)(2,1)S(1)}, u32[]{:S(2)}, u32[]{:S(2)}) async-start(bf16[16,160,128]{2,1,0:T(8,128)(2,1)} %get-tuple-element.12), calls=%async_computation.1 | async-start | bytes 1310720 | tf_op jit(solution)/shard_map/all_to_all | solution.py:315
  24.1 0.0 copy-start
  24.1 0.6 copy-done
  24.7 0.6 dynamic_slice.3
  27.3 10.9 %collective-permute-start = (bf16[16,64,128]{2,1,0:T(8,128)(2,1)S(1)}, bf16[16,64,128]{2,1,0:T(8,128)(2,1)S(1)}, u32[]{:S(2)}, u32[]{:S(2)}) collective-permute-start(bf16[16,64,128]{2,1,0:T(8,128)(2,1)S(1)} %get-tuple-element.23), channel_id=1, source_target_pairs={{0,448},{32,480},{64,0},{96,32},{128,64},{160,96},{192,128},{224,1... | collective-permute-start | bytes 786440 | tf_op jit(solution)/shard_map/ppermute | solution.py:274
  38.3 1.9 %collective-permute-start.2 = (bf16[16,64,128]{2,1,0:T(8,128)(2,1)S(1)}, bf16[16,64,128]{2,1,0:T(8,128)(2,1)S(1)}, u32[]{:S(2)}, u32[]{:S(2)}) collective-permute-start(bf16[16,64,128]{2,1,0:T(8,128)(2,1)S(1)} %get-tuple-element.22), channel_id=1, source_target_pairs={{0,64},{32,96},{64,128},{96,160},{128,192},{160,224},{192,256},{22... | collective-permute-start | bytes 786440 | tf_op jit(solution)/shard_map/ppermute | solution.py:274
  40.2 9.7 %collective-permute-done.r1 = bf16[16,64,128]{2,1,0:T(8,128)(2,1)S(1)} collective-permute-done((bf16[16,64,128]{2,1,0:T(8,128)(2,1)S(1)}, bf16[16,64,128]{2,1,0:T(8,128)(2,1)S(1)}, u32[]{:S(2)}, u32[]{:S(2)}) %collective-permute-start) | collective-permute-done | bytes 262176 | tf_op jit(solution)/shard_map/ppermute | solution.py:274
  49.9 6.3 %collective-permute-done.2.l1 = bf16[16,64,128]{2,1,0:T(8,128)(2,1)S(1)} collective-permute-done((bf16[16,64,128]{2,1,0:T(8,128)(2,1)S(1)}, bf16[16,64,128]{2,1,0:T(8,128)(2,1)S(1)}, u32[]{:S(2)}, u32[]{:S(2)}) %collective-permute-start.2) | collective-permute-done | bytes 262176 | tf_op jit(solution)/shard_map/ppermute | solution.py:274
  56.1 0.0 all-to-all-done.1.qv
  56.2 0.1 select_bitcast_fusion.1
  56.3 0.1 pad_maximum_fusion.1
  56.3 1.9 %collective-permute-start.1 = (bf16[2,16,64,128]{3,2,1,0:T(8,128)(2,1)S(1)}, bf16[2,16,64,128]{3,2,1,0:T(8,128)(2,1)S(1)}, u32[]{:S(2)}, u32[]{:S(2)}) collective-permute-start(bf16[2,16,64,128]{3,2,1,0:T(8,128)(2,1)S(1)} %pad_maximum_fusion.1), channel_id=1, source_target_pairs={{0,448},{32,480},{64,0},{96,32},{128,64},{160,96},{192,128},{224,1... | collective-permute-start | bytes 1572872 | tf_op jit(solution)/shard_map/ppermute | solution.py:274
  58.2 0.1 pad_maximum_fusion.2
  58.3 4.8 %collective-permute-start.3 = (bf16[2,16,64,128]{3,2,1,0:T(8,128)(2,1)S(1)}, bf16[2,16,64,128]{3,2,1,0:T(8,128)(2,1)S(1)}, u32[]{:S(2)}, u32[]{:S(2)}) collective-permute-start(bf16[2,16,64,128]{3,2,1,0:T(8,128)(2,1)S(1)} %pad_maximum_fusion.2), channel_id=1, source_target_pairs={{0,64},{32,96},{64,128},{96,160},{128,192},{160,224},{192,256},{22... | collective-permute-start | bytes 1572872 | tf_op jit(solution)/shard_map/ppermute | solution.py:274
  63.1 1.0 pad_maximum_fusion
  64.1 1.9 %collective-permute-start.4 = (bf16[3,16,64,128]{3,2,1,0:T(8,128)(2,1)}, bf16[3,16,64,128]{3,2,1,0:T(8,128)(2,1)S(1)}, u32[]{:S(2)}, u32[]{:S(2)}) collective-permute-start(bf16[3,16,64,128]{3,2,1,0:T(8,128)(2,1)} %pad_maximum_fusion), channel_id=1, source_target_pairs={{0,4},{4,0},{1,5},{5,1},{2,6},{6,2},{3,7},{7,3},{8,12},{12,8},{9,1... | collective-permute-start | bytes 2359304 | tf_op jit(solution)/shard_map/ppermute | solution.py:278
  66.0 13.4 %collective-permute-done.1.r2 = bf16[2,16,64,128]{3,2,1,0:T(8,128)(2,1)S(1)} collective-permute-done((bf16[2,16,64,128]{3,2,1,0:T(8,128)(2,1)S(1)}, bf16[2,16,64,128]{3,2,1,0:T(8,128)(2,1)S(1)}, u32[]{:S(2)}, u32[]{:S(2)}) %collective-permute-start.1) | collective-permute-done | bytes 524320 | tf_op jit(solution)/shard_map/ppermute | solution.py:274
  79.4 5.6 %collective-permute-done.3.l2 = bf16[2,16,64,128]{3,2,1,0:T(8,128)(2,1)S(1)} collective-permute-done((bf16[2,16,64,128]{3,2,1,0:T(8,128)(2,1)S(1)}, bf16[2,16,64,128]{3,2,1,0:T(8,128)(2,1)S(1)}, u32[]{:S(2)}, u32[]{:S(2)}) %collective-permute-start.3) | collective-permute-done | bytes 524320 | tf_op jit(solution)/shard_map/ppermute | solution.py:274
  85.0 0.7 fusion
  85.7 1.9 %collective-permute-start.5 = (bf16[16,64,128]{2,1,0:T(8,128)(2,1)}, bf16[16,64,128]{2,1,0:T(8,128)(2,1)}, u32[]{:S(2)}, u32[]{:S(2)}) collective-permute-start(bf16[16,64,128]{2,1,0:T(8,128)(2,1)} %fusion), channel_id=1, source_target_pairs={{0,4},{4,0},{1,5},{5,1},{2,6},{6,2},{3,7},{7,3},{8,12},{12,8},{9,1... | collective-permute-start | bytes 786440 | tf_op jit(solution)/shard_map/ppermute | solution.py:278
  87.6 0.8 copy.8.nb
  88.4 0.0 copy-start.1
  88.4 0.7 copy-done.1
  89.0 5.9 %attend_first.1 = (bf16[16,64,128]{2,1,0:T(8,128)(2,1)S(1)}, bf16[16,64,128]{2,1,0:T(8,128)(2,1)S(1)}) custom-call(s32[32]{0:T(128)S(1)} %copy-done.1, s32[32,9]{1,0:T(8,128)S(1)} %copy.8.nb, bf16[16,128,128]{2,1,0:T(8,128)(2,1)S(1)} %all_to_all.15.kv, bf16[16,160,128]{2,1,0:T(8,128)(2,1)S(1)} %all-to-all-done.1.qv, ...), custom_call_target="tpu_custom_call" | custom-call | tf_op jit(solution)/shard_map/attend_first/pallas_call | solution.py:288
  94.9 0.0 collective-permute-done.4.sw
  94.9 0.0 collective-permute-done.5.se
  95.0 1.0 attend_edge.1
  95.9 1.9 %collective-permute-start.6 = (bf16[16,64,128]{2,1,0:T(8,128)(2,1)S(1)}, bf16[16,64,128]{2,1,0:T(8,128)(2,1)S(1)}, u32[]{:S(2)}, u32[]{:S(2)}) collective-permute-start(bf16[16,64,128]{2,1,0:T(8,128)(2,1)S(1)} %attend_edge.1), channel_id=1, source_target_pairs={{0,448},{32,480},{64,0},{96,32},{128,64},{160,96},{192,128},{224,1... | collective-permute-start | bytes 786440 | tf_op jit(solution)/shard_map/ppermute | solution.py:274
  97.9 4.8 %collective-permute-start.7 = (bf16[16,64,128]{2,1,0:T(8,128)(2,1)S(1)}, bf16[16,64,128]{2,1,0:T(8,128)(2,1)S(1)}, u32[]{:S(2)}, u32[]{:S(2)}) collective-permute-start(bf16[16,64,128]{2,1,0:T(8,128)(2,1)S(1)} %attend_edge.1), channel_id=1, source_target_pairs={{0,64},{32,96},{64,128},{96,160},{128,192},{160,224},{192,256},{22... | collective-permute-start | bytes 786440 | tf_op jit(solution)/shard_map/ppermute | solution.py:274
  102.7 4.4 %attend_last.1 = (bf16[16,64,128]{2,1,0:T(8,128)(2,1)S(1)}, bf16[16,32,128]{2,1,0:T(8,128)(2,1)S(1)}) custom-call(s32[32]{0:T(128)S(1)} %copy-done.1, s32[32,9]{1,0:T(8,128)S(1)} %copy.8.nb, bf16[16,128,128]{2,1,0:T(8,128)(2,1)S(1)} %all_to_all.15.kv, bf16[16,160,128]{2,1,0:T(8,128)(2,1)S(1)} %all-to-all-done.1.qv, ...), custom_call_target="tpu_custom_call" | custom-call | tf_op jit(solution)/shard_map/attend_last/pallas_call | solution.py:288
  107.1 6.0 %collective-permute-done.6 = bf16[16,64,128]{2,1,0:T(8,128)(2,1)S(1)} collective-permute-done((bf16[16,64,128]{2,1,0:T(8,128)(2,1)S(1)}, bf16[16,64,128]{2,1,0:T(8,128)(2,1)S(1)}, u32[]{:S(2)}, u32[]{:S(2)}) %collective-permute-start.6) | collective-permute-done | bytes 262176 | tf_op jit(solution)/shard_map/ppermute | solution.py:274
  113.0 3.2 %collective-permute-done.7 = bf16[16,64,128]{2,1,0:T(8,128)(2,1)S(1)} collective-permute-done((bf16[16,64,128]{2,1,0:T(8,128)(2,1)S(1)}, bf16[16,64,128]{2,1,0:T(8,128)(2,1)S(1)}, u32[]{:S(2)}, u32[]{:S(2)}) %collective-permute-start.7) | collective-permute-done | bytes 262176 | tf_op jit(solution)/shard_map/ppermute | solution.py:274
  116.3 0.1 select_select_fusion
  116.4 14.1 %all_to_all.16.in_ref = bf16[16,96,128]{2,1,0:T(8,128)(2,1)S(1)} all-to-all(bf16[16,96,128]{2,1,0:T(8,128)(2,1)S(1)} %pad_maximum_fusion.3), channel_id=1, replica_groups=mesh['col'=8,'half'=2,'x'=4,'core'=2,'dp'=4] {'half','x','core'}, dimensions={0} | all-to-all | bytes 786432 | tf_op jit(solution)/shard_map/all_to_all | solution.py:359
  130.5 0.8 unpack.1
  (3 shorter events, 0.1 us)
Async XLA Ops:
  20.5 35.7 %all-to-all-start.1 = ((bf16[16,160,128]{2,1,0:T(8,128)(2,1)}), bf16[16,160,128]{2,1,0:T(8,128)(2,1)S(1)}, u32[]{:S(2)}, u32[]{:S(2)}) async-start(bf16[16,160,128]{2,1,0:T(8,128)(2,1)} %get-tuple-element.12), calls=%async_computation.1 | async-start | bytes 1310720 | tf_op jit(solution)/shard_map/all_to_all | solution.py:315
  24.1 0.7 copy-start
  27.3 22.6 %collective-permute-start = (bf16[16,64,128]{2,1,0:T(8,128)(2,1)S(1)}, bf16[16,64,128]{2,1,0:T(8,128)(2,1)S(1)}, u32[]{:S(2)}, u32[]{:S(2)}) collective-permute-start(bf16[16,64,128]{2,1,0:T(8,128)(2,1)S(1)} %get-tuple-element.23), channel_id=1, source_target_pairs={{0,448},{32,480},{64,0},{96,32},{128,64},{160,96},{192,128},{224,1... | collective-permute-start | bytes 786440 | tf_op jit(solution)/shard_map/ppermute | solution.py:274
  38.3 17.9 %collective-permute-start.2 = (bf16[16,64,128]{2,1,0:T(8,128)(2,1)S(1)}, bf16[16,64,128]{2,1,0:T(8,128)(2,1)S(1)}, u32[]{:S(2)}, u32[]{:S(2)}) collective-permute-start(bf16[16,64,128]{2,1,0:T(8,128)(2,1)S(1)} %get-tuple-element.22), channel_id=1, source_target_pairs={{0,64},{32,96},{64,128},{96,160},{128,192},{160,224},{192,256},{22... | collective-permute-start | bytes 786440 | tf_op jit(solution)/shard_map/ppermute | solution.py:274
  56.3 23.1 %collective-permute-start.1 = (bf16[2,16,64,128]{3,2,1,0:T(8,128)(2,1)S(1)}, bf16[2,16,64,128]{3,2,1,0:T(8,128)(2,1)S(1)}, u32[]{:S(2)}, u32[]{:S(2)}) collective-permute-start(bf16[2,16,64,128]{3,2,1,0:T(8,128)(2,1)S(1)} %pad_maximum_fusion.1), channel_id=1, source_target_pairs={{0,448},{32,480},{64,0},{96,32},{128,64},{160,96},{192,128},{224,1... | collective-permute-start | bytes 1572872 | tf_op jit(solution)/shard_map/ppermute | solution.py:274
  58.3 26.7 %collective-permute-start.3 = (bf16[2,16,64,128]{3,2,1,0:T(8,128)(2,1)S(1)}, bf16[2,16,64,128]{3,2,1,0:T(8,128)(2,1)S(1)}, u32[]{:S(2)}, u32[]{:S(2)}) collective-permute-start(bf16[2,16,64,128]{3,2,1,0:T(8,128)(2,1)S(1)} %pad_maximum_fusion.2), channel_id=1, source_target_pairs={{0,64},{32,96},{64,128},{96,160},{128,192},{160,224},{192,256},{22... | collective-permute-start | bytes 1572872 | tf_op jit(solution)/shard_map/ppermute | solution.py:274
  64.1 30.8 %collective-permute-start.4 = (bf16[3,16,64,128]{3,2,1,0:T(8,128)(2,1)}, bf16[3,16,64,128]{3,2,1,0:T(8,128)(2,1)S(1)}, u32[]{:S(2)}, u32[]{:S(2)}) collective-permute-start(bf16[3,16,64,128]{3,2,1,0:T(8,128)(2,1)} %pad_maximum_fusion), channel_id=1, source_target_pairs={{0,4},{4,0},{1,5},{5,1},{2,6},{6,2},{3,7},{7,3},{8,12},{12,8},{9,1... | collective-permute-start | bytes 2359304 | tf_op jit(solution)/shard_map/ppermute | solution.py:278
  85.7 9.3 %collective-permute-start.5 = (bf16[16,64,128]{2,1,0:T(8,128)(2,1)}, bf16[16,64,128]{2,1,0:T(8,128)(2,1)}, u32[]{:S(2)}, u32[]{:S(2)}) collective-permute-start(bf16[16,64,128]{2,1,0:T(8,128)(2,1)} %fusion), channel_id=1, source_target_pairs={{0,4},{4,0},{1,5},{5,1},{2,6},{6,2},{3,7},{7,3},{8,12},{12,8},{9,1... | collective-permute-start | bytes 786440 | tf_op jit(solution)/shard_map/ppermute | solution.py:278
  88.4 0.7 copy-start.1
  95.9 17.1 %collective-permute-start.6 = (bf16[16,64,128]{2,1,0:T(8,128)(2,1)S(1)}, bf16[16,64,128]{2,1,0:T(8,128)(2,1)S(1)}, u32[]{:S(2)}, u32[]{:S(2)}) collective-permute-start(bf16[16,64,128]{2,1,0:T(8,128)(2,1)S(1)} %attend_edge.1), channel_id=1, source_target_pairs={{0,448},{32,480},{64,0},{96,32},{128,64},{160,96},{192,128},{224,1... | collective-permute-start | bytes 786440 | tf_op jit(solution)/shard_map/ppermute | solution.py:274
  97.9 18.4 %collective-permute-start.7 = (bf16[16,64,128]{2,1,0:T(8,128)(2,1)S(1)}, bf16[16,64,128]{2,1,0:T(8,128)(2,1)S(1)}, u32[]{:S(2)}, u32[]{:S(2)}) collective-permute-start(bf16[16,64,128]{2,1,0:T(8,128)(2,1)S(1)} %attend_edge.1), channel_id=1, source_target_pairs={{0,64},{32,96},{64,128},{96,160},{128,192},{160,224},{192,256},{22... | collective-permute-start | bytes 786440 | tf_op jit(solution)/shard_map/ppermute | solution.py:274

commit v3 on v2

v3 whole, which is shorter than its diff:
```python
import jax
import jax.numpy as jnp
import numpy as np
from jax import lax
from jax.experimental import pallas as pl
from jax.experimental.pallas import tpu as pltpu
from jax.sharding import Mesh
from jax.sharding import PartitionSpec as P

HD = 128
TOK_TILE = 256
WIN = 9
COLS = 8
GROUP = ("half", "x", "core")
VMEM = pl.BlockSpec(memory_space=pltpu.VMEM)
SMEM = pl.BlockSpec(memory_space=pltpu.SMEM)
ANY = pl.BlockSpec(memory_space=pl.ANY)
BF = jnp.bfloat16
F32 = jnp.float32
MIB = 1024 * 1024
MAIN, VALUE, QUERY, REST = slice(0, 64), slice(64, 128), slice(128, 160), slice(160, 224)
AT_W, AT_HEAD, AT_SHARED = 0, 16, 96


def frequency_rows():
    pair = lax.broadcasted_iota(jnp.int32, (8, HD), 1) // 2
    nt = (HD - 4 * (HD // 6)) // 2
    ns = HD // 6
    rows = []
    for first, count in ((0, nt), (nt, ns), (nt + ns, ns)):
        within = (pair - first).astype(F32)
        freq = jnp.exp(within * float(-np.log(10000.0) / count))
        rows.append(jnp.where((pair >= first) & (pair < first + count), freq, 0.0)[0:1])
    return rows


def plan(order, nb, table):
    k = lax.axis_index("col")
    w = lax.rem(order[k * 4], COLS)
    table[AT_W] = w
    k_oth = lax.rem(jnp.where((w == 1) | (w == 7), k + 7, k + 1), COLS)
    near = jnp.where(w == 7, 7, 1)
    for u in range(8):
        slot = k_oth * 4 + u if u < 4 else k * 4 + u - 4
        for j in range(WIN):
            n = nb[j, slot]
            d = lax.rem(n // 4 - k + COLS, COLS)
            t = lax.rem(n, 4)
            table[AT_HEAD + WIN * u + j] = jnp.where(d == 0, 0, jnp.where(d == 1, 4, 8)) + t
            table[AT_SHARED + WIN * u + j] = jnp.where(d == 0, 0, jnp.where(d == near, 4, 8)) + t
    return w


def rotate_kernel(order, nb, q_hbm, k_hbm, v_hbm, one, two, table, held, sems):
    x = lax.axis_index("x")
    frame_in_tile = lax.rem(x, 2) * 2 + lax.axis_index("core")
    slot = lax.axis_index("col") * 4 + lax.axis_index("half") * 2 + x // 2
    rows = held.shape[1]
    width = 2 * 3 * HD
    copies = []
    for part in range(4):
        for which, ref in enumerate((k_hbm, q_hbm, v_hbm)):
            columns = pl.ds(part * width, width)
            copies.append(
                pltpu.make_async_copy(
                    ref.at[:, columns], held.at[which, :, columns], sems.at[3 * part + which]
                )
            )
    for copy in copies:
        copy.start()
    w = plan(order, nb, table)
    edge = (w == 0) | (w == 7)
    tile = order[slot]
    frame = (tile // 32 * 4 + frame_in_tile).astype(F32)
    row0 = (tile // 8 % 4 * 8).astype(F32)
    col0 = (tile % 8 * 8).astype(F32)
    token = lax.broadcasted_iota(jnp.int32, (rows, HD), 0)
    row = row0 + (token // 8).astype(F32)
    col = col0 + (token % 8).astype(F32)
    by_frame, by_row, by_col = frequency_rows()
    angle = frame * by_frame + row * by_row + col * by_col
    cosine = jnp.cos(angle)
    sine = jnp.sin(angle)
    even = lax.broadcasted_iota(jnp.int32, (rows, HD), 1) % 2 == 0
    from_next = jnp.where(even, -sine, 0.0)
    from_last = jnp.where(even, 0.0, sine)
    scale = HD ** (-0.5) * 1.4426950408889634

    def turned(x, c, n, l):
        x = x.astype(F32)
        return (x * c + pltpu.roll(x, HD - 1, 1) * n + pltpu.roll(x, 1, 1) * l).astype(BF)

    qc, qn, ql = cosine * scale, from_next * scale, from_last * scale
    for part in range(4):
        for which in range(3):
            copies[3 * part + which].wait()
        for g in range(2 * part, 2 * part + 2):
            for h in range(3):
                at = slice((3 * g + h) * HD, (3 * g + h + 1) * HD)
                key = turned(held[0, :, at], cosine, from_next, from_last)
                query = turned(held[1, :, at], qc, qn, ql)
                value = held[2, :, at]
                if h < 2:
                    to = 2 * g + h
                    two[to, VALUE, :] = value

                    @pl.when(edge)
                    def _(to=to, key=key, query=query):
                        one[to] = key
                        two[to, MAIN, :] = query

                    @pl.when(jnp.logical_not(edge))
                    def _(to=to, key=key, query=query):
                        two[to, MAIN, :] = key
                        two[to, REST, :] = query

                else:
                    for c in range(2):
                        to = 2 * g + c
                        part_of = slice(32 * c, 32 * c + 32)
                        two[to, QUERY, :] = query[part_of]

                        @pl.when(edge)
                        def _(to=to, part_of=part_of, key=key, value=value):
                            two[to, REST.start : REST.start + 32, :] = key[part_of]
                            two[to, REST.start + 32 : REST.stop, :] = value[part_of]

                        @pl.when(jnp.logical_not(edge))
                        def _(to=to, part_of=part_of, key=key, value=value):
                            one[to, 0:32, :] = key[part_of]
                            one[to, 32:64, :] = value[part_of]


def second_kernel(table, one, two, l1, r1, main_left, main_right, value_left, value_right, swap):
    w = table[AT_W]

    @pl.when(w == 1)
    def _():
        main_left[...] = r1[...]
        value_left[:, 0:32] = two[:, QUERY]
        value_left[:, 32:64] = two[:, QUERY]

    @pl.when(w != 1)
    def _():
        main_left[...] = two[:, MAIN]
        value_left[...] = two[:, VALUE]

    @pl.when(w == 6)
    def _():
        main_right[...] = l1[...]
        value_right[:, 0:32] = two[:, QUERY]
        value_right[:, 32:64] = two[:, QUERY]

    @pl.when(w != 6)
    def _():
        main_right[...] = two[:, MAIN]
        value_right[...] = two[:, VALUE]

    @pl.when((w == 0) | (w == 7))
    def _():
        swap[0] = two[:, REST]

    @pl.when((w != 0) & (w != 7))
    def _():
        swap[0] = one[...]

    swap[1] = l1[...]
    swap[2] = r1[...]


def attend(q, kp, vp, picks, s_ref):
    rows = q.shape[0]
    top = None
    for j in range(WIN):
        s = lax.dot_general(q, kp[picks[j]], (((1,), (1,)), ((), ())), preferred_element_type=F32)
        s_ref[j, 0:rows, :] = s
        top = s if top is None else jnp.maximum(top, s)
    top = jnp.max(top, axis=1, keepdims=True)
    total = jnp.zeros((rows, TOK_TILE), F32)
    acc = jnp.zeros((rows, HD), F32)
    for j in range(WIN):
        p = jnp.exp2(s_ref[j, 0:rows, :] - top)
        total = total + p
        acc = acc + jnp.dot(p.astype(BF), vp[picks[j]], preferred_element_type=F32)
    return (acc / jnp.sum(total, axis=1, keepdims=True)).astype(BF)


def picks_of(table, at, u):
    return [table[at + u * WIN + j] for j in range(WIN)]


def whole(ref, *index):
    return ref[index].reshape(-1, HD)


def fill_shared(base, mine, other, k2, v2):
    for t in range(4):
        four = slice(4 * t, 4 * t + 4)
        for pool, part in ((k2, slice(0, 32)), (v2, slice(32, 64))):
            pool[base + t, 0:128] = mine(four, part)
            pool[base + t, 128:256] = other(four, part)


def first_kernel(
    table, two, l1, r1, l2, r2, l3, r3, sw, se, sent, o_oth, kh, vh, k2, v2, s_ref
):
    w = table[AT_W]
    inner = (w == 1) | (w == 6)
    edge = (w == 0) | (w == 7)

    @pl.when(jnp.logical_not(edge))
    def _():
        for t in range(4):
            four = slice(4 * t, 4 * t + 4)
            kh[t] = whole(two, four, MAIN)
            vh[t] = whole(two, four, VALUE)
            vh[4 + t] = whole(r3, four)
            vh[8 + t] = whole(l3, four)
        for base, special, early, late in ((4, 6, r1, r2), (8, 1, l1, l2)):
            for condition, source in ((w == special, early), (w != special, late)):

                @pl.when(condition)
                def _(base=base, source=source):
                    for t in range(4):
                        kh[base + t] = whole(source, slice(4 * t, 4 * t + 4))

    @pl.when(inner)
    def _():
        @pl.loop(0, 4)
        def _(t):
            four = pl.ds(t * 4, 4)
            q = jnp.where(w == 1, whole(l2, four), whole(r2, four))
            o = attend(q, kh, vh, picks_of(table, AT_HEAD, t), s_ref)
            o_oth[four] = o.reshape(4, 64, HD)

    @pl.when(jnp.logical_not(inner | edge))
    def _():
        @pl.loop(0, 4)
        def _(t):
            four = pl.ds(t * 4, 4)
            o = attend(whole(two, four, REST), kh, vh, picks_of(table, AT_HEAD, 4 + t), s_ref)
            sent[four, 0:64] = o.reshape(4, 64, HD)

    @pl.when(edge)
    def _():
        fill_shared(
            0,
            lambda f, p: whole(two, f, slice(REST.start + p.start, REST.start + p.stop)),
            lambda f, p: whole(sw, 0, f, p),
            k2,
            v2,
        )

        @pl.when(w == 0)
        def _():
            fill_shared(4, lambda f, p: whole(r1, f, p), lambda f, p: whole(sw, 2, f, p), k2, v2)
            fill_shared(8, lambda f, p: whole(r2, f, p), lambda f, p: whole(se, f, p), k2, v2)

        @pl.when(w == 7)
        def _():
            fill_shared(4, lambda f, p: whole(l1, f, p), lambda f, p: whole(sw, 1, f, p), k2, v2)
            fill_shared(8, lambda f, p: whole(l2, f, p), lambda f, p: whole(se, f, p), k2, v2)

        @pl.loop(0, 4)
        def _(t):
            four = pl.ds(t * 4, 4)
            half = slice(0, 32)
            q = jnp.where(w == 7, whole(l3, four, half), whole(r3, four, half))
            o = attend(q, k2, v2, picks_of(table, AT_SHARED, t), s_ref)
            o_oth[four, 0:32] = o.reshape(4, 32, HD)

        @pl.loop(0, 4)
        def _(t):
            four = pl.ds(t * 4, 4)
            o = attend(whole(two, four, QUERY), k2, v2, picks_of(table, AT_SHARED, 4 + t), s_ref)
            sent[four, 64:96] = o.reshape(4, 32, HD)


def last_kernel(table, one, two, l1, r1, sw, kh, vh, sent_in, sent, k2, v2, s_ref):
    del sent_in
    w = table[AT_W]
    inner = (w == 1) | (w == 6)
    edge = (w == 0) | (w == 7)

    @pl.when(inner)
    def _():
        @pl.loop(0, 4)
        def _(t):
            four = pl.ds(t * 4, 4)
            o = attend(whole(two, four, REST), kh, vh, picks_of(table, AT_HEAD, 4 + t), s_ref)
            sent[four, 0:64] = o.reshape(4, 64, HD)

    @pl.when(jnp.logical_not(inner | edge))
    def _():
        fill_shared(0, lambda f, p: whole(one, f, p), lambda f, p: whole(sw, 0, f, p), k2, v2)
        fill_shared(4, lambda f, p: whole(r1, f, p), lambda f, p: whole(sw, 2, f, p), k2, v2)
        fill_shared(8, lambda f, p: whole(l1, f, p), lambda f, p: whole(sw, 1, f, p), k2, v2)

        @pl.loop(0, 4)
        def _(t):
            four = pl.ds(t * 4, 4)
            o = attend(whole(two, four, QUERY), k2, v2, picks_of(table, AT_SHARED, 4 + t), s_ref)
            sent[four, 64:96] = o.reshape(4, 32, HD)


def merge_kernel(table, o_left, o_right, sent_in, sent):
    del sent_in
    w = table[AT_W]

    @pl.when(w == 0)
    def _():
        sent[:, 0:64] = o_right[...]

    @pl.when(w == 7)
    def _():
        sent[:, 0:64] = o_left[...]

    @pl.when(w == 1)
    def _():
        sent[:, 64:96] = o_left[:, 0:32]

    @pl.when(w == 6)
    def _():
        sent[:, 64:96] = o_right[:, 0:32]


def unpack_kernel(in_ref, out_ref):
    for g in range(8):
        for h in range(2):
            out_ref[:, (3 * g + h) * HD : (3 * g + h + 1) * HD] = in_ref[2 * g + h, 0:64, :]
        last = slice((3 * g + 2) * HD, (3 * g + 3) * HD)
        out_ref[0:32, last] = in_ref[2 * g, 64:96, :]
        out_ref[32:64, last] = in_ref[2 * g + 1, 64:96, :]


def along_columns(block, distance):
    n = 2 * COLS
    return lax.ppermute(block, ("col", "half"), [(i, (i + 2 * distance) % n) for i in range(n)])


def swapped(block):
    return lax.ppermute(block, "core", [(0, 1), (1, 0)])


def exchanged(block):
    return lax.all_to_all(block, GROUP, split_axis=0, concat_axis=0, tiled=True)


POOL = (12, TOK_TILE, HD)
SCRATCH = [pltpu.VMEM(POOL, BF), pltpu.VMEM(POOL, BF), pltpu.VMEM((WIN, TOK_TILE, TOK_TILE), F32)]
SLOT = (16, 64, HD)


def kernel(body, name, outs, inputs, scratch=(), space=VMEM, limit=32, aliases={}):
    return pl.pallas_call(
        body,
        out_shape=tuple(
            jax.ShapeDtypeStruct(shape, BF if len(shape) > 1 else jnp.int32) for shape in outs
        ),
        in_specs=[SMEM if i.dtype == jnp.int32 else space for i in inputs],
        out_specs=tuple(VMEM if len(shape) > 1 else SMEM for shape in outs),
        scratch_shapes=list(scratch),
        input_output_aliases=aliases,
        compiler_params=pltpu.CompilerParams(vmem_limit_bytes=limit * MIB),
        name=name,
    )(*inputs)


def shards(queries, keys, values, order, nb):
    one, two, table = kernel(
        rotate_kernel,
        "rotate",
        (SLOT, (16, 224, HD), (256,)),
        (order, nb.T, queries, keys, values),
        (pltpu.VMEM((3,) + queries.shape, BF), pltpu.SemaphoreType.DMA((12,))),
        space=ANY,
        limit=60,
    )
    one = exchanged(one)
    l1, r1 = along_columns(one, 1), along_columns(one, -1)
    two = exchanged(two)
    main_left, main_right, value_left, value_right, swap = kernel(
        second_kernel, "second", (SLOT,) * 4 + ((3,) + SLOT,), (table, one, two, l1, r1)
    )
    l2, r2 = along_columns(main_right, 1), along_columns(main_left, -1)
    l3, r3 = along_columns(value_right, 1), along_columns(value_left, -1)
    sw = swapped(swap)
    se = swapped(jnp.where(table[AT_W] == 0, r2, l2))
    sent, o_oth, kh, vh = kernel(
        first_kernel,
        "attend_first",
        ((16, 96, HD), SLOT, POOL, POOL),
        (table, two, l1, r1, l2, r2, l3, r3, sw, se),
        SCRATCH,
    )
    o_left, o_right = along_columns(o_oth, 1), along_columns(o_oth, -1)
    (sent,) = kernel(
        last_kernel,
        "attend_last",
        ((16, 96, HD),),
        (table, one, two, l1, r1, sw, kh, vh, sent),
        SCRATCH,
        aliases={8: 0},
    )
    (sent,) = kernel(
        merge_kernel, "merge", ((16, 96, HD),), (table, o_left, o_right, sent), aliases={3: 0}
    )
    return kernel(unpack_kernel, "unpack", (queries.shape,), (exchanged(sent),))[0]


def solution(mesh):
    blk, uly, dp = (mesh.shape[name] for name in ("blk", "uly", "dp"))
    fine = Mesh(
        mesh.devices.reshape(blk // 2, 2, uly // 2, 2, dp), ("col", "half", "x", "core", "dp")
    )
    tokens = ("dp", "col", "half", "x", "core")
    placed = (P(tokens, None), P(tokens, None), P(tokens, None), P("dp"), P("dp", None))
    return jax.shard_map(
        shards, mesh=fine, in_specs=placed, out_specs=P(tokens, None), check_vma=False
    )
```

time: 132 us -> 131 us (level)
  starting transfers between devices: 33.8 us -> 43.4 us
  blocking collectives: 30.8 us -> 27.5 us
  local copies, waits for them, and re-layouts: 2.67 us -> 0.52 us
  other arithmetic: 2.08 us -> 0.03 us
  between operations: 2.14 us -> 0.8 us
    ppermute x6 -> x8, starting transfers between devices: 26.4 us -> 35.9 us  [along_columns(): lax.ppermute(block, ('col', 'half'), [(i, (i + 2 * distance) % n) for i i...]
    all_to_all x2, blocking collectives: 30.8 us -> 27.5 us  [exchanged(): return lax.all_to_all(block, GROUP, split_axis=0, concat_axis=0, tiled=True)]
    unnamed x5 -> x2, local copies, waits for them, and re-layouts: 2.08 us -> 0.01 us
    pallas_call x5 -> x6, Pallas kernels: 15.9 us -> 15 us  [kernel(): pl.pallas_call(body, out_shape=tuple((jax.ShapeDtypeStruct(shape, BF if l...]
    ppermute x6 -> x8, waiting for transfers between devices: 44 us -> 43.5 us  [along_columns(): lax.ppermute(block, ('col', 'half'), [(i, (i + 2 * distance) % n) for i i...]
  transfers between devices with their start and end apart: 9 -> 11, of which waited for: 6 -> 8; matrix products, arithmetic and copies ran while one was open for 2% -> 0% of each run, Pallas kernels for 8% -> 0%
where the time goes in v3:
time: 131 us
  waiting for transfers between devices  43.5 us (33%)
  starting transfers between devices  43.4 us (33%)
  blocking collectives  27.5 us (21%)
  Pallas kernels  15 us (11%)
    ppermute x8, waiting for transfers between devices, along_columns(): lax.ppermute(block, ('col', 'half'), [(i, (i + 2 * distance) % n) for i i...  43.5 us
    ppermute x8, starting transfers between devices, along_columns(): lax.ppermute(block, ('col', 'half'), [(i, (i + 2 * distance) % n) for i i...  35.9 us
    all_to_all x2, blocking collectives, exchanged(): return lax.all_to_all(block, GROUP, split_axis=0, concat_axis=0, tiled=True)  27.5 us
    pallas_call x6, Pallas kernels, kernel(): pl.pallas_call(body, out_shape=tuple((jax.ShapeDtypeStruct(shape, BF if l...  15 us
    ppermute x2, starting transfers between devices, swapped(): return lax.ppermute(block, 'core', [(0, 1), (1, 0)])  3.84 us
    all_to_all x1, starting transfers between devices, exchanged(): return lax.all_to_all(block, GROUP, split_axis=0, concat_axis=0, tiled=True)  3.63 us
  transfers between devices with their start and end apart: 11, of which 8 were waited for; matrix products, arithmetic and copies ran while one was open for 0% of the time, Pallas kernels for 0%

profile of v3, /device:TPU:24, one launch (start us, length us, event | category | flops | bytes accessed | tf_op | source)
XLA Modules:
  0.0 130.7 jit_solution(10198579706820894336)
XLA Ops:
  0.0 5.2 %rotate.1 = (bf16[16,64,128]{2,1,0:T(8,128)(2,1)}, bf16[16,224,128]{2,1,0:T(8,128)(2,1)}, s32[256]{0:T(256)}) custom-call(s32[32]{0:T(128)} %order.1, s32[9,32]{1,0:T(8,128)} %bitcast.2, bf16[64,3072]{1,0:T(8,128)(2,1)} %q_hbm.1, bf16[64,3072]{1,0:T(8,128)(2,1)} %k_hbm.1, bf16[64,3072]{1,0:T(8,128)(2,1)} %v_hbm.1), custom_call_target="tpu_custom_call" | custom-call | tf_op jit(solution)/shard_map/rotate/pallas_call | solution.py:355
  5.2 13.8 %all_to_all.15.one = bf16[16,64,128]{2,1,0:T(8,128)(2,1)S(1)} all-to-all(bf16[16,64,128]{2,1,0:T(8,128)(2,1)} %get-tuple-element.19), channel_id=1, replica_groups=mesh['col'=8,'half'=2,'x'=4,'core'=2,'dp'=4] {'half','x','core'}, dimensions={0} | all-to-all | bytes 524288 | tf_op jit(solution)/shard_map/all_to_all | solution.py:346
  19.0 3.6 %all-to-all-start = ((bf16[16,224,128]{2,1,0:T(8,128)(2,1)}), bf16[16,224,128]{2,1,0:T(8,128)(2,1)S(1)}, u32[]{:S(2)}, u32[]{:S(2)}) async-start(bf16[16,224,128]{2,1,0:T(8,128)(2,1)} %get-tuple-element.18), calls=%async_computation | async-start | bytes 1835008 | tf_op jit(solution)/shard_map/all_to_all | solution.py:346
  22.7 0.0 copy-start
  22.7 10.9 %collective-permute-start.1 = (bf16[16,64,128]{2,1,0:T(8,128)(2,1)S(1)}, bf16[16,64,128]{2,1,0:T(8,128)(2,1)S(1)}, u32[]{:S(2)}, u32[]{:S(2)}) collective-permute-start(bf16[16,64,128]{2,1,0:T(8,128)(2,1)S(1)} %all_to_all.15.one), channel_id=1, source_target_pairs={{0,448},{32,480},{64,0},{96,32},{128,64},{160,96},{192,128},{224,1... | collective-permute-start | bytes 786440 | tf_op jit(solution)/shard_map/ppermute | solution.py:338
  33.6 1.9 %collective-permute-start = (bf16[16,64,128]{2,1,0:T(8,128)(2,1)S(1)}, bf16[16,64,128]{2,1,0:T(8,128)(2,1)S(1)}, u32[]{:S(2)}, u32[]{:S(2)}) collective-permute-start(bf16[16,64,128]{2,1,0:T(8,128)(2,1)S(1)} %all_to_all.15.one), channel_id=1, source_target_pairs={{0,64},{32,96},{64,128},{96,160},{128,192},{160,224},{192,256},{22... | collective-permute-start | bytes 786440 | tf_op jit(solution)/shard_map/ppermute | solution.py:338
  35.6 4.1 %collective-permute-done.1.r1 = bf16[16,64,128]{2,1,0:T(8,128)(2,1)S(1)} collective-permute-done((bf16[16,64,128]{2,1,0:T(8,128)(2,1)S(1)}, bf16[16,64,128]{2,1,0:T(8,128)(2,1)S(1)}, u32[]{:S(2)}, u32[]{:S(2)}) %collective-permute-start.1) | collective-permute-done | bytes 262176 | tf_op jit(solution)/shard_map/ppermute | solution.py:338
  39.7 14.5 %collective-permute-done.l1 = bf16[16,64,128]{2,1,0:T(8,128)(2,1)S(1)} collective-permute-done((bf16[16,64,128]{2,1,0:T(8,128)(2,1)S(1)}, bf16[16,64,128]{2,1,0:T(8,128)(2,1)S(1)}, u32[]{:S(2)}, u32[]{:S(2)}) %collective-permute-start) | collective-permute-done | bytes 262176 | tf_op jit(solution)/shard_map/ppermute | solution.py:338
  54.2 0.0 all-to-all-done.two
  54.2 0.0 copy-done
  54.2 0.7 second.1
  54.9 1.9 %collective-permute-start.6 = (bf16[3,16,64,128]{3,2,1,0:T(8,128)(2,1)S(1)}, bf16[3,16,64,128]{3,2,1,0:T(8,128)(2,1)S(1)}, u32[]{:S(2)}, u32[]{:S(2)}) collective-permute-start(bf16[3,16,64,128]{3,2,1,0:T(8,128)(2,1)S(1)} %get-tuple-element.24), channel_id=1, source_target_pairs={{0,4},{4,0},{1,5},{5,1},{2,6},{6,2},{3,7},{7,3},{8,12},{12,8},{9,1... | collective-permute-start | bytes 2359304 | tf_op jit(solution)/shard_map/ppermute | solution.py:342
  56.8 1.9 %collective-permute-start.2 = (bf16[16,64,128]{2,1,0:T(8,128)(2,1)S(1)}, bf16[16,64,128]{2,1,0:T(8,128)(2,1)S(1)}, u32[]{:S(2)}, u32[]{:S(2)}) collective-permute-start(bf16[16,64,128]{2,1,0:T(8,128)(2,1)S(1)} %get-tuple-element.20), channel_id=1, source_target_pairs={{0,64},{32,96},{64,128},{96,160},{128,192},{160,224},{192,256},{22... | collective-permute-start | bytes 786440 | tf_op jit(solution)/shard_map/ppermute | solution.py:338
  58.7 6.0 %collective-permute-start.3 = (bf16[16,64,128]{2,1,0:T(8,128)(2,1)S(1)}, bf16[16,64,128]{2,1,0:T(8,128)(2,1)S(1)}, u32[]{:S(2)}, u32[]{:S(2)}) collective-permute-start(bf16[16,64,128]{2,1,0:T(8,128)(2,1)S(1)} %get-tuple-element.21), channel_id=1, source_target_pairs={{0,448},{32,480},{64,0},{96,32},{128,64},{160,96},{192,128},{224,1... | collective-permute-start | bytes 786440 | tf_op jit(solution)/shard_map/ppermute | solution.py:338
  64.8 0.5 slice.3
  65.9 1.9 %collective-permute-start.4 = (bf16[16,64,128]{2,1,0:T(8,128)(2,1)S(1)}, bf16[16,64,128]{2,1,0:T(8,128)(2,1)S(1)}, u32[]{:S(2)}, u32[]{:S(2)}) collective-permute-start(bf16[16,64,128]{2,1,0:T(8,128)(2,1)S(1)} %get-tuple-element.22), channel_id=1, source_target_pairs={{0,64},{32,96},{64,128},{96,160},{128,192},{160,224},{192,256},{22... | collective-permute-start | bytes 786440 | tf_op jit(solution)/shard_map/ppermute | solution.py:338
  67.8 6.0 %collective-permute-start.5 = (bf16[16,64,128]{2,1,0:T(8,128)(2,1)S(1)}, bf16[16,64,128]{2,1,0:T(8,128)(2,1)S(1)}, u32[]{:S(2)}, u32[]{:S(2)}) collective-permute-start(bf16[16,64,128]{2,1,0:T(8,128)(2,1)S(1)} %get-tuple-element.23), channel_id=1, source_target_pairs={{0,448},{32,480},{64,0},{96,32},{128,64},{160,96},{192,128},{224,1... | collective-permute-start | bytes 786440 | tf_op jit(solution)/shard_map/ppermute | solution.py:338
  73.9 1.0 collective-permute-done.2.l2
  74.9 3.8 %collective-permute-done.3.r2 = bf16[16,64,128]{2,1,0:T(8,128)(2,1)S(1)} collective-permute-done((bf16[16,64,128]{2,1,0:T(8,128)(2,1)S(1)}, bf16[16,64,128]{2,1,0:T(8,128)(2,1)S(1)}, u32[]{:S(2)}, u32[]{:S(2)}) %collective-permute-start.3) | collective-permute-done | bytes 262176 | tf_op jit(solution)/shard_map/ppermute | solution.py:338
  78.7 1.9 %collective-permute-start.7 = (bf16[16,64,128]{2,1,0:T(8,128)(2,1)S(1)}, bf16[16,64,128]{2,1,0:T(8,128)(2,1)S(1)}, u32[]{:S(2)}, u32[]{:S(2)}) collective-permute-start(bf16[16,64,128]{2,1,0:T(8,128)(2,1)S(1)} %broadcast_select_fusion), channel_id=1, source_target_pairs={{0,4},{4,0},{1,5},{5,1},{2,6},{6,2},{3,7},{7,3},{8,12},{12,8},{9,1... | collective-permute-start | bytes 786440 | tf_op jit(solution)/shard_map/ppermute | solution.py:342
  80.7 4.7 %collective-permute-done.4.l3 = bf16[16,64,128]{2,1,0:T(8,128)(2,1)S(1)} collective-permute-done((bf16[16,64,128]{2,1,0:T(8,128)(2,1)S(1)}, bf16[16,64,128]{2,1,0:T(8,128)(2,1)S(1)}, u32[]{:S(2)}, u32[]{:S(2)}) %collective-permute-start.4) | collective-permute-done | bytes 262176 | tf_op jit(solution)/shard_map/ppermute | solution.py:338
  85.4 1.7 %collective-permute-done.5.r3 = bf16[16,64,128]{2,1,0:T(8,128)(2,1)S(1)} collective-permute-done((bf16[16,64,128]{2,1,0:T(8,128)(2,1)S(1)}, bf16[16,64,128]{2,1,0:T(8,128)(2,1)S(1)}, u32[]{:S(2)}, u32[]{:S(2)}) %collective-permute-start.5) | collective-permute-done | bytes 262176 | tf_op jit(solution)/shard_map/ppermute | solution.py:338
  87.1 0.0 collective-permute-done.7.se
  87.1 0.0 collective-permute-done.6.sw
  87.1 7.1 %attend_first.1 = (bf16[16,96,128]{2,1,0:T(8,128)(2,1)S(1)}, bf16[16,64,128]{2,1,0:T(8,128)(2,1)S(1)}, bf16[12,256,128]{2,1,0:T(8,128)(2,1)S(1)}, bf16[12,256,128]{2,1,0:T(8,128)(2,1)S(1)}) custom-call(s32[256]{0:T(256)S(1)} %copy-done, bf16[16,224,128]{2,1,0:T(8,128)(2,1)S(1)} %all-to-all-done.two, bf16[16,64,128]{2,1,0:T(8,128)(2,1)S(1)} %collective-permute-done.l1, ...), custom_call_target="tpu_custom_call" | custom-call | tf_op jit(solution)/shard_map/attend_first/pallas_call | solution.py:355
  94.2 5.2 %collective-permute-start.9 = (bf16[16,64,128]{2,1,0:T(8,128)(2,1)S(1)}, bf16[16,64,128]{2,1,0:T(8,128)(2,1)S(1)}, u32[]{:S(2)}, u32[]{:S(2)}) collective-permute-start(bf16[16,64,128]{2,1,0:T(8,128)(2,1)S(1)} %get-tuple-element.25), channel_id=1, source_target_pairs={{0,448},{32,480},{64,0},{96,32},{128,64},{160,96},{192,128},{224,1... | collective-permute-start | bytes 786440 | tf_op jit(solution)/shard_map/ppermute | solution.py:338
  99.4 1.9 %collective-permute-start.8 = (bf16[16,64,128]{2,1,0:T(8,128)(2,1)S(1)}, bf16[16,64,128]{2,1,0:T(8,128)(2,1)S(1)}, u32[]{:S(2)}, u32[]{:S(2)}) collective-permute-start(bf16[16,64,128]{2,1,0:T(8,128)(2,1)S(1)} %get-tuple-element.25), channel_id=1, source_target_pairs={{0,64},{32,96},{64,128},{96,160},{128,192},{160,224},{192,256},{22... | collective-permute-start | bytes 786440 | tf_op jit(solution)/shard_map/ppermute | solution.py:338
  101.4 0.6 attend_last.1.sent_in
  102.0 5.5 %collective-permute-done.9.o_right = bf16[16,64,128]{2,1,0:T(8,128)(2,1)S(1)} collective-permute-done((bf16[16,64,128]{2,1,0:T(8,128)(2,1)S(1)}, bf16[16,64,128]{2,1,0:T(8,128)(2,1)S(1)}, u32[]{:S(2)}, u32[]{:S(2)}) %collective-permute-start.9) | collective-permute-done | bytes 262176 | tf_op jit(solution)/shard_map/ppermute | solution.py:338
  107.5 8.2 %collective-permute-done.8.o_left = bf16[16,64,128]{2,1,0:T(8,128)(2,1)S(1)} collective-permute-done((bf16[16,64,128]{2,1,0:T(8,128)(2,1)S(1)}, bf16[16,64,128]{2,1,0:T(8,128)(2,1)S(1)}, u32[]{:S(2)}, u32[]{:S(2)}) %collective-permute-start.8) | collective-permute-done | bytes 262176 | tf_op jit(solution)/shard_map/ppermute | solution.py:338
  115.6 0.6 merge.1
  116.2 13.6 %all_to_all.16.in_ref = bf16[16,96,128]{2,1,0:T(8,128)(2,1)S(1)} all-to-all(bf16[16,96,128]{2,1,0:T(8,128)(2,1)S(1)} %merge.1), channel_id=1, replica_groups=mesh['col'=8,'half'=2,'x'=4,'core'=2,'dp'=4] {'half','x','core'}, dimensions={0} | all-to-all | bytes 786432 | tf_op jit(solution)/shard_map/all_to_all | solution.py:346
  129.9 0.8 unpack.1
  (1 shorter events, 0.0 us)
Async XLA Ops:
  19.0 35.1 %all-to-all-start = ((bf16[16,224,128]{2,1,0:T(8,128)(2,1)}), bf16[16,224,128]{2,1,0:T(8,128)(2,1)S(1)}, u32[]{:S(2)}, u32[]{:S(2)}) async-start(bf16[16,224,128]{2,1,0:T(8,128)(2,1)} %get-tuple-element.18), calls=%async_computation | async-start | bytes 1835008 | tf_op jit(solution)/shard_map/all_to_all | solution.py:346
  22.7 31.5 %copy-start = (s32[256]{0:T(256)S(1)}, s32[256]{0:T(256)}, u32[]{:S(2)}) copy-start(s32[256]{0:T(256)} %get-tuple-element.17.table) | copy-start | bytes 3076
  22.7 17.0 %collective-permute-start.1 = (bf16[16,64,128]{2,1,0:T(8,128)(2,1)S(1)}, bf16[16,64,128]{2,1,0:T(8,128)(2,1)S(1)}, u32[]{:S(2)}, u32[]{:S(2)}) collective-permute-start(bf16[16,64,128]{2,1,0:T(8,128)(2,1)S(1)} %all_to_all.15.one), channel_id=1, source_target_pairs={{0,448},{32,480},{64,0},{96,32},{128,64},{160,96},{192,128},{224,1... | collective-permute-start | bytes 786440 | tf_op jit(solution)/shard_map/ppermute | solution.py:338
  33.6 20.5 %collective-permute-start = (bf16[16,64,128]{2,1,0:T(8,128)(2,1)S(1)}, bf16[16,64,128]{2,1,0:T(8,128)(2,1)S(1)}, u32[]{:S(2)}, u32[]{:S(2)}) collective-permute-start(bf16[16,64,128]{2,1,0:T(8,128)(2,1)S(1)} %all_to_all.15.one), channel_id=1, source_target_pairs={{0,64},{32,96},{64,128},{96,160},{128,192},{160,224},{192,256},{22... | collective-permute-start | bytes 786440 | tf_op jit(solution)/shard_map/ppermute | solution.py:338
  54.9 32.2 %collective-permute-start.6 = (bf16[3,16,64,128]{3,2,1,0:T(8,128)(2,1)S(1)}, bf16[3,16,64,128]{3,2,1,0:T(8,128)(2,1)S(1)}, u32[]{:S(2)}, u32[]{:S(2)}) collective-permute-start(bf16[3,16,64,128]{3,2,1,0:T(8,128)(2,1)S(1)} %get-tuple-element.24), channel_id=1, source_target_pairs={{0,4},{4,0},{1,5},{5,1},{2,6},{6,2},{3,7},{7,3},{8,12},{12,8},{9,1... | collective-permute-start | bytes 2359304 | tf_op jit(solution)/shard_map/ppermute | solution.py:342
  56.8 18.1 %collective-permute-start.2 = (bf16[16,64,128]{2,1,0:T(8,128)(2,1)S(1)}, bf16[16,64,128]{2,1,0:T(8,128)(2,1)S(1)}, u32[]{:S(2)}, u32[]{:S(2)}) collective-permute-start(bf16[16,64,128]{2,1,0:T(8,128)(2,1)S(1)} %get-tuple-element.20), channel_id=1, source_target_pairs={{0,64},{32,96},{64,128},{96,160},{128,192},{160,224},{192,256},{22... | collective-permute-start | bytes 786440 | tf_op jit(solution)/shard_map/ppermute | solution.py:338
  58.7 20.0 %collective-permute-start.3 = (bf16[16,64,128]{2,1,0:T(8,128)(2,1)S(1)}, bf16[16,64,128]{2,1,0:T(8,128)(2,1)S(1)}, u32[]{:S(2)}, u32[]{:S(2)}) collective-permute-start(bf16[16,64,128]{2,1,0:T(8,128)(2,1)S(1)} %get-tuple-element.21), channel_id=1, source_target_pairs={{0,448},{32,480},{64,0},{96,32},{128,64},{160,96},{192,128},{224,1... | collective-permute-start | bytes 786440 | tf_op jit(solution)/shard_map/ppermute | solution.py:338
  65.9 19.5 %collective-permute-start.4 = (bf16[16,64,128]{2,1,0:T(8,128)(2,1)S(1)}, bf16[16,64,128]{2,1,0:T(8,128)(2,1)S(1)}, u32[]{:S(2)}, u32[]{:S(2)}) collective-permute-start(bf16[16,64,128]{2,1,0:T(8,128)(2,1)S(1)} %get-tuple-element.22), channel_id=1, source_target_pairs={{0,64},{32,96},{64,128},{96,160},{128,192},{160,224},{192,256},{22... | collective-permute-start | bytes 786440 | tf_op jit(solution)/shard_map/ppermute | solution.py:338
  67.8 19.2 %collective-permute-start.5 = (bf16[16,64,128]{2,1,0:T(8,128)(2,1)S(1)}, bf16[16,64,128]{2,1,0:T(8,128)(2,1)S(1)}, u32[]{:S(2)}, u32[]{:S(2)}) collective-permute-start(bf16[16,64,128]{2,1,0:T(8,128)(2,1)S(1)} %get-tuple-element.23), channel_id=1, source_target_pairs={{0,448},{32,480},{64,0},{96,32},{128,64},{160,96},{192,128},{224,1... | collective-permute-start | bytes 786440 | tf_op jit(solution)/shard_map/ppermute | solution.py:338
  78.7 8.3 %collective-permute-start.7 = (bf16[16,64,128]{2,1,0:T(8,128)(2,1)S(1)}, bf16[16,64,128]{2,1,0:T(8,128)(2,1)S(1)}, u32[]{:S(2)}, u32[]{:S(2)}) collective-permute-start(bf16[16,64,128]{2,1,0:T(8,128)(2,1)S(1)} %broadcast_select_fusion), channel_id=1, source_target_pairs={{0,4},{4,0},{1,5},{5,1},{2,6},{6,2},{3,7},{7,3},{8,12},{12,8},{9,1... | collective-permute-start | bytes 786440 | tf_op jit(solution)/shard_map/ppermute | solution.py:342
  94.2 13.3 %collective-permute-start.9 = (bf16[16,64,128]{2,1,0:T(8,128)(2,1)S(1)}, bf16[16,64,128]{2,1,0:T(8,128)(2,1)S(1)}, u32[]{:S(2)}, u32[]{:S(2)}) collective-permute-start(bf16[16,64,128]{2,1,0:T(8,128)(2,1)S(1)} %get-tuple-element.25), channel_id=1, source_target_pairs={{0,448},{32,480},{64,0},{96,32},{128,64},{160,96},{192,128},{224,1... | collective-permute-start | bytes 786440 | tf_op jit(solution)/shard_map/ppermute | solution.py:338
  99.4 16.2 %collective-permute-start.8 = (bf16[16,64,128]{2,1,0:T(8,128)(2,1)S(1)}, bf16[16,64,128]{2,1,0:T(8,128)(2,1)S(1)}, u32[]{:S(2)}, u32[]{:S(2)}) collective-permute-start(bf16[16,64,128]{2,1,0:T(8,128)(2,1)S(1)} %get-tuple-element.25), channel_id=1, source_target_pairs={{0,64},{32,96},{64,128},{96,160},{128,192},{160,224},{192,256},{22... | collective-permute-start | bytes 786440 | tf_op jit(solution)/shard_map/ppermute | solution.py:338

commit v4 on v3

--- a/solution.py
+++ b/solution.py
@@ -18,7 +18,8 @@
 BF = jnp.bfloat16
 F32 = jnp.float32
 MIB = 1024 * 1024
-MAIN, VALUE, QUERY, REST = slice(0, 64), slice(64, 128), slice(128, 160), slice(160, 224)
+ONE, MAIN, VALUE = slice(0, 64), slice(64, 128), slice(128, 192)
+QUERY, REST = slice(192, 224), slice(224, 288)
 AT_W, AT_HEAD, AT_SHARED = 0, 16, 96
 
 
@@ -51,7 +52,7 @@
     return w
 
 
-def rotate_kernel(order, nb, q_hbm, k_hbm, v_hbm, one, two, table, held, sems):
+def rotate_kernel(order, nb, q_hbm, k_hbm, v_hbm, two, table, held, sems):
     x = lax.axis_index("x")
     frame_in_tile = lax.rem(x, 2) * 2 + lax.axis_index("core")
     slot = lax.axis_index("col") * 4 + lax.axis_index("half") * 2 + x // 2
@@ -106,7 +107,7 @@
 
                     @pl.when(edge)
                     def _(to=to, key=key, query=query):
-                        one[to] = key
+                        two[to, ONE, :] = key
                         two[to, MAIN, :] = query
 
                     @pl.when(jnp.logical_not(edge))
@@ -127,34 +128,36 @@
 
                         @pl.when(jnp.logical_not(edge))
                         def _(to=to, part_of=part_of, key=key, value=value):
-                            one[to, 0:32, :] = key[part_of]
-                            one[to, 32:64, :] = value[part_of]
-
-
-def second_kernel(table, one, two, l1, r1, main_left, main_right, value_left, value_right, swap):
-    w = table[AT_W]
-
-    @pl.when(w == 1)
-    def _():
-        main_left[...] = r1[...]
-        value_left[:, 0:32] = two[:, QUERY]
-        value_left[:, 32:64] = two[:, QUERY]
-
-    @pl.when(w != 1)
-    def _():
-        main_left[...] = two[:, MAIN]
-        value_left[...] = two[:, VALUE]
-
-    @pl.when(w == 6)
-    def _():
-        main_right[...] = l1[...]
-        value_right[:, 0:32] = two[:, QUERY]
-        value_right[:, 32:64] = two[:, QUERY]
-
-    @pl.when(w != 6)
-    def _():
-        main_right[...] = two[:, MAIN]
-        value_right[...] = two[:, VALUE]
+                            two[to, 0:32, :] = key[part_of]
+                            two[to, 32:64, :] = value[part_of]
+
+
+def early_kernel(table, two, one, value_left, value_right):
+    w = table[AT_W]
+    one[...] = two[:, ONE]
+    for out, special in ((value_left, 1), (value_right, 6)):
+
+        @pl.when(w == special)
+        def _(out=out):
+            out[:, 0:32] = two[:, QUERY]
+            out[:, 32:64] = two[:, QUERY]
+
+        @pl.when(w != special)
+        def _(out=out):
+            out[...] = two[:, VALUE]
+
+
+def late_kernel(table, two, l1, r1, main_left, main_right, swap):
+    w = table[AT_W]
+    for out, special, source in ((main_left, 1, r1), (main_right, 6, l1)):
+
+        @pl.when(w == special)
+        def _(out=out, source=source):
+            out[...] = source[...]
+
+        @pl.when(w != special)
+        def _(out=out):
+            out[...] = two[:, MAIN]
 
     @pl.when((w == 0) | (w == 7))
     def _():
@@ -162,7 +165,7 @@
 
     @pl.when((w != 0) & (w != 7))
     def _():
-        swap[0] = one[...]
+        swap[0] = two[:, ONE]
 
     swap[1] = l1[...]
     swap[2] = r1[...]
@@ -201,9 +204,28 @@
             pool[base + t, 128:256] = other(four, part)
 
 
-def first_kernel(
-    table, two, l1, r1, l2, r2, l3, r3, sw, se, sent, o_oth, kh, vh, k2, v2, s_ref
-):
+def value_kernel(two, l3, r3, vh):
+    for t in range(4):
+        four = slice(4 * t, 4 * t + 4)
+        vh[t] = whole(two, four, VALUE)
+        vh[4 + t] = whole(r3, four)
+        vh[8 + t] = whole(l3, four)
+
+
+def forwarded_kernel(table, l2, r2, vh, out):
+    del vh
+    w = table[AT_W]
+
+    @pl.when(w == 0)
+    def _():
+        out[...] = r2[...]
+
+    @pl.when(w == 7)
+    def _():
+        out[...] = l2[...]
+
+
+def first_kernel(table, two, l1, r1, l2, r2, vh, sent, o_oth, kh, s_ref):
     w = table[AT_W]
     inner = (w == 1) | (w == 6)
     edge = (w == 0) | (w == 7)
@@ -213,9 +235,6 @@
         for t in range(4):
             four = slice(4 * t, 4 * t + 4)
             kh[t] = whole(two, four, MAIN)
-            vh[t] = whole(two, four, VALUE)
-            vh[4 + t] = whole(r3, four)
-            vh[8 + t] = whole(l3, four)
         for base, special, early, late in ((4, 6, r1, r2), (8, 1, l1, l2)):
             for condition, source in ((w == special, early), (w != special, late)):
 
@@ -241,7 +260,14 @@
             o = attend(whole(two, four, REST), kh, vh, picks_of(table, AT_HEAD, 4 + t), s_ref)
             sent[four, 0:64] = o.reshape(4, 64, HD)
 
-    @pl.when(edge)
+
+def edge_kernel(
+    table, two, l1, r1, l2, r2, l3, r3, sw, se, sent_in, oth_in, sent, o_oth, k2, v2, s_ref
+):
+    del sent_in, oth_in
+    w = table[AT_W]
+
+    @pl.when((w == 0) | (w == 7))
     def _():
         fill_shared(
             0,
@@ -276,7 +302,7 @@
             sent[four, 64:96] = o.reshape(4, 32, HD)
 
 
-def last_kernel(table, one, two, l1, r1, sw, kh, vh, sent_in, sent, k2, v2, s_ref):
+def last_kernel(table, two, l1, r1, sw, kh, vh, sent_in, sent, k2, v2, s_ref):
     del sent_in
     w = table[AT_W]
     inner = (w == 1) | (w == 6)
@@ -292,7 +318,7 @@
 
     @pl.when(jnp.logical_not(inner | edge))
     def _():
-        fill_shared(0, lambda f, p: whole(one, f, p), lambda f, p: whole(sw, 0, f, p), k2, v2)
+        fill_shared(0, lambda f, p: whole(two, f, p), lambda f, p: whole(sw, 0, f, p), k2, v2)
         fill_shared(4, lambda f, p: whole(r1, f, p), lambda f, p: whole(sw, 2, f, p), k2, v2)
         fill_shared(8, lambda f, p: whole(l1, f, p), lambda f, p: whole(sw, 1, f, p), k2, v2)
 
@@ -349,9 +375,10 @@
 POOL = (12, TOK_TILE, HD)
 SCRATCH = [pltpu.VMEM(POOL, BF), pltpu.VMEM(POOL, BF), pltpu.VMEM((WIN, TOK_TILE, TOK_TILE), F32)]
 SLOT = (16, 64, HD)
-
-
-def kernel(body, name, outs, inputs, scratch=(), space=VMEM, limit=32, aliases={}):
+FLOPS = 20_000_000_000
+
+
+def kernel(body, name, outs, inputs, scratch=(), space=VMEM, limit=32, aliases={}, flops=None):
     return pl.pallas_call(
         body,
         out_shape=tuple(
@@ -362,45 +389,57 @@
         scratch_shapes=list(scratch),
         input_output_aliases=aliases,
         compiler_params=pltpu.CompilerParams(vmem_limit_bytes=limit * MIB),
+        cost_estimate=flops and pl.CostEstimate(flops=flops, bytes_accessed=0, transcendentals=0),
         name=name,
     )(*inputs)
 
 
 def shards(queries, keys, values, order, nb):
-    one, two, table = kernel(
+    two, table = kernel(
         rotate_kernel,
         "rotate",
-        (SLOT, (16, 224, HD), (256,)),
+        ((16, 288, HD), (256,)),
         (order, nb.T, queries, keys, values),
         (pltpu.VMEM((3,) + queries.shape, BF), pltpu.SemaphoreType.DMA((12,))),
         space=ANY,
         limit=60,
     )
-    one = exchanged(one)
+    two = exchanged(two)
+    one, value_left, value_right = kernel(early_kernel, "early", (SLOT,) * 3, (table, two))
     l1, r1 = along_columns(one, 1), along_columns(one, -1)
-    two = exchanged(two)
-    main_left, main_right, value_left, value_right, swap = kernel(
-        second_kernel, "second", (SLOT,) * 4 + ((3,) + SLOT,), (table, one, two, l1, r1)
+    l3, r3 = along_columns(value_right, 1), along_columns(value_left, -1)
+    main_left, main_right, swap = kernel(
+        late_kernel, "late", (SLOT, SLOT, (3,) + SLOT), (table, two, l1, r1)
     )
     l2, r2 = along_columns(main_right, 1), along_columns(main_left, -1)
-    l3, r3 = along_columns(value_right, 1), along_columns(value_left, -1)
     sw = swapped(swap)
-    se = swapped(jnp.where(table[AT_W] == 0, r2, l2))
-    sent, o_oth, kh, vh = kernel(
+    (vh,) = kernel(value_kernel, "values", (POOL,), (two, l3, r3), flops=FLOPS)
+    (se,) = kernel(forwarded_kernel, "forwarded", (SLOT,), (table, l2, r2, vh))
+    se = swapped(se)
+    sent, o_oth, kh = kernel(
         first_kernel,
         "attend_first",
-        ((16, 96, HD), SLOT, POOL, POOL),
-        (table, two, l1, r1, l2, r2, l3, r3, sw, se),
+        ((16, 96, HD), SLOT, POOL),
+        (table, two, l1, r1, l2, r2, vh),
+        SCRATCH[2:],
+        flops=FLOPS,
+    )
+    sent, o_oth = kernel(
+        edge_kernel,
+        "attend_edge",
+        ((16, 96, HD), SLOT),
+        (table, two, l1, r1, l2, r2, l3, r3, sw, se, sent, o_oth),
         SCRATCH,
+        aliases={10: 0, 11: 1},
     )
     o_left, o_right = along_columns(o_oth, 1), along_columns(o_oth, -1)
     (sent,) = kernel(
         last_kernel,
         "attend_last",
         ((16, 96, HD),),
-        (table, one, two, l1, r1, sw, kh, vh, sent),
+        (table, two, l1, r1, sw, kh, vh, sent),
         SCRATCH,
-        aliases={8: 0},
+        aliases={7: 0},
     )
     (sent,) = kernel(
         merge_kernel, "merge", ((16, 96, HD),), (table, o_left, o_right, sent), aliases={3: 0}

time: 131 us -> 127 us (0.969); the launches traced: 131 us -> 125 us
  waiting for transfers between devices: 43.5 us -> 31.1 us
  blocking collectives: 27.5 us -> 37.7 us
  starting transfers between devices: 43.4 us -> 39.4 us
  Pallas kernels: 15 us -> 16.7 us
    ppermute x8, waiting for transfers between devices: 43.5 us -> 30.2 us  [along_columns(): lax.ppermute(block, ('col', 'half'), [(i, (i + 2 * distance) % n) for i i...]
    all_to_all x2, blocking collectives: 27.5 us -> 37.7 us  [exchanged(): return lax.all_to_all(block, GROUP, split_axis=0, concat_axis=0, tiled=True)]
    all_to_all x1 -> x0, starting transfers between devices: 3.63 us -> none  [exchanged(): return lax.all_to_all(block, GROUP, split_axis=0, concat_axis=0, tiled=True)]
    pallas_call x6 -> x10, Pallas kernels: 15 us -> 16.7 us  [kernel(): pl.pallas_call(body, out_shape=tuple((jax.ShapeDtypeStruct(shape, BF if l...]
  transfers between devices with their start and end apart: 11 -> 10, of which waited for: 8 -> 5; matrix products, arithmetic and copies ran while one was open for 0% -> 0% of each run, Pallas kernels for 0% -> 2%
where the time goes in v4:
time: 127 us; the launch traced here: 125 us
  starting transfers between devices  39.4 us (31%)
  blocking collectives  37.7 us (30%)
  waiting for transfers between devices  31.1 us (24%)
  Pallas kernels  16.7 us (13%)
    all_to_all x2, blocking collectives, exchanged(): return lax.all_to_all(block, GROUP, split_axis=0, concat_axis=0, tiled=True)  37.7 us
    ppermute x8, starting transfers between devices, along_columns(): lax.ppermute(block, ('col', 'half'), [(i, (i + 2 * distance) % n) for i i...  35.5 us
    ppermute x8, waiting for transfers between devices, along_columns(): lax.ppermute(block, ('col', 'half'), [(i, (i + 2 * distance) % n) for i i...  30.2 us
    pallas_call x10, Pallas kernels, kernel(): pl.pallas_call(body, out_shape=tuple((jax.ShapeDtypeStruct(shape, BF if l...  16.7 us
    ppermute x2, starting transfers between devices, swapped(): return lax.ppermute(block, 'core', [(0, 1), (1, 0)])  3.84 us
  transfers between devices with their start and end apart: 10, of which 5 were waited for; matrix products, arithmetic and copies ran while one was open for 0% of the time, Pallas kernels for 2%

profile of v4, /device:TPU:24, one launch (start us, length us, event | category | flops | bytes accessed | tf_op | source)
XLA Modules:
  0.0 125.1 jit_solution(16558129498625590614)
XLA Ops:
  0.0 5.2 %rotate.1 = (bf16[16,288,128]{2,1,0:T(8,128)(2,1)}, s32[256]{0:T(256)}) custom-call(s32[32]{0:T(128)} %order.1, s32[9,32]{1,0:T(8,128)} %bitcast.1, bf16[64,3072]{1,0:T(8,128)(2,1)} %q_hbm.1, bf16[64,3072]{1,0:T(8,128)(2,1)} %k_hbm.1, bf16[64,3072]{1,0:T(8,128)(2,1)} %v_hbm.1), custom_call_target="tpu_custom_call" | custom-call | tf_op jit(solution)/shard_map/rotate/pallas_call | solution.py:382
  5.2 0.0 copy-start
  5.2 23.7 %all_to_all.10.two = bf16[16,288,128]{2,1,0:T(8,128)(2,1)S(1)} all-to-all(bf16[16,288,128]{2,1,0:T(8,128)(2,1)} %get-tuple-element.19), channel_id=1, replica_groups=mesh['col'=8,'half'=2,'x'=4,'core'=2,'dp'=4] {'half','x','core'}, dimensions={0} | all-to-all | bytes 2359296 | tf_op jit(solution)/shard_map/all_to_all | solution.py:372
  29.0 0.0 copy-done
  29.0 0.6 early.1
  29.6 11.0 %collective-permute-start.1 = (bf16[16,64,128]{2,1,0:T(8,128)(2,1)S(1)}, bf16[16,64,128]{2,1,0:T(8,128)(2,1)S(1)}, u32[]{:S(2)}, u32[]{:S(2)}) collective-permute-start(bf16[16,64,128]{2,1,0:T(8,128)(2,1)S(1)} %get-tuple-element.20), channel_id=1, source_target_pairs={{0,448},{32,480},{64,0},{96,32},{128,64},{160,96},{192,128},{224,1... | collective-permute-start | bytes 786440 | tf_op jit(solution)/shard_map/ppermute | solution.py:364
  40.6 1.9 %collective-permute-start = (bf16[16,64,128]{2,1,0:T(8,128)(2,1)S(1)}, bf16[16,64,128]{2,1,0:T(8,128)(2,1)S(1)}, u32[]{:S(2)}, u32[]{:S(2)}) collective-permute-start(bf16[16,64,128]{2,1,0:T(8,128)(2,1)S(1)} %get-tuple-element.20), channel_id=1, source_target_pairs={{0,64},{32,96},{64,128},{96,160},{128,192},{160,224},{192,256},{22... | collective-permute-start | bytes 786440 | tf_op jit(solution)/shard_map/ppermute | solution.py:364
  42.5 1.9 %collective-permute-start.4 = (bf16[16,64,128]{2,1,0:T(8,128)(2,1)S(1)}, bf16[16,64,128]{2,1,0:T(8,128)(2,1)S(1)}, u32[]{:S(2)}, u32[]{:S(2)}) collective-permute-start(bf16[16,64,128]{2,1,0:T(8,128)(2,1)S(1)} %get-tuple-element.23), channel_id=1, source_target_pairs={{0,64},{32,96},{64,128},{96,160},{128,192},{160,224},{192,256},{22... | collective-permute-start | bytes 786440 | tf_op jit(solution)/shard_map/ppermute | solution.py:364
  44.4 6.0 %collective-permute-start.5 = (bf16[16,64,128]{2,1,0:T(8,128)(2,1)S(1)}, bf16[16,64,128]{2,1,0:T(8,128)(2,1)S(1)}, u32[]{:S(2)}, u32[]{:S(2)}) collective-permute-start(bf16[16,64,128]{2,1,0:T(8,128)(2,1)S(1)} %get-tuple-element.24), channel_id=1, source_target_pairs={{0,448},{32,480},{64,0},{96,32},{128,64},{160,96},{192,128},{224,1... | collective-permute-start | bytes 786440 | tf_op jit(solution)/shard_map/ppermute | solution.py:364
  50.5 0.0 collective-permute-done.1.r1
  50.5 5.7 %collective-permute-done.l1 = bf16[16,64,128]{2,1,0:T(8,128)(2,1)S(1)} collective-permute-done((bf16[16,64,128]{2,1,0:T(8,128)(2,1)S(1)}, bf16[16,64,128]{2,1,0:T(8,128)(2,1)S(1)}, u32[]{:S(2)}, u32[]{:S(2)}) %collective-permute-start) | collective-permute-done | bytes 262176 | tf_op jit(solution)/shard_map/ppermute | solution.py:364
  56.2 0.7 late.1
  56.8 1.9 %collective-permute-start.2 = (bf16[16,64,128]{2,1,0:T(8,128)(2,1)S(1)}, bf16[16,64,128]{2,1,0:T(8,128)(2,1)S(1)}, u32[]{:S(2)}, u32[]{:S(2)}) collective-permute-start(bf16[16,64,128]{2,1,0:T(8,128)(2,1)S(1)} %get-tuple-element.21), channel_id=1, source_target_pairs={{0,64},{32,96},{64,128},{96,160},{128,192},{160,224},{192,256},{22... | collective-permute-start | bytes 786440 | tf_op jit(solution)/shard_map/ppermute | solution.py:364
  58.8 6.0 %collective-permute-start.3 = (bf16[16,64,128]{2,1,0:T(8,128)(2,1)S(1)}, bf16[16,64,128]{2,1,0:T(8,128)(2,1)S(1)}, u32[]{:S(2)}, u32[]{:S(2)}) collective-permute-start(bf16[16,64,128]{2,1,0:T(8,128)(2,1)S(1)} %get-tuple-element.22), channel_id=1, source_target_pairs={{0,448},{32,480},{64,0},{96,32},{128,64},{160,96},{192,128},{224,1... | collective-permute-start | bytes 786440 | tf_op jit(solution)/shard_map/ppermute | solution.py:364
  64.8 1.9 %collective-permute-start.6 = (bf16[3,16,64,128]{3,2,1,0:T(8,128)(2,1)S(1)}, bf16[3,16,64,128]{3,2,1,0:T(8,128)(2,1)S(1)}, u32[]{:S(2)}, u32[]{:S(2)}) collective-permute-start(bf16[3,16,64,128]{3,2,1,0:T(8,128)(2,1)S(1)} %get-tuple-element.25), channel_id=1, source_target_pairs={{0,4},{4,0},{1,5},{5,1},{2,6},{6,2},{3,7},{7,3},{8,12},{12,8},{9,1... | collective-permute-start | bytes 2359304 | tf_op jit(solution)/shard_map/ppermute | solution.py:368
  66.7 0.0 collective-permute-done.4.l3
  66.8 0.0 collective-permute-done.5.r3
  66.8 0.1 values.1.vh
  66.8 12.9 %collective-permute-done.2.l2 = bf16[16,64,128]{2,1,0:T(8,128)(2,1)S(1)} collective-permute-done((bf16[16,64,128]{2,1,0:T(8,128)(2,1)S(1)}, bf16[16,64,128]{2,1,0:T(8,128)(2,1)S(1)}, u32[]{:S(2)}, u32[]{:S(2)}) %collective-permute-start.2) | collective-permute-done | bytes 262176 | tf_op jit(solution)/shard_map/ppermute | solution.py:364
  79.7 0.0 collective-permute-done.3.r2
  79.7 0.6 forwarded.1
  80.3 1.9 %collective-permute-start.7 = (bf16[16,64,128]{2,1,0:T(8,128)(2,1)S(1)}, bf16[16,64,128]{2,1,0:T(8,128)(2,1)S(1)}, u32[]{:S(2)}, u32[]{:S(2)}) collective-permute-start(bf16[16,64,128]{2,1,0:T(8,128)(2,1)S(1)} %forwarded.1), channel_id=1, source_target_pairs={{0,4},{4,0},{1,5},{5,1},{2,6},{6,2},{3,7},{7,3},{8,12},{12,8},{9,1... | collective-permute-start | bytes 786440 | tf_op jit(solution)/shard_map/ppermute | solution.py:368
  82.2 0.6 attend_first.1
  82.8 0.9 collective-permute-done.7.se
  83.7 0.0 collective-permute-done.6.sw
  83.7 7.0 %attend_edge.1 = (bf16[16,96,128]{2,1,0:T(8,128)(2,1)S(1)}, bf16[16,64,128]{2,1,0:T(8,128)(2,1)S(1)}) custom-call(s32[256]{0:T(256)S(1)} %copy-done, bf16[16,288,128]{2,1,0:T(8,128)(2,1)S(1)} %all_to_all.10.two, bf16[16,64,128]{2,1,0:T(8,128)(2,1)S(1)} %collective-permute-done.l1, ...), custom_call_target="tpu_custom_call", output_to_operand_aliasing={{0}: (10, {}), {1}: (11, {})} | custom-call | tf_op jit(solution)/shard_map/attend_edge/pallas_call | solution.py:382
  90.8 1.9 %collective-permute-start.9 = (bf16[16,64,128]{2,1,0:T(8,128)(2,1)S(1)}, bf16[16,64,128]{2,1,0:T(8,128)(2,1)S(1)}, u32[]{:S(2)}, u32[]{:S(2)}) collective-permute-start(bf16[16,64,128]{2,1,0:T(8,128)(2,1)S(1)} %get-tuple-element.28), channel_id=1, source_target_pairs={{0,448},{32,480},{64,0},{96,32},{128,64},{160,96},{192,128},{224,1... | collective-permute-start | bytes 786440 | tf_op jit(solution)/shard_map/ppermute | solution.py:364
  92.7 4.8 %collective-permute-start.8 = (bf16[16,64,128]{2,1,0:T(8,128)(2,1)S(1)}, bf16[16,64,128]{2,1,0:T(8,128)(2,1)S(1)}, u32[]{:S(2)}, u32[]{:S(2)}) collective-permute-start(bf16[16,64,128]{2,1,0:T(8,128)(2,1)S(1)} %get-tuple-element.28), channel_id=1, source_target_pairs={{0,64},{32,96},{64,128},{96,160},{128,192},{160,224},{192,256},{22... | collective-permute-start | bytes 786440 | tf_op jit(solution)/shard_map/ppermute | solution.py:364
  97.5 0.6 attend_last.1.sent_in
  98.1 9.4 %collective-permute-done.9.o_right = bf16[16,64,128]{2,1,0:T(8,128)(2,1)S(1)} collective-permute-done((bf16[16,64,128]{2,1,0:T(8,128)(2,1)S(1)}, bf16[16,64,128]{2,1,0:T(8,128)(2,1)S(1)}, u32[]{:S(2)}, u32[]{:S(2)}) %collective-permute-start.9) | collective-permute-done | bytes 262176 | tf_op jit(solution)/shard_map/ppermute | solution.py:364
  107.5 2.1 %collective-permute-done.8.o_left = bf16[16,64,128]{2,1,0:T(8,128)(2,1)S(1)} collective-permute-done((bf16[16,64,128]{2,1,0:T(8,128)(2,1)S(1)}, bf16[16,64,128]{2,1,0:T(8,128)(2,1)S(1)}, u32[]{:S(2)}, u32[]{:S(2)}) %collective-permute-start.8) | collective-permute-done | bytes 262176 | tf_op jit(solution)/shard_map/ppermute | solution.py:364
  109.7 0.6 merge.1
  110.3 14.0 %all_to_all.11.in_ref = bf16[16,96,128]{2,1,0:T(8,128)(2,1)S(1)} all-to-all(bf16[16,96,128]{2,1,0:T(8,128)(2,1)S(1)} %merge.1), channel_id=1, replica_groups=mesh['col'=8,'half'=2,'x'=4,'core'=2,'dp'=4] {'half','x','core'}, dimensions={0} | all-to-all | bytes 786432 | tf_op jit(solution)/shard_map/all_to_all | solution.py:372
  124.3 0.8 unpack.1
Async XLA Ops:
  5.2 23.7 %copy-start = (s32[256]{0:T(256)S(1)}, s32[256]{0:T(256)}, u32[]{:S(2)}) copy-start(s32[256]{0:T(256)} %get-tuple-element.18.table) | copy-start | bytes 3076
  29.6 20.9 %collective-permute-start.1 = (bf16[16,64,128]{2,1,0:T(8,128)(2,1)S(1)}, bf16[16,64,128]{2,1,0:T(8,128)(2,1)S(1)}, u32[]{:S(2)}, u32[]{:S(2)}) collective-permute-start(bf16[16,64,128]{2,1,0:T(8,128)(2,1)S(1)} %get-tuple-element.20), channel_id=1, source_target_pairs={{0,448},{32,480},{64,0},{96,32},{128,64},{160,96},{192,128},{224,1... | collective-permute-start | bytes 786440 | tf_op jit(solution)/shard_map/ppermute | solution.py:364
  40.6 15.6 %collective-permute-start = (bf16[16,64,128]{2,1,0:T(8,128)(2,1)S(1)}, bf16[16,64,128]{2,1,0:T(8,128)(2,1)S(1)}, u32[]{:S(2)}, u32[]{:S(2)}) collective-permute-start(bf16[16,64,128]{2,1,0:T(8,128)(2,1)S(1)} %get-tuple-element.20), channel_id=1, source_target_pairs={{0,64},{32,96},{64,128},{96,160},{128,192},{160,224},{192,256},{22... | collective-permute-start | bytes 786440 | tf_op jit(solution)/shard_map/ppermute | solution.py:364
  42.5 24.3 %collective-permute-start.4 = (bf16[16,64,128]{2,1,0:T(8,128)(2,1)S(1)}, bf16[16,64,128]{2,1,0:T(8,128)(2,1)S(1)}, u32[]{:S(2)}, u32[]{:S(2)}) collective-permute-start(bf16[16,64,128]{2,1,0:T(8,128)(2,1)S(1)} %get-tuple-element.23), channel_id=1, source_target_pairs={{0,64},{32,96},{64,128},{96,160},{128,192},{160,224},{192,256},{22... | collective-permute-start | bytes 786440 | tf_op jit(solution)/shard_map/ppermute | solution.py:364
  44.4 22.3 %collective-permute-start.5 = (bf16[16,64,128]{2,1,0:T(8,128)(2,1)S(1)}, bf16[16,64,128]{2,1,0:T(8,128)(2,1)S(1)}, u32[]{:S(2)}, u32[]{:S(2)}) collective-permute-start(bf16[16,64,128]{2,1,0:T(8,128)(2,1)S(1)} %get-tuple-element.24), channel_id=1, source_target_pairs={{0,448},{32,480},{64,0},{96,32},{128,64},{160,96},{192,128},{224,1... | collective-permute-start | bytes 786440 | tf_op jit(solution)/shard_map/ppermute | solution.py:364
  56.8 22.9 %collective-permute-start.2 = (bf16[16,64,128]{2,1,0:T(8,128)(2,1)S(1)}, bf16[16,64,128]{2,1,0:T(8,128)(2,1)S(1)}, u32[]{:S(2)}, u32[]{:S(2)}) collective-permute-start(bf16[16,64,128]{2,1,0:T(8,128)(2,1)S(1)} %get-tuple-element.21), channel_id=1, source_target_pairs={{0,64},{32,96},{64,128},{96,160},{128,192},{160,224},{192,256},{22... | collective-permute-start | bytes 786440 | tf_op jit(solution)/shard_map/ppermute | solution.py:364
  58.8 20.9 %collective-permute-start.3 = (bf16[16,64,128]{2,1,0:T(8,128)(2,1)S(1)}, bf16[16,64,128]{2,1,0:T(8,128)(2,1)S(1)}, u32[]{:S(2)}, u32[]{:S(2)}) collective-permute-start(bf16[16,64,128]{2,1,0:T(8,128)(2,1)S(1)} %get-tuple-element.22), channel_id=1, source_target_pairs={{0,448},{32,480},{64,0},{96,32},{128,64},{160,96},{192,128},{224,1... | collective-permute-start | bytes 786440 | tf_op jit(solution)/shard_map/ppermute | solution.py:364
  64.8 18.9 %collective-permute-start.6 = (bf16[3,16,64,128]{3,2,1,0:T(8,128)(2,1)S(1)}, bf16[3,16,64,128]{3,2,1,0:T(8,128)(2,1)S(1)}, u32[]{:S(2)}, u32[]{:S(2)}) collective-permute-start(bf16[3,16,64,128]{3,2,1,0:T(8,128)(2,1)S(1)} %get-tuple-element.25), channel_id=1, source_target_pairs={{0,4},{4,0},{1,5},{5,1},{2,6},{6,2},{3,7},{7,3},{8,12},{12,8},{9,1... | collective-permute-start | bytes 2359304 | tf_op jit(solution)/shard_map/ppermute | solution.py:368
  80.3 3.4 %collective-permute-start.7 = (bf16[16,64,128]{2,1,0:T(8,128)(2,1)S(1)}, bf16[16,64,128]{2,1,0:T(8,128)(2,1)S(1)}, u32[]{:S(2)}, u32[]{:S(2)}) collective-permute-start(bf16[16,64,128]{2,1,0:T(8,128)(2,1)S(1)} %forwarded.1), channel_id=1, source_target_pairs={{0,4},{4,0},{1,5},{5,1},{2,6},{6,2},{3,7},{7,3},{8,12},{12,8},{9,1... | collective-permute-start | bytes 786440 | tf_op jit(solution)/shard_map/ppermute | solution.py:368
  90.8 16.8 %collective-permute-start.9 = (bf16[16,64,128]{2,1,0:T(8,128)(2,1)S(1)}, bf16[16,64,128]{2,1,0:T(8,128)(2,1)S(1)}, u32[]{:S(2)}, u32[]{:S(2)}) collective-permute-start(bf16[16,64,128]{2,1,0:T(8,128)(2,1)S(1)} %get-tuple-element.28), channel_id=1, source_target_pairs={{0,448},{32,480},{64,0},{96,32},{128,64},{160,96},{192,128},{224,1... | collective-permute-start | bytes 786440 | tf_op jit(solution)/shard_map/ppermute | solution.py:364
  92.7 17.0 %collective-permute-start.8 = (bf16[16,64,128]{2,1,0:T(8,128)(2,1)S(1)}, bf16[16,64,128]{2,1,0:T(8,128)(2,1)S(1)}, u32[]{:S(2)}, u32[]{:S(2)}) collective-permute-start(bf16[16,64,128]{2,1,0:T(8,128)(2,1)S(1)} %get-tuple-element.28), channel_id=1, source_target_pairs={{0,64},{32,96},{64,128},{96,160},{128,192},{160,224},{192,256},{22... | collective-permute-start | bytes 786440 | tf_op jit(solution)/shard_map/ppermute | solution.py:364

commit v5 on v4

v5 whole, which is shorter than its diff:
```python
import jax
import jax.numpy as jnp
import numpy as np
from jax import lax
from jax.experimental import pallas as pl
from jax.experimental.pallas import tpu as pltpu
from jax.sharding import Mesh
from jax.sharding import PartitionSpec as P

HD = 128
TOK_TILE = 256
WIN = 9
COLS = 8
GROUP = ("half", "x", "core")
VMEM = pl.BlockSpec(memory_space=pltpu.VMEM)
SMEM = pl.BlockSpec(memory_space=pltpu.SMEM)
ANY = pl.BlockSpec(memory_space=pl.ANY)
BF = jnp.bfloat16
F32 = jnp.float32
MIB = 1024 * 1024
ONE, MAIN, VALUE = slice(0, 64), slice(64, 128), slice(128, 192)
QUERY, REST = slice(192, 224), slice(224, 288)
VALUE_A, VALUE_B = slice(128, 160), slice(160, 192)
AT_W, AT_TILE, AT_HEAD, AT_SHARED = 0, 8, 16, 64
OTHER, THIS = 0, 1


def frequency_rows():
    pair = lax.broadcasted_iota(jnp.int32, (8, HD), 1) // 2
    nt = (HD - 4 * (HD // 6)) // 2
    ns = HD // 6
    rows = []
    for first, count in ((0, nt), (nt, ns), (nt + ns, ns)):
        within = (pair - first).astype(F32)
        freq = jnp.exp(within * float(-np.log(10000.0) / count))
        rows.append(jnp.where((pair >= first) & (pair < first + count), freq, 0.0)[0:1])
    return rows


def plan(order, nb, table):
    k = lax.axis_index("col")
    w = lax.rem(order[k * 4], COLS)
    table[AT_W] = w
    k_oth = lax.rem(jnp.where((w == 1) | (w == 7), k + 7, k + 1), COLS)
    near = jnp.where(w == 7, 7, 1)
    for column, base in ((OTHER, k_oth), (THIS, k)):
        low, high = 0, 2
        first = [0, 0]
        for t in range(4):
            upper = lax.rem(order[base * 4 + t] // 8, 4) < 2
            table[AT_TILE + 4 * column + jnp.where(upper, low, high)] = t
            first = [jnp.where(upper, t, first[0]), jnp.where(upper, first[1], t)]
            low, high = low + upper.astype(jnp.int32), high + 1 - upper.astype(jnp.int32)
        for p in range(2):
            for j in range(WIN):
                n = nb[j, base * 4 + first[p]]
                d = lax.rem(n // 4 - k + COLS, COLS)
                t = lax.rem(n, 4)
                at = WIN * (2 * column + p) + j
                table[AT_HEAD + at] = jnp.where(d == 0, 0, jnp.where(d == 1, 4, 8)) + t
                table[AT_SHARED + at] = jnp.where(d == 0, 0, jnp.where(d == near, 4, 8)) + t
    return w


def rotate_kernel(order, nb, q_hbm, k_hbm, v_hbm, out_hbm, table, held, packed, sems, out_sems):
    x = lax.axis_index("x")
    frame_in_tile = lax.rem(x, 2) * 2 + lax.axis_index("core")
    slot = lax.axis_index("col") * 4 + lax.axis_index("half") * 2 + x // 2
    rows = held.shape[1]
    width = 2 * 3 * HD
    copies = []
    for part in range(4):
        for which, ref in enumerate((k_hbm, q_hbm, v_hbm)):
            columns = pl.ds(part * width, width)
            copies.append(
                pltpu.make_async_copy(
                    ref.at[:, columns], held.at[which, :, columns], sems.at[3 * part + which]
                )
            )
    for copy in copies:
        copy.start()
    w = plan(order, nb, table)
    edge = (w == 0) | (w == 7)
    tile = order[slot]
    frame = (tile // 32 * 4 + frame_in_tile).astype(F32)
    row0 = (tile // 8 % 4 * 8).astype(F32)
    col0 = (tile % 8 * 8).astype(F32)
    token = lax.broadcasted_iota(jnp.int32, (rows, HD), 0)
    row = row0 + (token // 8).astype(F32)
    col = col0 + (token % 8).astype(F32)
    by_frame, by_row, by_col = frequency_rows()
    angle = frame * by_frame + row * by_row + col * by_col
    cosine = jnp.cos(angle)
    sine = jnp.sin(angle)
    even = lax.broadcasted_iota(jnp.int32, (rows, HD), 1) % 2 == 0
    from_next = jnp.where(even, -sine, 0.0)
    from_last = jnp.where(even, 0.0, sine)
    scale = HD ** (-0.5) * 1.4426950408889634

    def turned(x, c, n, l):
        x = x.astype(F32)
        return (x * c + pltpu.roll(x, HD - 1, 1) * n + pltpu.roll(x, 1, 1) * l).astype(BF)

    qc, qn, ql = cosine * scale, from_next * scale, from_last * scale
    outs = []
    for part in range(4):
        for which in range(3):
            copies[3 * part + which].wait()
        for g in range(2 * part, 2 * part + 2):
            at = [slice((3 * g + h) * HD, (3 * g + h + 1) * HD) for h in range(3)]
            key = [turned(held[0, :, a], cosine, from_next, from_last) for a in at]
            query = [turned(held[1, :, a], qc, qn, ql) for a in at]
            value = [held[2, :, a] for a in at]
            for c in range(2):
                to = 2 * g + c
                mine = slice(32 * c, 32 * c + 32)
                shared = jnp.concatenate([key[2][mine], value[2][mine]])
                packed[to, ONE, :] = jnp.where(edge, key[c], shared)
                packed[to, MAIN, :] = jnp.where(edge, query[c], key[c])
                packed[to, VALUE, :] = value[c]
                packed[to, QUERY, :] = query[2][mine]
                packed[to, REST, :] = jnp.where(edge, shared, query[c])
        four = pl.ds(4 * part, 4)
        outs.append(
            pltpu.make_async_copy(packed.at[four], out_hbm.at[four], out_sems.at[part])
        )
        outs[-1].start()
    for out in outs:
        out.wait()


def early_kernel(table, two, one, value_left, value_right):
    w = table[AT_W]
    one[...] = two[:, ONE]
    for out, special in ((value_left, 1), (value_right, 6)):

        @pl.when(w == special)
        def _(out=out):
            out[...] = two[:, QUERY]

        @pl.when(w != special)
        def _(out=out):
            out[...] = two[:, VALUE_A]


def late_kernel(table, two, l1, r1, main_left, main_right, swap):
    w = table[AT_W]
    for out, special, source in ((main_left, 1, r1), (main_right, 6, l1)):
        out[:, 64:96] = two[:, VALUE_B]

        @pl.when(w == special)
        def _(out=out, source=source):
            out[:, 0:64] = source[...]

        @pl.when(w != special)
        def _(out=out):
            out[:, 0:64] = two[:, MAIN]

    @pl.when((w == 0) | (w == 7))
    def _():
        swap[0] = two[:, REST]

    @pl.when((w != 0) & (w != 7))
    def _():
        swap[0] = two[:, ONE]

    swap[1] = l1[...]
    swap[2] = r1[...]


def attend(q, kp, vp, picks):
    top = weights = acc = None
    for pick in picks:
        s = lax.dot_general(q, kp[pick], (((1,), (1,)), ((), ())), preferred_element_type=F32)
        high = jnp.max(s, axis=1, keepdims=True)
        new = high if top is None else jnp.maximum(top, high)
        p = jnp.exp2(s - new)
        part = jnp.dot(p.astype(BF), whole(vp, pick), preferred_element_type=F32)
        if top is None:
            weights, acc = p, part
        else:
            shrink = jnp.exp2(top - new)
            weights, acc = weights * shrink + p, acc * shrink + part
        top = new
    return (acc / jnp.sum(weights, axis=1, keepdims=True)).astype(BF)


def whole(ref, *index):
    return ref[index].reshape(-1, HD)


def attend_column(table, column, at, query, kp, vp, store):
    @pl.loop(0, 2)
    def _(p):
        fours = [pl.ds(table[AT_TILE + 4 * column + 2 * p + i] * 4, 4) for i in range(2)]
        picks = [table[at + (2 * column + p) * WIN + j] for j in range(WIN)]
        o = attend(jnp.concatenate([query(four) for four in fours]), kp, vp, picks)
        half = o.shape[0] // 2
        for i, four in enumerate(fours):
            store(four, o[i * half : (i + 1) * half].reshape(4, -1, HD))


def fill_shared(base, mine, other, k2, v2):
    for t in range(4):
        four = slice(4 * t, 4 * t + 4)
        for pool, part in ((k2, slice(0, 32)), (v2, slice(32, 64))):
            pool[base + t, 0:128] = mine(four, part)
            pool[base + t, 128:256] = other(four, part)


def value_kernel(two, l3, r3, vh):
    for t in range(4):
        four = slice(4 * t, 4 * t + 4)
        vh[t] = two[four, VALUE]
        vh[4 + t, :, 0:32] = r3[four]
        vh[8 + t, :, 0:32] = l3[four]


def forwarded_kernel(table, l2, r2, vh, out):
    del vh
    w = table[AT_W]

    @pl.when(w == 0)
    def _():
        out[...] = r2[:, 0:64]

    @pl.when(w == 7)
    def _():
        out[...] = l2[:, 0:64]


def first_kernel(table, two, l1, r1, l2, r2, vh_in, sent, o_oth, kh, vh):
    del vh_in
    w = table[AT_W]
    inner = (w == 1) | (w == 6)
    edge = (w == 0) | (w == 7)

    @pl.when(jnp.logical_not(edge))
    def _():
        for t in range(4):
            four = slice(4 * t, 4 * t + 4)
            kh[t] = whole(two, four, MAIN)
            vh[4 + t, :, 32:64] = r2[four, 64:96]
            vh[8 + t, :, 32:64] = l2[four, 64:96]
        for base, special, early, late in ((4, 6, r1, r2), (8, 1, l1, l2)):

            @pl.when(w == special)
            def _(base=base, early=early):
                for t in range(4):
                    kh[base + t] = whole(early, slice(4 * t, 4 * t + 4))

            @pl.when(w != special)
            def _(base=base, late=late):
                for t in range(4):
                    kh[base + t] = whole(late, slice(4 * t, 4 * t + 4), slice(0, 64))

    def to_other(four, o):
        o_oth[four] = o

    def to_sent(four, o):
        sent[four, 0:64] = o

    for special, source in ((1, l2), (6, r2)):

        @pl.when(w == special)
        def _(source=source):
            query = lambda four: whole(source, four, slice(0, 64))
            attend_column(table, OTHER, AT_HEAD, query, kh, vh, to_other)

    @pl.when(jnp.logical_not(inner | edge))
    def _():
        query = lambda four: whole(two, four, REST)
        attend_column(table, THIS, AT_HEAD, query, kh, vh, to_sent)


def edge_kernel(table, two, l1, r1, l2, r2, l3, r3, sw, se, oth_in, o_oth, k2, v2):
    del oth_in
    w = table[AT_W]

    def to_other(four, o):
        o_oth[four, 0:32] = o

    for special, near, far, asked, swapped_near in ((0, r1, r2, r3, 2), (7, l1, l2, l3, 1)):

        @pl.when(w == special)
        def _(near=near, far=far, asked=asked, swapped_near=swapped_near):
            own = lambda f, p: whole(two, f, slice(REST.start + p.start, REST.start + p.stop))
            fill_shared(0, own, lambda f, p: whole(sw, 0, f, p), k2, v2)
            fill_shared(
                4, lambda f, p: whole(near, f, p), lambda f, p: whole(sw, swapped_near, f, p), k2, v2
            )
            fill_shared(8, lambda f, p: whole(far, f, p), lambda f, p: whole(se, f, p), k2, v2)
            query = lambda four: whole(asked, four)
            attend_column(table, OTHER, AT_SHARED, query, k2, v2, to_other)


def last_kernel(table, two, l1, r1, sw, kh, vh, k2, v2, sent_in, sent, k3, v3):
    del sent_in
    w = table[AT_W]
    inner = (w == 1) | (w == 6)
    edge = (w == 0) | (w == 7)

    def to_head(four, o):
        sent[four, 0:64] = o

    def to_shared(four, o):
        sent[four, 64:96] = o

    shared_query = lambda four: whole(two, four, QUERY)

    @pl.when(inner)
    def _():
        query = lambda four: whole(two, four, REST)
        attend_column(table, THIS, AT_HEAD, query, kh, vh, to_head)

    @pl.when(edge)
    def _():
        attend_column(table, THIS, AT_SHARED, shared_query, k2, v2, to_shared)

    @pl.when(jnp.logical_not(inner | edge))
    def _():
        fill_shared(0, lambda f, p: whole(two, f, p), lambda f, p: whole(sw, 0, f, p), k3, v3)
        fill_shared(4, lambda f, p: whole(r1, f, p), lambda f, p: whole(sw, 2, f, p), k3, v3)
        fill_shared(8, lambda f, p: whole(l1, f, p), lambda f, p: whole(sw, 1, f, p), k3, v3)
        attend_column(table, THIS, AT_SHARED, shared_query, k3, v3, to_shared)


def merge_kernel(table, o_left, o_right, sent_in, sent):
    del sent_in
    w = table[AT_W]

    @pl.when(w == 0)
    def _():
        sent[:, 0:64] = o_right[...]

    @pl.when(w == 7)
    def _():
        sent[:, 0:64] = o_left[...]

    @pl.when(w == 1)
    def _():
        sent[:, 64:96] = o_left[:, 0:32]

    @pl.when(w == 6)
    def _():
        sent[:, 64:96] = o_right[:, 0:32]


def unpack_kernel(in_ref, out_ref):
    for g in range(8):
        for h in range(2):
            out_ref[:, (3 * g + h) * HD : (3 * g + h + 1) * HD] = in_ref[2 * g + h, 0:64, :]
        last = slice((3 * g + 2) * HD, (3 * g + 3) * HD)
        out_ref[0:32, last] = in_ref[2 * g, 64:96, :]
        out_ref[32:64, last] = in_ref[2 * g + 1, 64:96, :]


def along_columns(block, distance):
    n = 2 * COLS
    return lax.ppermute(block, ("col", "half"), [(i, (i + 2 * distance) % n) for i in range(n)])


def swapped(block):
    return lax.ppermute(block, "core", [(0, 1), (1, 0)])


def exchanged(block):
    return lax.all_to_all(block, GROUP, split_axis=0, concat_axis=0, tiled=True)


SLOT = (16, 64, HD)
SENT = (16, 96, HD)
POOL = (12, TOK_TILE, HD)
PARTS = (12, 4, 64, HD)
FLOPS = 20_000_000_000


def kernel(body, name, outs, inputs, scratch=(), limit=32, aliases={}, flops=None, space=VMEM):
    return pl.pallas_call(
        body,
        out_shape=tuple(
            jax.ShapeDtypeStruct(shape, BF if len(shape) > 1 else jnp.int32) for shape in outs
        ),
        in_specs=[SMEM if i.dtype == jnp.int32 else space for i in inputs],
        out_specs=tuple(space if len(shape) > 1 else SMEM for shape in outs),
        scratch_shapes=list(scratch),
        input_output_aliases=aliases,
        compiler_params=pltpu.CompilerParams(vmem_limit_bytes=limit * MIB),
        cost_estimate=flops and pl.CostEstimate(flops=flops, bytes_accessed=0, transcendentals=0),
        name=name,
    )(*inputs)


def shards(queries, keys, values, order, nb):
    two, table = kernel(
        rotate_kernel,
        "rotate",
        ((16, 288, HD), (128,)),
        (order, nb.T, queries, keys, values),
        (
            pltpu.VMEM((3,) + queries.shape, BF),
            pltpu.VMEM((16, 288, HD), BF),
            pltpu.SemaphoreType.DMA((12,)),
            pltpu.SemaphoreType.DMA((4,)),
        ),
        limit=60,
        space=ANY,
    )
    two = exchanged(two)
    one, value_left, value_right = kernel(
        early_kernel, "early", (SLOT, (16, 32, HD), (16, 32, HD)), (table, two)
    )
    l1, r1 = along_columns(one, 1), along_columns(one, -1)
    l3, r3 = along_columns(value_right, 1), along_columns(value_left, -1)
    main_left, main_right, swap = kernel(
        late_kernel, "late", (SENT, SENT, (3,) + SLOT), (table, two, l1, r1)
    )
    l2, r2 = along_columns(main_right, 1), along_columns(main_left, -1)
    sw = swapped(swap)
    (vh,) = kernel(value_kernel, "values", (PARTS,), (two, l3, r3), flops=FLOPS)
    (se,) = kernel(forwarded_kernel, "forwarded", (SLOT,), (table, l2, r2, vh))
    se = swapped(se)
    sent, o_oth, kh, vh = kernel(
        first_kernel,
        "attend_first",
        (SENT, SLOT, POOL, PARTS),
        (table, two, l1, r1, l2, r2, vh),
        aliases={6: 3},
        flops=FLOPS,
    )
    o_oth, k2, v2 = kernel(
        edge_kernel,
        "attend_edge",
        (SLOT, POOL, POOL),
        (table, two, l1, r1, l2, r2, l3, r3, sw, se, o_oth),
        aliases={10: 0},
    )
    o_left, o_right = along_columns(o_oth, 1), along_columns(o_oth, -1)
    (sent,) = kernel(
        last_kernel,
        "attend_last",
        (SENT,),
        (table, two, l1, r1, sw, kh, vh, k2, v2, sent),
        (pltpu.VMEM(POOL, BF), pltpu.VMEM(POOL, BF)),
        aliases={9: 0},
    )
    (sent,) = kernel(merge_kernel, "merge", (SENT,), (table, o_left, o_right, sent), aliases={3: 0})
    return kernel(unpack_kernel, "unpack", (queries.shape,), (exchanged(sent),))[0]


def solution(mesh):
    blk, uly, dp = (mesh.shape[name] for name in ("blk", "uly", "dp"))
    fine = Mesh(
        mesh.devices.reshape(blk // 2, 2, uly // 2, 2, dp), ("col", "half", "x", "core", "dp")
    )
    tokens = ("dp", "col", "half", "x", "core")
    placed = (P(tokens, None), P(tokens, None), P(tokens, None), P("dp"), P("dp", None))
    return jax.shard_map(
        shards, mesh=fine, in_specs=placed, out_specs=P(tokens, None), check_vma=False
    )
```

time: 127 us -> 123 us (0.969); the launches traced: 125 us -> 123 us
  waiting for transfers between devices: 31.1 us -> 28.5 us
  starting transfers between devices: 39.4 us -> 41 us
    ppermute x8, starting transfers between devices: 35.5 us -> 37.2 us  [along_columns(): lax.ppermute(block, ('col', 'half'), [(i, (i + 2 * distance) % n) for i i...]
    ppermute x8, waiting for transfers between devices: 30.2 us -> 28.5 us  [along_columns(): lax.ppermute(block, ('col', 'half'), [(i, (i + 2 * distance) % n) for i i...]
  transfers between devices with their start and end apart: 10 -> 10, of which waited for: 5 -> 5; matrix products, arithmetic and copies ran while one was open for 0% -> 0% of each run, Pallas kernels for 2% -> 8%
where the time goes in v5:
time: 123 us
  starting transfers between devices  41 us (33%)
  blocking collectives  36.8 us (30%)
  waiting for transfers between devices  28.5 us (23%)
  Pallas kernels  16 us (13%)
    ppermute x8, starting transfers between devices, along_columns(): lax.ppermute(block, ('col', 'half'), [(i, (i + 2 * distance) % n) for i i...  37.2 us
    all_to_all x2, blocking collectives, exchanged(): return lax.all_to_all(block, GROUP, split_axis=0, concat_axis=0, tiled=True)  36.8 us
    ppermute x8, waiting for transfers between devices, along_columns(): lax.ppermute(block, ('col', 'half'), [(i, (i + 2 * distance) % n) for i i...  28.5 us
    pallas_call x10, Pallas kernels, kernel(): pl.pallas_call(body, out_shape=tuple((jax.ShapeDtypeStruct(shape, BF if l...  16 us
    ppermute x2, starting transfers between devices, swapped(): return lax.ppermute(block, 'core', [(0, 1), (1, 0)])  3.84 us
  transfers between devices with their start and end apart: 10, of which 5 were waited for; matrix products, arithmetic and copies ran while one was open for 0% of the time, Pallas kernels for 8%

profile of v5, /device:TPU:24, one launch (start us, length us, event | category | flops | bytes accessed | tf_op | source)
XLA Modules:
  0.0 122.6 jit_solution(17918787442697655926)
XLA Ops:
  0.0 4.0 %rotate.1 = (bf16[16,288,128]{2,1,0:T(8,128)(2,1)}, s32[128]{0:T(128)}) custom-call(s32[32]{0:T(128)} %order.1, s32[9,32]{1,0:T(8,128)} %bitcast.1, bf16[64,3072]{1,0:T(8,128)(2,1)} %q_hbm.1, bf16[64,3072]{1,0:T(8,128)(2,1)} %k_hbm.1, bf16[64,3072]{1,0:T(8,128)(2,1)} %v_hbm.1), custom_call_target="tpu_custom_call" | custom-call | tf_op jit(solution)/shard_map/rotate/pallas_call | solution.py:379
  4.0 0.0 copy-start
  4.0 23.7 %all_to_all.10.two = bf16[16,288,128]{2,1,0:T(8,128)(2,1)S(1)} all-to-all(bf16[16,288,128]{2,1,0:T(8,128)(2,1)} %get-tuple-element.21), channel_id=1, replica_groups=mesh['col'=8,'half'=2,'x'=4,'core'=2,'dp'=4] {'half','x','core'}, dimensions={0} | all-to-all | bytes 2359296 | tf_op jit(solution)/shard_map/all_to_all | solution.py:368
  27.7 0.0 copy-done
  27.7 0.6 early.1
  28.3 10.9 %collective-permute-start.1 = (bf16[16,64,128]{2,1,0:T(8,128)(2,1)S(1)}, bf16[16,64,128]{2,1,0:T(8,128)(2,1)S(1)}, u32[]{:S(2)}, u32[]{:S(2)}) collective-permute-start(bf16[16,64,128]{2,1,0:T(8,128)(2,1)S(1)} %get-tuple-element.22), channel_id=1, source_target_pairs={{0,448},{32,480},{64,0},{96,32},{128,64},{160,96},{192,128},{224,1... | collective-permute-start | bytes 786440 | tf_op jit(solution)/shard_map/ppermute | solution.py:360
  39.3 1.9 %collective-permute-start = (bf16[16,64,128]{2,1,0:T(8,128)(2,1)S(1)}, bf16[16,64,128]{2,1,0:T(8,128)(2,1)S(1)}, u32[]{:S(2)}, u32[]{:S(2)}) collective-permute-start(bf16[16,64,128]{2,1,0:T(8,128)(2,1)S(1)} %get-tuple-element.22), channel_id=1, source_target_pairs={{0,64},{32,96},{64,128},{96,160},{128,192},{160,224},{192,256},{22... | collective-permute-start | bytes 786440 | tf_op jit(solution)/shard_map/ppermute | solution.py:360
  41.2 1.9 %collective-permute-start.4 = (bf16[16,32,128]{2,1,0:T(8,128)(2,1)S(1)}, bf16[16,32,128]{2,1,0:T(8,128)(2,1)S(1)}, u32[]{:S(2)}, u32[]{:S(2)}) collective-permute-start(bf16[16,32,128]{2,1,0:T(8,128)(2,1)S(1)} %get-tuple-element.25), channel_id=1, source_target_pairs={{0,64},{32,96},{64,128},{96,160},{128,192},{160,224},{192,256},{22... | collective-permute-start | bytes 393224 | tf_op jit(solution)/shard_map/ppermute | solution.py:360
  43.1 6.0 %collective-permute-start.5 = (bf16[16,32,128]{2,1,0:T(8,128)(2,1)S(1)}, bf16[16,32,128]{2,1,0:T(8,128)(2,1)S(1)}, u32[]{:S(2)}, u32[]{:S(2)}) collective-permute-start(bf16[16,32,128]{2,1,0:T(8,128)(2,1)S(1)} %get-tuple-element.26), channel_id=1, source_target_pairs={{0,448},{32,480},{64,0},{96,32},{128,64},{160,96},{192,128},{224,1... | collective-permute-start | bytes 393224 | tf_op jit(solution)/shard_map/ppermute | solution.py:360
  49.2 0.0 collective-permute-done.1.r1
  49.2 5.7 %collective-permute-done.l1 = bf16[16,64,128]{2,1,0:T(8,128)(2,1)S(1)} collective-permute-done((bf16[16,64,128]{2,1,0:T(8,128)(2,1)S(1)}, bf16[16,64,128]{2,1,0:T(8,128)(2,1)S(1)}, u32[]{:S(2)}, u32[]{:S(2)}) %collective-permute-start) | collective-permute-done | bytes 262176 | tf_op jit(solution)/shard_map/ppermute | solution.py:360
  54.9 0.7 late.1
  55.6 1.9 %collective-permute-start.2 = (bf16[16,96,128]{2,1,0:T(8,128)(2,1)S(1)}, bf16[16,96,128]{2,1,0:T(8,128)(2,1)S(1)}, u32[]{:S(2)}, u32[]{:S(2)}) collective-permute-start(bf16[16,96,128]{2,1,0:T(8,128)(2,1)S(1)} %get-tuple-element.23), channel_id=1, source_target_pairs={{0,64},{32,96},{64,128},{96,160},{128,192},{160,224},{192,256},{22... | collective-permute-start | bytes 1179656 | tf_op jit(solution)/shard_map/ppermute | solution.py:360
  57.5 6.0 %collective-permute-start.3 = (bf16[16,96,128]{2,1,0:T(8,128)(2,1)S(1)}, bf16[16,96,128]{2,1,0:T(8,128)(2,1)S(1)}, u32[]{:S(2)}, u32[]{:S(2)}) collective-permute-start(bf16[16,96,128]{2,1,0:T(8,128)(2,1)S(1)} %get-tuple-element.24), channel_id=1, source_target_pairs={{0,448},{32,480},{64,0},{96,32},{128,64},{160,96},{192,128},{224,1... | collective-permute-start | bytes 1179656 | tf_op jit(solution)/shard_map/ppermute | solution.py:360
  63.5 0.0 collective-permute-done.4.l3
  63.5 0.0 collective-permute-done.5.r3
  63.6 1.9 %collective-permute-start.6 = (bf16[3,16,64,128]{3,2,1,0:T(8,128)(2,1)S(1)}, bf16[3,16,64,128]{3,2,1,0:T(8,128)(2,1)S(1)}, u32[]{:S(2)}, u32[]{:S(2)}) collective-permute-start(bf16[3,16,64,128]{3,2,1,0:T(8,128)(2,1)S(1)} %get-tuple-element.27), channel_id=1, source_target_pairs={{0,4},{4,0},{1,5},{5,1},{2,6},{6,2},{3,7},{7,3},{8,12},{12,8},{9,1... | collective-permute-start | bytes 2359304 | tf_op jit(solution)/shard_map/ppermute | solution.py:364
  65.5 5.5 %collective-permute-done.2.l2 = bf16[16,96,128]{2,1,0:T(8,128)(2,1)S(1)} collective-permute-done((bf16[16,96,128]{2,1,0:T(8,128)(2,1)S(1)}, bf16[16,96,128]{2,1,0:T(8,128)(2,1)S(1)}, u32[]{:S(2)}, u32[]{:S(2)}) %collective-permute-start.2) | collective-permute-done | bytes 393248 | tf_op jit(solution)/shard_map/ppermute | solution.py:360
  71.0 6.3 %collective-permute-done.3.r2 = bf16[16,96,128]{2,1,0:T(8,128)(2,1)S(1)} collective-permute-done((bf16[16,96,128]{2,1,0:T(8,128)(2,1)S(1)}, bf16[16,96,128]{2,1,0:T(8,128)(2,1)S(1)}, u32[]{:S(2)}, u32[]{:S(2)}) %collective-permute-start.3) | collective-permute-done | bytes 393248 | tf_op jit(solution)/shard_map/ppermute | solution.py:360
  77.3 0.6 forwarded.1
  77.8 1.9 %collective-permute-start.7 = (bf16[16,64,128]{2,1,0:T(8,128)(2,1)S(1)}, bf16[16,64,128]{2,1,0:T(8,128)(2,1)S(1)}, u32[]{:S(2)}, u32[]{:S(2)}) collective-permute-start(bf16[16,64,128]{2,1,0:T(8,128)(2,1)S(1)} %forwarded.1), channel_id=1, source_target_pairs={{0,4},{4,0},{1,5},{5,1},{2,6},{6,2},{3,7},{7,3},{8,12},{12,8},{9,1... | collective-permute-start | bytes 786440 | tf_op jit(solution)/shard_map/ppermute | solution.py:364
  79.8 4.1 %attend_first.1 = (bf16[16,96,128]{2,1,0:T(8,128)(2,1)S(1)}, bf16[16,64,128]{2,1,0:T(8,128)(2,1)S(1)}, bf16[12,256,128]{2,1,0:T(8,128)(2,1)S(1)}, bf16[12,4,64,128]{3,2,1,0:T(8,128)(2,1)S(1)}) custom-call(s32[128]{0:T(128)S(1)} %copy-done, bf16[16,288,128]{2,1,0:T(8,128)(2,1)S(1)} %all_to_all.10.two, ...), custom_call_target="tpu_custom_call", output_to_operand_aliasing={{3}: (6, {})} | custom-call | flops 20000000000 | tf_op jit(solution)/shard_map/attend_first/pallas_call | solution.py:379
  83.8 0.0 collective-permute-done.7.se
  83.9 0.0 collective-permute-done.6.sw
  83.9 0.6 attend_edge.1
  84.4 6.5 %collective-permute-start.9 = (bf16[16,64,128]{2,1,0:T(8,128)(2,1)S(1)}, bf16[16,64,128]{2,1,0:T(8,128)(2,1)S(1)}, u32[]{:S(2)}, u32[]{:S(2)}) collective-permute-start(bf16[16,64,128]{2,1,0:T(8,128)(2,1)S(1)} %get-tuple-element.29), channel_id=1, source_target_pairs={{0,448},{32,480},{64,0},{96,32},{128,64},{160,96},{192,128},{224,1... | collective-permute-start | bytes 786440 | tf_op jit(solution)/shard_map/ppermute | solution.py:360
  90.9 1.9 %collective-permute-start.8 = (bf16[16,64,128]{2,1,0:T(8,128)(2,1)S(1)}, bf16[16,64,128]{2,1,0:T(8,128)(2,1)S(1)}, u32[]{:S(2)}, u32[]{:S(2)}) collective-permute-start(bf16[16,64,128]{2,1,0:T(8,128)(2,1)S(1)} %get-tuple-element.29), channel_id=1, source_target_pairs={{0,64},{32,96},{64,128},{96,160},{128,192},{160,224},{192,256},{22... | collective-permute-start | bytes 786440 | tf_op jit(solution)/shard_map/ppermute | solution.py:360
  92.9 4.2 %attend_last.1.sent_in = bf16[16,96,128]{2,1,0:T(8,128)(2,1)S(1)} custom-call(s32[128]{0:T(128)S(1)} %copy-done, bf16[16,288,128]{2,1,0:T(8,128)(2,1)S(1)} %all_to_all.10.two, bf16[16,64,128]{2,1,0:T(8,128)(2,1)S(1)} %collective-permute-done.l1, bf16[16,64,128]{2,1,0:T(8,128)(2,1)S(1)} %collective-permute-done.1.r1, ...), custom_call_target="tpu_custom_call", output_to_operand_aliasing={{}: (9, {})} | custom-call | tf_op jit(solution)/shard_map/attend_last/pallas_call | solution.py:379
  97.1 5.7 %collective-permute-done.9.o_right = bf16[16,64,128]{2,1,0:T(8,128)(2,1)S(1)} collective-permute-done((bf16[16,64,128]{2,1,0:T(8,128)(2,1)S(1)}, bf16[16,64,128]{2,1,0:T(8,128)(2,1)S(1)}, u32[]{:S(2)}, u32[]{:S(2)}) %collective-permute-start.9) | collective-permute-done | bytes 262176 | tf_op jit(solution)/shard_map/ppermute | solution.py:360
  102.8 5.4 %collective-permute-done.8.o_left = bf16[16,64,128]{2,1,0:T(8,128)(2,1)S(1)} collective-permute-done((bf16[16,64,128]{2,1,0:T(8,128)(2,1)S(1)}, bf16[16,64,128]{2,1,0:T(8,128)(2,1)S(1)}, u32[]{:S(2)}, u32[]{:S(2)}) %collective-permute-start.8) | collective-permute-done | bytes 262176 | tf_op jit(solution)/shard_map/ppermute | solution.py:360
  108.1 0.6 merge.1
  108.7 13.1 %all_to_all.11.in_ref = bf16[16,96,128]{2,1,0:T(8,128)(2,1)S(1)} all-to-all(bf16[16,96,128]{2,1,0:T(8,128)(2,1)S(1)} %merge.1), channel_id=1, replica_groups=mesh['col'=8,'half'=2,'x'=4,'core'=2,'dp'=4] {'half','x','core'}, dimensions={0} | all-to-all | bytes 786432 | tf_op jit(solution)/shard_map/all_to_all | solution.py:368
  121.8 0.8 unpack.1
  (1 shorter events, 0.0 us)
Async XLA Ops:
  4.0 23.7 %copy-start = (s32[128]{0:T(128)S(1)}, s32[128]{0:T(128)}, u32[]{:S(2)}) copy-start(s32[128]{0:T(128)} %get-tuple-element.20.table) | copy-start | bytes 1540
  28.3 20.9 %collective-permute-start.1 = (bf16[16,64,128]{2,1,0:T(8,128)(2,1)S(1)}, bf16[16,64,128]{2,1,0:T(8,128)(2,1)S(1)}, u32[]{:S(2)}, u32[]{:S(2)}) collective-permute-start(bf16[16,64,128]{2,1,0:T(8,128)(2,1)S(1)} %get-tuple-element.22), channel_id=1, source_target_pairs={{0,448},{32,480},{64,0},{96,32},{128,64},{160,96},{192,128},{224,1... | collective-permute-start | bytes 786440 | tf_op jit(solution)/shard_map/ppermute | solution.py:360
  39.3 15.6 %collective-permute-start = (bf16[16,64,128]{2,1,0:T(8,128)(2,1)S(1)}, bf16[16,64,128]{2,1,0:T(8,128)(2,1)S(1)}, u32[]{:S(2)}, u32[]{:S(2)}) collective-permute-start(bf16[16,64,128]{2,1,0:T(8,128)(2,1)S(1)} %get-tuple-element.22), channel_id=1, source_target_pairs={{0,64},{32,96},{64,128},{96,160},{128,192},{160,224},{192,256},{22... | collective-permute-start | bytes 786440 | tf_op jit(solution)/shard_map/ppermute | solution.py:360
  41.2 22.3 %collective-permute-start.4 = (bf16[16,32,128]{2,1,0:T(8,128)(2,1)S(1)}, bf16[16,32,128]{2,1,0:T(8,128)(2,1)S(1)}, u32[]{:S(2)}, u32[]{:S(2)}) collective-permute-start(bf16[16,32,128]{2,1,0:T(8,128)(2,1)S(1)} %get-tuple-element.25), channel_id=1, source_target_pairs={{0,64},{32,96},{64,128},{96,160},{128,192},{160,224},{192,256},{22... | collective-permute-start | bytes 393224 | tf_op jit(solution)/shard_map/ppermute | solution.py:360
  43.1 20.4 %collective-permute-start.5 = (bf16[16,32,128]{2,1,0:T(8,128)(2,1)S(1)}, bf16[16,32,128]{2,1,0:T(8,128)(2,1)S(1)}, u32[]{:S(2)}, u32[]{:S(2)}) collective-permute-start(bf16[16,32,128]{2,1,0:T(8,128)(2,1)S(1)} %get-tuple-element.26), channel_id=1, source_target_pairs={{0,448},{32,480},{64,0},{96,32},{128,64},{160,96},{192,128},{224,1... | collective-permute-start | bytes 393224 | tf_op jit(solution)/shard_map/ppermute | solution.py:360
  55.6 15.4 %collective-permute-start.2 = (bf16[16,96,128]{2,1,0:T(8,128)(2,1)S(1)}, bf16[16,96,128]{2,1,0:T(8,128)(2,1)S(1)}, u32[]{:S(2)}, u32[]{:S(2)}) collective-permute-start(bf16[16,96,128]{2,1,0:T(8,128)(2,1)S(1)} %get-tuple-element.23), channel_id=1, source_target_pairs={{0,64},{32,96},{64,128},{96,160},{128,192},{160,224},{192,256},{22... | collective-permute-start | bytes 1179656 | tf_op jit(solution)/shard_map/ppermute | solution.py:360
  57.5 19.8 %collective-permute-start.3 = (bf16[16,96,128]{2,1,0:T(8,128)(2,1)S(1)}, bf16[16,96,128]{2,1,0:T(8,128)(2,1)S(1)}, u32[]{:S(2)}, u32[]{:S(2)}) collective-permute-start(bf16[16,96,128]{2,1,0:T(8,128)(2,1)S(1)} %get-tuple-element.24), channel_id=1, source_target_pairs={{0,448},{32,480},{64,0},{96,32},{128,64},{160,96},{192,128},{224,1... | collective-permute-start | bytes 1179656 | tf_op jit(solution)/shard_map/ppermute | solution.py:360
  63.6 20.3 %collective-permute-start.6 = (bf16[3,16,64,128]{3,2,1,0:T(8,128)(2,1)S(1)}, bf16[3,16,64,128]{3,2,1,0:T(8,128)(2,1)S(1)}, u32[]{:S(2)}, u32[]{:S(2)}) collective-permute-start(bf16[3,16,64,128]{3,2,1,0:T(8,128)(2,1)S(1)} %get-tuple-element.27), channel_id=1, source_target_pairs={{0,4},{4,0},{1,5},{5,1},{2,6},{6,2},{3,7},{7,3},{8,12},{12,8},{9,1... | collective-permute-start | bytes 2359304 | tf_op jit(solution)/shard_map/ppermute | solution.py:364
  77.8 6.0 %collective-permute-start.7 = (bf16[16,64,128]{2,1,0:T(8,128)(2,1)S(1)}, bf16[16,64,128]{2,1,0:T(8,128)(2,1)S(1)}, u32[]{:S(2)}, u32[]{:S(2)}) collective-permute-start(bf16[16,64,128]{2,1,0:T(8,128)(2,1)S(1)} %forwarded.1), channel_id=1, source_target_pairs={{0,4},{4,0},{1,5},{5,1},{2,6},{6,2},{3,7},{7,3},{8,12},{12,8},{9,1... | collective-permute-start | bytes 786440 | tf_op jit(solution)/shard_map/ppermute | solution.py:364
  84.4 18.3 %collective-permute-start.9 = (bf16[16,64,128]{2,1,0:T(8,128)(2,1)S(1)}, bf16[16,64,128]{2,1,0:T(8,128)(2,1)S(1)}, u32[]{:S(2)}, u32[]{:S(2)}) collective-permute-start(bf16[16,64,128]{2,1,0:T(8,128)(2,1)S(1)} %get-tuple-element.29), channel_id=1, source_target_pairs={{0,448},{32,480},{64,0},{96,32},{128,64},{160,96},{192,128},{224,1... | collective-permute-start | bytes 786440 | tf_op jit(solution)/shard_map/ppermute | solution.py:360
  90.9 17.2 %collective-permute-start.8 = (bf16[16,64,128]{2,1,0:T(8,128)(2,1)S(1)}, bf16[16,64,128]{2,1,0:T(8,128)(2,1)S(1)}, u32[]{:S(2)}, u32[]{:S(2)}) collective-permute-start(bf16[16,64,128]{2,1,0:T(8,128)(2,1)S(1)} %get-tuple-element.29), channel_id=1, source_target_pairs={{0,64},{32,96},{64,128},{96,160},{128,192},{160,224},{192,256},{22... | collective-permute-start | bytes 786440 | tf_op jit(solution)/shard_map/ppermute | solution.py:360

commit v6 on v5

--- a/solution.py
+++ b/solution.py
@@ -20,7 +20,6 @@
 MIB = 1024 * 1024
 ONE, MAIN, VALUE = slice(0, 64), slice(64, 128), slice(128, 192)
 QUERY, REST = slice(192, 224), slice(224, 288)
-VALUE_A, VALUE_B = slice(128, 160), slice(160, 192)
 AT_W, AT_TILE, AT_HEAD, AT_SHARED = 0, 8, 16, 64
 OTHER, THIS = 0, 1
 
@@ -35,6 +34,27 @@
         freq = jnp.exp(within * float(-np.log(10000.0) / count))
         rows.append(jnp.where((pair >= first) & (pair < first + count), freq, 0.0)[0:1])
     return rows
+
+
+def turns(tile, frame_in_tile, scale):
+    frame = (tile // 32 * 4 + frame_in_tile).astype(F32)
+    row0 = (tile // 8 % 4 * 8).astype(F32)
+    col0 = (tile % 8 * 8).astype(F32)
+    token = lax.broadcasted_iota(jnp.int32, (64, HD), 0)
+    row = row0 + (token // 8).astype(F32)
+    col = col0 + (token % 8).astype(F32)
+    by_frame, by_row, by_col = frequency_rows()
+    angle = frame * by_frame + row * by_row + col * by_col
+    cosine = jnp.cos(angle) * scale
+    sine = jnp.sin(angle) * scale
+    even = lax.broadcasted_iota(jnp.int32, (64, HD), 1) % 2 == 0
+    return cosine, jnp.where(even, -sine, 0.0), jnp.where(even, 0.0, sine)
+
+
+def turned(x, factors):
+    here, after, before = factors
+    x = x.astype(F32)
+    return (x * here + pltpu.roll(x, HD - 1, 1) * after + pltpu.roll(x, 1, 1) * before).astype(BF)
 
 
 def plan(order, nb, table):
@@ -66,7 +86,6 @@
     x = lax.axis_index("x")
     frame_in_tile = lax.rem(x, 2) * 2 + lax.axis_index("core")
     slot = lax.axis_index("col") * 4 + lax.axis_index("half") * 2 + x // 2
-    rows = held.shape[1]
     width = 2 * 3 * HD
     copies = []
     for part in range(4):
@@ -81,35 +100,15 @@
         copy.start()
     w = plan(order, nb, table)
     edge = (w == 0) | (w == 7)
-    tile = order[slot]
-    frame = (tile // 32 * 4 + frame_in_tile).astype(F32)
-    row0 = (tile // 8 % 4 * 8).astype(F32)
-    col0 = (tile % 8 * 8).astype(F32)
-    token = lax.broadcasted_iota(jnp.int32, (rows, HD), 0)
-    row = row0 + (token // 8).astype(F32)
-    col = col0 + (token % 8).astype(F32)
-    by_frame, by_row, by_col = frequency_rows()
-    angle = frame * by_frame + row * by_row + col * by_col
-    cosine = jnp.cos(angle)
-    sine = jnp.sin(angle)
-    even = lax.broadcasted_iota(jnp.int32, (rows, HD), 1) % 2 == 0
-    from_next = jnp.where(even, -sine, 0.0)
-    from_last = jnp.where(even, 0.0, sine)
-    scale = HD ** (-0.5) * 1.4426950408889634
-
-    def turned(x, c, n, l):
-        x = x.astype(F32)
-        return (x * c + pltpu.roll(x, HD - 1, 1) * n + pltpu.roll(x, 1, 1) * l).astype(BF)
-
-    qc, qn, ql = cosine * scale, from_next * scale, from_last * scale
+    factors = turns(order[slot], frame_in_tile, 1.0)
     outs = []
     for part in range(4):
         for which in range(3):
             copies[3 * part + which].wait()
         for g in range(2 * part, 2 * part + 2):
             at = [slice((3 * g + h) * HD, (3 * g + h + 1) * HD) for h in range(3)]
-            key = [turned(held[0, :, a], cosine, from_next, from_last) for a in at]
-            query = [turned(held[1, :, a], qc, qn, ql) for a in at]
+            key = [turned(held[0, :, a], factors) for a in at]
+            query = [held[1, :, a] for a in at]
             value = [held[2, :, a] for a in at]
             for c in range(2):
                 to = 2 * g + c
@@ -129,43 +128,64 @@
         out.wait()
 
 
-def early_kernel(table, two, one, value_left, value_right):
+def early_kernel(table, two, one, own):
     w = table[AT_W]
     one[...] = two[:, ONE]
+
+    @pl.when((w == 0) | (w == 7))
+    def _():
+        own[...] = two[:, REST]
+
+    @pl.when((w != 0) & (w != 7))
+    def _():
+        own[...] = two[:, ONE]
+
+
+def middle_kernel(table, order, two, q_head, q_shared, value_left, value_right):
+    w = table[AT_W]
+    edge = (w == 0) | (w == 7)
+    col, core = lax.axis_index("col"), lax.axis_index("core")
+
+    @pl.loop(0, 16)
+    def _(source):
+        scale = HD ** (-0.5) * 1.4426950408889634
+        factors = turns(order[col * 4 + source // 4], lax.rem(source, 4), scale)
+        held = two[source]
+        q_head[source] = turned(jnp.where(edge, held[MAIN], held[REST]), factors)
+        mine = [jnp.where(core == 0, f[0:32], f[32:64]) for f in factors]
+        q_shared[source] = turned(held[QUERY], mine)
+
     for out, special in ((value_left, 1), (value_right, 6)):
 
         @pl.when(w == special)
         def _(out=out):
-            out[...] = two[:, QUERY]
+            out[:, 0:32] = q_shared[...]
+            out[:, 32:64] = q_shared[...]
 
         @pl.when(w != special)
         def _(out=out):
-            out[...] = two[:, VALUE_A]
-
-
-def late_kernel(table, two, l1, r1, main_left, main_right, swap):
-    w = table[AT_W]
+            out[...] = two[:, VALUE]
+
+
+def late_kernel(table, two, q_head, l1, r1, main_left, main_right, swap):
+    w = table[AT_W]
+    edge = (w == 0) | (w == 7)
     for out, special, source in ((main_left, 1, r1), (main_right, 6, l1)):
-        out[:, 64:96] = two[:, VALUE_B]
 
         @pl.when(w == special)
         def _(out=out, source=source):
-            out[:, 0:64] = source[...]
-
-        @pl.when(w != special)
+            out[...] = source[...]
+
+        @pl.when(edge)
         def _(out=out):
-            out[:, 0:64] = two[:, MAIN]
-
-    @pl.when((w == 0) | (w == 7))
-    def _():
-        swap[0] = two[:, REST]
-
-    @pl.when((w != 0) & (w != 7))
-    def _():
-        swap[0] = two[:, ONE]
-
-    swap[1] = l1[...]
-    swap[2] = r1[...]
+            out[...] = q_head[...]
+
+        @pl.when((w != special) & jnp.logical_not(edge))
+        def _(out=out):
+            out[...] = two[:, MAIN]
+
+    swap[0] = l1[...]
+    swap[1] = r1[...]
 
 
 def attend(q, kp, vp, picks):
@@ -212,8 +232,8 @@
     for t in range(4):
         four = slice(4 * t, 4 * t + 4)
         vh[t] = two[four, VALUE]
-        vh[4 + t, :, 0:32] = r3[four]
-        vh[8 + t, :, 0:32] = l3[four]
+        vh[4 + t] = r3[four]
+        vh[8 + t] = l3[four]
 
 
 def forwarded_kernel(table, l2, r2, vh, out):
@@ -222,15 +242,14 @@
 
     @pl.when(w == 0)
     def _():
-        out[...] = r2[:, 0:64]
+        out[...] = r2[...]
 
     @pl.when(w == 7)
     def _():
-        out[...] = l2[:, 0:64]
-
-
-def first_kernel(table, two, l1, r1, l2, r2, vh_in, sent, o_oth, kh, vh):
-    del vh_in
+        out[...] = l2[...]
+
+
+def first_kernel(table, two, q_head, l1, r1, l2, r2, vh, sent, o_oth, kh):
     w = table[AT_W]
     inner = (w == 1) | (w == 6)
     edge = (w == 0) | (w == 7)
@@ -240,8 +259,6 @@
         for t in range(4):
             four = slice(4 * t, 4 * t + 4)
             kh[t] = whole(two, four, MAIN)
-            vh[4 + t, :, 32:64] = r2[four, 64:96]
-            vh[8 + t, :, 32:64] = l2[four, 64:96]
         for base, special, early, late in ((4, 6, r1, r2), (8, 1, l1, l2)):
 
             @pl.when(w == special)
@@ -252,7 +269,7 @@
             @pl.when(w != special)
             def _(base=base, late=late):
                 for t in range(4):
-                    kh[base + t] = whole(late, slice(4 * t, 4 * t + 4), slice(0, 64))
+                    kh[base + t] = whole(late, slice(4 * t, 4 * t + 4))
 
     def to_other(four, o):
         o_oth[four] = o
@@ -264,37 +281,37 @@
 
         @pl.when(w == special)
         def _(source=source):
-            query = lambda four: whole(source, four, slice(0, 64))
+            query = lambda four: whole(source, four)
             attend_column(table, OTHER, AT_HEAD, query, kh, vh, to_other)
 
     @pl.when(jnp.logical_not(inner | edge))
     def _():
-        query = lambda four: whole(two, four, REST)
+        query = lambda four: whole(q_head, four)
         attend_column(table, THIS, AT_HEAD, query, kh, vh, to_sent)
 
 
-def edge_kernel(table, two, l1, r1, l2, r2, l3, r3, sw, se, oth_in, o_oth, k2, v2):
+def edge_kernel(table, two, l1, r1, l2, r2, l3, r3, s0, sw, se, oth_in, o_oth, k2, v2):
     del oth_in
     w = table[AT_W]
 
     def to_other(four, o):
         o_oth[four, 0:32] = o
 
-    for special, near, far, asked, swapped_near in ((0, r1, r2, r3, 2), (7, l1, l2, l3, 1)):
+    for special, near, far, asked, swapped_near in ((0, r1, r2, r3, 1), (7, l1, l2, l3, 0)):
 
         @pl.when(w == special)
         def _(near=near, far=far, asked=asked, swapped_near=swapped_near):
             own = lambda f, p: whole(two, f, slice(REST.start + p.start, REST.start + p.stop))
-            fill_shared(0, own, lambda f, p: whole(sw, 0, f, p), k2, v2)
+            fill_shared(0, own, lambda f, p: whole(s0, f, p), k2, v2)
             fill_shared(
                 4, lambda f, p: whole(near, f, p), lambda f, p: whole(sw, swapped_near, f, p), k2, v2
             )
             fill_shared(8, lambda f, p: whole(far, f, p), lambda f, p: whole(se, f, p), k2, v2)
-            query = lambda four: whole(asked, four)
+            query = lambda four: whole(asked, four, slice(0, 32))
             attend_column(table, OTHER, AT_SHARED, query, k2, v2, to_other)
 
 
-def last_kernel(table, two, l1, r1, sw, kh, vh, k2, v2, sent_in, sent, k3, v3):
+def last_kernel(table, two, q_head, q_shared, l1, r1, s0, sw, kh, vh, k2, v2, sent_in, sent, k3, v3):
     del sent_in
     w = table[AT_W]
     inner = (w == 1) | (w == 6)
@@ -306,11 +323,11 @@
     def to_shared(four, o):
         sent[four, 64:96] = o
 
-    shared_query = lambda four: whole(two, four, QUERY)
+    shared_query = lambda four: whole(q_shared, four)
 
     @pl.when(inner)
     def _():
-        query = lambda four: whole(two, four, REST)
+        query = lambda four: whole(q_head, four)
         attend_column(table, THIS, AT_HEAD, query, kh, vh, to_head)
 
     @pl.when(edge)
@@ -319,9 +336,9 @@
 
     @pl.when(jnp.logical_not(inner | edge))
     def _():
-        fill_shared(0, lambda f, p: whole(two, f, p), lambda f, p: whole(sw, 0, f, p), k3, v3)
-        fill_shared(4, lambda f, p: whole(r1, f, p), lambda f, p: whole(sw, 2, f, p), k3, v3)
-        fill_shared(8, lambda f, p: whole(l1, f, p), lambda f, p: whole(sw, 1, f, p), k3, v3)
+        fill_shared(0, lambda f, p: whole(two, f, p), lambda f, p: whole(s0, f, p), k3, v3)
+        fill_shared(4, lambda f, p: whole(r1, f, p), lambda f, p: whole(sw, 1, f, p), k3, v3)
+        fill_shared(8, lambda f, p: whole(l1, f, p), lambda f, p: whole(sw, 0, f, p), k3, v3)
         attend_column(table, THIS, AT_SHARED, shared_query, k3, v3, to_shared)
 
 
@@ -407,42 +424,43 @@
         space=ANY,
     )
     two = exchanged(two)
-    one, value_left, value_right = kernel(
-        early_kernel, "early", (SLOT, (16, 32, HD), (16, 32, HD)), (table, two)
-    )
+    one, own = kernel(early_kernel, "early", (SLOT, SLOT), (table, two))
     l1, r1 = along_columns(one, 1), along_columns(one, -1)
+    q_head, q_shared, value_left, value_right = kernel(
+        middle_kernel, "middle", (SLOT, (16, 32, HD), SLOT, SLOT), (table, order, two), flops=FLOPS
+    )
     l3, r3 = along_columns(value_right, 1), along_columns(value_left, -1)
     main_left, main_right, swap = kernel(
-        late_kernel, "late", (SENT, SENT, (3,) + SLOT), (table, two, l1, r1)
+        late_kernel, "late", (SLOT, SLOT, (2,) + SLOT), (table, two, q_head, l1, r1)
     )
     l2, r2 = along_columns(main_right, 1), along_columns(main_left, -1)
     sw = swapped(swap)
+    s0 = swapped(own)
     (vh,) = kernel(value_kernel, "values", (PARTS,), (two, l3, r3), flops=FLOPS)
     (se,) = kernel(forwarded_kernel, "forwarded", (SLOT,), (table, l2, r2, vh))
     se = swapped(se)
-    sent, o_oth, kh, vh = kernel(
+    sent, o_oth, kh = kernel(
         first_kernel,
         "attend_first",
-        (SENT, SLOT, POOL, PARTS),
-        (table, two, l1, r1, l2, r2, vh),
-        aliases={6: 3},
+        (SENT, SLOT, POOL),
+        (table, two, q_head, l1, r1, l2, r2, vh),
         flops=FLOPS,
     )
     o_oth, k2, v2 = kernel(
         edge_kernel,
         "attend_edge",
         (SLOT, POOL, POOL),
-        (table, two, l1, r1, l2, r2, l3, r3, sw, se, o_oth),
-        aliases={10: 0},
+        (table, two, l1, r1, l2, r2, l3, r3, s0, sw, se, o_oth),
+        aliases={11: 0},
     )
     o_left, o_right = along_columns(o_oth, 1), along_columns(o_oth, -1)
     (sent,) = kernel(
         last_kernel,
         "attend_last",
         (SENT,),
-        (table, two, l1, r1, sw, kh, vh, k2, v2, sent),
+        (table, two, q_head, q_shared, l1, r1, s0, sw, kh, vh, k2, v2, sent),
         (pltpu.VMEM(POOL, BF), pltpu.VMEM(POOL, BF)),
-        aliases={9: 0},
+        aliases={12: 0},
     )
     (sent,) = kernel(merge_kernel, "merge", (SENT,), (table, o_left, o_right, sent), aliases={3: 0})
     return kernel(unpack_kernel, "unpack", (queries.shape,), (exchanged(sent),))[0]

time: 123 us -> 121 us (0.984)
  waiting for transfers between devices: 28.5 us -> 25.2 us
  Pallas kernels: 16 us -> 18.3 us
    ppermute x8, waiting for transfers between devices: 28.5 us -> 25.2 us  [along_columns(): lax.ppermute(block, ('col', 'half'), [(i, (i + 2 * distance) % n) for i i...]
    pallas_call x10 -> x11, Pallas kernels: 16 us -> 18.3 us  [kernel(): pl.pallas_call(body, out_shape=tuple((jax.ShapeDtypeStruct(shape, BF if l...]
    ppermute x2 -> x3, starting transfers between devices: 3.84 us -> 5.75 us  [swapped(): return lax.ppermute(block, 'core', [(0, 1), (1, 0)])]
    ppermute x8, starting transfers between devices: 37.2 us -> 35.5 us  [along_columns(): lax.ppermute(block, ('col', 'half'), [(i, (i + 2 * distance) % n) for i i...]
  transfers between devices with their start and end apart: 10 -> 11, of which waited for: 5 -> 5; matrix products, arithmetic and copies ran while one was open for 0% -> 0% of each run, Pallas kernels for 8% -> 10%
where the time goes in v6:
time: 121 us
  starting transfers between devices  41.3 us (34%)
  blocking collectives  35.8 us (30%)
  waiting for transfers between devices  25.2 us (21%)
  Pallas kernels  18.3 us (15%)
    all_to_all x2, blocking collectives, exchanged(): return lax.all_to_all(block, GROUP, split_axis=0, concat_axis=0, tiled=True)  35.8 us
    ppermute x8, starting transfers between devices, along_columns(): lax.ppermute(block, ('col', 'half'), [(i, (i + 2 * distance) % n) for i i...  35.5 us
    ppermute x8, waiting for transfers between devices, along_columns(): lax.ppermute(block, ('col', 'half'), [(i, (i + 2 * distance) % n) for i i...  25.2 us
    pallas_call x11, Pallas kernels, kernel(): pl.pallas_call(body, out_shape=tuple((jax.ShapeDtypeStruct(shape, BF if l...  18.3 us
    ppermute x3, starting transfers between devices, swapped(): return lax.ppermute(block, 'core', [(0, 1), (1, 0)])  5.75 us
  transfers between devices with their start and end apart: 11, of which 5 were waited for; matrix products, arithmetic and copies ran while one was open for 0% of the time, Pallas kernels for 10%

profile of v6, /device:TPU:24, one launch (start us, length us, event | category | flops | bytes accessed | tf_op | source)
XLA Modules:
  0.0 120.8 jit_solution(17545270585964989792)
XLA Ops:
  0.0 3.7 %rotate.1 = (bf16[16,288,128]{2,1,0:T(8,128)(2,1)}, s32[128]{0:T(128)}) custom-call(s32[32]{0:T(128)} %order.3, s32[9,32]{1,0:T(8,128)} %bitcast.1, bf16[64,3072]{1,0:T(8,128)(2,1)} %q_hbm.1, bf16[64,3072]{1,0:T(8,128)(2,1)} %k_hbm.1, bf16[64,3072]{1,0:T(8,128)(2,1)} %v_hbm.1), custom_call_target="tpu_custom_call" | custom-call | tf_op jit(solution)/shard_map/rotate/pallas_call | solution.py:396
  3.7 0.0 copy-start
  3.8 23.7 %all_to_all.10.two = bf16[16,288,128]{2,1,0:T(8,128)(2,1)S(1)} all-to-all(bf16[16,288,128]{2,1,0:T(8,128)(2,1)} %get-tuple-element.23), channel_id=1, replica_groups=mesh['col'=8,'half'=2,'x'=4,'core'=2,'dp'=4] {'half','x','core'}, dimensions={0} | all-to-all | bytes 2359296 | tf_op jit(solution)/shard_map/all_to_all | solution.py:385
  27.5 0.0 copy-start.1
  27.5 0.0 copy-done
  27.5 0.6 early.1
  28.1 10.9 %collective-permute-start.1 = (bf16[16,64,128]{2,1,0:T(8,128)(2,1)S(1)}, bf16[16,64,128]{2,1,0:T(8,128)(2,1)S(1)}, u32[]{:S(2)}, u32[]{:S(2)}) collective-permute-start(bf16[16,64,128]{2,1,0:T(8,128)(2,1)S(1)} %get-tuple-element.24), channel_id=1, source_target_pairs={{0,448},{32,480},{64,0},{96,32},{128,64},{160,96},{192,128},{224,1... | collective-permute-start | bytes 786440 | tf_op jit(solution)/shard_map/ppermute | solution.py:377
  39.0 1.9 %collective-permute-start = (bf16[16,64,128]{2,1,0:T(8,128)(2,1)S(1)}, bf16[16,64,128]{2,1,0:T(8,128)(2,1)S(1)}, u32[]{:S(2)}, u32[]{:S(2)}) collective-permute-start(bf16[16,64,128]{2,1,0:T(8,128)(2,1)S(1)} %get-tuple-element.24), channel_id=1, source_target_pairs={{0,64},{32,96},{64,128},{96,160},{128,192},{160,224},{192,256},{22... | collective-permute-start | bytes 786440 | tf_op jit(solution)/shard_map/ppermute | solution.py:377
  40.9 0.0 copy-done.1
  41.0 3.5 %middle.1 = (bf16[16,64,128]{2,1,0:T(8,128)(2,1)S(1)}, bf16[16,32,128]{2,1,0:T(8,128)(2,1)S(1)}, bf16[16,64,128]{2,1,0:T(8,128)(2,1)S(1)}, bf16[16,64,128]{2,1,0:T(8,128)(2,1)S(1)}) custom-call(s32[128]{0:T(128)S(1)} %copy-done, s32[32]{0:T(128)S(1)} %copy-done.1, bf16[16,288,128]{2,1,0:T(8,128)(2,1)S(1)} %all_to_all.10.two), custom_call_target="tpu_custom_call" | custom-call | flops 20000000000 | tf_op jit(solution)/shard_map/middle/pallas_call | solution.py:396
  44.4 1.9 %collective-permute-start.4 = (bf16[16,64,128]{2,1,0:T(8,128)(2,1)S(1)}, bf16[16,64,128]{2,1,0:T(8,128)(2,1)S(1)}, u32[]{:S(2)}, u32[]{:S(2)}) collective-permute-start(bf16[16,64,128]{2,1,0:T(8,128)(2,1)S(1)} %get-tuple-element.28), channel_id=1, source_target_pairs={{0,64},{32,96},{64,128},{96,160},{128,192},{160,224},{192,256},{22... | collective-permute-start | bytes 786440 | tf_op jit(solution)/shard_map/ppermute | solution.py:377
  46.4 6.1 %collective-permute-start.5 = (bf16[16,64,128]{2,1,0:T(8,128)(2,1)S(1)}, bf16[16,64,128]{2,1,0:T(8,128)(2,1)S(1)}, u32[]{:S(2)}, u32[]{:S(2)}) collective-permute-start(bf16[16,64,128]{2,1,0:T(8,128)(2,1)S(1)} %get-tuple-element.29), channel_id=1, source_target_pairs={{0,448},{32,480},{64,0},{96,32},{128,64},{160,96},{192,128},{224,1... | collective-permute-start | bytes 786440 | tf_op jit(solution)/shard_map/ppermute | solution.py:377
  52.4 1.9 %collective-permute-start.6 = (bf16[16,64,128]{2,1,0:T(8,128)(2,1)S(1)}, bf16[16,64,128]{2,1,0:T(8,128)(2,1)S(1)}, u32[]{:S(2)}, u32[]{:S(2)}) collective-permute-start(bf16[16,64,128]{2,1,0:T(8,128)(2,1)S(1)} %get-tuple-element.30), channel_id=1, source_target_pairs={{0,4},{4,0},{1,5},{5,1},{2,6},{6,2},{3,7},{7,3},{8,12},{12,8},{9,1... | collective-permute-start | bytes 786440 | tf_op jit(solution)/shard_map/ppermute | solution.py:381
  54.3 0.0 collective-permute-done.1.r1
  54.4 0.3 collective-permute-done.l1
  54.6 0.6 late.1
  55.3 1.9 %collective-permute-start.2 = (bf16[16,64,128]{2,1,0:T(8,128)(2,1)S(1)}, bf16[16,64,128]{2,1,0:T(8,128)(2,1)S(1)}, u32[]{:S(2)}, u32[]{:S(2)}) collective-permute-start(bf16[16,64,128]{2,1,0:T(8,128)(2,1)S(1)} %get-tuple-element.26), channel_id=1, source_target_pairs={{0,64},{32,96},{64,128},{96,160},{128,192},{160,224},{192,256},{22... | collective-permute-start | bytes 786440 | tf_op jit(solution)/shard_map/ppermute | solution.py:377
  57.2 6.0 %collective-permute-start.3 = (bf16[16,64,128]{2,1,0:T(8,128)(2,1)S(1)}, bf16[16,64,128]{2,1,0:T(8,128)(2,1)S(1)}, u32[]{:S(2)}, u32[]{:S(2)}) collective-permute-start(bf16[16,64,128]{2,1,0:T(8,128)(2,1)S(1)} %get-tuple-element.27), channel_id=1, source_target_pairs={{0,448},{32,480},{64,0},{96,32},{128,64},{160,96},{192,128},{224,1... | collective-permute-start | bytes 786440 | tf_op jit(solution)/shard_map/ppermute | solution.py:377
  63.3 0.7 collective-permute-done.4.l3
  64.0 1.9 %collective-permute-start.7 = (bf16[2,16,64,128]{3,2,1,0:T(8,128)(2,1)S(1)}, bf16[2,16,64,128]{3,2,1,0:T(8,128)(2,1)S(1)}, u32[]{:S(2)}, u32[]{:S(2)}) collective-permute-start(bf16[2,16,64,128]{3,2,1,0:T(8,128)(2,1)S(1)} %get-tuple-element.31), channel_id=1, source_target_pairs={{0,4},{4,0},{1,5},{5,1},{2,6},{6,2},{3,7},{7,3},{8,12},{12,8},{9,1... | collective-permute-start | bytes 1572872 | tf_op jit(solution)/shard_map/ppermute | solution.py:381
  65.9 0.0 collective-permute-done.5.r3
  65.9 0.1 values.1.vh
  66.0 12.2 %collective-permute-done.2.l2 = bf16[16,64,128]{2,1,0:T(8,128)(2,1)S(1)} collective-permute-done((bf16[16,64,128]{2,1,0:T(8,128)(2,1)S(1)}, bf16[16,64,128]{2,1,0:T(8,128)(2,1)S(1)}, u32[]{:S(2)}, u32[]{:S(2)}) %collective-permute-start.2) | collective-permute-done | bytes 262176 | tf_op jit(solution)/shard_map/ppermute | solution.py:377
  78.2 0.0 collective-permute-done.3.r2
  78.2 0.6 forwarded.1
  78.7 1.9 %collective-permute-start.8 = (bf16[16,64,128]{2,1,0:T(8,128)(2,1)S(1)}, bf16[16,64,128]{2,1,0:T(8,128)(2,1)S(1)}, u32[]{:S(2)}, u32[]{:S(2)}) collective-permute-start(bf16[16,64,128]{2,1,0:T(8,128)(2,1)S(1)} %forwarded.1), channel_id=1, source_target_pairs={{0,4},{4,0},{1,5},{5,1},{2,6},{6,2},{3,7},{7,3},{8,12},{12,8},{9,1... | collective-permute-start | bytes 786440 | tf_op jit(solution)/shard_map/ppermute | solution.py:381
  80.7 4.1 %attend_first.1 = (bf16[16,96,128]{2,1,0:T(8,128)(2,1)S(1)}, bf16[16,64,128]{2,1,0:T(8,128)(2,1)S(1)}, bf16[12,256,128]{2,1,0:T(8,128)(2,1)S(1)}) custom-call(s32[128]{0:T(128)S(1)} %copy-done, bf16[16,288,128]{2,1,0:T(8,128)(2,1)S(1)} %all_to_all.10.two, bf16[16,64,128]{2,1,0:T(8,128)(2,1)S(1)} %get-tuple-element.25.q_head, ...), custom_call_target="tpu_custom_call" | custom-call | flops 20000000000 | tf_op jit(solution)/shard_map/attend_first/pallas_call | solution.py:396
  84.7 0.0 collective-permute-done.6.s0
  84.7 0.0 collective-permute-done.7.sw
  84.8 0.0 collective-permute-done.8.se
  84.8 0.6 attend_edge.1
  85.3 4.0 %collective-permute-start.10 = (bf16[16,64,128]{2,1,0:T(8,128)(2,1)S(1)}, bf16[16,64,128]{2,1,0:T(8,128)(2,1)S(1)}, u32[]{:S(2)}, u32[]{:S(2)}) collective-permute-start(bf16[16,64,128]{2,1,0:T(8,128)(2,1)S(1)} %get-tuple-element.33), channel_id=1, source_target_pairs={{0,448},{32,480},{64,0},{96,32},{128,64},{160,96},{192,128},{224,1... | collective-permute-start | bytes 786440 | tf_op jit(solution)/shard_map/ppermute | solution.py:377
  89.3 2.8 %collective-permute-start.9 = (bf16[16,64,128]{2,1,0:T(8,128)(2,1)S(1)}, bf16[16,64,128]{2,1,0:T(8,128)(2,1)S(1)}, u32[]{:S(2)}, u32[]{:S(2)}) collective-permute-start(bf16[16,64,128]{2,1,0:T(8,128)(2,1)S(1)} %get-tuple-element.33), channel_id=1, source_target_pairs={{0,64},{32,96},{64,128},{96,160},{128,192},{160,224},{192,256},{22... | collective-permute-start | bytes 786440 | tf_op jit(solution)/shard_map/ppermute | solution.py:377
  92.1 3.3 %attend_last.1.sent_in = bf16[16,96,128]{2,1,0:T(8,128)(2,1)S(1)} custom-call(s32[128]{0:T(128)S(1)} %copy-done, bf16[16,288,128]{2,1,0:T(8,128)(2,1)S(1)} %all_to_all.10.two, bf16[16,64,128]{2,1,0:T(8,128)(2,1)S(1)} %get-tuple-element.25.q_head, bf16[16,32,128]{2,1,0:T(8,128)(2,1)S(1)} %get-tuple-element.34.q_shared, ...), custom_call_target="tpu_custom_call", output_to_operand_aliasing={{}: (12, {})} | custom-call | tf_op jit(solution)/shard_map/attend_last/pallas_call | solution.py:396
  95.4 7.0 %collective-permute-done.10.o_right = bf16[16,64,128]{2,1,0:T(8,128)(2,1)S(1)} collective-permute-done((bf16[16,64,128]{2,1,0:T(8,128)(2,1)S(1)}, bf16[16,64,128]{2,1,0:T(8,128)(2,1)S(1)}, u32[]{:S(2)}, u32[]{:S(2)}) %collective-permute-start.10) | collective-permute-done | bytes 262176 | tf_op jit(solution)/shard_map/ppermute | solution.py:377
  102.4 4.9 %collective-permute-done.9.o_left = bf16[16,64,128]{2,1,0:T(8,128)(2,1)S(1)} collective-permute-done((bf16[16,64,128]{2,1,0:T(8,128)(2,1)S(1)}, bf16[16,64,128]{2,1,0:T(8,128)(2,1)S(1)}, u32[]{:S(2)}, u32[]{:S(2)}) %collective-permute-start.9) | collective-permute-done | bytes 262176 | tf_op jit(solution)/shard_map/ppermute | solution.py:377
  107.4 0.6 merge.1
  107.9 12.1 %all_to_all.11.in_ref = bf16[16,96,128]{2,1,0:T(8,128)(2,1)S(1)} all-to-all(bf16[16,96,128]{2,1,0:T(8,128)(2,1)S(1)} %merge.1), channel_id=1, replica_groups=mesh['col'=8,'half'=2,'x'=4,'core'=2,'dp'=4] {'half','x','core'}, dimensions={0} | all-to-all | bytes 786432 | tf_op jit(solution)/shard_map/all_to_all | solution.py:385
  120.0 0.8 unpack.1
Async XLA Ops:
  3.7 23.7 %copy-start = (s32[128]{0:T(128)S(1)}, s32[128]{0:T(128)}, u32[]{:S(2)}) copy-start(s32[128]{0:T(128)} %get-tuple-element.22.table) | copy-start | bytes 1540
  27.5 13.5 %copy-start.1 = (s32[32]{0:T(128)S(1)}, s32[32]{0:T(128)}, u32[]{:S(2)}) copy-start(s32[32]{0:T(128)} %order.3) | copy-start | bytes 388
  28.1 26.3 %collective-permute-start.1 = (bf16[16,64,128]{2,1,0:T(8,128)(2,1)S(1)}, bf16[16,64,128]{2,1,0:T(8,128)(2,1)S(1)}, u32[]{:S(2)}, u32[]{:S(2)}) collective-permute-start(bf16[16,64,128]{2,1,0:T(8,128)(2,1)S(1)} %get-tuple-element.24), channel_id=1, source_target_pairs={{0,448},{32,480},{64,0},{96,32},{128,64},{160,96},{192,128},{224,1... | collective-permute-start | bytes 786440 | tf_op jit(solution)/shard_map/ppermute | solution.py:377
  39.0 15.6 %collective-permute-start = (bf16[16,64,128]{2,1,0:T(8,128)(2,1)S(1)}, bf16[16,64,128]{2,1,0:T(8,128)(2,1)S(1)}, u32[]{:S(2)}, u32[]{:S(2)}) collective-permute-start(bf16[16,64,128]{2,1,0:T(8,128)(2,1)S(1)} %get-tuple-element.24), channel_id=1, source_target_pairs={{0,64},{32,96},{64,128},{96,160},{128,192},{160,224},{192,256},{22... | collective-permute-start | bytes 786440 | tf_op jit(solution)/shard_map/ppermute | solution.py:377
  44.4 19.5 %collective-permute-start.4 = (bf16[16,64,128]{2,1,0:T(8,128)(2,1)S(1)}, bf16[16,64,128]{2,1,0:T(8,128)(2,1)S(1)}, u32[]{:S(2)}, u32[]{:S(2)}) collective-permute-start(bf16[16,64,128]{2,1,0:T(8,128)(2,1)S(1)} %get-tuple-element.28), channel_id=1, source_target_pairs={{0,64},{32,96},{64,128},{96,160},{128,192},{160,224},{192,256},{22... | collective-permute-start | bytes 786440 | tf_op jit(solution)/shard_map/ppermute | solution.py:377
  46.4 19.5 %collective-permute-start.5 = (bf16[16,64,128]{2,1,0:T(8,128)(2,1)S(1)}, bf16[16,64,128]{2,1,0:T(8,128)(2,1)S(1)}, u32[]{:S(2)}, u32[]{:S(2)}) collective-permute-start(bf16[16,64,128]{2,1,0:T(8,128)(2,1)S(1)} %get-tuple-element.29), channel_id=1, source_target_pairs={{0,448},{32,480},{64,0},{96,32},{128,64},{160,96},{192,128},{224,1... | collective-permute-start | bytes 786440 | tf_op jit(solution)/shard_map/ppermute | solution.py:377
  52.4 32.3 %collective-permute-start.6 = (bf16[16,64,128]{2,1,0:T(8,128)(2,1)S(1)}, bf16[16,64,128]{2,1,0:T(8,128)(2,1)S(1)}, u32[]{:S(2)}, u32[]{:S(2)}) collective-permute-start(bf16[16,64,128]{2,1,0:T(8,128)(2,1)S(1)} %get-tuple-element.30), channel_id=1, source_target_pairs={{0,4},{4,0},{1,5},{5,1},{2,6},{6,2},{3,7},{7,3},{8,12},{12,8},{9,1... | collective-permute-start | bytes 786440 | tf_op jit(solution)/shard_map/ppermute | solution.py:381
  55.3 22.9 %collective-permute-start.2 = (bf16[16,64,128]{2,1,0:T(8,128)(2,1)S(1)}, bf16[16,64,128]{2,1,0:T(8,128)(2,1)S(1)}, u32[]{:S(2)}, u32[]{:S(2)}) collective-permute-start(bf16[16,64,128]{2,1,0:T(8,128)(2,1)S(1)} %get-tuple-element.26), channel_id=1, source_target_pairs={{0,64},{32,96},{64,128},{96,160},{128,192},{160,224},{192,256},{22... | collective-permute-start | bytes 786440 | tf_op jit(solution)/shard_map/ppermute | solution.py:377
  57.2 21.0 %collective-permute-start.3 = (bf16[16,64,128]{2,1,0:T(8,128)(2,1)S(1)}, bf16[16,64,128]{2,1,0:T(8,128)(2,1)S(1)}, u32[]{:S(2)}, u32[]{:S(2)}) collective-permute-start(bf16[16,64,128]{2,1,0:T(8,128)(2,1)S(1)} %get-tuple-element.27), channel_id=1, source_target_pairs={{0,448},{32,480},{64,0},{96,32},{128,64},{160,96},{192,128},{224,1... | collective-permute-start | bytes 786440 | tf_op jit(solution)/shard_map/ppermute | solution.py:377
  64.0 20.8 %collective-permute-start.7 = (bf16[2,16,64,128]{3,2,1,0:T(8,128)(2,1)S(1)}, bf16[2,16,64,128]{3,2,1,0:T(8,128)(2,1)S(1)}, u32[]{:S(2)}, u32[]{:S(2)}) collective-permute-start(bf16[2,16,64,128]{3,2,1,0:T(8,128)(2,1)S(1)} %get-tuple-element.31), channel_id=1, source_target_pairs={{0,4},{4,0},{1,5},{5,1},{2,6},{6,2},{3,7},{7,3},{8,12},{12,8},{9,1... | collective-permute-start | bytes 1572872 | tf_op jit(solution)/shard_map/ppermute | solution.py:381
  78.7 6.0 %collective-permute-start.8 = (bf16[16,64,128]{2,1,0:T(8,128)(2,1)S(1)}, bf16[16,64,128]{2,1,0:T(8,128)(2,1)S(1)}, u32[]{:S(2)}, u32[]{:S(2)}) collective-permute-start(bf16[16,64,128]{2,1,0:T(8,128)(2,1)S(1)} %forwarded.1), channel_id=1, source_target_pairs={{0,4},{4,0},{1,5},{5,1},{2,6},{6,2},{3,7},{7,3},{8,12},{12,8},{9,1... | collective-permute-start | bytes 786440 | tf_op jit(solution)/shard_map/ppermute | solution.py:381
  85.3 17.1 %collective-permute-start.10 = (bf16[16,64,128]{2,1,0:T(8,128)(2,1)S(1)}, bf16[16,64,128]{2,1,0:T(8,128)(2,1)S(1)}, u32[]{:S(2)}, u32[]{:S(2)}) collective-permute-start(bf16[16,64,128]{2,1,0:T(8,128)(2,1)S(1)} %get-tuple-element.33), channel_id=1, source_target_pairs={{0,448},{32,480},{64,0},{96,32},{128,64},{160,96},{192,128},{224,1... | collective-permute-start | bytes 786440 | tf_op jit(solution)/shard_map/ppermute | solution.py:377
  89.3 18.0 %collective-permute-start.9 = (bf16[16,64,128]{2,1,0:T(8,128)(2,1)S(1)}, bf16[16,64,128]{2,1,0:T(8,128)(2,1)S(1)}, u32[]{:S(2)}, u32[]{:S(2)}) collective-permute-start(bf16[16,64,128]{2,1,0:T(8,128)(2,1)S(1)} %get-tuple-element.33), channel_id=1, source_target_pairs={{0,64},{32,96},{64,128},{96,160},{128,192},{160,224},{192,256},{22... | collective-permute-start | bytes 786440 | tf_op jit(solution)/shard_map/ppermute | solution.py:377

commit v7 on v6

--- a/solution.py
+++ b/solution.py
@@ -18,6 +18,7 @@
 BF = jnp.bfloat16
 F32 = jnp.float32
 MIB = 1024 * 1024
+POWER = HD ** (-0.5) * 1.4426950408889634
 ONE, MAIN, VALUE = slice(0, 64), slice(64, 128), slice(128, 192)
 QUERY, REST = slice(192, 224), slice(224, 288)
 AT_W, AT_TILE, AT_HEAD, AT_SHARED = 0, 8, 16, 64
@@ -36,7 +37,7 @@
     return rows
 
 
-def turns(tile, frame_in_tile, scale):
+def turns(tile, frame_in_tile):
     frame = (tile // 32 * 4 + frame_in_tile).astype(F32)
     row0 = (tile // 8 % 4 * 8).astype(F32)
     col0 = (tile % 8 * 8).astype(F32)
@@ -45,8 +46,8 @@
     col = col0 + (token % 8).astype(F32)
     by_frame, by_row, by_col = frequency_rows()
     angle = frame * by_frame + row * by_row + col * by_col
-    cosine = jnp.cos(angle) * scale
-    sine = jnp.sin(angle) * scale
+    cosine = jnp.cos(angle)
+    sine = jnp.sin(angle)
     even = lax.broadcasted_iota(jnp.int32, (64, HD), 1) % 2 == 0
     return cosine, jnp.where(even, -sine, 0.0), jnp.where(even, 0.0, sine)
 
@@ -100,7 +101,7 @@
         copy.start()
     w = plan(order, nb, table)
     edge = (w == 0) | (w == 7)
-    factors = turns(order[slot], frame_in_tile, 1.0)
+    factors = turns(order[slot], frame_in_tile)
     outs = []
     for part in range(4):
         for which in range(3):
@@ -128,17 +129,8 @@
         out.wait()
 
 
-def early_kernel(table, two, one, own):
-    w = table[AT_W]
+def early_kernel(two, one):
     one[...] = two[:, ONE]
-
-    @pl.when((w == 0) | (w == 7))
-    def _():
-        own[...] = two[:, REST]
-
-    @pl.when((w != 0) & (w != 7))
-    def _():
-        own[...] = two[:, ONE]
 
 
 def middle_kernel(table, order, two, q_head, q_shared, value_left, value_right):
@@ -148,8 +140,7 @@
 
     @pl.loop(0, 16)
     def _(source):
-        scale = HD ** (-0.5) * 1.4426950408889634
-        factors = turns(order[col * 4 + source // 4], lax.rem(source, 4), scale)
+        factors = turns(order[col * 4 + source // 4], lax.rem(source, 4))
         held = two[source]
         q_head[source] = turned(jnp.where(edge, held[MAIN], held[REST]), factors)
         mine = [jnp.where(core == 0, f[0:32], f[32:64]) for f in factors]
@@ -184,8 +175,16 @@
         def _(out=out):
             out[...] = two[:, MAIN]
 
-    swap[0] = l1[...]
-    swap[1] = r1[...]
+    @pl.when(edge)
+    def _():
+        swap[0] = two[:, REST]
+
+    @pl.when(jnp.logical_not(edge))
+    def _():
+        swap[0] = two[:, ONE]
+
+    swap[1] = l1[...]
+    swap[2] = r1[...]
 
 
 def attend(q, kp, vp, picks):
@@ -194,12 +193,12 @@
         s = lax.dot_general(q, kp[pick], (((1,), (1,)), ((), ())), preferred_element_type=F32)
         high = jnp.max(s, axis=1, keepdims=True)
         new = high if top is None else jnp.maximum(top, high)
-        p = jnp.exp2(s - new)
+        p = jnp.exp2((s - new) * POWER)
         part = jnp.dot(p.astype(BF), whole(vp, pick), preferred_element_type=F32)
         if top is None:
             weights, acc = p, part
         else:
-            shrink = jnp.exp2(top - new)
+            shrink = jnp.exp2((top - new) * POWER)
             weights, acc = weights * shrink + p, acc * shrink + part
         top = new
     return (acc / jnp.sum(weights, axis=1, keepdims=True)).astype(BF)
@@ -236,8 +235,35 @@
         vh[8 + t] = l3[four]
 
 
-def forwarded_kernel(table, l2, r2, vh, out):
-    del vh
+def shared_kernel(table, two, l1, r1, sw, k2, v2):
+    w = table[AT_W]
+    edge = (w == 0) | (w == 7)
+    left = (lambda f, p: whole(l1, f, p)), (lambda f, p: whole(sw, 1, f, p))
+    right = (lambda f, p: whole(r1, f, p)), (lambda f, p: whole(sw, 2, f, p))
+
+    def own(rows):
+        mine = lambda f, p: whole(two, f, slice(rows.start + p.start, rows.start + p.stop))
+        fill_shared(0, mine, lambda f, p: whole(sw, 0, f, p), k2, v2)
+
+    @pl.when(jnp.logical_not(edge))
+    def _():
+        own(ONE)
+        fill_shared(4, *right, k2, v2)
+        fill_shared(8, *left, k2, v2)
+
+    @pl.when(w == 0)
+    def _():
+        own(REST)
+        fill_shared(4, *right, k2, v2)
+
+    @pl.when(w == 7)
+    def _():
+        own(REST)
+        fill_shared(4, *left, k2, v2)
+
+
+def forwarded_kernel(table, l2, r2, vh, k2, out):
+    del vh, k2
     w = table[AT_W]
 
     @pl.when(w == 0)
@@ -290,32 +316,26 @@
         attend_column(table, THIS, AT_HEAD, query, kh, vh, to_sent)
 
 
-def edge_kernel(table, two, l1, r1, l2, r2, l3, r3, s0, sw, se, oth_in, o_oth, k2, v2):
-    del oth_in
+def edge_kernel(table, l2, r2, l3, r3, se, oth_in, k_in, v_in, o_oth, k2, v2):
+    del oth_in, k_in, v_in
     w = table[AT_W]
 
     def to_other(four, o):
         o_oth[four, 0:32] = o
 
-    for special, near, far, asked, swapped_near in ((0, r1, r2, r3, 1), (7, l1, l2, l3, 0)):
+    for special, far, asked in ((0, r2, r3), (7, l2, l3)):
 
         @pl.when(w == special)
-        def _(near=near, far=far, asked=asked, swapped_near=swapped_near):
-            own = lambda f, p: whole(two, f, slice(REST.start + p.start, REST.start + p.stop))
-            fill_shared(0, own, lambda f, p: whole(s0, f, p), k2, v2)
-            fill_shared(
-                4, lambda f, p: whole(near, f, p), lambda f, p: whole(sw, swapped_near, f, p), k2, v2
-            )
+        def _(far=far, asked=asked):
             fill_shared(8, lambda f, p: whole(far, f, p), lambda f, p: whole(se, f, p), k2, v2)
             query = lambda four: whole(asked, four, slice(0, 32))
             attend_column(table, OTHER, AT_SHARED, query, k2, v2, to_other)
 
 
-def last_kernel(table, two, q_head, q_shared, l1, r1, s0, sw, kh, vh, k2, v2, sent_in, sent, k3, v3):
+def last_kernel(table, q_head, q_shared, kh, vh, k2, v2, sent_in, sent):
     del sent_in
     w = table[AT_W]
     inner = (w == 1) | (w == 6)
-    edge = (w == 0) | (w == 7)
 
     def to_head(four, o):
         sent[four, 0:64] = o
@@ -323,23 +343,15 @@
     def to_shared(four, o):
         sent[four, 64:96] = o
 
-    shared_query = lambda four: whole(q_shared, four)
-
     @pl.when(inner)
     def _():
         query = lambda four: whole(q_head, four)
         attend_column(table, THIS, AT_HEAD, query, kh, vh, to_head)
 
-    @pl.when(edge)
-    def _():
-        attend_column(table, THIS, AT_SHARED, shared_query, k2, v2, to_shared)
-
-    @pl.when(jnp.logical_not(inner | edge))
-    def _():
-        fill_shared(0, lambda f, p: whole(two, f, p), lambda f, p: whole(s0, f, p), k3, v3)
-        fill_shared(4, lambda f, p: whole(r1, f, p), lambda f, p: whole(sw, 1, f, p), k3, v3)
-        fill_shared(8, lambda f, p: whole(l1, f, p), lambda f, p: whole(sw, 0, f, p), k3, v3)
-        attend_column(table, THIS, AT_SHARED, shared_query, k3, v3, to_shared)
+    @pl.when(jnp.logical_not(inner))
+    def _():
+        query = lambda four: whole(q_shared, four)
+        attend_column(table, THIS, AT_SHARED, query, k2, v2, to_shared)
 
 
 def merge_kernel(table, o_left, o_right, sent_in, sent):
@@ -424,20 +436,22 @@
         space=ANY,
     )
     two = exchanged(two)
-    one, own = kernel(early_kernel, "early", (SLOT, SLOT), (table, two))
+    (one,) = kernel(early_kernel, "early", (SLOT,), (two,))
     l1, r1 = along_columns(one, 1), along_columns(one, -1)
     q_head, q_shared, value_left, value_right = kernel(
         middle_kernel, "middle", (SLOT, (16, 32, HD), SLOT, SLOT), (table, order, two), flops=FLOPS
     )
     l3, r3 = along_columns(value_right, 1), along_columns(value_left, -1)
     main_left, main_right, swap = kernel(
-        late_kernel, "late", (SLOT, SLOT, (2,) + SLOT), (table, two, q_head, l1, r1)
+        late_kernel, "late", (SLOT, SLOT, (3,) + SLOT), (table, two, q_head, l1, r1)
     )
     l2, r2 = along_columns(main_right, 1), along_columns(main_left, -1)
     sw = swapped(swap)
-    s0 = swapped(own)
     (vh,) = kernel(value_kernel, "values", (PARTS,), (two, l3, r3), flops=FLOPS)
-    (se,) = kernel(forwarded_kernel, "forwarded", (SLOT,), (table, l2, r2, vh))
+    k2, v2 = kernel(shared_kernel, "shared", (POOL, POOL), (table, two, l1, r1, sw))
+    (se,) = kernel(
+        forwarded_kernel, "forwarded", (SLOT,), (table, l2, r2, vh, k2), space=VMEM
+    )
     se = swapped(se)
     sent, o_oth, kh = kernel(
         first_kernel,
@@ -450,17 +464,16 @@
         edge_kernel,
         "attend_edge",
         (SLOT, POOL, POOL),
-        (table, two, l1, r1, l2, r2, l3, r3, s0, sw, se, o_oth),
-        aliases={11: 0},
+        (table, l2, r2, l3, r3, se, o_oth, k2, v2),
+        aliases={6: 0, 7: 1, 8: 2},
     )
     o_left, o_right = along_columns(o_oth, 1), along_columns(o_oth, -1)
     (sent,) = kernel(
         last_kernel,
         "attend_last",
         (SENT,),
-        (table, two, q_head, q_shared, l1, r1, s0, sw, kh, vh, k2, v2, sent),
-        (pltpu.VMEM(POOL, BF), pltpu.VMEM(POOL, BF)),
-        aliases={12: 0},
+        (table, q_head, q_shared, kh, vh, k2, v2, sent),
+        aliases={7: 0},
     )
     (sent,) = kernel(merge_kernel, "merge", (SENT,), (table, o_left, o_right, sent), aliases={3: 0})
     return kernel(unpack_kernel, "unpack", (queries.shape,), (exchanged(sent),))[0]

time: 121 us -> 121 us (level); the launches traced: 121 us -> 120 us
  waiting for transfers between devices: 25.2 us -> 20.3 us
  blocking collectives: 35.8 us -> 39.6 us
  starting transfers between devices: 41.3 us -> 39.4 us
  Pallas kernels: 18.3 us -> 20.1 us
    ppermute x8, waiting for transfers between devices: 25.2 us -> 19.8 us  [along_columns(): lax.ppermute(block, ('col', 'half'), [(i, (i + 2 * distance) % n) for i i...]
    all_to_all x2, blocking collectives: 35.8 us -> 39.6 us  [exchanged(): return lax.all_to_all(block, GROUP, split_axis=0, concat_axis=0, tiled=True)]
    ppermute x3 -> x2, starting transfers between devices: 5.75 us -> 3.84 us  [swapped(): return lax.ppermute(block, 'core', [(0, 1), (1, 0)])]
    pallas_call x11 -> x12, Pallas kernels: 18.3 us -> 20.1 us  [kernel(): pl.pallas_call(body, out_shape=tuple((jax.ShapeDtypeStruct(shape, BF if l...]
  transfers between devices with their start and end apart: 11 -> 10, of which waited for: 5 -> 5; matrix products, arithmetic and copies ran while one was open for 0% -> 0% of each run, Pallas kernels for 10% -> 12%
where the time goes in v7:
time: 121 us; the launch traced here: 120 us
  blocking collectives  39.6 us (33%)
  starting transfers between devices  39.4 us (33%)
  waiting for transfers between devices  20.3 us (17%)
  Pallas kernels  20.1 us (17%)
    all_to_all x2, blocking collectives, exchanged(): return lax.all_to_all(block, GROUP, split_axis=0, concat_axis=0, tiled=True)  39.6 us
    ppermute x8, starting transfers between devices, along_columns(): lax.ppermute(block, ('col', 'half'), [(i, (i + 2 * distance) % n) for i i...  35.5 us
    pallas_call x12, Pallas kernels, kernel(): pl.pallas_call(body, out_shape=tuple((jax.ShapeDtypeStruct(shape, BF if l...  20.1 us
    ppermute x8, waiting for transfers between devices, along_columns(): lax.ppermute(block, ('col', 'half'), [(i, (i + 2 * distance) % n) for i i...  19.8 us
    ppermute x2, starting transfers between devices, swapped(): return lax.ppermute(block, 'core', [(0, 1), (1, 0)])  3.84 us
  transfers between devices with their start and end apart: 10, of which 5 were waited for; matrix products, arithmetic and copies ran while one was open for 0% of the time, Pallas kernels for 12%

profile of v7, /device:TPU:24, one launch (start us, length us, event | category | flops | bytes accessed | tf_op | source)
XLA Modules:
  0.0 119.5 jit_solution(12697024559951611231)
XLA Ops:
  0.0 3.7 %rotate.1 = (bf16[16,288,128]{2,1,0:T(8,128)(2,1)}, s32[128]{0:T(128)}) custom-call(s32[32]{0:T(128)} %order.3, s32[9,32]{1,0:T(8,128)} %bitcast.1, bf16[64,3072]{1,0:T(8,128)(2,1)} %q_hbm.1, bf16[64,3072]{1,0:T(8,128)(2,1)} %k_hbm.1, bf16[64,3072]{1,0:T(8,128)(2,1)} %v_hbm.1), custom_call_target="tpu_custom_call" | custom-call | tf_op jit(solution)/shard_map/rotate/pallas_call | solution.py:408
  3.7 23.7 %all_to_all.10.two = bf16[16,288,128]{2,1,0:T(8,128)(2,1)S(1)} all-to-all(bf16[16,288,128]{2,1,0:T(8,128)(2,1)} %get-tuple-element.23), channel_id=1, replica_groups=mesh['col'=8,'half'=2,'x'=4,'core'=2,'dp'=4] {'half','x','core'}, dimensions={0} | all-to-all | bytes 2359296 | tf_op jit(solution)/shard_map/all_to_all | solution.py:397
  27.5 0.0 copy-start
  27.5 0.0 copy-start.1
  27.5 10.9 %collective-permute-start.1 = (bf16[16,64,128]{2,1,0:T(8,128)(2,1)S(1)}, bf16[16,64,128]{2,1,0:T(8,128)(2,1)S(1)}, u32[]{:S(2)}, u32[]{:S(2)}) collective-permute-start(bf16[16,64,128]{2,1,0:T(8,128)(2,1)S(1)} %early.1), channel_id=1, source_target_pairs={{0,448},{32,480},{64,0},{96,32},{128,64},{160,96},{192,128},{224,1... | collective-permute-start | bytes 786440 | tf_op jit(solution)/shard_map/ppermute | solution.py:389
  38.4 1.9 %collective-permute-start = (bf16[16,64,128]{2,1,0:T(8,128)(2,1)S(1)}, bf16[16,64,128]{2,1,0:T(8,128)(2,1)S(1)}, u32[]{:S(2)}, u32[]{:S(2)}) collective-permute-start(bf16[16,64,128]{2,1,0:T(8,128)(2,1)S(1)} %early.1), channel_id=1, source_target_pairs={{0,64},{32,96},{64,128},{96,160},{128,192},{160,224},{192,256},{22... | collective-permute-start | bytes 786440 | tf_op jit(solution)/shard_map/ppermute | solution.py:389
  40.4 0.0 copy-done
  40.4 0.0 copy-done.1
  40.4 3.4 %middle.1 = (bf16[16,64,128]{2,1,0:T(8,128)(2,1)S(1)}, bf16[16,32,128]{2,1,0:T(8,128)(2,1)S(1)}, bf16[16,64,128]{2,1,0:T(8,128)(2,1)S(1)}, bf16[16,64,128]{2,1,0:T(8,128)(2,1)S(1)}) custom-call(s32[128]{0:T(128)S(1)} %copy-done, s32[32]{0:T(128)S(1)} %copy-done.1, bf16[16,288,128]{2,1,0:T(8,128)(2,1)S(1)} %all_to_all.10.two), custom_call_target="tpu_custom_call" | custom-call | flops 20000000000 | tf_op jit(solution)/shard_map/middle/pallas_call | solution.py:408
  43.8 1.9 %collective-permute-start.4 = (bf16[16,64,128]{2,1,0:T(8,128)(2,1)S(1)}, bf16[16,64,128]{2,1,0:T(8,128)(2,1)S(1)}, u32[]{:S(2)}, u32[]{:S(2)}) collective-permute-start(bf16[16,64,128]{2,1,0:T(8,128)(2,1)S(1)} %get-tuple-element.27), channel_id=1, source_target_pairs={{0,64},{32,96},{64,128},{96,160},{128,192},{160,224},{192,256},{22... | collective-permute-start | bytes 786440 | tf_op jit(solution)/shard_map/ppermute | solution.py:389
  45.8 6.0 %collective-permute-start.5 = (bf16[16,64,128]{2,1,0:T(8,128)(2,1)S(1)}, bf16[16,64,128]{2,1,0:T(8,128)(2,1)S(1)}, u32[]{:S(2)}, u32[]{:S(2)}) collective-permute-start(bf16[16,64,128]{2,1,0:T(8,128)(2,1)S(1)} %get-tuple-element.28), channel_id=1, source_target_pairs={{0,448},{32,480},{64,0},{96,32},{128,64},{160,96},{192,128},{224,1... | collective-permute-start | bytes 786440 | tf_op jit(solution)/shard_map/ppermute | solution.py:389
  51.8 0.0 collective-permute-done.1.r1
  51.8 2.2 %collective-permute-done.l1 = bf16[16,64,128]{2,1,0:T(8,128)(2,1)S(1)} collective-permute-done((bf16[16,64,128]{2,1,0:T(8,128)(2,1)S(1)}, bf16[16,64,128]{2,1,0:T(8,128)(2,1)S(1)}, u32[]{:S(2)}, u32[]{:S(2)}) %collective-permute-start) | collective-permute-done | bytes 262176 | tf_op jit(solution)/shard_map/ppermute | solution.py:389
  54.1 0.7 late.1
  54.7 1.9 %collective-permute-start.2 = (bf16[16,64,128]{2,1,0:T(8,128)(2,1)S(1)}, bf16[16,64,128]{2,1,0:T(8,128)(2,1)S(1)}, u32[]{:S(2)}, u32[]{:S(2)}) collective-permute-start(bf16[16,64,128]{2,1,0:T(8,128)(2,1)S(1)} %get-tuple-element.25), channel_id=1, source_target_pairs={{0,64},{32,96},{64,128},{96,160},{128,192},{160,224},{192,256},{22... | collective-permute-start | bytes 786440 | tf_op jit(solution)/shard_map/ppermute | solution.py:389
  56.7 6.0 %collective-permute-start.3 = (bf16[16,64,128]{2,1,0:T(8,128)(2,1)S(1)}, bf16[16,64,128]{2,1,0:T(8,128)(2,1)S(1)}, u32[]{:S(2)}, u32[]{:S(2)}) collective-permute-start(bf16[16,64,128]{2,1,0:T(8,128)(2,1)S(1)} %get-tuple-element.26), channel_id=1, source_target_pairs={{0,448},{32,480},{64,0},{96,32},{128,64},{160,96},{192,128},{224,1... | collective-permute-start | bytes 786440 | tf_op jit(solution)/shard_map/ppermute | solution.py:389
  62.7 1.9 %collective-permute-start.6 = (bf16[3,16,64,128]{3,2,1,0:T(8,128)(2,1)S(1)}, bf16[3,16,64,128]{3,2,1,0:T(8,128)(2,1)S(1)}, u32[]{:S(2)}, u32[]{:S(2)}) collective-permute-start(bf16[3,16,64,128]{3,2,1,0:T(8,128)(2,1)S(1)} %get-tuple-element.29), channel_id=1, source_target_pairs={{0,4},{4,0},{1,5},{5,1},{2,6},{6,2},{3,7},{7,3},{8,12},{12,8},{9,1... | collective-permute-start | bytes 2359304 | tf_op jit(solution)/shard_map/ppermute | solution.py:393
  64.6 1.7 %collective-permute-done.4.l3 = bf16[16,64,128]{2,1,0:T(8,128)(2,1)S(1)} collective-permute-done((bf16[16,64,128]{2,1,0:T(8,128)(2,1)S(1)}, bf16[16,64,128]{2,1,0:T(8,128)(2,1)S(1)}, u32[]{:S(2)}, u32[]{:S(2)}) %collective-permute-start.4) | collective-permute-done | bytes 262176 | tf_op jit(solution)/shard_map/ppermute | solution.py:389
  66.3 0.0 collective-permute-done.5.r3
  66.3 0.1 values.1.vh
  66.4 0.5 collective-permute-done.6.sw
  66.9 0.7 shared.1
  67.5 10.1 %collective-permute-done.2.l2 = bf16[16,64,128]{2,1,0:T(8,128)(2,1)S(1)} collective-permute-done((bf16[16,64,128]{2,1,0:T(8,128)(2,1)S(1)}, bf16[16,64,128]{2,1,0:T(8,128)(2,1)S(1)}, u32[]{:S(2)}, u32[]{:S(2)}) %collective-permute-start.2) | collective-permute-done | bytes 262176 | tf_op jit(solution)/shard_map/ppermute | solution.py:389
  77.6 0.0 collective-permute-done.3.r2
  77.6 0.6 forwarded.1
  78.2 1.9 %collective-permute-start.7 = (bf16[16,64,128]{2,1,0:T(8,128)(2,1)S(1)}, bf16[16,64,128]{2,1,0:T(8,128)(2,1)S(1)}, u32[]{:S(2)}, u32[]{:S(2)}) collective-permute-start(bf16[16,64,128]{2,1,0:T(8,128)(2,1)S(1)} %forwarded.1), channel_id=1, source_target_pairs={{0,4},{4,0},{1,5},{5,1},{2,6},{6,2},{3,7},{7,3},{8,12},{12,8},{9,1... | collective-permute-start | bytes 786440 | tf_op jit(solution)/shard_map/ppermute | solution.py:393
  80.1 4.5 %attend_first.1 = (bf16[16,96,128]{2,1,0:T(8,128)(2,1)S(1)}, bf16[16,64,128]{2,1,0:T(8,128)(2,1)S(1)}, bf16[12,256,128]{2,1,0:T(8,128)(2,1)S(1)}) custom-call(s32[128]{0:T(128)S(1)} %copy-done, bf16[16,288,128]{2,1,0:T(8,128)(2,1)S(1)} %all_to_all.10.two, bf16[16,64,128]{2,1,0:T(8,128)(2,1)S(1)} %get-tuple-element.24.q_head, ...), custom_call_target="tpu_custom_call" | custom-call | flops 20000000000 | tf_op jit(solution)/shard_map/attend_first/pallas_call | solution.py:408
  84.6 0.0 collective-permute-done.7.se
  84.6 0.6 attend_edge.1
  85.2 1.9 %collective-permute-start.9 = (bf16[16,64,128]{2,1,0:T(8,128)(2,1)S(1)}, bf16[16,64,128]{2,1,0:T(8,128)(2,1)S(1)}, u32[]{:S(2)}, u32[]{:S(2)}) collective-permute-start(bf16[16,64,128]{2,1,0:T(8,128)(2,1)S(1)} %get-tuple-element.33), channel_id=1, source_target_pairs={{0,448},{32,480},{64,0},{96,32},{128,64},{160,96},{192,128},{224,1... | collective-permute-start | bytes 786440 | tf_op jit(solution)/shard_map/ppermute | solution.py:389
  87.1 4.8 %collective-permute-start.8 = (bf16[16,64,128]{2,1,0:T(8,128)(2,1)S(1)}, bf16[16,64,128]{2,1,0:T(8,128)(2,1)S(1)}, u32[]{:S(2)}, u32[]{:S(2)}) collective-permute-start(bf16[16,64,128]{2,1,0:T(8,128)(2,1)S(1)} %get-tuple-element.33), channel_id=1, source_target_pairs={{0,64},{32,96},{64,128},{96,160},{128,192},{160,224},{192,256},{22... | collective-permute-start | bytes 786440 | tf_op jit(solution)/shard_map/ppermute | solution.py:389
  91.9 4.6 %attend_last.1.sent_in = bf16[16,96,128]{2,1,0:T(8,128)(2,1)S(1)} custom-call(s32[128]{0:T(128)S(1)} %copy-done, bf16[16,64,128]{2,1,0:T(8,128)(2,1)S(1)} %get-tuple-element.24.q_head, bf16[16,32,128]{2,1,0:T(8,128)(2,1)S(1)} %get-tuple-element.34.q_shared, bf16[12,256,128]{2,1,0:T(8,128)(2,1)S(1)} %get-tuple-element.35.kh, ...), custom_call_target="tpu_custom_call", output_to_operand_aliasing={{}: (7, {})} | custom-call | tf_op jit(solution)/shard_map/attend_last/pallas_call | solution.py:408
  96.5 5.8 %collective-permute-done.9.o_right = bf16[16,64,128]{2,1,0:T(8,128)(2,1)S(1)} collective-permute-done((bf16[16,64,128]{2,1,0:T(8,128)(2,1)S(1)}, bf16[16,64,128]{2,1,0:T(8,128)(2,1)S(1)}, u32[]{:S(2)}, u32[]{:S(2)}) %collective-permute-start.9) | collective-permute-done | bytes 262176 | tf_op jit(solution)/shard_map/ppermute | solution.py:389
  102.3 0.0 collective-permute-done.8.o_left
  102.3 0.6 merge.1
  102.9 15.9 %all_to_all.11.in_ref = bf16[16,96,128]{2,1,0:T(8,128)(2,1)S(1)} all-to-all(bf16[16,96,128]{2,1,0:T(8,128)(2,1)S(1)} %merge.1), channel_id=1, replica_groups=mesh['col'=8,'half'=2,'x'=4,'core'=2,'dp'=4] {'half','x','core'}, dimensions={0} | all-to-all | bytes 786432 | tf_op jit(solution)/shard_map/all_to_all | solution.py:397
  118.7 0.8 unpack.1
  (1 shorter events, 0.0 us)
Async XLA Ops:
  27.5 12.9 %copy-start = (s32[128]{0:T(128)S(1)}, s32[128]{0:T(128)}, u32[]{:S(2)}) copy-start(s32[128]{0:T(128)} %get-tuple-element.22.table) | copy-start | bytes 1540
  27.5 12.9 %copy-start.1 = (s32[32]{0:T(128)S(1)}, s32[32]{0:T(128)}, u32[]{:S(2)}) copy-start(s32[32]{0:T(128)} %order.3) | copy-start | bytes 388
  27.5 24.3 %collective-permute-start.1 = (bf16[16,64,128]{2,1,0:T(8,128)(2,1)S(1)}, bf16[16,64,128]{2,1,0:T(8,128)(2,1)S(1)}, u32[]{:S(2)}, u32[]{:S(2)}) collective-permute-start(bf16[16,64,128]{2,1,0:T(8,128)(2,1)S(1)} %early.1), channel_id=1, source_target_pairs={{0,448},{32,480},{64,0},{96,32},{128,64},{160,96},{192,128},{224,1... | collective-permute-start | bytes 786440 | tf_op jit(solution)/shard_map/ppermute | solution.py:389
  38.4 15.6 %collective-permute-start = (bf16[16,64,128]{2,1,0:T(8,128)(2,1)S(1)}, bf16[16,64,128]{2,1,0:T(8,128)(2,1)S(1)}, u32[]{:S(2)}, u32[]{:S(2)}) collective-permute-start(bf16[16,64,128]{2,1,0:T(8,128)(2,1)S(1)} %early.1), channel_id=1, source_target_pairs={{0,64},{32,96},{64,128},{96,160},{128,192},{160,224},{192,256},{22... | collective-permute-start | bytes 786440 | tf_op jit(solution)/shard_map/ppermute | solution.py:389
  43.8 22.5 %collective-permute-start.4 = (bf16[16,64,128]{2,1,0:T(8,128)(2,1)S(1)}, bf16[16,64,128]{2,1,0:T(8,128)(2,1)S(1)}, u32[]{:S(2)}, u32[]{:S(2)}) collective-permute-start(bf16[16,64,128]{2,1,0:T(8,128)(2,1)S(1)} %get-tuple-element.27), channel_id=1, source_target_pairs={{0,64},{32,96},{64,128},{96,160},{128,192},{160,224},{192,256},{22... | collective-permute-start | bytes 786440 | tf_op jit(solution)/shard_map/ppermute | solution.py:389
  45.8 20.6 %collective-permute-start.5 = (bf16[16,64,128]{2,1,0:T(8,128)(2,1)S(1)}, bf16[16,64,128]{2,1,0:T(8,128)(2,1)S(1)}, u32[]{:S(2)}, u32[]{:S(2)}) collective-permute-start(bf16[16,64,128]{2,1,0:T(8,128)(2,1)S(1)} %get-tuple-element.28), channel_id=1, source_target_pairs={{0,448},{32,480},{64,0},{96,32},{128,64},{160,96},{192,128},{224,1... | collective-permute-start | bytes 786440 | tf_op jit(solution)/shard_map/ppermute | solution.py:389
  54.7 22.9 %collective-permute-start.2 = (bf16[16,64,128]{2,1,0:T(8,128)(2,1)S(1)}, bf16[16,64,128]{2,1,0:T(8,128)(2,1)S(1)}, u32[]{:S(2)}, u32[]{:S(2)}) collective-permute-start(bf16[16,64,128]{2,1,0:T(8,128)(2,1)S(1)} %get-tuple-element.25), channel_id=1, source_target_pairs={{0,64},{32,96},{64,128},{96,160},{128,192},{160,224},{192,256},{22... | collective-permute-start | bytes 786440 | tf_op jit(solution)/shard_map/ppermute | solution.py:389
  56.7 21.0 %collective-permute-start.3 = (bf16[16,64,128]{2,1,0:T(8,128)(2,1)S(1)}, bf16[16,64,128]{2,1,0:T(8,128)(2,1)S(1)}, u32[]{:S(2)}, u32[]{:S(2)}) collective-permute-start(bf16[16,64,128]{2,1,0:T(8,128)(2,1)S(1)} %get-tuple-element.26), channel_id=1, source_target_pairs={{0,448},{32,480},{64,0},{96,32},{128,64},{160,96},{192,128},{224,1... | collective-permute-start | bytes 786440 | tf_op jit(solution)/shard_map/ppermute | solution.py:389
  62.7 4.2 %collective-permute-start.6 = (bf16[3,16,64,128]{3,2,1,0:T(8,128)(2,1)S(1)}, bf16[3,16,64,128]{3,2,1,0:T(8,128)(2,1)S(1)}, u32[]{:S(2)}, u32[]{:S(2)}) collective-permute-start(bf16[3,16,64,128]{3,2,1,0:T(8,128)(2,1)S(1)} %get-tuple-element.29), channel_id=1, source_target_pairs={{0,4},{4,0},{1,5},{5,1},{2,6},{6,2},{3,7},{7,3},{8,12},{12,8},{9,1... | collective-permute-start | bytes 2359304 | tf_op jit(solution)/shard_map/ppermute | solution.py:393
  78.2 6.4 %collective-permute-start.7 = (bf16[16,64,128]{2,1,0:T(8,128)(2,1)S(1)}, bf16[16,64,128]{2,1,0:T(8,128)(2,1)S(1)}, u32[]{:S(2)}, u32[]{:S(2)}) collective-permute-start(bf16[16,64,128]{2,1,0:T(8,128)(2,1)S(1)} %forwarded.1), channel_id=1, source_target_pairs={{0,4},{4,0},{1,5},{5,1},{2,6},{6,2},{3,7},{7,3},{8,12},{12,8},{9,1... | collective-permute-start | bytes 786440 | tf_op jit(solution)/shard_map/ppermute | solution.py:393
  85.2 17.1 %collective-permute-start.9 = (bf16[16,64,128]{2,1,0:T(8,128)(2,1)S(1)}, bf16[16,64,128]{2,1,0:T(8,128)(2,1)S(1)}, u32[]{:S(2)}, u32[]{:S(2)}) collective-permute-start(bf16[16,64,128]{2,1,0:T(8,128)(2,1)S(1)} %get-tuple-element.33), channel_id=1, source_target_pairs={{0,448},{32,480},{64,0},{96,32},{128,64},{160,96},{192,128},{224,1... | collective-permute-start | bytes 786440 | tf_op jit(solution)/shard_map/ppermute | solution.py:389
  87.1 15.2 %collective-permute-start.8 = (bf16[16,64,128]{2,1,0:T(8,128)(2,1)S(1)}, bf16[16,64,128]{2,1,0:T(8,128)(2,1)S(1)}, u32[]{:S(2)}, u32[]{:S(2)}) collective-permute-start(bf16[16,64,128]{2,1,0:T(8,128)(2,1)S(1)} %get-tuple-element.33), channel_id=1, source_target_pairs={{0,64},{32,96},{64,128},{96,160},{128,192},{160,224},{192,256},{22... | collective-permute-start | bytes 786440 | tf_op jit(solution)/shard_map/ppermute | solution.py:389

commit v8 on v7

--- a/solution.py
+++ b/solution.py
@@ -73,13 +73,17 @@
             first = [jnp.where(upper, t, first[0]), jnp.where(upper, first[1], t)]
             low, high = low + upper.astype(jnp.int32), high + 1 - upper.astype(jnp.int32)
         for p in range(2):
+            counts = [0, 0, 0]
             for j in range(WIN):
                 n = nb[j, base * 4 + first[p]]
                 d = lax.rem(n // 4 - k + COLS, COLS)
                 t = lax.rem(n, 4)
-                at = WIN * (2 * column + p) + j
-                table[AT_HEAD + at] = jnp.where(d == 0, 0, jnp.where(d == 1, 4, 8)) + t
-                table[AT_SHARED + at] = jnp.where(d == 0, 0, jnp.where(d == near, 4, 8)) + t
+                at = WIN * (2 * column + p)
+                table[AT_HEAD + at + j] = jnp.where(d == 0, 0, jnp.where(d == 1, 4, 8)) + t
+                group = jnp.where(d == 0, 0, jnp.where(d == near, 1, 2))
+                count = jnp.where(group == 0, counts[0], jnp.where(group == 1, counts[1], counts[2]))
+                table[AT_SHARED + at + 3 * group + count] = 4 * group + t
+                counts = [c + (group == g).astype(jnp.int32) for g, c in enumerate(counts)]
     return w
 
 
@@ -133,7 +137,7 @@
     one[...] = two[:, ONE]
 
 
-def middle_kernel(table, order, two, q_head, q_shared, value_left, value_right):
+def middle_kernel(table, order, two, q_head, q_shared, main_left, main_right):
     w = table[AT_W]
     edge = (w == 0) | (w == 7)
     col, core = lax.axis_index("col"), lax.axis_index("core")
@@ -146,35 +150,35 @@
         mine = [jnp.where(core == 0, f[0:32], f[32:64]) for f in factors]
         q_shared[source] = turned(held[QUERY], mine)
 
-    for out, special in ((value_left, 1), (value_right, 6)):
+    for out, special in ((main_left, 1), (main_right, 6)):
 
         @pl.when(w == special)
         def _(out=out):
             out[:, 0:32] = q_shared[...]
             out[:, 32:64] = q_shared[...]
 
+        @pl.when(edge)
+        def _(out=out):
+            out[...] = q_head[...]
+
+        @pl.when((w != special) & jnp.logical_not(edge))
+        def _(out=out):
+            out[...] = two[:, MAIN]
+
+
+def late_kernel(table, two, l1, r1, value_left, value_right, swap):
+    w = table[AT_W]
+    edge = (w == 0) | (w == 7)
+    for out, special, source in ((value_left, 1, r1), (value_right, 6, l1)):
+
+        @pl.when(w == special)
+        def _(out=out, source=source):
+            out[...] = source[...]
+
         @pl.when(w != special)
         def _(out=out):
             out[...] = two[:, VALUE]
 
-
-def late_kernel(table, two, q_head, l1, r1, main_left, main_right, swap):
-    w = table[AT_W]
-    edge = (w == 0) | (w == 7)
-    for out, special, source in ((main_left, 1, r1), (main_right, 6, l1)):
-
-        @pl.when(w == special)
-        def _(out=out, source=source):
-            out[...] = source[...]
-
-        @pl.when(edge)
-        def _(out=out):
-            out[...] = q_head[...]
-
-        @pl.when((w != special) & jnp.logical_not(edge))
-        def _(out=out):
-            out[...] = two[:, MAIN]
-
     @pl.when(edge)
     def _():
         swap[0] = two[:, REST]
@@ -187,8 +191,8 @@
     swap[2] = r1[...]
 
 
-def attend(q, kp, vp, picks):
-    top = weights = acc = None
+def steps(q, kp, vp, picks, state):
+    top, weights, acc = state
     for pick in picks:
         s = lax.dot_general(q, kp[pick], (((1,), (1,)), ((), ())), preferred_element_type=F32)
         high = jnp.max(s, axis=1, keepdims=True)
@@ -201,22 +205,35 @@
             shrink = jnp.exp2((top - new) * POWER)
             weights, acc = weights * shrink + p, acc * shrink + part
         top = new
+    return top, weights, acc
+
+
+def finished(state):
+    _, weights, acc = state
     return (acc / jnp.sum(weights, axis=1, keepdims=True)).astype(BF)
 
 
 def whole(ref, *index):
     return ref[index].reshape(-1, HD)
+
+
+def pair_of(table, column, at, p):
+    fours = [pl.ds(table[AT_TILE + 4 * column + 2 * p + i] * 4, 4) for i in range(2)]
+    return fours, [table[at + (2 * column + p) * WIN + j] for j in range(WIN)]
+
+
+def store_pair(store, fours, o):
+    half = o.shape[0] // 2
+    for i, four in enumerate(fours):
+        store(four, o[i * half : (i + 1) * half].reshape(4, -1, HD))
 
 
 def attend_column(table, column, at, query, kp, vp, store):
     @pl.loop(0, 2)
     def _(p):
-        fours = [pl.ds(table[AT_TILE + 4 * column + 2 * p + i] * 4, 4) for i in range(2)]
-        picks = [table[at + (2 * column + p) * WIN + j] for j in range(WIN)]
-        o = attend(jnp.concatenate([query(four) for four in fours]), kp, vp, picks)
-        half = o.shape[0] // 2
-        for i, four in enumerate(fours):
-            store(four, o[i * half : (i + 1) * half].reshape(4, -1, HD))
+        fours, picks = pair_of(table, column, at, p)
+        q = jnp.concatenate([query(four) for four in fours])
+        store_pair(store, fours, finished(steps(q, kp, vp, picks, (None, None, None))))
 
 
 def fill_shared(base, mine, other, k2, v2):
@@ -227,55 +244,7 @@
             pool[base + t, 128:256] = other(four, part)
 
 
-def value_kernel(two, l3, r3, vh):
-    for t in range(4):
-        four = slice(4 * t, 4 * t + 4)
-        vh[t] = two[four, VALUE]
-        vh[4 + t] = r3[four]
-        vh[8 + t] = l3[four]
-
-
-def shared_kernel(table, two, l1, r1, sw, k2, v2):
-    w = table[AT_W]
-    edge = (w == 0) | (w == 7)
-    left = (lambda f, p: whole(l1, f, p)), (lambda f, p: whole(sw, 1, f, p))
-    right = (lambda f, p: whole(r1, f, p)), (lambda f, p: whole(sw, 2, f, p))
-
-    def own(rows):
-        mine = lambda f, p: whole(two, f, slice(rows.start + p.start, rows.start + p.stop))
-        fill_shared(0, mine, lambda f, p: whole(sw, 0, f, p), k2, v2)
-
-    @pl.when(jnp.logical_not(edge))
-    def _():
-        own(ONE)
-        fill_shared(4, *right, k2, v2)
-        fill_shared(8, *left, k2, v2)
-
-    @pl.when(w == 0)
-    def _():
-        own(REST)
-        fill_shared(4, *right, k2, v2)
-
-    @pl.when(w == 7)
-    def _():
-        own(REST)
-        fill_shared(4, *left, k2, v2)
-
-
-def forwarded_kernel(table, l2, r2, vh, k2, out):
-    del vh, k2
-    w = table[AT_W]
-
-    @pl.when(w == 0)
-    def _():
-        out[...] = r2[...]
-
-    @pl.when(w == 7)
-    def _():
-        out[...] = l2[...]
-
-
-def first_kernel(table, two, q_head, l1, r1, l2, r2, vh, sent, o_oth, kh):
+def scores_kernel(table, two, q_head, l1, r1, l3, r3, kh, prob, total, s_ref):
     w = table[AT_W]
     inner = (w == 1) | (w == 6)
     edge = (w == 0) | (w == 7)
@@ -283,9 +252,8 @@
     @pl.when(jnp.logical_not(edge))
     def _():
         for t in range(4):
-            four = slice(4 * t, 4 * t + 4)
-            kh[t] = whole(two, four, MAIN)
-        for base, special, early, late in ((4, 6, r1, r2), (8, 1, l1, l2)):
+            kh[t] = whole(two, slice(4 * t, 4 * t + 4), MAIN)
+        for base, special, early, later in ((4, 6, r1, r3), (8, 1, l1, l3)):
 
             @pl.when(w == special)
             def _(base=base, early=early):
@@ -293,9 +261,112 @@
                     kh[base + t] = whole(early, slice(4 * t, 4 * t + 4))
 
             @pl.when(w != special)
-            def _(base=base, late=late):
+            def _(base=base, later=later):
                 for t in range(4):
-                    kh[base + t] = whole(late, slice(4 * t, 4 * t + 4))
+                    kh[base + t] = whole(later, slice(4 * t, 4 * t + 4))
+
+    def weigh(column, query):
+        @pl.loop(0, 2)
+        def _(p):
+            fours, picks = pair_of(table, column, AT_HEAD, p)
+            for i, four in enumerate(fours):
+                rows = slice(i * TOK_TILE, (i + 1) * TOK_TILE)
+                q = query(four)
+                top = None
+                for j, pick in enumerate(picks):
+                    s = lax.dot_general(
+                        q, kh[pick], (((1,), (1,)), ((), ())), preferred_element_type=F32
+                    )
+                    s_ref[i, j] = s
+                    top = s if top is None else jnp.maximum(top, s)
+                top = jnp.max(top, axis=1, keepdims=True)
+                sums = None
+                for j in range(WIN):
+                    weights = jnp.exp2((s_ref[i, j] - top) * POWER)
+                    sums = weights if sums is None else sums + weights
+                    prob[p, j, rows, :] = weights.astype(BF)
+                sums = jnp.sum(sums, axis=1, keepdims=True)
+                total[p, rows, :] = jnp.broadcast_to(sums, (TOK_TILE, HD))
+
+    for special, source in ((1, l3), (6, r3)):
+
+        @pl.when(w == special)
+        def _(source=source):
+            weigh(OTHER, lambda four: whole(source, four))
+
+    @pl.when(jnp.logical_not(inner | edge))
+    def _():
+        weigh(THIS, lambda four: whole(q_head, four))
+
+
+def shared_kernel(table, two, l1, r1, l3, r3, sw, k2, v2, tops, weights, accs):
+    w = table[AT_W]
+    edge = (w == 0) | (w == 7)
+    left = (lambda f, p: whole(l1, f, p)), (lambda f, p: whole(sw, 1, f, p))
+    right = (lambda f, p: whole(r1, f, p)), (lambda f, p: whole(sw, 2, f, p))
+
+    def own(rows):
+        mine = lambda f, p: whole(two, f, slice(rows.start + p.start, rows.start + p.stop))
+        fill_shared(0, mine, lambda f, p: whole(sw, 0, f, p), k2, v2)
+
+    @pl.when(jnp.logical_not(edge))
+    def _():
+        own(ONE)
+        fill_shared(4, *right, k2, v2)
+        fill_shared(8, *left, k2, v2)
+
+    for special, near, asked in ((0, right, r3), (7, left, l3)):
+
+        @pl.when(w == special)
+        def _(near=near, asked=asked):
+            own(REST)
+            fill_shared(4, *near, k2, v2)
+
+            @pl.loop(0, 2)
+            def _(p):
+                fours, picks = pair_of(table, OTHER, AT_SHARED, p)
+                q = jnp.concatenate([whole(asked, four, slice(0, 32)) for four in fours])
+                top, sums, acc = steps(q, k2, v2, picks[0:6], (None, None, None))
+                tops[p] = jnp.broadcast_to(top, acc.shape)
+                weights[p] = sums
+                accs[p] = acc
+
+
+def forwarded_kernel(table, l2, r2, kh, k2, out):
+    del kh, k2
+    w = table[AT_W]
+
+    @pl.when(w == 0)
+    def _():
+        out[...] = r2[...]
+
+    @pl.when(w == 7)
+    def _():
+        out[...] = l2[...]
+
+
+def first_kernel(table, two, l2, r2, prob, total, sent, o_oth, vh):
+    w = table[AT_W]
+    inner = (w == 1) | (w == 6)
+    edge = (w == 0) | (w == 7)
+
+    @pl.when(jnp.logical_not(edge))
+    def _():
+        for t in range(4):
+            four = slice(4 * t, 4 * t + 4)
+            vh[t] = two[four, VALUE]
+            vh[4 + t] = r2[four]
+            vh[8 + t] = l2[four]
+
+    def gather(column, store):
+        @pl.loop(0, 2)
+        def _(p):
+            fours, picks = pair_of(table, column, AT_HEAD, p)
+            acc = None
+            for j, pick in enumerate(picks):
+                part = jnp.dot(prob[p, j], whole(vh, pick), preferred_element_type=F32)
+                acc = part if acc is None else acc + part
+            store_pair(store, fours, (acc / total[p]).astype(BF))
 
     def to_other(four, o):
         o_oth[four] = o
@@ -303,20 +374,18 @@
     def to_sent(four, o):
         sent[four, 0:64] = o
 
-    for special, source in ((1, l2), (6, r2)):
-
-        @pl.when(w == special)
-        def _(source=source):
-            query = lambda four: whole(source, four)
-            attend_column(table, OTHER, AT_HEAD, query, kh, vh, to_other)
+    @pl.when(inner)
+    def _():
+        gather(OTHER, to_other)
 
     @pl.when(jnp.logical_not(inner | edge))
     def _():
-        query = lambda four: whole(q_head, four)
-        attend_column(table, THIS, AT_HEAD, query, kh, vh, to_sent)
-
-
-def edge_kernel(table, l2, r2, l3, r3, se, oth_in, k_in, v_in, o_oth, k2, v2):
+        gather(THIS, to_sent)
+
+
+def edge_kernel(
+    table, l2, r2, l3, r3, se, tops, weights, accs, oth_in, k_in, v_in, o_oth, k2, v2
+):
     del oth_in, k_in, v_in
     w = table[AT_W]
 
@@ -328,8 +397,13 @@
         @pl.when(w == special)
         def _(far=far, asked=asked):
             fill_shared(8, lambda f, p: whole(far, f, p), lambda f, p: whole(se, f, p), k2, v2)
-            query = lambda four: whole(asked, four, slice(0, 32))
-            attend_column(table, OTHER, AT_SHARED, query, k2, v2, to_other)
+
+            @pl.loop(0, 2)
+            def _(p):
+                fours, picks = pair_of(table, OTHER, AT_SHARED, p)
+                q = jnp.concatenate([whole(asked, four, slice(0, 32)) for four in fours])
+                state = tops[p, :, 0:1], weights[p], accs[p]
+                store_pair(to_other, fours, finished(steps(q, k2, v2, picks[6:9], state)))
 
 
 def last_kernel(table, q_head, q_shared, kh, vh, k2, v2, sent_in, sent):
@@ -405,13 +479,17 @@
 
 
 def kernel(body, name, outs, inputs, scratch=(), limit=32, aliases={}, flops=None, space=VMEM):
+    outs = [
+        out
+        if isinstance(out, jax.ShapeDtypeStruct)
+        else jax.ShapeDtypeStruct(out, BF if len(out) > 1 else jnp.int32)
+        for out in outs
+    ]
     return pl.pallas_call(
         body,
-        out_shape=tuple(
-            jax.ShapeDtypeStruct(shape, BF if len(shape) > 1 else jnp.int32) for shape in outs
-        ),
+        out_shape=tuple(outs),
         in_specs=[SMEM if i.dtype == jnp.int32 else space for i in inputs],
-        out_specs=tuple(space if len(shape) > 1 else SMEM for shape in outs),
+        out_specs=tuple(SMEM if out.dtype == jnp.int32 else space for out in outs),
         scratch_shapes=list(scratch),
         input_output_aliases=aliases,
         compiler_params=pltpu.CompilerParams(vmem_limit_bytes=limit * MIB),
@@ -438,34 +516,42 @@
     two = exchanged(two)
     (one,) = kernel(early_kernel, "early", (SLOT,), (two,))
     l1, r1 = along_columns(one, 1), along_columns(one, -1)
-    q_head, q_shared, value_left, value_right = kernel(
+    q_head, q_shared, main_left, main_right = kernel(
         middle_kernel, "middle", (SLOT, (16, 32, HD), SLOT, SLOT), (table, order, two), flops=FLOPS
     )
-    l3, r3 = along_columns(value_right, 1), along_columns(value_left, -1)
-    main_left, main_right, swap = kernel(
-        late_kernel, "late", (SLOT, SLOT, (3,) + SLOT), (table, two, q_head, l1, r1)
-    )
-    l2, r2 = along_columns(main_right, 1), along_columns(main_left, -1)
+    l3, r3 = along_columns(main_right, 1), along_columns(main_left, -1)
+    value_left, value_right, swap = kernel(
+        late_kernel, "late", (SLOT, SLOT, (3,) + SLOT), (table, two, l1, r1)
+    )
+    l2, r2 = along_columns(value_right, 1), along_columns(value_left, -1)
     sw = swapped(swap)
-    (vh,) = kernel(value_kernel, "values", (PARTS,), (two, l3, r3), flops=FLOPS)
-    k2, v2 = kernel(shared_kernel, "shared", (POOL, POOL), (table, two, l1, r1, sw))
-    (se,) = kernel(
-        forwarded_kernel, "forwarded", (SLOT,), (table, l2, r2, vh, k2), space=VMEM
-    )
+    kh, prob, total = kernel(
+        scores_kernel,
+        "scores",
+        (POOL, (2, WIN, 512, TOK_TILE), jax.ShapeDtypeStruct((2, 512, HD), F32)),
+        (table, two, q_head, l1, r1, l3, r3),
+        (pltpu.VMEM((2, WIN, TOK_TILE, TOK_TILE), F32),),
+        flops=FLOPS,
+    )
+    state = [jax.ShapeDtypeStruct((2, TOK_TILE, n), F32) for n in (HD, TOK_TILE, HD)]
+    k2, v2, *state = kernel(
+        shared_kernel, "shared", (POOL, POOL, *state), (table, two, l1, r1, l3, r3, sw)
+    )
+    (se,) = kernel(forwarded_kernel, "forwarded", (SLOT,), (table, l2, r2, kh, k2))
     se = swapped(se)
-    sent, o_oth, kh = kernel(
+    sent, o_oth, vh = kernel(
         first_kernel,
         "attend_first",
-        (SENT, SLOT, POOL),
-        (table, two, q_head, l1, r1, l2, r2, vh),
+        (SENT, SLOT, PARTS),
+        (table, two, l2, r2, prob, total),
         flops=FLOPS,
     )
     o_oth, k2, v2 = kernel(
         edge_kernel,
         "attend_edge",
         (SLOT, POOL, POOL),
-        (table, l2, r2, l3, r3, se, o_oth, k2, v2),
-        aliases={6: 0, 7: 1, 8: 2},
+        (table, l2, r2, l3, r3, se, *state, o_oth, k2, v2),
+        aliases={9: 0, 10: 1, 11: 2},
     )
     o_left, o_right = along_columns(o_oth, 1), along_columns(o_oth, -1)
     (sent,) = kernel(

time: 121 us -> 121 us (level)
  blocking collectives: 39.6 us -> 35.9 us
  starting transfers between devices: 39.4 us -> 41.3 us
    all_to_all x2, blocking collectives: 39.6 us -> 35.9 us  [exchanged(): return lax.all_to_all(block, GROUP, split_axis=0, concat_axis=0, tiled=True)]
    ppermute x8, starting transfers between devices: 35.5 us -> 37.5 us  [along_columns(): lax.ppermute(block, ('col', 'half'), [(i, (i + 2 * distance) % n) for i i...]
  transfers between devices with their start and end apart: 10 -> 10, of which waited for: 5 -> 6; matrix products, arithmetic and copies ran while one was open for 0% -> 0% of each run, Pallas kernels for 12% -> 12%
where the time goes in v8:
time: 121 us; the launch traced here: 120 us
  starting transfers between devices  41.3 us (34%)
  blocking collectives  35.9 us (30%)
  Pallas kernels  21.1 us (17%)
  waiting for transfers between devices  21 us (17%)
    ppermute x8, starting transfers between devices, along_columns(): lax.ppermute(block, ('col', 'half'), [(i, (i + 2 * distance) % n) for i i...  37.5 us
    all_to_all x2, blocking collectives, exchanged(): return lax.all_to_all(block, GROUP, split_axis=0, concat_axis=0, tiled=True)  35.9 us
    pallas_call x12, Pallas kernels, kernel(): pl.pallas_call(body, out_shape=tuple(outs), in_specs=[SMEM if i.dtype ==...  21.1 us
    ppermute x8, waiting for transfers between devices, along_columns(): lax.ppermute(block, ('col', 'half'), [(i, (i + 2 * distance) % n) for i i...  21 us
    ppermute x2, starting transfers between devices, swapped(): return lax.ppermute(block, 'core', [(0, 1), (1, 0)])  3.84 us
  transfers between devices with their start and end apart: 10, of which 6 were waited for; matrix products, arithmetic and copies ran while one was open for 0% of the time, Pallas kernels for 12%

profile of v8, /device:TPU:24, one launch (start us, length us, event | category | flops | bytes accessed | tf_op | source)
XLA Modules:
  0.0 119.6 jit_solution(11902012661755526363)
XLA Ops:
  0.0 3.7 %rotate.1 = (bf16[16,288,128]{2,1,0:T(8,128)(2,1)}, s32[128]{0:T(128)}) custom-call(s32[32]{0:T(128)} %order.3, s32[9,32]{1,0:T(8,128)} %bitcast.1, bf16[64,3072]{1,0:T(8,128)(2,1)} %q_hbm.1, bf16[64,3072]{1,0:T(8,128)(2,1)} %k_hbm.1, bf16[64,3072]{1,0:T(8,128)(2,1)} %v_hbm.1), custom_call_target="tpu_custom_call" | custom-call | tf_op jit(solution)/shard_map/rotate/pallas_call | solution.py:488
  3.7 23.7 %all_to_all.10.two = bf16[16,288,128]{2,1,0:T(8,128)(2,1)S(1)} all-to-all(bf16[16,288,128]{2,1,0:T(8,128)(2,1)} %get-tuple-element.29), channel_id=1, replica_groups=mesh['col'=8,'half'=2,'x'=4,'core'=2,'dp'=4] {'half','x','core'}, dimensions={0} | all-to-all | bytes 2359296 | tf_op jit(solution)/shard_map/all_to_all | solution.py:471
  27.5 0.0 copy-start
  27.5 0.0 copy-start.1
  27.5 5.2 %collective-permute-start = (bf16[16,64,128]{2,1,0:T(8,128)(2,1)S(1)}, bf16[16,64,128]{2,1,0:T(8,128)(2,1)S(1)}, u32[]{:S(2)}, u32[]{:S(2)}) collective-permute-start(bf16[16,64,128]{2,1,0:T(8,128)(2,1)S(1)} %early.1), channel_id=1, source_target_pairs={{0,64},{32,96},{64,128},{96,160},{128,192},{160,224},{192,256},{22... | collective-permute-start | bytes 786440 | tf_op jit(solution)/shard_map/ppermute | solution.py:463
  32.7 7.7 %collective-permute-start.1 = (bf16[16,64,128]{2,1,0:T(8,128)(2,1)S(1)}, bf16[16,64,128]{2,1,0:T(8,128)(2,1)S(1)}, u32[]{:S(2)}, u32[]{:S(2)}) collective-permute-start(bf16[16,64,128]{2,1,0:T(8,128)(2,1)S(1)} %early.1), channel_id=1, source_target_pairs={{0,448},{32,480},{64,0},{96,32},{128,64},{160,96},{192,128},{224,1... | collective-permute-start | bytes 786440 | tf_op jit(solution)/shard_map/ppermute | solution.py:463
  40.4 0.0 copy-done
  40.4 0.0 copy-done.1
  40.4 3.4 %middle.1 = (bf16[16,64,128]{2,1,0:T(8,128)(2,1)S(1)}, bf16[16,32,128]{2,1,0:T(8,128)(2,1)S(1)}, bf16[16,64,128]{2,1,0:T(8,128)(2,1)S(1)}, bf16[16,64,128]{2,1,0:T(8,128)(2,1)S(1)}) custom-call(s32[128]{0:T(128)S(1)} %copy-done, s32[32]{0:T(128)S(1)} %copy-done.1, bf16[16,288,128]{2,1,0:T(8,128)(2,1)S(1)} %all_to_all.10.two), custom_call_target="tpu_custom_call" | custom-call | flops 20000000000 | tf_op jit(solution)/shard_map/middle/pallas_call | solution.py:488
  43.8 1.9 %collective-permute-start.4 = (bf16[16,64,128]{2,1,0:T(8,128)(2,1)S(1)}, bf16[16,64,128]{2,1,0:T(8,128)(2,1)S(1)}, u32[]{:S(2)}, u32[]{:S(2)}) collective-permute-start(bf16[16,64,128]{2,1,0:T(8,128)(2,1)S(1)} %get-tuple-element.32), channel_id=1, source_target_pairs={{0,64},{32,96},{64,128},{96,160},{128,192},{160,224},{192,256},{22... | collective-permute-start | bytes 786440 | tf_op jit(solution)/shard_map/ppermute | solution.py:463
  45.8 6.0 %collective-permute-start.5 = (bf16[16,64,128]{2,1,0:T(8,128)(2,1)S(1)}, bf16[16,64,128]{2,1,0:T(8,128)(2,1)S(1)}, u32[]{:S(2)}, u32[]{:S(2)}) collective-permute-start(bf16[16,64,128]{2,1,0:T(8,128)(2,1)S(1)} %get-tuple-element.33), channel_id=1, source_target_pairs={{0,448},{32,480},{64,0},{96,32},{128,64},{160,96},{192,128},{224,1... | collective-permute-start | bytes 786440 | tf_op jit(solution)/shard_map/ppermute | solution.py:463
  51.8 0.0 collective-permute-done.l1
  51.8 0.0 collective-permute-done.1.r1
  51.8 0.6 late.1
  52.5 5.0 %collective-permute-start.2 = (bf16[16,64,128]{2,1,0:T(8,128)(2,1)S(1)}, bf16[16,64,128]{2,1,0:T(8,128)(2,1)S(1)}, u32[]{:S(2)}, u32[]{:S(2)}) collective-permute-start(bf16[16,64,128]{2,1,0:T(8,128)(2,1)S(1)} %get-tuple-element.30), channel_id=1, source_target_pairs={{0,64},{32,96},{64,128},{96,160},{128,192},{160,224},{192,256},{22... | collective-permute-start | bytes 786440 | tf_op jit(solution)/shard_map/ppermute | solution.py:463
  57.5 2.9 %collective-permute-start.3 = (bf16[16,64,128]{2,1,0:T(8,128)(2,1)S(1)}, bf16[16,64,128]{2,1,0:T(8,128)(2,1)S(1)}, u32[]{:S(2)}, u32[]{:S(2)}) collective-permute-start(bf16[16,64,128]{2,1,0:T(8,128)(2,1)S(1)} %get-tuple-element.31), channel_id=1, source_target_pairs={{0,448},{32,480},{64,0},{96,32},{128,64},{160,96},{192,128},{224,1... | collective-permute-start | bytes 786440 | tf_op jit(solution)/shard_map/ppermute | solution.py:463
  60.5 1.9 %collective-permute-start.6 = (bf16[3,16,64,128]{3,2,1,0:T(8,128)(2,1)S(1)}, bf16[3,16,64,128]{3,2,1,0:T(8,128)(2,1)S(1)}, u32[]{:S(2)}, u32[]{:S(2)}) collective-permute-start(bf16[3,16,64,128]{3,2,1,0:T(8,128)(2,1)S(1)} %get-tuple-element.36), channel_id=1, source_target_pairs={{0,4},{4,0},{1,5},{5,1},{2,6},{6,2},{3,7},{7,3},{8,12},{12,8},{9,1... | collective-permute-start | bytes 2359304 | tf_op jit(solution)/shard_map/ppermute | solution.py:467
  62.4 0.7 collective-permute-done.4.l3
  63.1 2.3 %collective-permute-done.5.r3 = bf16[16,64,128]{2,1,0:T(8,128)(2,1)S(1)} collective-permute-done((bf16[16,64,128]{2,1,0:T(8,128)(2,1)S(1)}, bf16[16,64,128]{2,1,0:T(8,128)(2,1)S(1)}, u32[]{:S(2)}, u32[]{:S(2)}) %collective-permute-start.5) | collective-permute-done | bytes 262176 | tf_op jit(solution)/shard_map/ppermute | solution.py:463
  65.4 3.4 %scores.1 = (bf16[12,256,128]{2,1,0:T(8,128)(2,1)S(1)}, bf16[2,9,512,256]{3,2,1,0:T(8,128)(2,1)S(1)}, f32[2,512,128]{2,1,0:T(8,128)S(1)}) custom-call(s32[128]{0:T(128)S(1)} %copy-done, bf16[16,288,128]{2,1,0:T(8,128)(2,1)S(1)} %all_to_all.10.two, bf16[16,64,128]{2,1,0:T(8,128)(2,1)S(1)} %get-tuple-element.34.q_head, ...), custom_call_target="tpu_custom_call" | custom-call | flops 20000000000 | tf_op jit(solution)/shard_map/scores/pallas_call | solution.py:488
  68.8 0.0 collective-permute-done.6.sw
  68.8 0.7 shared.1
  69.5 0.6 collective-permute-done.2.l2
  70.1 6.5 %collective-permute-done.3.r2 = bf16[16,64,128]{2,1,0:T(8,128)(2,1)S(1)} collective-permute-done((bf16[16,64,128]{2,1,0:T(8,128)(2,1)S(1)}, bf16[16,64,128]{2,1,0:T(8,128)(2,1)S(1)}, u32[]{:S(2)}, u32[]{:S(2)}) %collective-permute-start.3) | collective-permute-done | bytes 262176 | tf_op jit(solution)/shard_map/ppermute | solution.py:463
  76.6 0.6 forwarded.1
  77.1 1.9 %collective-permute-start.7 = (bf16[16,64,128]{2,1,0:T(8,128)(2,1)S(1)}, bf16[16,64,128]{2,1,0:T(8,128)(2,1)S(1)}, u32[]{:S(2)}, u32[]{:S(2)}) collective-permute-start(bf16[16,64,128]{2,1,0:T(8,128)(2,1)S(1)} %forwarded.1), channel_id=1, source_target_pairs={{0,4},{4,0},{1,5},{5,1},{2,6},{6,2},{3,7},{7,3},{8,12},{12,8},{9,1... | collective-permute-start | bytes 786440 | tf_op jit(solution)/shard_map/ppermute | solution.py:467
  79.1 2.2 %attend_first.1 = (bf16[16,96,128]{2,1,0:T(8,128)(2,1)S(1)}, bf16[16,64,128]{2,1,0:T(8,128)(2,1)S(1)}, bf16[12,4,64,128]{3,2,1,0:T(8,128)(2,1)S(1)}) custom-call(s32[128]{0:T(128)S(1)} %copy-done, bf16[16,288,128]{2,1,0:T(8,128)(2,1)S(1)} %all_to_all.10.two, bf16[16,64,128]{2,1,0:T(8,128)(2,1)S(1)} %collective-permute-done.2.l2, ...), custom_call_target="tpu_custom_call" | custom-call | flops 20000000000 | tf_op jit(solution)/shard_map/attend_first/pallas_call | solution.py:488
  81.2 0.0 collective-permute-done.7.se
  81.2 0.7 attend_edge.1
  82.0 6.8 %collective-permute-start.8 = (bf16[16,64,128]{2,1,0:T(8,128)(2,1)S(1)}, bf16[16,64,128]{2,1,0:T(8,128)(2,1)S(1)}, u32[]{:S(2)}, u32[]{:S(2)}) collective-permute-start(bf16[16,64,128]{2,1,0:T(8,128)(2,1)S(1)} %get-tuple-element.45), channel_id=1, source_target_pairs={{0,64},{32,96},{64,128},{96,160},{128,192},{160,224},{192,256},{22... | collective-permute-start | bytes 786440 | tf_op jit(solution)/shard_map/ppermute | solution.py:463
  88.8 1.9 %collective-permute-start.9 = (bf16[16,64,128]{2,1,0:T(8,128)(2,1)S(1)}, bf16[16,64,128]{2,1,0:T(8,128)(2,1)S(1)}, u32[]{:S(2)}, u32[]{:S(2)}) collective-permute-start(bf16[16,64,128]{2,1,0:T(8,128)(2,1)S(1)} %get-tuple-element.45), channel_id=1, source_target_pairs={{0,448},{32,480},{64,0},{96,32},{128,64},{160,96},{192,128},{224,1... | collective-permute-start | bytes 786440 | tf_op jit(solution)/shard_map/ppermute | solution.py:463
  90.7 4.4 %attend_last.1.sent_in = bf16[16,96,128]{2,1,0:T(8,128)(2,1)S(1)} custom-call(s32[128]{0:T(128)S(1)} %copy-done, bf16[16,64,128]{2,1,0:T(8,128)(2,1)S(1)} %get-tuple-element.34.q_head, bf16[16,32,128]{2,1,0:T(8,128)(2,1)S(1)} %get-tuple-element.46.q_shared, bf16[12,256,128]{2,1,0:T(8,128)(2,1)S(1)} %get-tuple-element.35.kh, ...), custom_call_target="tpu_custom_call", output_to_operand_aliasing={{}: (7, {})} | custom-call | tf_op jit(solution)/shard_map/attend_last/pallas_call | solution.py:488
  95.1 5.0 %collective-permute-done.8.o_left = bf16[16,64,128]{2,1,0:T(8,128)(2,1)S(1)} collective-permute-done((bf16[16,64,128]{2,1,0:T(8,128)(2,1)S(1)}, bf16[16,64,128]{2,1,0:T(8,128)(2,1)S(1)}, u32[]{:S(2)}, u32[]{:S(2)}) %collective-permute-start.8) | collective-permute-done | bytes 262176 | tf_op jit(solution)/shard_map/ppermute | solution.py:463
  100.1 5.9 %collective-permute-done.9.o_right = bf16[16,64,128]{2,1,0:T(8,128)(2,1)S(1)} collective-permute-done((bf16[16,64,128]{2,1,0:T(8,128)(2,1)S(1)}, bf16[16,64,128]{2,1,0:T(8,128)(2,1)S(1)}, u32[]{:S(2)}, u32[]{:S(2)}) %collective-permute-start.9) | collective-permute-done | bytes 262176 | tf_op jit(solution)/shard_map/ppermute | solution.py:463
  106.0 0.6 merge.1
  106.6 12.2 %all_to_all.11.in_ref = bf16[16,96,128]{2,1,0:T(8,128)(2,1)S(1)} all-to-all(bf16[16,96,128]{2,1,0:T(8,128)(2,1)S(1)} %merge.1), channel_id=1, replica_groups=mesh['col'=8,'half'=2,'x'=4,'core'=2,'dp'=4] {'half','x','core'}, dimensions={0} | all-to-all | bytes 786432 | tf_op jit(solution)/shard_map/all_to_all | solution.py:471
  118.8 0.8 unpack.1
  (1 shorter events, 0.0 us)
Async XLA Ops:
  27.5 12.9 %copy-start = (s32[128]{0:T(128)S(1)}, s32[128]{0:T(128)}, u32[]{:S(2)}) copy-start(s32[128]{0:T(128)} %get-tuple-element.28.table) | copy-start | bytes 1540
  27.5 12.9 %copy-start.1 = (s32[32]{0:T(128)S(1)}, s32[32]{0:T(128)}, u32[]{:S(2)}) copy-start(s32[32]{0:T(128)} %order.3) | copy-start | bytes 388
  27.5 24.3 %collective-permute-start = (bf16[16,64,128]{2,1,0:T(8,128)(2,1)S(1)}, bf16[16,64,128]{2,1,0:T(8,128)(2,1)S(1)}, u32[]{:S(2)}, u32[]{:S(2)}) collective-permute-start(bf16[16,64,128]{2,1,0:T(8,128)(2,1)S(1)} %early.1), channel_id=1, source_target_pairs={{0,64},{32,96},{64,128},{96,160},{128,192},{160,224},{192,256},{22... | collective-permute-start | bytes 786440 | tf_op jit(solution)/shard_map/ppermute | solution.py:463
  32.7 19.2 %collective-permute-start.1 = (bf16[16,64,128]{2,1,0:T(8,128)(2,1)S(1)}, bf16[16,64,128]{2,1,0:T(8,128)(2,1)S(1)}, u32[]{:S(2)}, u32[]{:S(2)}) collective-permute-start(bf16[16,64,128]{2,1,0:T(8,128)(2,1)S(1)} %early.1), channel_id=1, source_target_pairs={{0,448},{32,480},{64,0},{96,32},{128,64},{160,96},{192,128},{224,1... | collective-permute-start | bytes 786440 | tf_op jit(solution)/shard_map/ppermute | solution.py:463
  43.8 19.2 %collective-permute-start.4 = (bf16[16,64,128]{2,1,0:T(8,128)(2,1)S(1)}, bf16[16,64,128]{2,1,0:T(8,128)(2,1)S(1)}, u32[]{:S(2)}, u32[]{:S(2)}) collective-permute-start(bf16[16,64,128]{2,1,0:T(8,128)(2,1)S(1)} %get-tuple-element.32), channel_id=1, source_target_pairs={{0,64},{32,96},{64,128},{96,160},{128,192},{160,224},{192,256},{22... | collective-permute-start | bytes 786440 | tf_op jit(solution)/shard_map/ppermute | solution.py:463
  45.8 19.6 %collective-permute-start.5 = (bf16[16,64,128]{2,1,0:T(8,128)(2,1)S(1)}, bf16[16,64,128]{2,1,0:T(8,128)(2,1)S(1)}, u32[]{:S(2)}, u32[]{:S(2)}) collective-permute-start(bf16[16,64,128]{2,1,0:T(8,128)(2,1)S(1)} %get-tuple-element.33), channel_id=1, source_target_pairs={{0,448},{32,480},{64,0},{96,32},{128,64},{160,96},{192,128},{224,1... | collective-permute-start | bytes 786440 | tf_op jit(solution)/shard_map/ppermute | solution.py:463
  52.5 17.6 %collective-permute-start.2 = (bf16[16,64,128]{2,1,0:T(8,128)(2,1)S(1)}, bf16[16,64,128]{2,1,0:T(8,128)(2,1)S(1)}, u32[]{:S(2)}, u32[]{:S(2)}) collective-permute-start(bf16[16,64,128]{2,1,0:T(8,128)(2,1)S(1)} %get-tuple-element.30), channel_id=1, source_target_pairs={{0,64},{32,96},{64,128},{96,160},{128,192},{160,224},{192,256},{22... | collective-permute-start | bytes 786440 | tf_op jit(solution)/shard_map/ppermute | solution.py:463
  57.5 19.1 %collective-permute-start.3 = (bf16[16,64,128]{2,1,0:T(8,128)(2,1)S(1)}, bf16[16,64,128]{2,1,0:T(8,128)(2,1)S(1)}, u32[]{:S(2)}, u32[]{:S(2)}) collective-permute-start(bf16[16,64,128]{2,1,0:T(8,128)(2,1)S(1)} %get-tuple-element.31), channel_id=1, source_target_pairs={{0,448},{32,480},{64,0},{96,32},{128,64},{160,96},{192,128},{224,1... | collective-permute-start | bytes 786440 | tf_op jit(solution)/shard_map/ppermute | solution.py:463
  60.5 8.3 %collective-permute-start.6 = (bf16[3,16,64,128]{3,2,1,0:T(8,128)(2,1)S(1)}, bf16[3,16,64,128]{3,2,1,0:T(8,128)(2,1)S(1)}, u32[]{:S(2)}, u32[]{:S(2)}) collective-permute-start(bf16[3,16,64,128]{3,2,1,0:T(8,128)(2,1)S(1)} %get-tuple-element.36), channel_id=1, source_target_pairs={{0,4},{4,0},{1,5},{5,1},{2,6},{6,2},{3,7},{7,3},{8,12},{12,8},{9,1... | collective-permute-start | bytes 2359304 | tf_op jit(solution)/shard_map/ppermute | solution.py:467
  77.1 4.1 %collective-permute-start.7 = (bf16[16,64,128]{2,1,0:T(8,128)(2,1)S(1)}, bf16[16,64,128]{2,1,0:T(8,128)(2,1)S(1)}, u32[]{:S(2)}, u32[]{:S(2)}) collective-permute-start(bf16[16,64,128]{2,1,0:T(8,128)(2,1)S(1)} %forwarded.1), channel_id=1, source_target_pairs={{0,4},{4,0},{1,5},{5,1},{2,6},{6,2},{3,7},{7,3},{8,12},{12,8},{9,1... | collective-permute-start | bytes 786440 | tf_op jit(solution)/shard_map/ppermute | solution.py:467
  82.0 18.1 %collective-permute-start.8 = (bf16[16,64,128]{2,1,0:T(8,128)(2,1)S(1)}, bf16[16,64,128]{2,1,0:T(8,128)(2,1)S(1)}, u32[]{:S(2)}, u32[]{:S(2)}) collective-permute-start(bf16[16,64,128]{2,1,0:T(8,128)(2,1)S(1)} %get-tuple-element.45), channel_id=1, source_target_pairs={{0,64},{32,96},{64,128},{96,160},{128,192},{160,224},{192,256},{22... | collective-permute-start | bytes 786440 | tf_op jit(solution)/shard_map/ppermute | solution.py:463
  88.8 17.2 %collective-permute-start.9 = (bf16[16,64,128]{2,1,0:T(8,128)(2,1)S(1)}, bf16[16,64,128]{2,1,0:T(8,128)(2,1)S(1)}, u32[]{:S(2)}, u32[]{:S(2)}) collective-permute-start(bf16[16,64,128]{2,1,0:T(8,128)(2,1)S(1)} %get-tuple-element.45), channel_id=1, source_target_pairs={{0,448},{32,480},{64,0},{96,32},{128,64},{160,96},{192,128},{224,1... | collective-permute-start | bytes 786440 | tf_op jit(solution)/shard_map/ppermute | solution.py:463

commit v9 on v8

--- a/solution.py
+++ b/solution.py
@@ -217,8 +217,9 @@
     return ref[index].reshape(-1, HD)
 
 
-def pair_of(table, column, at, p):
-    fours = [pl.ds(table[AT_TILE + 4 * column + 2 * p + i] * 4, 4) for i in range(2)]
+def pair_of(table, column, at, p, only=None):
+    tiles = range(2) if only is None else (only,)
+    fours = [pl.ds(table[AT_TILE + 4 * column + 2 * p + i] * 4, 4) for i in tiles]
     return fours, [table[at + (2 * column + p) * WIN + j] for j in range(WIN)]
 
 
@@ -265,38 +266,30 @@
                 for t in range(4):
                     kh[base + t] = whole(later, slice(4 * t, 4 * t + 4))
 
-    def weigh(column, query):
-        @pl.loop(0, 2)
-        def _(p):
-            fours, picks = pair_of(table, column, AT_HEAD, p)
-            for i, four in enumerate(fours):
-                rows = slice(i * TOK_TILE, (i + 1) * TOK_TILE)
-                q = query(four)
-                top = None
-                for j, pick in enumerate(picks):
-                    s = lax.dot_general(
-                        q, kh[pick], (((1,), (1,)), ((), ())), preferred_element_type=F32
-                    )
-                    s_ref[i, j] = s
-                    top = s if top is None else jnp.maximum(top, s)
-                top = jnp.max(top, axis=1, keepdims=True)
-                sums = None
-                for j in range(WIN):
-                    weights = jnp.exp2((s_ref[i, j] - top) * POWER)
-                    sums = weights if sums is None else sums + weights
-                    prob[p, j, rows, :] = weights.astype(BF)
-                sums = jnp.sum(sums, axis=1, keepdims=True)
-                total[p, rows, :] = jnp.broadcast_to(sums, (TOK_TILE, HD))
-
-    for special, source in ((1, l3), (6, r3)):
-
-        @pl.when(w == special)
-        def _(source=source):
-            weigh(OTHER, lambda four: whole(source, four))
-
-    @pl.when(jnp.logical_not(inner | edge))
-    def _():
-        weigh(THIS, lambda four: whole(q_head, four))
+    @pl.when(jnp.logical_not(edge))
+    def _():
+        column = jnp.where(inner, OTHER, THIS)
+
+        @pl.loop(0, 4)
+        def _(n):
+            p, i = n // 2, lax.rem(n, 2)
+            fours, picks = pair_of(table, column, AT_HEAD, p, i)
+            four = fours[0]
+            q = jnp.where(w == 1, whole(l3, four), jnp.where(w == 6, whole(r3, four), whole(q_head, four)))
+            rows = pl.ds(pl.multiple_of(i * TOK_TILE, TOK_TILE), TOK_TILE)
+            top = None
+            for j, pick in enumerate(picks):
+                s = lax.dot_general(q, kh[pick], (((1,), (1,)), ((), ())), preferred_element_type=F32)
+                s_ref[j] = s
+                top = s if top is None else jnp.maximum(top, s)
+            top = jnp.max(top, axis=1, keepdims=True)
+            sums = None
+            for j in range(WIN):
+                weights = jnp.exp2((s_ref[j] - top) * POWER)
+                sums = weights if sums is None else sums + weights
+                prob[p, j, rows, :] = weights.astype(BF)
+            sums = jnp.sum(sums, axis=1, keepdims=True)
+            total[p, rows, :] = jnp.broadcast_to(sums, (TOK_TILE, HD))
 
 
 def shared_kernel(table, two, l1, r1, l3, r3, sw, k2, v2, tops, weights, accs):
@@ -315,21 +308,29 @@
         fill_shared(4, *right, k2, v2)
         fill_shared(8, *left, k2, v2)
 
-    for special, near, asked in ((0, right, r3), (7, left, l3)):
-
-        @pl.when(w == special)
-        def _(near=near, asked=asked):
-            own(REST)
-            fill_shared(4, *near, k2, v2)
-
-            @pl.loop(0, 2)
-            def _(p):
-                fours, picks = pair_of(table, OTHER, AT_SHARED, p)
-                q = jnp.concatenate([whole(asked, four, slice(0, 32)) for four in fours])
-                top, sums, acc = steps(q, k2, v2, picks[0:6], (None, None, None))
-                tops[p] = jnp.broadcast_to(top, acc.shape)
-                weights[p] = sums
-                accs[p] = acc
+    @pl.when(edge)
+    def _():
+        own(REST)
+        for special, near in ((0, right), (7, left)):
+
+            @pl.when(w == special)
+            def _(near=near):
+                fill_shared(4, *near, k2, v2)
+
+        @pl.loop(0, 2)
+        def _(p):
+            fours, picks = pair_of(table, OTHER, AT_SHARED, p)
+            top, sums, acc = steps(asked(w, l3, r3, fours), k2, v2, picks[0:6], (None, None, None))
+            tops[p] = jnp.broadcast_to(top, acc.shape)
+            weights[p] = sums
+            accs[p] = acc
+
+
+def asked(w, l3, r3, fours):
+    half = slice(0, 32)
+    return jnp.concatenate(
+        [jnp.where(w == 7, whole(l3, four, half), whole(r3, four, half)) for four in fours]
+    )
 
 
 def forwarded_kernel(table, l2, r2, kh, k2, out):
@@ -358,7 +359,8 @@
             vh[4 + t] = r2[four]
             vh[8 + t] = l2[four]
 
-    def gather(column, store):
+        column = jnp.where(inner, OTHER, THIS)
+
         @pl.loop(0, 2)
         def _(p):
             fours, picks = pair_of(table, column, AT_HEAD, p)
@@ -366,44 +368,31 @@
             for j, pick in enumerate(picks):
                 part = jnp.dot(prob[p, j], whole(vh, pick), preferred_element_type=F32)
                 acc = part if acc is None else acc + part
+
+            def store(four, o):
+                o_oth[four] = o
+                sent[four, 0:64] = o
+
             store_pair(store, fours, (acc / total[p]).astype(BF))
 
-    def to_other(four, o):
-        o_oth[four] = o
-
-    def to_sent(four, o):
-        sent[four, 0:64] = o
-
-    @pl.when(inner)
-    def _():
-        gather(OTHER, to_other)
-
-    @pl.when(jnp.logical_not(inner | edge))
-    def _():
-        gather(THIS, to_sent)
-
-
-def edge_kernel(
-    table, l2, r2, l3, r3, se, tops, weights, accs, oth_in, k_in, v_in, o_oth, k2, v2
-):
+
+def edge_kernel(table, far, l3, r3, se, tops, weights, accs, oth_in, k_in, v_in, o_oth, k2, v2):
     del oth_in, k_in, v_in
     w = table[AT_W]
 
     def to_other(four, o):
         o_oth[four, 0:32] = o
 
-    for special, far, asked in ((0, r2, r3), (7, l2, l3)):
-
-        @pl.when(w == special)
-        def _(far=far, asked=asked):
-            fill_shared(8, lambda f, p: whole(far, f, p), lambda f, p: whole(se, f, p), k2, v2)
-
-            @pl.loop(0, 2)
-            def _(p):
-                fours, picks = pair_of(table, OTHER, AT_SHARED, p)
-                q = jnp.concatenate([whole(asked, four, slice(0, 32)) for four in fours])
-                state = tops[p, :, 0:1], weights[p], accs[p]
-                store_pair(to_other, fours, finished(steps(q, k2, v2, picks[6:9], state)))
+    @pl.when((w == 0) | (w == 7))
+    def _():
+        fill_shared(8, lambda f, p: whole(far, f, p), lambda f, p: whole(se, f, p), k2, v2)
+
+        @pl.loop(0, 2)
+        def _(p):
+            fours, picks = pair_of(table, OTHER, AT_SHARED, p)
+            state = tops[p, :, 0:1], weights[p], accs[p]
+            q = asked(w, l3, r3, fours)
+            store_pair(to_other, fours, finished(steps(q, k2, v2, picks[6:9], state)))
 
 
 def last_kernel(table, q_head, q_shared, kh, vh, k2, v2, sent_in, sent):
@@ -530,15 +519,15 @@
         "scores",
         (POOL, (2, WIN, 512, TOK_TILE), jax.ShapeDtypeStruct((2, 512, HD), F32)),
         (table, two, q_head, l1, r1, l3, r3),
-        (pltpu.VMEM((2, WIN, TOK_TILE, TOK_TILE), F32),),
+        (pltpu.VMEM((WIN, TOK_TILE, TOK_TILE), F32),),
         flops=FLOPS,
     )
     state = [jax.ShapeDtypeStruct((2, TOK_TILE, n), F32) for n in (HD, TOK_TILE, HD)]
     k2, v2, *state = kernel(
         shared_kernel, "shared", (POOL, POOL, *state), (table, two, l1, r1, l3, r3, sw)
     )
-    (se,) = kernel(forwarded_kernel, "forwarded", (SLOT,), (table, l2, r2, kh, k2))
-    se = swapped(se)
+    (far,) = kernel(forwarded_kernel, "forwarded", (SLOT,), (table, l2, r2, kh, k2))
+    se = swapped(far)
     sent, o_oth, vh = kernel(
         first_kernel,
         "attend_first",
@@ -550,8 +539,8 @@
         edge_kernel,
         "attend_edge",
         (SLOT, POOL, POOL),
-        (table, l2, r2, l3, r3, se, *state, o_oth, k2, v2),
-        aliases={9: 0, 10: 1, 11: 2},
+        (table, far, l3, r3, se, *state, o_oth, k2, v2),
+        aliases={8: 0, 9: 1, 10: 2},
     )
     o_left, o_right = along_columns(o_oth, 1), along_columns(o_oth, -1)
     (sent,) = kernel(

time: 121 us -> 121 us (level)
  transfers between devices with their start and end apart: 10 -> 10, of which waited for: 6 -> 5; matrix products, arithmetic and copies ran while one was open for 0% -> 0% of each run, Pallas kernels for 12% -> 12%
where the time goes in v9:
time: 121 us; the launch traced here: 119 us
  starting transfers between devices  40.6 us (34%)
  blocking collectives  35.9 us (30%)
  waiting for transfers between devices  22.2 us (18%)
  Pallas kernels  20.5 us (17%)
    ppermute x8, starting transfers between devices, along_columns(): lax.ppermute(block, ('col', 'half'), [(i, (i + 2 * distance) % n) for i i...  36.7 us
    all_to_all x2, blocking collectives, exchanged(): return lax.all_to_all(block, GROUP, split_axis=0, concat_axis=0, tiled=True)  35.9 us
    ppermute x8, waiting for transfers between devices, along_columns(): lax.ppermute(block, ('col', 'half'), [(i, (i + 2 * distance) % n) for i i...  22.2 us
    pallas_call x12, Pallas kernels, kernel(): pl.pallas_call(body, out_shape=tuple(outs), in_specs=[SMEM if i.dtype ==...  20.5 us
    ppermute x2, starting transfers between devices, swapped(): return lax.ppermute(block, 'core', [(0, 1), (1, 0)])  3.84 us
  transfers between devices with their start and end apart: 10, of which 5 were waited for; matrix products, arithmetic and copies ran while one was open for 0% of the time, Pallas kernels for 12%

profile of v9, /device:TPU:24, one launch (start us, length us, event | category | flops | bytes accessed | tf_op | source)
XLA Modules:
  0.0 119.4 jit_solution(1771788969581827726)
XLA Ops:
  0.0 3.7 %rotate.1 = (bf16[16,288,128]{2,1,0:T(8,128)(2,1)}, s32[128]{0:T(128)}) custom-call(s32[32]{0:T(128)} %order.3, s32[9,32]{1,0:T(8,128)} %bitcast.1, bf16[64,3072]{1,0:T(8,128)(2,1)} %q_hbm.1, bf16[64,3072]{1,0:T(8,128)(2,1)} %k_hbm.1, bf16[64,3072]{1,0:T(8,128)(2,1)} %v_hbm.1), custom_call_target="tpu_custom_call" | custom-call | tf_op jit(solution)/shard_map/rotate/pallas_call | solution.py:477
  3.7 23.7 %all_to_all.10.two = bf16[16,288,128]{2,1,0:T(8,128)(2,1)S(1)} all-to-all(bf16[16,288,128]{2,1,0:T(8,128)(2,1)} %get-tuple-element.29), channel_id=1, replica_groups=mesh['col'=8,'half'=2,'x'=4,'core'=2,'dp'=4] {'half','x','core'}, dimensions={0} | all-to-all | bytes 2359296 | tf_op jit(solution)/shard_map/all_to_all | solution.py:460
  27.5 0.0 copy-start
  27.5 0.0 copy-start.1
  27.5 5.2 %collective-permute-start = (bf16[16,64,128]{2,1,0:T(8,128)(2,1)S(1)}, bf16[16,64,128]{2,1,0:T(8,128)(2,1)S(1)}, u32[]{:S(2)}, u32[]{:S(2)}) collective-permute-start(bf16[16,64,128]{2,1,0:T(8,128)(2,1)S(1)} %early.1), channel_id=1, source_target_pairs={{0,64},{32,96},{64,128},{96,160},{128,192},{160,224},{192,256},{22... | collective-permute-start | bytes 786440 | tf_op jit(solution)/shard_map/ppermute | solution.py:452
  32.7 7.7 %collective-permute-start.1 = (bf16[16,64,128]{2,1,0:T(8,128)(2,1)S(1)}, bf16[16,64,128]{2,1,0:T(8,128)(2,1)S(1)}, u32[]{:S(2)}, u32[]{:S(2)}) collective-permute-start(bf16[16,64,128]{2,1,0:T(8,128)(2,1)S(1)} %early.1), channel_id=1, source_target_pairs={{0,448},{32,480},{64,0},{96,32},{128,64},{160,96},{192,128},{224,1... | collective-permute-start | bytes 786440 | tf_op jit(solution)/shard_map/ppermute | solution.py:452
  40.4 0.0 copy-done
  40.4 0.0 copy-done.1
  40.4 3.4 %middle.1 = (bf16[16,64,128]{2,1,0:T(8,128)(2,1)S(1)}, bf16[16,32,128]{2,1,0:T(8,128)(2,1)S(1)}, bf16[16,64,128]{2,1,0:T(8,128)(2,1)S(1)}, bf16[16,64,128]{2,1,0:T(8,128)(2,1)S(1)}) custom-call(s32[128]{0:T(128)S(1)} %copy-done, s32[32]{0:T(128)S(1)} %copy-done.1, bf16[16,288,128]{2,1,0:T(8,128)(2,1)S(1)} %all_to_all.10.two), custom_call_target="tpu_custom_call" | custom-call | flops 20000000000 | tf_op jit(solution)/shard_map/middle/pallas_call | solution.py:477
  43.8 1.9 %collective-permute-start.4 = (bf16[16,64,128]{2,1,0:T(8,128)(2,1)S(1)}, bf16[16,64,128]{2,1,0:T(8,128)(2,1)S(1)}, u32[]{:S(2)}, u32[]{:S(2)}) collective-permute-start(bf16[16,64,128]{2,1,0:T(8,128)(2,1)S(1)} %get-tuple-element.33), channel_id=1, source_target_pairs={{0,64},{32,96},{64,128},{96,160},{128,192},{160,224},{192,256},{22... | collective-permute-start | bytes 786440 | tf_op jit(solution)/shard_map/ppermute | solution.py:452
  45.8 6.0 %collective-permute-start.5 = (bf16[16,64,128]{2,1,0:T(8,128)(2,1)S(1)}, bf16[16,64,128]{2,1,0:T(8,128)(2,1)S(1)}, u32[]{:S(2)}, u32[]{:S(2)}) collective-permute-start(bf16[16,64,128]{2,1,0:T(8,128)(2,1)S(1)} %get-tuple-element.34), channel_id=1, source_target_pairs={{0,448},{32,480},{64,0},{96,32},{128,64},{160,96},{192,128},{224,1... | collective-permute-start | bytes 786440 | tf_op jit(solution)/shard_map/ppermute | solution.py:452
  51.8 0.0 collective-permute-done.l1
  51.8 0.0 collective-permute-done.1.r1
  51.8 0.6 late.1
  52.5 5.0 %collective-permute-start.2 = (bf16[16,64,128]{2,1,0:T(8,128)(2,1)S(1)}, bf16[16,64,128]{2,1,0:T(8,128)(2,1)S(1)}, u32[]{:S(2)}, u32[]{:S(2)}) collective-permute-start(bf16[16,64,128]{2,1,0:T(8,128)(2,1)S(1)} %get-tuple-element.30), channel_id=1, source_target_pairs={{0,64},{32,96},{64,128},{96,160},{128,192},{160,224},{192,256},{22... | collective-permute-start | bytes 786440 | tf_op jit(solution)/shard_map/ppermute | solution.py:452
  57.5 2.9 %collective-permute-start.3 = (bf16[16,64,128]{2,1,0:T(8,128)(2,1)S(1)}, bf16[16,64,128]{2,1,0:T(8,128)(2,1)S(1)}, u32[]{:S(2)}, u32[]{:S(2)}) collective-permute-start(bf16[16,64,128]{2,1,0:T(8,128)(2,1)S(1)} %get-tuple-element.31), channel_id=1, source_target_pairs={{0,448},{32,480},{64,0},{96,32},{128,64},{160,96},{192,128},{224,1... | collective-permute-start | bytes 786440 | tf_op jit(solution)/shard_map/ppermute | solution.py:452
  60.4 1.9 %collective-permute-start.6 = (bf16[3,16,64,128]{3,2,1,0:T(8,128)(2,1)S(1)}, bf16[3,16,64,128]{3,2,1,0:T(8,128)(2,1)S(1)}, u32[]{:S(2)}, u32[]{:S(2)}) collective-permute-start(bf16[3,16,64,128]{3,2,1,0:T(8,128)(2,1)S(1)} %get-tuple-element.36), channel_id=1, source_target_pairs={{0,4},{4,0},{1,5},{5,1},{2,6},{6,2},{3,7},{7,3},{8,12},{12,8},{9,1... | collective-permute-start | bytes 2359304 | tf_op jit(solution)/shard_map/ppermute | solution.py:456
  62.4 0.7 collective-permute-done.4.l3
  63.1 2.3 %collective-permute-done.5.r3 = bf16[16,64,128]{2,1,0:T(8,128)(2,1)S(1)} collective-permute-done((bf16[16,64,128]{2,1,0:T(8,128)(2,1)S(1)}, bf16[16,64,128]{2,1,0:T(8,128)(2,1)S(1)}, u32[]{:S(2)}, u32[]{:S(2)}) %collective-permute-start.5) | collective-permute-done | bytes 262176 | tf_op jit(solution)/shard_map/ppermute | solution.py:452
  65.4 4.2 %scores.1 = (bf16[12,256,128]{2,1,0:T(8,128)(2,1)S(1)}, bf16[2,9,512,256]{3,2,1,0:T(8,128)(2,1)S(1)}, f32[2,512,128]{2,1,0:T(8,128)S(1)}) custom-call(s32[128]{0:T(128)S(1)} %copy-done, bf16[16,288,128]{2,1,0:T(8,128)(2,1)S(1)} %all_to_all.10.two, bf16[16,64,128]{2,1,0:T(8,128)(2,1)S(1)} %get-tuple-element.32.q_head, ...), custom_call_target="tpu_custom_call" | custom-call | flops 20000000000 | tf_op jit(solution)/shard_map/scores/pallas_call | solution.py:477
  69.6 0.0 collective-permute-done.6.sw
  69.6 0.7 shared.1
  70.3 0.0 collective-permute-done.2.l2
  70.3 6.3 %collective-permute-done.3.r2 = bf16[16,64,128]{2,1,0:T(8,128)(2,1)S(1)} collective-permute-done((bf16[16,64,128]{2,1,0:T(8,128)(2,1)S(1)}, bf16[16,64,128]{2,1,0:T(8,128)(2,1)S(1)}, u32[]{:S(2)}, u32[]{:S(2)}) %collective-permute-start.3) | collective-permute-done | bytes 262176 | tf_op jit(solution)/shard_map/ppermute | solution.py:452
  76.6 0.6 forwarded.1.far
  77.1 1.9 %collective-permute-start.7 = (bf16[16,64,128]{2,1,0:T(8,128)(2,1)S(1)}, bf16[16,64,128]{2,1,0:T(8,128)(2,1)S(1)}, u32[]{:S(2)}, u32[]{:S(2)}) collective-permute-start(bf16[16,64,128]{2,1,0:T(8,128)(2,1)S(1)} %forwarded.1.far), channel_id=1, source_target_pairs={{0,4},{4,0},{1,5},{5,1},{2,6},{6,2},{3,7},{7,3},{8,12},{12,8},{9,1... | collective-permute-start | bytes 786440 | tf_op jit(solution)/shard_map/ppermute | solution.py:456
  79.1 2.2 %attend_first.1 = (bf16[16,96,128]{2,1,0:T(8,128)(2,1)S(1)}, bf16[16,64,128]{2,1,0:T(8,128)(2,1)S(1)}, bf16[12,4,64,128]{3,2,1,0:T(8,128)(2,1)S(1)}) custom-call(s32[128]{0:T(128)S(1)} %copy-done, bf16[16,288,128]{2,1,0:T(8,128)(2,1)S(1)} %all_to_all.10.two, bf16[16,64,128]{2,1,0:T(8,128)(2,1)S(1)} %collective-permute-done.2.l2, ...), custom_call_target="tpu_custom_call" | custom-call | flops 20000000000 | tf_op jit(solution)/shard_map/attend_first/pallas_call | solution.py:477
  81.2 0.0 collective-permute-done.7.se
  81.2 0.6 attend_edge.1
  81.8 4.8 %collective-permute-start.8 = (bf16[16,64,128]{2,1,0:T(8,128)(2,1)S(1)}, bf16[16,64,128]{2,1,0:T(8,128)(2,1)S(1)}, u32[]{:S(2)}, u32[]{:S(2)}) collective-permute-start(bf16[16,64,128]{2,1,0:T(8,128)(2,1)S(1)} %get-tuple-element.45), channel_id=1, source_target_pairs={{0,64},{32,96},{64,128},{96,160},{128,192},{160,224},{192,256},{22... | collective-permute-start | bytes 786440 | tf_op jit(solution)/shard_map/ppermute | solution.py:452
  86.6 3.1 %collective-permute-start.9 = (bf16[16,64,128]{2,1,0:T(8,128)(2,1)S(1)}, bf16[16,64,128]{2,1,0:T(8,128)(2,1)S(1)}, u32[]{:S(2)}, u32[]{:S(2)}) collective-permute-start(bf16[16,64,128]{2,1,0:T(8,128)(2,1)S(1)} %get-tuple-element.45), channel_id=1, source_target_pairs={{0,448},{32,480},{64,0},{96,32},{128,64},{160,96},{192,128},{224,1... | collective-permute-start | bytes 786440 | tf_op jit(solution)/shard_map/ppermute | solution.py:452
  89.8 3.2 %attend_last.1.sent_in = bf16[16,96,128]{2,1,0:T(8,128)(2,1)S(1)} custom-call(s32[128]{0:T(128)S(1)} %copy-done, bf16[16,64,128]{2,1,0:T(8,128)(2,1)S(1)} %get-tuple-element.32.q_head, bf16[16,32,128]{2,1,0:T(8,128)(2,1)S(1)} %get-tuple-element.46.q_shared, bf16[12,256,128]{2,1,0:T(8,128)(2,1)S(1)} %get-tuple-element.35.kh, ...), custom_call_target="tpu_custom_call", output_to_operand_aliasing={{}: (7, {})} | custom-call | tf_op jit(solution)/shard_map/attend_last/pallas_call | solution.py:477
  92.9 3.9 %collective-permute-done.8.o_left = bf16[16,64,128]{2,1,0:T(8,128)(2,1)S(1)} collective-permute-done((bf16[16,64,128]{2,1,0:T(8,128)(2,1)S(1)}, bf16[16,64,128]{2,1,0:T(8,128)(2,1)S(1)}, u32[]{:S(2)}, u32[]{:S(2)}) %collective-permute-start.8) | collective-permute-done | bytes 262176 | tf_op jit(solution)/shard_map/ppermute | solution.py:452
  96.8 9.0 %collective-permute-done.9.o_right = bf16[16,64,128]{2,1,0:T(8,128)(2,1)S(1)} collective-permute-done((bf16[16,64,128]{2,1,0:T(8,128)(2,1)S(1)}, bf16[16,64,128]{2,1,0:T(8,128)(2,1)S(1)}, u32[]{:S(2)}, u32[]{:S(2)}) %collective-permute-start.9) | collective-permute-done | bytes 262176 | tf_op jit(solution)/shard_map/ppermute | solution.py:452
  105.8 0.6 merge.1
  106.4 12.2 %all_to_all.11.in_ref = bf16[16,96,128]{2,1,0:T(8,128)(2,1)S(1)} all-to-all(bf16[16,96,128]{2,1,0:T(8,128)(2,1)S(1)} %merge.1), channel_id=1, replica_groups=mesh['col'=8,'half'=2,'x'=4,'core'=2,'dp'=4] {'half','x','core'}, dimensions={0} | all-to-all | bytes 786432 | tf_op jit(solution)/shard_map/all_to_all | solution.py:460
  118.6 0.8 unpack.1
  (1 shorter events, 0.0 us)
Async XLA Ops:
  27.5 12.9 %copy-start = (s32[128]{0:T(128)S(1)}, s32[128]{0:T(128)}, u32[]{:S(2)}) copy-start(s32[128]{0:T(128)} %get-tuple-element.28.table) | copy-start | bytes 1540
  27.5 12.9 %copy-start.1 = (s32[32]{0:T(128)S(1)}, s32[32]{0:T(128)}, u32[]{:S(2)}) copy-start(s32[32]{0:T(128)} %order.3) | copy-start | bytes 388
  27.5 24.3 %collective-permute-start = (bf16[16,64,128]{2,1,0:T(8,128)(2,1)S(1)}, bf16[16,64,128]{2,1,0:T(8,128)(2,1)S(1)}, u32[]{:S(2)}, u32[]{:S(2)}) collective-permute-start(bf16[16,64,128]{2,1,0:T(8,128)(2,1)S(1)} %early.1), channel_id=1, source_target_pairs={{0,64},{32,96},{64,128},{96,160},{128,192},{160,224},{192,256},{22... | collective-permute-start | bytes 786440 | tf_op jit(solution)/shard_map/ppermute | solution.py:452
  32.7 19.1 %collective-permute-start.1 = (bf16[16,64,128]{2,1,0:T(8,128)(2,1)S(1)}, bf16[16,64,128]{2,1,0:T(8,128)(2,1)S(1)}, u32[]{:S(2)}, u32[]{:S(2)}) collective-permute-start(bf16[16,64,128]{2,1,0:T(8,128)(2,1)S(1)} %early.1), channel_id=1, source_target_pairs={{0,448},{32,480},{64,0},{96,32},{128,64},{160,96},{192,128},{224,1... | collective-permute-start | bytes 786440 | tf_op jit(solution)/shard_map/ppermute | solution.py:452
  43.8 19.3 %collective-permute-start.4 = (bf16[16,64,128]{2,1,0:T(8,128)(2,1)S(1)}, bf16[16,64,128]{2,1,0:T(8,128)(2,1)S(1)}, u32[]{:S(2)}, u32[]{:S(2)}) collective-permute-start(bf16[16,64,128]{2,1,0:T(8,128)(2,1)S(1)} %get-tuple-element.33), channel_id=1, source_target_pairs={{0,64},{32,96},{64,128},{96,160},{128,192},{160,224},{192,256},{22... | collective-permute-start | bytes 786440 | tf_op jit(solution)/shard_map/ppermute | solution.py:452
  45.8 19.6 %collective-permute-start.5 = (bf16[16,64,128]{2,1,0:T(8,128)(2,1)S(1)}, bf16[16,64,128]{2,1,0:T(8,128)(2,1)S(1)}, u32[]{:S(2)}, u32[]{:S(2)}) collective-permute-start(bf16[16,64,128]{2,1,0:T(8,128)(2,1)S(1)} %get-tuple-element.34), channel_id=1, source_target_pairs={{0,448},{32,480},{64,0},{96,32},{128,64},{160,96},{192,128},{224,1... | collective-permute-start | bytes 786440 | tf_op jit(solution)/shard_map/ppermute | solution.py:452
  52.5 17.8 %collective-permute-start.2 = (bf16[16,64,128]{2,1,0:T(8,128)(2,1)S(1)}, bf16[16,64,128]{2,1,0:T(8,128)(2,1)S(1)}, u32[]{:S(2)}, u32[]{:S(2)}) collective-permute-start(bf16[16,64,128]{2,1,0:T(8,128)(2,1)S(1)} %get-tuple-element.30), channel_id=1, source_target_pairs={{0,64},{32,96},{64,128},{96,160},{128,192},{160,224},{192,256},{22... | collective-permute-start | bytes 786440 | tf_op jit(solution)/shard_map/ppermute | solution.py:452
  57.5 19.1 %collective-permute-start.3 = (bf16[16,64,128]{2,1,0:T(8,128)(2,1)S(1)}, bf16[16,64,128]{2,1,0:T(8,128)(2,1)S(1)}, u32[]{:S(2)}, u32[]{:S(2)}) collective-permute-start(bf16[16,64,128]{2,1,0:T(8,128)(2,1)S(1)} %get-tuple-element.31), channel_id=1, source_target_pairs={{0,448},{32,480},{64,0},{96,32},{128,64},{160,96},{192,128},{224,1... | collective-permute-start | bytes 786440 | tf_op jit(solution)/shard_map/ppermute | solution.py:452
  60.4 9.2 %collective-permute-start.6 = (bf16[3,16,64,128]{3,2,1,0:T(8,128)(2,1)S(1)}, bf16[3,16,64,128]{3,2,1,0:T(8,128)(2,1)S(1)}, u32[]{:S(2)}, u32[]{:S(2)}) collective-permute-start(bf16[3,16,64,128]{3,2,1,0:T(8,128)(2,1)S(1)} %get-tuple-element.36), channel_id=1, source_target_pairs={{0,4},{4,0},{1,5},{5,1},{2,6},{6,2},{3,7},{7,3},{8,12},{12,8},{9,1... | collective-permute-start | bytes 2359304 | tf_op jit(solution)/shard_map/ppermute | solution.py:456
  77.1 4.1 %collective-permute-start.7 = (bf16[16,64,128]{2,1,0:T(8,128)(2,1)S(1)}, bf16[16,64,128]{2,1,0:T(8,128)(2,1)S(1)}, u32[]{:S(2)}, u32[]{:S(2)}) collective-permute-start(bf16[16,64,128]{2,1,0:T(8,128)(2,1)S(1)} %forwarded.1.far), channel_id=1, source_target_pairs={{0,4},{4,0},{1,5},{5,1},{2,6},{6,2},{3,7},{7,3},{8,12},{12,8},{9,1... | collective-permute-start | bytes 786440 | tf_op jit(solution)/shard_map/ppermute | solution.py:456
  81.8 15.0 %collective-permute-start.8 = (bf16[16,64,128]{2,1,0:T(8,128)(2,1)S(1)}, bf16[16,64,128]{2,1,0:T(8,128)(2,1)S(1)}, u32[]{:S(2)}, u32[]{:S(2)}) collective-permute-start(bf16[16,64,128]{2,1,0:T(8,128)(2,1)S(1)} %get-tuple-element.45), channel_id=1, source_target_pairs={{0,64},{32,96},{64,128},{96,160},{128,192},{160,224},{192,256},{22... | collective-permute-start | bytes 786440 | tf_op jit(solution)/shard_map/ppermute | solution.py:452
  86.6 19.2 %collective-permute-start.9 = (bf16[16,64,128]{2,1,0:T(8,128)(2,1)S(1)}, bf16[16,64,128]{2,1,0:T(8,128)(2,1)S(1)}, u32[]{:S(2)}, u32[]{:S(2)}) collective-permute-start(bf16[16,64,128]{2,1,0:T(8,128)(2,1)S(1)} %get-tuple-element.45), channel_id=1, source_target_pairs={{0,448},{32,480},{64,0},{96,32},{128,64},{160,96},{192,128},{224,1... | collective-permute-start | bytes 786440 | tf_op jit(solution)/shard_map/ppermute | solution.py:452

commit v10 on v9

--- a/solution.py
+++ b/solution.py
@@ -191,19 +191,30 @@
     swap[2] = r1[...]
 
 
-def steps(q, kp, vp, picks, state):
+def steps(q, kp, vp, picks, state, at_once=1):
     top, weights, acc = state
-    for pick in picks:
-        s = lax.dot_general(q, kp[pick], (((1,), (1,)), ((), ())), preferred_element_type=F32)
-        high = jnp.max(s, axis=1, keepdims=True)
+    for start in range(0, len(picks), at_once):
+        some = picks[start : start + at_once]
+        scores = [
+            lax.dot_general(q, kp[pick], (((1,), (1,)), ((), ())), preferred_element_type=F32)
+            for pick in some
+        ]
+        high = scores[0]
+        for s in scores[1:]:
+            high = jnp.maximum(high, s)
+        high = jnp.max(high, axis=1, keepdims=True)
         new = high if top is None else jnp.maximum(top, high)
-        p = jnp.exp2((s - new) * POWER)
-        part = jnp.dot(p.astype(BF), whole(vp, pick), preferred_element_type=F32)
+        sums = part = None
+        for pick, s in zip(some, scores):
+            p = jnp.exp2((s - new) * POWER)
+            product = jnp.dot(p.astype(BF), whole(vp, pick), preferred_element_type=F32)
+            sums = p if sums is None else sums + p
+            part = product if part is None else part + product
         if top is None:
-            weights, acc = p, part
+            weights, acc = sums, part
         else:
             shrink = jnp.exp2((top - new) * POWER)
-            weights, acc = weights * shrink + p, acc * shrink + part
+            weights, acc = weights * shrink + sums, acc * shrink + part
         top = new
     return top, weights, acc
 
@@ -387,12 +398,14 @@
     def _():
         fill_shared(8, lambda f, p: whole(far, f, p), lambda f, p: whole(se, f, p), k2, v2)
 
-        @pl.loop(0, 2)
-        def _(p):
+        done = []
+        for p in range(2):
             fours, picks = pair_of(table, OTHER, AT_SHARED, p)
             state = tops[p, :, 0:1], weights[p], accs[p]
             q = asked(w, l3, r3, fours)
-            store_pair(to_other, fours, finished(steps(q, k2, v2, picks[6:9], state)))
+            done.append((fours, finished(steps(q, k2, v2, picks[6:9], state, 3))))
+        for fours, o in done:
+            store_pair(to_other, fours, o)
 
 
 def last_kernel(table, q_head, q_shared, kh, vh, k2, v2, sent_in, sent):

time: 121 us -> 119 us (0.983)
  waiting for transfers between devices: 22.2 us -> 20.6 us
    ppermute x8, waiting for transfers between devices: 22.2 us -> 20.6 us  [along_columns(): lax.ppermute(block, ('col', 'half'), [(i, (i + 2 * distance) % n) for i i...]
where the time goes in v10:
time: 119 us; the launch traced here: 118 us
  starting transfers between devices  40.6 us (34%)
  blocking collectives  36 us (30%)
  waiting for transfers between devices  20.6 us (17%)
  Pallas kernels  20.5 us (17%)
    ppermute x8, starting transfers between devices, along_columns(): lax.ppermute(block, ('col', 'half'), [(i, (i + 2 * distance) % n) for i i...  36.7 us
    all_to_all x2, blocking collectives, exchanged(): return lax.all_to_all(block, GROUP, split_axis=0, concat_axis=0, tiled=True)  36 us
    ppermute x8, waiting for transfers between devices, along_columns(): lax.ppermute(block, ('col', 'half'), [(i, (i + 2 * distance) % n) for i i...  20.6 us
    pallas_call x12, Pallas kernels, kernel(): pl.pallas_call(body, out_shape=tuple(outs), in_specs=[SMEM if i.dtype ==...  20.5 us
    ppermute x2, starting transfers between devices, swapped(): return lax.ppermute(block, 'core', [(0, 1), (1, 0)])  3.84 us
  transfers between devices with their start and end apart: 10, of which 5 were waited for; matrix products, arithmetic and copies ran while one was open for 0% of the time, Pallas kernels for 12%

profile of v10, /device:TPU:24, one launch (start us, length us, event | category | flops | bytes accessed | tf_op | source)
XLA Modules:
  0.0 117.8 jit_solution(17474762661769783163)
XLA Ops:
  0.0 3.7 %rotate.1 = (bf16[16,288,128]{2,1,0:T(8,128)(2,1)}, s32[128]{0:T(128)}) custom-call(s32[32]{0:T(128)} %order.3, s32[9,32]{1,0:T(8,128)} %bitcast.1, bf16[64,3072]{1,0:T(8,128)(2,1)} %q_hbm.1, bf16[64,3072]{1,0:T(8,128)(2,1)} %k_hbm.1, bf16[64,3072]{1,0:T(8,128)(2,1)} %v_hbm.1), custom_call_target="tpu_custom_call" | custom-call | tf_op jit(solution)/shard_map/rotate/pallas_call | solution.py:490
  3.7 23.7 %all_to_all.10.two = bf16[16,288,128]{2,1,0:T(8,128)(2,1)S(1)} all-to-all(bf16[16,288,128]{2,1,0:T(8,128)(2,1)} %get-tuple-element.29), channel_id=1, replica_groups=mesh['col'=8,'half'=2,'x'=4,'core'=2,'dp'=4] {'half','x','core'}, dimensions={0} | all-to-all | bytes 2359296 | tf_op jit(solution)/shard_map/all_to_all | solution.py:473
  27.5 0.0 copy-start
  27.5 0.0 copy-start.1
  27.5 5.2 %collective-permute-start = (bf16[16,64,128]{2,1,0:T(8,128)(2,1)S(1)}, bf16[16,64,128]{2,1,0:T(8,128)(2,1)S(1)}, u32[]{:S(2)}, u32[]{:S(2)}) collective-permute-start(bf16[16,64,128]{2,1,0:T(8,128)(2,1)S(1)} %early.1), channel_id=1, source_target_pairs={{0,64},{32,96},{64,128},{96,160},{128,192},{160,224},{192,256},{22... | collective-permute-start | bytes 786440 | tf_op jit(solution)/shard_map/ppermute | solution.py:465
  32.7 7.7 %collective-permute-start.1 = (bf16[16,64,128]{2,1,0:T(8,128)(2,1)S(1)}, bf16[16,64,128]{2,1,0:T(8,128)(2,1)S(1)}, u32[]{:S(2)}, u32[]{:S(2)}) collective-permute-start(bf16[16,64,128]{2,1,0:T(8,128)(2,1)S(1)} %early.1), channel_id=1, source_target_pairs={{0,448},{32,480},{64,0},{96,32},{128,64},{160,96},{192,128},{224,1... | collective-permute-start | bytes 786440 | tf_op jit(solution)/shard_map/ppermute | solution.py:465
  40.4 0.0 copy-done
  40.4 0.0 copy-done.1
  40.4 3.4 %middle.1 = (bf16[16,64,128]{2,1,0:T(8,128)(2,1)S(1)}, bf16[16,32,128]{2,1,0:T(8,128)(2,1)S(1)}, bf16[16,64,128]{2,1,0:T(8,128)(2,1)S(1)}, bf16[16,64,128]{2,1,0:T(8,128)(2,1)S(1)}) custom-call(s32[128]{0:T(128)S(1)} %copy-done, s32[32]{0:T(128)S(1)} %copy-done.1, bf16[16,288,128]{2,1,0:T(8,128)(2,1)S(1)} %all_to_all.10.two), custom_call_target="tpu_custom_call" | custom-call | flops 20000000000 | tf_op jit(solution)/shard_map/middle/pallas_call | solution.py:490
  43.8 1.9 %collective-permute-start.4 = (bf16[16,64,128]{2,1,0:T(8,128)(2,1)S(1)}, bf16[16,64,128]{2,1,0:T(8,128)(2,1)S(1)}, u32[]{:S(2)}, u32[]{:S(2)}) collective-permute-start(bf16[16,64,128]{2,1,0:T(8,128)(2,1)S(1)} %get-tuple-element.33), channel_id=1, source_target_pairs={{0,64},{32,96},{64,128},{96,160},{128,192},{160,224},{192,256},{22... | collective-permute-start | bytes 786440 | tf_op jit(solution)/shard_map/ppermute | solution.py:465
  45.8 6.0 %collective-permute-start.5 = (bf16[16,64,128]{2,1,0:T(8,128)(2,1)S(1)}, bf16[16,64,128]{2,1,0:T(8,128)(2,1)S(1)}, u32[]{:S(2)}, u32[]{:S(2)}) collective-permute-start(bf16[16,64,128]{2,1,0:T(8,128)(2,1)S(1)} %get-tuple-element.34), channel_id=1, source_target_pairs={{0,448},{32,480},{64,0},{96,32},{128,64},{160,96},{192,128},{224,1... | collective-permute-start | bytes 786440 | tf_op jit(solution)/shard_map/ppermute | solution.py:465
  51.8 0.0 collective-permute-done.l1
  51.8 0.0 collective-permute-done.1.r1
  51.8 0.6 late.1
  52.5 5.0 %collective-permute-start.2 = (bf16[16,64,128]{2,1,0:T(8,128)(2,1)S(1)}, bf16[16,64,128]{2,1,0:T(8,128)(2,1)S(1)}, u32[]{:S(2)}, u32[]{:S(2)}) collective-permute-start(bf16[16,64,128]{2,1,0:T(8,128)(2,1)S(1)} %get-tuple-element.30), channel_id=1, source_target_pairs={{0,64},{32,96},{64,128},{96,160},{128,192},{160,224},{192,256},{22... | collective-permute-start | bytes 786440 | tf_op jit(solution)/shard_map/ppermute | solution.py:465
  57.5 2.9 %collective-permute-start.3 = (bf16[16,64,128]{2,1,0:T(8,128)(2,1)S(1)}, bf16[16,64,128]{2,1,0:T(8,128)(2,1)S(1)}, u32[]{:S(2)}, u32[]{:S(2)}) collective-permute-start(bf16[16,64,128]{2,1,0:T(8,128)(2,1)S(1)} %get-tuple-element.31), channel_id=1, source_target_pairs={{0,448},{32,480},{64,0},{96,32},{128,64},{160,96},{192,128},{224,1... | collective-permute-start | bytes 786440 | tf_op jit(solution)/shard_map/ppermute | solution.py:465
  60.4 1.9 %collective-permute-start.6 = (bf16[3,16,64,128]{3,2,1,0:T(8,128)(2,1)S(1)}, bf16[3,16,64,128]{3,2,1,0:T(8,128)(2,1)S(1)}, u32[]{:S(2)}, u32[]{:S(2)}) collective-permute-start(bf16[3,16,64,128]{3,2,1,0:T(8,128)(2,1)S(1)} %get-tuple-element.36), channel_id=1, source_target_pairs={{0,4},{4,0},{1,5},{5,1},{2,6},{6,2},{3,7},{7,3},{8,12},{12,8},{9,1... | collective-permute-start | bytes 2359304 | tf_op jit(solution)/shard_map/ppermute | solution.py:469
  62.4 0.7 collective-permute-done.4.l3
  63.1 2.3 %collective-permute-done.5.r3 = bf16[16,64,128]{2,1,0:T(8,128)(2,1)S(1)} collective-permute-done((bf16[16,64,128]{2,1,0:T(8,128)(2,1)S(1)}, bf16[16,64,128]{2,1,0:T(8,128)(2,1)S(1)}, u32[]{:S(2)}, u32[]{:S(2)}) %collective-permute-start.5) | collective-permute-done | bytes 262176 | tf_op jit(solution)/shard_map/ppermute | solution.py:465
  65.4 4.2 %scores.1 = (bf16[12,256,128]{2,1,0:T(8,128)(2,1)S(1)}, bf16[2,9,512,256]{3,2,1,0:T(8,128)(2,1)S(1)}, f32[2,512,128]{2,1,0:T(8,128)S(1)}) custom-call(s32[128]{0:T(128)S(1)} %copy-done, bf16[16,288,128]{2,1,0:T(8,128)(2,1)S(1)} %all_to_all.10.two, bf16[16,64,128]{2,1,0:T(8,128)(2,1)S(1)} %get-tuple-element.32.q_head, ...), custom_call_target="tpu_custom_call" | custom-call | flops 20000000000 | tf_op jit(solution)/shard_map/scores/pallas_call | solution.py:490
  69.6 0.0 collective-permute-done.6.sw
  69.6 0.7 shared.1
  70.3 0.0 collective-permute-done.2.l2
  70.3 6.3 %collective-permute-done.3.r2 = bf16[16,64,128]{2,1,0:T(8,128)(2,1)S(1)} collective-permute-done((bf16[16,64,128]{2,1,0:T(8,128)(2,1)S(1)}, bf16[16,64,128]{2,1,0:T(8,128)(2,1)S(1)}, u32[]{:S(2)}, u32[]{:S(2)}) %collective-permute-start.3) | collective-permute-done | bytes 262176 | tf_op jit(solution)/shard_map/ppermute | solution.py:465
  76.6 0.6 forwarded.1.far
  77.1 1.9 %collective-permute-start.7 = (bf16[16,64,128]{2,1,0:T(8,128)(2,1)S(1)}, bf16[16,64,128]{2,1,0:T(8,128)(2,1)S(1)}, u32[]{:S(2)}, u32[]{:S(2)}) collective-permute-start(bf16[16,64,128]{2,1,0:T(8,128)(2,1)S(1)} %forwarded.1.far), channel_id=1, source_target_pairs={{0,4},{4,0},{1,5},{5,1},{2,6},{6,2},{3,7},{7,3},{8,12},{12,8},{9,1... | collective-permute-start | bytes 786440 | tf_op jit(solution)/shard_map/ppermute | solution.py:469
  79.1 2.2 %attend_first.1 = (bf16[16,96,128]{2,1,0:T(8,128)(2,1)S(1)}, bf16[16,64,128]{2,1,0:T(8,128)(2,1)S(1)}, bf16[12,4,64,128]{3,2,1,0:T(8,128)(2,1)S(1)}) custom-call(s32[128]{0:T(128)S(1)} %copy-done, bf16[16,288,128]{2,1,0:T(8,128)(2,1)S(1)} %all_to_all.10.two, bf16[16,64,128]{2,1,0:T(8,128)(2,1)S(1)} %collective-permute-done.2.l2, ...), custom_call_target="tpu_custom_call" | custom-call | flops 20000000000 | tf_op jit(solution)/shard_map/attend_first/pallas_call | solution.py:490
  81.2 0.0 collective-permute-done.7.se
  81.2 0.6 attend_edge.1
  81.8 4.8 %collective-permute-start.8 = (bf16[16,64,128]{2,1,0:T(8,128)(2,1)S(1)}, bf16[16,64,128]{2,1,0:T(8,128)(2,1)S(1)}, u32[]{:S(2)}, u32[]{:S(2)}) collective-permute-start(bf16[16,64,128]{2,1,0:T(8,128)(2,1)S(1)} %get-tuple-element.45), channel_id=1, source_target_pairs={{0,64},{32,96},{64,128},{96,160},{128,192},{160,224},{192,256},{22... | collective-permute-start | bytes 786440 | tf_op jit(solution)/shard_map/ppermute | solution.py:465
  86.6 3.1 %collective-permute-start.9 = (bf16[16,64,128]{2,1,0:T(8,128)(2,1)S(1)}, bf16[16,64,128]{2,1,0:T(8,128)(2,1)S(1)}, u32[]{:S(2)}, u32[]{:S(2)}) collective-permute-start(bf16[16,64,128]{2,1,0:T(8,128)(2,1)S(1)} %get-tuple-element.45), channel_id=1, source_target_pairs={{0,448},{32,480},{64,0},{96,32},{128,64},{160,96},{192,128},{224,1... | collective-permute-start | bytes 786440 | tf_op jit(solution)/shard_map/ppermute | solution.py:465
  89.8 3.2 %attend_last.1.sent_in = bf16[16,96,128]{2,1,0:T(8,128)(2,1)S(1)} custom-call(s32[128]{0:T(128)S(1)} %copy-done, bf16[16,64,128]{2,1,0:T(8,128)(2,1)S(1)} %get-tuple-element.32.q_head, bf16[16,32,128]{2,1,0:T(8,128)(2,1)S(1)} %get-tuple-element.46.q_shared, bf16[12,256,128]{2,1,0:T(8,128)(2,1)S(1)} %get-tuple-element.35.kh, ...), custom_call_target="tpu_custom_call", output_to_operand_aliasing={{}: (7, {})} | custom-call | tf_op jit(solution)/shard_map/attend_last/pallas_call | solution.py:490
  92.9 4.3 %collective-permute-done.8.o_left = bf16[16,64,128]{2,1,0:T(8,128)(2,1)S(1)} collective-permute-done((bf16[16,64,128]{2,1,0:T(8,128)(2,1)S(1)}, bf16[16,64,128]{2,1,0:T(8,128)(2,1)S(1)}, u32[]{:S(2)}, u32[]{:S(2)}) %collective-permute-start.8) | collective-permute-done | bytes 262176 | tf_op jit(solution)/shard_map/ppermute | solution.py:465
  97.2 7.0 %collective-permute-done.9.o_right = bf16[16,64,128]{2,1,0:T(8,128)(2,1)S(1)} collective-permute-done((bf16[16,64,128]{2,1,0:T(8,128)(2,1)S(1)}, bf16[16,64,128]{2,1,0:T(8,128)(2,1)S(1)}, u32[]{:S(2)}, u32[]{:S(2)}) %collective-permute-start.9) | collective-permute-done | bytes 262176 | tf_op jit(solution)/shard_map/ppermute | solution.py:465
  104.2 0.6 merge.1
  104.8 12.2 %all_to_all.11.in_ref = bf16[16,96,128]{2,1,0:T(8,128)(2,1)S(1)} all-to-all(bf16[16,96,128]{2,1,0:T(8,128)(2,1)S(1)} %merge.1), channel_id=1, replica_groups=mesh['col'=8,'half'=2,'x'=4,'core'=2,'dp'=4] {'half','x','core'}, dimensions={0} | all-to-all | bytes 786432 | tf_op jit(solution)/shard_map/all_to_all | solution.py:473
  117.0 0.8 unpack.1
  (1 shorter events, 0.0 us)
Async XLA Ops:
  27.5 12.9 %copy-start = (s32[128]{0:T(128)S(1)}, s32[128]{0:T(128)}, u32[]{:S(2)}) copy-start(s32[128]{0:T(128)} %get-tuple-element.28.table) | copy-start | bytes 1540
  27.5 12.9 %copy-start.1 = (s32[32]{0:T(128)S(1)}, s32[32]{0:T(128)}, u32[]{:S(2)}) copy-start(s32[32]{0:T(128)} %order.3) | copy-start | bytes 388
  27.5 24.3 %collective-permute-start = (bf16[16,64,128]{2,1,0:T(8,128)(2,1)S(1)}, bf16[16,64,128]{2,1,0:T(8,128)(2,1)S(1)}, u32[]{:S(2)}, u32[]{:S(2)}) collective-permute-start(bf16[16,64,128]{2,1,0:T(8,128)(2,1)S(1)} %early.1), channel_id=1, source_target_pairs={{0,64},{32,96},{64,128},{96,160},{128,192},{160,224},{192,256},{22... | collective-permute-start | bytes 786440 | tf_op jit(solution)/shard_map/ppermute | solution.py:465
  32.7 19.1 %collective-permute-start.1 = (bf16[16,64,128]{2,1,0:T(8,128)(2,1)S(1)}, bf16[16,64,128]{2,1,0:T(8,128)(2,1)S(1)}, u32[]{:S(2)}, u32[]{:S(2)}) collective-permute-start(bf16[16,64,128]{2,1,0:T(8,128)(2,1)S(1)} %early.1), channel_id=1, source_target_pairs={{0,448},{32,480},{64,0},{96,32},{128,64},{160,96},{192,128},{224,1... | collective-permute-start | bytes 786440 | tf_op jit(solution)/shard_map/ppermute | solution.py:465
  43.8 19.3 %collective-permute-start.4 = (bf16[16,64,128]{2,1,0:T(8,128)(2,1)S(1)}, bf16[16,64,128]{2,1,0:T(8,128)(2,1)S(1)}, u32[]{:S(2)}, u32[]{:S(2)}) collective-permute-start(bf16[16,64,128]{2,1,0:T(8,128)(2,1)S(1)} %get-tuple-element.33), channel_id=1, source_target_pairs={{0,64},{32,96},{64,128},{96,160},{128,192},{160,224},{192,256},{22... | collective-permute-start | bytes 786440 | tf_op jit(solution)/shard_map/ppermute | solution.py:465
  45.8 19.6 %collective-permute-start.5 = (bf16[16,64,128]{2,1,0:T(8,128)(2,1)S(1)}, bf16[16,64,128]{2,1,0:T(8,128)(2,1)S(1)}, u32[]{:S(2)}, u32[]{:S(2)}) collective-permute-start(bf16[16,64,128]{2,1,0:T(8,128)(2,1)S(1)} %get-tuple-element.34), channel_id=1, source_target_pairs={{0,448},{32,480},{64,0},{96,32},{128,64},{160,96},{192,128},{224,1... | collective-permute-start | bytes 786440 | tf_op jit(solution)/shard_map/ppermute | solution.py:465
  52.5 17.8 %collective-permute-start.2 = (bf16[16,64,128]{2,1,0:T(8,128)(2,1)S(1)}, bf16[16,64,128]{2,1,0:T(8,128)(2,1)S(1)}, u32[]{:S(2)}, u32[]{:S(2)}) collective-permute-start(bf16[16,64,128]{2,1,0:T(8,128)(2,1)S(1)} %get-tuple-element.30), channel_id=1, source_target_pairs={{0,64},{32,96},{64,128},{96,160},{128,192},{160,224},{192,256},{22... | collective-permute-start | bytes 786440 | tf_op jit(solution)/shard_map/ppermute | solution.py:465
  57.5 19.1 %collective-permute-start.3 = (bf16[16,64,128]{2,1,0:T(8,128)(2,1)S(1)}, bf16[16,64,128]{2,1,0:T(8,128)(2,1)S(1)}, u32[]{:S(2)}, u32[]{:S(2)}) collective-permute-start(bf16[16,64,128]{2,1,0:T(8,128)(2,1)S(1)} %get-tuple-element.31), channel_id=1, source_target_pairs={{0,448},{32,480},{64,0},{96,32},{128,64},{160,96},{192,128},{224,1... | collective-permute-start | bytes 786440 | tf_op jit(solution)/shard_map/ppermute | solution.py:465
  60.4 9.2 %collective-permute-start.6 = (bf16[3,16,64,128]{3,2,1,0:T(8,128)(2,1)S(1)}, bf16[3,16,64,128]{3,2,1,0:T(8,128)(2,1)S(1)}, u32[]{:S(2)}, u32[]{:S(2)}) collective-permute-start(bf16[3,16,64,128]{3,2,1,0:T(8,128)(2,1)S(1)} %get-tuple-element.36), channel_id=1, source_target_pairs={{0,4},{4,0},{1,5},{5,1},{2,6},{6,2},{3,7},{7,3},{8,12},{12,8},{9,1... | collective-permute-start | bytes 2359304 | tf_op jit(solution)/shard_map/ppermute | solution.py:469
  77.1 4.1 %collective-permute-start.7 = (bf16[16,64,128]{2,1,0:T(8,128)(2,1)S(1)}, bf16[16,64,128]{2,1,0:T(8,128)(2,1)S(1)}, u32[]{:S(2)}, u32[]{:S(2)}) collective-permute-start(bf16[16,64,128]{2,1,0:T(8,128)(2,1)S(1)} %forwarded.1.far), channel_id=1, source_target_pairs={{0,4},{4,0},{1,5},{5,1},{2,6},{6,2},{3,7},{7,3},{8,12},{12,8},{9,1... | collective-permute-start | bytes 786440 | tf_op jit(solution)/shard_map/ppermute | solution.py:469
  81.8 15.4 %collective-permute-start.8 = (bf16[16,64,128]{2,1,0:T(8,128)(2,1)S(1)}, bf16[16,64,128]{2,1,0:T(8,128)(2,1)S(1)}, u32[]{:S(2)}, u32[]{:S(2)}) collective-permute-start(bf16[16,64,128]{2,1,0:T(8,128)(2,1)S(1)} %get-tuple-element.45), channel_id=1, source_target_pairs={{0,64},{32,96},{64,128},{96,160},{128,192},{160,224},{192,256},{22... | collective-permute-start | bytes 786440 | tf_op jit(solution)/shard_map/ppermute | solution.py:465
  86.6 17.6 %collective-permute-start.9 = (bf16[16,64,128]{2,1,0:T(8,128)(2,1)S(1)}, bf16[16,64,128]{2,1,0:T(8,128)(2,1)S(1)}, u32[]{:S(2)}, u32[]{:S(2)}) collective-permute-start(bf16[16,64,128]{2,1,0:T(8,128)(2,1)S(1)} %get-tuple-element.45), channel_id=1, source_target_pairs={{0,448},{32,480},{64,0},{96,32},{128,64},{160,96},{192,128},{224,1... | collective-permute-start | bytes 786440 | tf_op jit(solution)/shard_map/ppermute | solution.py:465

commit v11 on v10

--- a/solution.py
+++ b/solution.py
@@ -37,19 +37,22 @@
     return rows
 
 
-def turns(tile, frame_in_tile):
-    frame = (tile // 32 * 4 + frame_in_tile).astype(F32)
+def turns(tile, frames):
     row0 = (tile // 8 % 4 * 8).astype(F32)
     col0 = (tile % 8 * 8).astype(F32)
     token = lax.broadcasted_iota(jnp.int32, (64, HD), 0)
     row = row0 + (token // 8).astype(F32)
     col = col0 + (token % 8).astype(F32)
     by_frame, by_row, by_col = frequency_rows()
-    angle = frame * by_frame + row * by_row + col * by_col
-    cosine = jnp.cos(angle)
-    sine = jnp.sin(angle)
+    angle = row * by_row + col * by_col
+    cosine, sine = jnp.cos(angle), jnp.sin(angle)
     even = lax.broadcasted_iota(jnp.int32, (64, HD), 1) % 2 == 0
-    return cosine, jnp.where(even, -sine, 0.0), jnp.where(even, 0.0, sine)
+    found = []
+    for frame in frames:
+        turn = (tile // 32 * 4 + frame).astype(F32) * by_frame
+        c, s = cosine * jnp.cos(turn), sine + jnp.sin(turn)
+        found.append((c, jnp.where(even, -s, 0.0), jnp.where(even, 0.0, s)))
+    return found
 
 
 def turned(x, factors):
@@ -105,7 +108,7 @@
         copy.start()
     w = plan(order, nb, table)
     edge = (w == 0) | (w == 7)
-    factors = turns(order[slot], frame_in_tile)
+    (factors,) = turns(order[slot], [frame_in_tile])
     outs = []
     for part in range(4):
         for which in range(3):
@@ -142,13 +145,14 @@
     edge = (w == 0) | (w == 7)
     col, core = lax.axis_index("col"), lax.axis_index("core")
 
-    @pl.loop(0, 16)
-    def _(source):
-        factors = turns(order[col * 4 + source // 4], lax.rem(source, 4))
-        held = two[source]
-        q_head[source] = turned(jnp.where(edge, held[MAIN], held[REST]), factors)
-        mine = [jnp.where(core == 0, f[0:32], f[32:64]) for f in factors]
-        q_shared[source] = turned(held[QUERY], mine)
+    @pl.loop(0, 4)
+    def _(t):
+        for frame, factors in enumerate(turns(order[col * 4 + t], range(4))):
+            source = t * 4 + frame
+            held = two[source]
+            q_head[source] = turned(jnp.where(edge, held[MAIN], held[REST]), factors)
+            mine = [jnp.where(core == 0, f[0:32], f[32:64]) for f in factors]
+            q_shared[source] = turned(held[QUERY], mine)
 
     for out, special in ((main_left, 1), (main_right, 6)):
 

time: 119 us -> 119 us (level)
  Pallas kernels: 20.5 us -> 18.9 us
  waiting for transfers between devices: 20.6 us -> 22 us
    pallas_call x12, Pallas kernels: 20.5 us -> 18.9 us  [kernel(): pl.pallas_call(body, out_shape=tuple(outs), in_specs=[SMEM if i.dtype ==...]
    ppermute x8, waiting for transfers between devices: 20.6 us -> 22 us  [along_columns(): lax.ppermute(block, ('col', 'half'), [(i, (i + 2 * distance) % n) for i i...]
  transfers between devices with their start and end apart: 10 -> 10, of which waited for: 5 -> 6; matrix products, arithmetic and copies ran while one was open for 0% -> 0% of each run, Pallas kernels for 12% -> 11%
where the time goes in v11:
time: 119 us; the launch traced here: 118 us
  starting transfers between devices  40.6 us (34%)
  blocking collectives  35.8 us (30%)
  waiting for transfers between devices  22 us (18%)
  Pallas kernels  18.9 us (16%)
    ppermute x8, starting transfers between devices, along_columns(): lax.ppermute(block, ('col', 'half'), [(i, (i + 2 * distance) % n) for i i...  36.7 us
    all_to_all x2, blocking collectives, exchanged(): return lax.all_to_all(block, GROUP, split_axis=0, concat_axis=0, tiled=True)  35.8 us
    ppermute x8, waiting for transfers between devices, along_columns(): lax.ppermute(block, ('col', 'half'), [(i, (i + 2 * distance) % n) for i i...  22 us
    pallas_call x12, Pallas kernels, kernel(): pl.pallas_call(body, out_shape=tuple(outs), in_specs=[SMEM if i.dtype ==...  18.9 us
    ppermute x2, starting transfers between devices, swapped(): return lax.ppermute(block, 'core', [(0, 1), (1, 0)])  3.84 us
  transfers between devices with their start and end apart: 10, of which 6 were waited for; matrix products, arithmetic and copies ran while one was open for 0% of the time, Pallas kernels for 11%

profile of v11, /device:TPU:24, one launch (start us, length us, event | category | flops | bytes accessed | tf_op | source)
XLA Modules:
  0.0 117.5 jit_solution(16374880681481862290)
XLA Ops:
  0.0 3.7 %rotate.1 = (bf16[16,288,128]{2,1,0:T(8,128)(2,1)}, s32[128]{0:T(128)}) custom-call(s32[32]{0:T(128)} %order.3, s32[9,32]{1,0:T(8,128)} %bitcast.1, bf16[64,3072]{1,0:T(8,128)(2,1)} %q_hbm.1, bf16[64,3072]{1,0:T(8,128)(2,1)} %k_hbm.1, bf16[64,3072]{1,0:T(8,128)(2,1)} %v_hbm.1), custom_call_target="tpu_custom_call" | custom-call | tf_op jit(solution)/shard_map/rotate/pallas_call | solution.py:494
  3.7 23.7 %all_to_all.10.two = bf16[16,288,128]{2,1,0:T(8,128)(2,1)S(1)} all-to-all(bf16[16,288,128]{2,1,0:T(8,128)(2,1)} %get-tuple-element.29), channel_id=1, replica_groups=mesh['col'=8,'half'=2,'x'=4,'core'=2,'dp'=4] {'half','x','core'}, dimensions={0} | all-to-all | bytes 2359296 | tf_op jit(solution)/shard_map/all_to_all | solution.py:477
  27.5 0.0 copy-start
  27.5 0.0 copy-start.1
  27.5 5.2 %collective-permute-start = (bf16[16,64,128]{2,1,0:T(8,128)(2,1)S(1)}, bf16[16,64,128]{2,1,0:T(8,128)(2,1)S(1)}, u32[]{:S(2)}, u32[]{:S(2)}) collective-permute-start(bf16[16,64,128]{2,1,0:T(8,128)(2,1)S(1)} %early.1), channel_id=1, source_target_pairs={{0,64},{32,96},{64,128},{96,160},{128,192},{160,224},{192,256},{22... | collective-permute-start | bytes 786440 | tf_op jit(solution)/shard_map/ppermute | solution.py:469
  32.7 7.7 %collective-permute-start.1 = (bf16[16,64,128]{2,1,0:T(8,128)(2,1)S(1)}, bf16[16,64,128]{2,1,0:T(8,128)(2,1)S(1)}, u32[]{:S(2)}, u32[]{:S(2)}) collective-permute-start(bf16[16,64,128]{2,1,0:T(8,128)(2,1)S(1)} %early.1), channel_id=1, source_target_pairs={{0,448},{32,480},{64,0},{96,32},{128,64},{160,96},{192,128},{224,1... | collective-permute-start | bytes 786440 | tf_op jit(solution)/shard_map/ppermute | solution.py:469
  40.4 0.0 copy-done
  40.4 0.0 copy-done.1
  40.4 1.9 %middle.1 = (bf16[16,64,128]{2,1,0:T(8,128)(2,1)S(1)}, bf16[16,32,128]{2,1,0:T(8,128)(2,1)S(1)}, bf16[16,64,128]{2,1,0:T(8,128)(2,1)S(1)}, bf16[16,64,128]{2,1,0:T(8,128)(2,1)S(1)}) custom-call(s32[128]{0:T(128)S(1)} %copy-done, s32[32]{0:T(128)S(1)} %copy-done.1, bf16[16,288,128]{2,1,0:T(8,128)(2,1)S(1)} %all_to_all.10.two), custom_call_target="tpu_custom_call" | custom-call | flops 20000000000 | tf_op jit(solution)/shard_map/middle/pallas_call | solution.py:494
  42.3 1.9 %collective-permute-start.4 = (bf16[16,64,128]{2,1,0:T(8,128)(2,1)S(1)}, bf16[16,64,128]{2,1,0:T(8,128)(2,1)S(1)}, u32[]{:S(2)}, u32[]{:S(2)}) collective-permute-start(bf16[16,64,128]{2,1,0:T(8,128)(2,1)S(1)} %get-tuple-element.33), channel_id=1, source_target_pairs={{0,64},{32,96},{64,128},{96,160},{128,192},{160,224},{192,256},{22... | collective-permute-start | bytes 786440 | tf_op jit(solution)/shard_map/ppermute | solution.py:469
  44.2 6.0 %collective-permute-start.5 = (bf16[16,64,128]{2,1,0:T(8,128)(2,1)S(1)}, bf16[16,64,128]{2,1,0:T(8,128)(2,1)S(1)}, u32[]{:S(2)}, u32[]{:S(2)}) collective-permute-start(bf16[16,64,128]{2,1,0:T(8,128)(2,1)S(1)} %get-tuple-element.34), channel_id=1, source_target_pairs={{0,448},{32,480},{64,0},{96,32},{128,64},{160,96},{192,128},{224,1... | collective-permute-start | bytes 786440 | tf_op jit(solution)/shard_map/ppermute | solution.py:469
  50.2 0.0 collective-permute-done.l1
  50.2 0.9 collective-permute-done.1.r1
  51.1 0.6 late.1
  51.8 5.8 %collective-permute-start.2 = (bf16[16,64,128]{2,1,0:T(8,128)(2,1)S(1)}, bf16[16,64,128]{2,1,0:T(8,128)(2,1)S(1)}, u32[]{:S(2)}, u32[]{:S(2)}) collective-permute-start(bf16[16,64,128]{2,1,0:T(8,128)(2,1)S(1)} %get-tuple-element.30), channel_id=1, source_target_pairs={{0,64},{32,96},{64,128},{96,160},{128,192},{160,224},{192,256},{22... | collective-permute-start | bytes 786440 | tf_op jit(solution)/shard_map/ppermute | solution.py:469
  57.5 2.2 %collective-permute-start.3 = (bf16[16,64,128]{2,1,0:T(8,128)(2,1)S(1)}, bf16[16,64,128]{2,1,0:T(8,128)(2,1)S(1)}, u32[]{:S(2)}, u32[]{:S(2)}) collective-permute-start(bf16[16,64,128]{2,1,0:T(8,128)(2,1)S(1)} %get-tuple-element.31), channel_id=1, source_target_pairs={{0,448},{32,480},{64,0},{96,32},{128,64},{160,96},{192,128},{224,1... | collective-permute-start | bytes 786440 | tf_op jit(solution)/shard_map/ppermute | solution.py:469
  59.7 1.9 %collective-permute-start.6 = (bf16[3,16,64,128]{3,2,1,0:T(8,128)(2,1)S(1)}, bf16[3,16,64,128]{3,2,1,0:T(8,128)(2,1)S(1)}, u32[]{:S(2)}, u32[]{:S(2)}) collective-permute-start(bf16[3,16,64,128]{3,2,1,0:T(8,128)(2,1)S(1)} %get-tuple-element.36), channel_id=1, source_target_pairs={{0,4},{4,0},{1,5},{5,1},{2,6},{6,2},{3,7},{7,3},{8,12},{12,8},{9,1... | collective-permute-start | bytes 2359304 | tf_op jit(solution)/shard_map/ppermute | solution.py:473
  61.7 1.1 collective-permute-done.4.l3
  62.8 0.0 collective-permute-done.5.r3
  62.8 4.2 %scores.1 = (bf16[12,256,128]{2,1,0:T(8,128)(2,1)S(1)}, bf16[2,9,512,256]{3,2,1,0:T(8,128)(2,1)S(1)}, f32[2,512,128]{2,1,0:T(8,128)S(1)}) custom-call(s32[128]{0:T(128)S(1)} %copy-done, bf16[16,288,128]{2,1,0:T(8,128)(2,1)S(1)} %all_to_all.10.two, bf16[16,64,128]{2,1,0:T(8,128)(2,1)S(1)} %get-tuple-element.32.q_head, ...), custom_call_target="tpu_custom_call" | custom-call | flops 20000000000 | tf_op jit(solution)/shard_map/scores/pallas_call | solution.py:494
  67.0 0.0 collective-permute-done.6.sw
  67.0 0.7 shared.1
  67.7 0.1 collective-permute-done.2.l2
  67.8 8.6 %collective-permute-done.3.r2 = bf16[16,64,128]{2,1,0:T(8,128)(2,1)S(1)} collective-permute-done((bf16[16,64,128]{2,1,0:T(8,128)(2,1)S(1)}, bf16[16,64,128]{2,1,0:T(8,128)(2,1)S(1)}, u32[]{:S(2)}, u32[]{:S(2)}) %collective-permute-start.3) | collective-permute-done | bytes 262176 | tf_op jit(solution)/shard_map/ppermute | solution.py:469
  76.4 0.6 forwarded.1.far
  76.9 1.9 %collective-permute-start.7 = (bf16[16,64,128]{2,1,0:T(8,128)(2,1)S(1)}, bf16[16,64,128]{2,1,0:T(8,128)(2,1)S(1)}, u32[]{:S(2)}, u32[]{:S(2)}) collective-permute-start(bf16[16,64,128]{2,1,0:T(8,128)(2,1)S(1)} %forwarded.1.far), channel_id=1, source_target_pairs={{0,4},{4,0},{1,5},{5,1},{2,6},{6,2},{3,7},{7,3},{8,12},{12,8},{9,1... | collective-permute-start | bytes 786440 | tf_op jit(solution)/shard_map/ppermute | solution.py:473
  78.9 2.2 %attend_first.1 = (bf16[16,96,128]{2,1,0:T(8,128)(2,1)S(1)}, bf16[16,64,128]{2,1,0:T(8,128)(2,1)S(1)}, bf16[12,4,64,128]{3,2,1,0:T(8,128)(2,1)S(1)}) custom-call(s32[128]{0:T(128)S(1)} %copy-done, bf16[16,288,128]{2,1,0:T(8,128)(2,1)S(1)} %all_to_all.10.two, bf16[16,64,128]{2,1,0:T(8,128)(2,1)S(1)} %collective-permute-done.2.l2, ...), custom_call_target="tpu_custom_call" | custom-call | flops 20000000000 | tf_op jit(solution)/shard_map/attend_first/pallas_call | solution.py:494
  81.0 0.0 collective-permute-done.7.se
  81.0 0.6 attend_edge.1
  81.6 2.5 %collective-permute-start.8 = (bf16[16,64,128]{2,1,0:T(8,128)(2,1)S(1)}, bf16[16,64,128]{2,1,0:T(8,128)(2,1)S(1)}, u32[]{:S(2)}, u32[]{:S(2)}) collective-permute-start(bf16[16,64,128]{2,1,0:T(8,128)(2,1)S(1)} %get-tuple-element.45), channel_id=1, source_target_pairs={{0,64},{32,96},{64,128},{96,160},{128,192},{160,224},{192,256},{22... | collective-permute-start | bytes 786440 | tf_op jit(solution)/shard_map/ppermute | solution.py:469
  84.1 5.4 %collective-permute-start.9 = (bf16[16,64,128]{2,1,0:T(8,128)(2,1)S(1)}, bf16[16,64,128]{2,1,0:T(8,128)(2,1)S(1)}, u32[]{:S(2)}, u32[]{:S(2)}) collective-permute-start(bf16[16,64,128]{2,1,0:T(8,128)(2,1)S(1)} %get-tuple-element.45), channel_id=1, source_target_pairs={{0,448},{32,480},{64,0},{96,32},{128,64},{160,96},{192,128},{224,1... | collective-permute-start | bytes 786440 | tf_op jit(solution)/shard_map/ppermute | solution.py:469
  89.6 3.2 %attend_last.1.sent_in = bf16[16,96,128]{2,1,0:T(8,128)(2,1)S(1)} custom-call(s32[128]{0:T(128)S(1)} %copy-done, bf16[16,64,128]{2,1,0:T(8,128)(2,1)S(1)} %get-tuple-element.32.q_head, bf16[16,32,128]{2,1,0:T(8,128)(2,1)S(1)} %get-tuple-element.46.q_shared, bf16[12,256,128]{2,1,0:T(8,128)(2,1)S(1)} %get-tuple-element.35.kh, ...), custom_call_target="tpu_custom_call", output_to_operand_aliasing={{}: (7, {})} | custom-call | tf_op jit(solution)/shard_map/attend_last/pallas_call | solution.py:494
  92.7 7.2 %collective-permute-done.8.o_left = bf16[16,64,128]{2,1,0:T(8,128)(2,1)S(1)} collective-permute-done((bf16[16,64,128]{2,1,0:T(8,128)(2,1)S(1)}, bf16[16,64,128]{2,1,0:T(8,128)(2,1)S(1)}, u32[]{:S(2)}, u32[]{:S(2)}) %collective-permute-start.8) | collective-permute-done | bytes 262176 | tf_op jit(solution)/shard_map/ppermute | solution.py:469
  100.0 4.0 %collective-permute-done.9.o_right = bf16[16,64,128]{2,1,0:T(8,128)(2,1)S(1)} collective-permute-done((bf16[16,64,128]{2,1,0:T(8,128)(2,1)S(1)}, bf16[16,64,128]{2,1,0:T(8,128)(2,1)S(1)}, u32[]{:S(2)}, u32[]{:S(2)}) %collective-permute-start.9) | collective-permute-done | bytes 262176 | tf_op jit(solution)/shard_map/ppermute | solution.py:469
  104.0 0.6 merge.1
  104.6 12.1 %all_to_all.11.in_ref = bf16[16,96,128]{2,1,0:T(8,128)(2,1)S(1)} all-to-all(bf16[16,96,128]{2,1,0:T(8,128)(2,1)S(1)} %merge.1), channel_id=1, replica_groups=mesh['col'=8,'half'=2,'x'=4,'core'=2,'dp'=4] {'half','x','core'}, dimensions={0} | all-to-all | bytes 786432 | tf_op jit(solution)/shard_map/all_to_all | solution.py:477
  116.7 0.8 unpack.1
  (1 shorter events, 0.0 us)
Async XLA Ops:
  27.5 12.9 %copy-start = (s32[128]{0:T(128)S(1)}, s32[128]{0:T(128)}, u32[]{:S(2)}) copy-start(s32[128]{0:T(128)} %get-tuple-element.28.table) | copy-start | bytes 1540
  27.5 12.9 %copy-start.1 = (s32[32]{0:T(128)S(1)}, s32[32]{0:T(128)}, u32[]{:S(2)}) copy-start(s32[32]{0:T(128)} %order.3) | copy-start | bytes 388
  27.5 22.7 %collective-permute-start = (bf16[16,64,128]{2,1,0:T(8,128)(2,1)S(1)}, bf16[16,64,128]{2,1,0:T(8,128)(2,1)S(1)}, u32[]{:S(2)}, u32[]{:S(2)}) collective-permute-start(bf16[16,64,128]{2,1,0:T(8,128)(2,1)S(1)} %early.1), channel_id=1, source_target_pairs={{0,64},{32,96},{64,128},{96,160},{128,192},{160,224},{192,256},{22... | collective-permute-start | bytes 786440 | tf_op jit(solution)/shard_map/ppermute | solution.py:469
  32.7 18.4 %collective-permute-start.1 = (bf16[16,64,128]{2,1,0:T(8,128)(2,1)S(1)}, bf16[16,64,128]{2,1,0:T(8,128)(2,1)S(1)}, u32[]{:S(2)}, u32[]{:S(2)}) collective-permute-start(bf16[16,64,128]{2,1,0:T(8,128)(2,1)S(1)} %early.1), channel_id=1, source_target_pairs={{0,448},{32,480},{64,0},{96,32},{128,64},{160,96},{192,128},{224,1... | collective-permute-start | bytes 786440 | tf_op jit(solution)/shard_map/ppermute | solution.py:469
  42.3 20.5 %collective-permute-start.4 = (bf16[16,64,128]{2,1,0:T(8,128)(2,1)S(1)}, bf16[16,64,128]{2,1,0:T(8,128)(2,1)S(1)}, u32[]{:S(2)}, u32[]{:S(2)}) collective-permute-start(bf16[16,64,128]{2,1,0:T(8,128)(2,1)S(1)} %get-tuple-element.33), channel_id=1, source_target_pairs={{0,64},{32,96},{64,128},{96,160},{128,192},{160,224},{192,256},{22... | collective-permute-start | bytes 786440 | tf_op jit(solution)/shard_map/ppermute | solution.py:469
  44.2 18.6 %collective-permute-start.5 = (bf16[16,64,128]{2,1,0:T(8,128)(2,1)S(1)}, bf16[16,64,128]{2,1,0:T(8,128)(2,1)S(1)}, u32[]{:S(2)}, u32[]{:S(2)}) collective-permute-start(bf16[16,64,128]{2,1,0:T(8,128)(2,1)S(1)} %get-tuple-element.34), channel_id=1, source_target_pairs={{0,448},{32,480},{64,0},{96,32},{128,64},{160,96},{192,128},{224,1... | collective-permute-start | bytes 786440 | tf_op jit(solution)/shard_map/ppermute | solution.py:469
  51.8 16.0 %collective-permute-start.2 = (bf16[16,64,128]{2,1,0:T(8,128)(2,1)S(1)}, bf16[16,64,128]{2,1,0:T(8,128)(2,1)S(1)}, u32[]{:S(2)}, u32[]{:S(2)}) collective-permute-start(bf16[16,64,128]{2,1,0:T(8,128)(2,1)S(1)} %get-tuple-element.30), channel_id=1, source_target_pairs={{0,64},{32,96},{64,128},{96,160},{128,192},{160,224},{192,256},{22... | collective-permute-start | bytes 786440 | tf_op jit(solution)/shard_map/ppermute | solution.py:469
  57.5 18.8 %collective-permute-start.3 = (bf16[16,64,128]{2,1,0:T(8,128)(2,1)S(1)}, bf16[16,64,128]{2,1,0:T(8,128)(2,1)S(1)}, u32[]{:S(2)}, u32[]{:S(2)}) collective-permute-start(bf16[16,64,128]{2,1,0:T(8,128)(2,1)S(1)} %get-tuple-element.31), channel_id=1, source_target_pairs={{0,448},{32,480},{64,0},{96,32},{128,64},{160,96},{192,128},{224,1... | collective-permute-start | bytes 786440 | tf_op jit(solution)/shard_map/ppermute | solution.py:469
  59.7 7.3 %collective-permute-start.6 = (bf16[3,16,64,128]{3,2,1,0:T(8,128)(2,1)S(1)}, bf16[3,16,64,128]{3,2,1,0:T(8,128)(2,1)S(1)}, u32[]{:S(2)}, u32[]{:S(2)}) collective-permute-start(bf16[3,16,64,128]{3,2,1,0:T(8,128)(2,1)S(1)} %get-tuple-element.36), channel_id=1, source_target_pairs={{0,4},{4,0},{1,5},{5,1},{2,6},{6,2},{3,7},{7,3},{8,12},{12,8},{9,1... | collective-permute-start | bytes 2359304 | tf_op jit(solution)/shard_map/ppermute | solution.py:473
  76.9 4.1 %collective-permute-start.7 = (bf16[16,64,128]{2,1,0:T(8,128)(2,1)S(1)}, bf16[16,64,128]{2,1,0:T(8,128)(2,1)S(1)}, u32[]{:S(2)}, u32[]{:S(2)}) collective-permute-start(bf16[16,64,128]{2,1,0:T(8,128)(2,1)S(1)} %forwarded.1.far), channel_id=1, source_target_pairs={{0,4},{4,0},{1,5},{5,1},{2,6},{6,2},{3,7},{7,3},{8,12},{12,8},{9,1... | collective-permute-start | bytes 786440 | tf_op jit(solution)/shard_map/ppermute | solution.py:473
  81.6 18.4 %collective-permute-start.8 = (bf16[16,64,128]{2,1,0:T(8,128)(2,1)S(1)}, bf16[16,64,128]{2,1,0:T(8,128)(2,1)S(1)}, u32[]{:S(2)}, u32[]{:S(2)}) collective-permute-start(bf16[16,64,128]{2,1,0:T(8,128)(2,1)S(1)} %get-tuple-element.45), channel_id=1, source_target_pairs={{0,64},{32,96},{64,128},{96,160},{128,192},{160,224},{192,256},{22... | collective-permute-start | bytes 786440 | tf_op jit(solution)/shard_map/ppermute | solution.py:469
  84.1 19.9 %collective-permute-start.9 = (bf16[16,64,128]{2,1,0:T(8,128)(2,1)S(1)}, bf16[16,64,128]{2,1,0:T(8,128)(2,1)S(1)}, u32[]{:S(2)}, u32[]{:S(2)}) collective-permute-start(bf16[16,64,128]{2,1,0:T(8,128)(2,1)S(1)} %get-tuple-element.45), channel_id=1, source_target_pairs={{0,448},{32,480},{64,0},{96,32},{128,64},{160,96},{192,128},{224,1... | collective-permute-start | bytes 786440 | tf_op jit(solution)/shard_map/ppermute | solution.py:469
